TPU v7x, 32 devices: a whole 2x2x4 slice. The times are simulated.
32 devices in a mesh: dp: 8 (over y, x, core), seq: 4 (over z).
Axes of the slice: x: 2, y: 2, z: 4, core: 2. Of those that a mesh axis runs over, the one named last changes fastest.
Arguments:
- tokens: bfloat16 [8, 1024, 5120], P('dp', 'seq'), may hold values from -6 to 6
- queries: bfloat16 [8, 1024, 2560], P('dp', 'seq'), may hold values from -400 to 400
- cotangent: bfloat16 [8, 1024, 2560], P('dp', 'seq'), may hold values from -6 to 6
- kv_weight: bfloat16 [5120, 1024], P('dp'), may hold values from -0.078125 to 0.078125
- active: int32 [8, 4], P('dp'), may hold values from 0 to 7, as said below
Outputs:
- query_grads: bfloat16 [8, 1024, 2560], P('dp', 'seq')
- token_grads: bfloat16 [8, 1024, 5120], P('dp', 'seq')
- weight_grad: float32 [5120, 1024], P('dp', 'seq')
Inputs may be any that keep to these rules, and one draw needn't show every extreme that they name: active[p] lists 4 different blocks of sequence p in increasing order; blocks 0 and 7 are always among them.
All inputs are finite; a program needn't handle non-finite values.
Results may differ from a plain program's by a relative error of at most 0.019.
The roundings to bfloat16 on the way count: a program that leaves them out, or rounds other values in their place, can miss the bound.
Values may be sent and summed in bfloat16 or wider, within the bound.
No kernel may reach another device: no remote copies, remote signals or barrier semaphores. Data moves between devices by JAX's collectives and lax.ppermute only.
A program may use at most 128 MiB of HBM per device.

v0:
```python
import math

import jax
import jax.numpy as jnp
from jax import lax
from jax.sharding import PartitionSpec as P

HEAD_SIZE = 128
BLK = 128


def body(tokens, queries, cotangent, kv_weight, active):
    seq_count = lax.axis_size("seq")
    seq_rank = lax.axis_index("seq")
    tok_dev = tokens.shape[1]
    qwidth = queries.shape[2]
    kvwidth = kv_weight.shape[1]
    row_count = BLK // seq_count
    blocks_dev = tok_dev // BLK
    block_total = blocks_dev * seq_count
    act_total = active.shape[1]
    kv_heads = kvwidth // (2 * HEAD_SIZE)
    head_group = qwidth // (HEAD_SIZE * kv_heads)
    scale = 1.0 / math.sqrt(HEAD_SIZE)
    weight_full = lax.all_gather(kv_weight, "dp", axis=0, tiled=True)
    x_local = tokens[0]
    keyval = jnp.dot(x_local, weight_full, preferred_element_type=jnp.float32).astype(jnp.bfloat16)

    def spread(values_in):
        return values_in.reshape(blocks_dev, seq_count, row_count, values_in.shape[-1])

    q_in, g_in, kv_in = (
        lax.all_to_all(spread(queries[0]), "seq", split_axis=1, concat_axis=0, tiled=True),
        lax.all_to_all(spread(cotangent[0]), "seq", split_axis=1, concat_axis=0, tiled=True),
        lax.all_to_all(spread(keyval), "seq", split_axis=1, concat_axis=0, tiled=True),
    )
    block_ids = active[0]
    active_query = q_in.reshape(block_total, row_count, qwidth)[block_ids]
    active_gradient = g_in.reshape(block_total, row_count, qwidth)[block_ids]
    kv_act = kv_in.reshape(block_total, row_count, kvwidth)[block_ids]
    kv_all = lax.all_gather(kv_act, "seq", axis=1, tiled=True)
    query_rows = act_total * row_count
    key_count = act_total * BLK
    kv_flat = kv_all.reshape(key_count, kvwidth)
    key_matrix = kv_flat[:, : kv_heads * HEAD_SIZE].reshape(key_count, kv_heads, HEAD_SIZE)
    value_matrix = kv_flat[:, kv_heads * HEAD_SIZE :].reshape(key_count, kv_heads, HEAD_SIZE)
    q_heads = active_query.reshape(query_rows, kv_heads, head_group, HEAD_SIZE)
    g_heads = active_gradient.reshape(query_rows, kv_heads, head_group, HEAD_SIZE)
    scores = (
        jnp.einsum("mkgd,nkd->kgmn", q_heads, key_matrix, preferred_element_type=jnp.float32)
        * scale
    )
    query_pos = (
        jnp.arange(act_total, dtype=jnp.int32)[:, None] * BLK
        + seq_rank * row_count
        + jnp.arange(row_count, dtype=jnp.int32)[None, :]
    ).reshape(query_rows)
    causal = jnp.arange(key_count, dtype=jnp.int32)[None, :] <= query_pos[:, None]
    scores = jnp.where(causal, scores, -1e30)
    row_max = jnp.max(scores, axis=-1, keepdims=True)
    exponent = jnp.exp(scores - row_max)
    probs = exponent / jnp.sum(exponent, axis=-1, keepdims=True)
    probs_low = probs.astype(jnp.bfloat16)
    attended = jnp.einsum(
        "kgmn,nkd->mkgd", probs_low, value_matrix, preferred_element_type=jnp.float32
    )
    row_delta = jnp.einsum("mkgd,mkgd->kgm", g_heads.astype(jnp.float32), attended)
    dprobs = jnp.einsum("mkgd,nkd->kgmn", g_heads, value_matrix, preferred_element_type=jnp.float32)
    dscores = (probs * (dprobs - row_delta[..., None]) * scale).astype(jnp.bfloat16)
    query_grad = jnp.einsum(
        "kgmn,nkd->mkgd", dscores, key_matrix, preferred_element_type=jnp.float32
    ).astype(jnp.bfloat16)
    query_grad = query_grad.reshape(act_total, row_count, qwidth)
    key_gradient = jnp.einsum(
        "kgmn,mkgd->nkd", dscores, q_heads, preferred_element_type=jnp.float32
    )
    value_gradient = jnp.einsum(
        "kgmn,mkgd->nkd", probs_low, g_heads, preferred_element_type=jnp.float32
    )
    kv_terms = jnp.concatenate(
        [
            key_gradient.reshape(key_count, kv_heads * HEAD_SIZE),
            value_gradient.reshape(key_count, kv_heads * HEAD_SIZE),
        ],
        axis=1,
    )
    kv_terms = kv_terms.reshape(act_total, BLK, kvwidth)
    kv_mine = lax.psum_scatter(kv_terms, "seq", scatter_dimension=1, tiled=True).astype(
        jnp.bfloat16
    )

    def padded(values_in):
        width_here = values_in.shape[-1]
        placed = (
            jnp.zeros((block_total, row_count, width_here), jnp.bfloat16)
            .at[block_ids]
            .set(values_in)
        )
        return placed.reshape(seq_count, blocks_dev, 1, row_count, width_here)

    query_back, kv_back = (
        lax.all_to_all(padded(query_grad), "seq", split_axis=0, concat_axis=2, tiled=True),
        lax.all_to_all(padded(kv_mine), "seq", split_axis=0, concat_axis=2, tiled=True),
    )
    query_back = query_back.reshape(tok_dev, qwidth)
    kv_back = kv_back.reshape(tok_dev, kvwidth)
    token_grad = lax.dot_general(
        kv_back, weight_full, (((1,), (1,)), ((), ())), preferred_element_type=jnp.float32
    ).astype(jnp.bfloat16)
    partial_value = lax.dot_general(
        x_local, kv_back, (((0,), (0,)), ((), ())), preferred_element_type=jnp.float32
    )
    part_sum = lax.psum_scatter(
        partial_value.astype(jnp.bfloat16), "dp", scatter_dimension=0, tiled=True
    ).astype(jnp.float32)
    weight_part = lax.psum_scatter(part_sum, "seq", scatter_dimension=1, tiled=True)
    return (query_back[None], token_grad[None], weight_part)


def solution(mesh):
    in_specs = (
        P("dp", "seq", None),
        P("dp", "seq", None),
        P("dp", "seq", None),
        P("dp", None),
        P("dp", None),
    )
    out_specs = (P("dp", "seq", None), P("dp", "seq", None), P("dp", "seq"))
    return jax.shard_map(body, mesh=mesh, in_specs=in_specs, out_specs=out_specs, check_vma=False)
```

profile of v0, /device:TPU:8, one launch (start us, length us, event | category | flops | bytes accessed | tf_op | source)
XLA Modules:
  0.0 462.1 jit_solution(7797930070945867866)
XLA Ops:
  7.9 2.5 copy.59
  10.4 5.3 %all-to-all-start.2 = ((bf16[2,4,32,2560]{3,2,0,1:T(8,128)(2,1)}), bf16[2,4,32,2560]{3,2,0,1:T(8,128)(2,1)}, u32[]{:S(2)}, u32[]{:S(2)}) async-start(bf16[2,4,32,2560]{3,2,0,1:T(8,128)(2,1)} %copy.59), calls=%async_computation.2 | async-start | bytes 2621440 | tf_op jit(solution)/shard_map/all_to_all | solution.py:34
  15.7 58.6 %all-gather.4.cloned.1.call-done = bf16[5120,1024]{1,0:T(8,128)(2,1)} async-done(((bf16[640,1024]{1,0:T(8,128)(2,1)}), bf16[5120,1024]{1,0:T(8,128)(2,1)}) %all-gather.4.cloned.1.call-update) | async-done | bytes 10485776 | tf_op jit(solution)/shard_map/all_gather | solution.py:25
  74.4 6.8 %fusion.14 = bf16[256,1024]{1,0:T(8,128)(2,1)S(1)} fusion(bf16[5120,1024]{1,0:T(8,128)(2,1)} %all-gather.4.cloned.1.call-done, bf16[1,256,5120]{2,1,0:T(8,128)(2,1)S(1)} %copy-done), kind=kOutput, calls=%fused_computation.30 | convolution fusion | flops 2684616704 | bytes 13631488 | tf_op jit(solution)/shard_map/dot_general | solution.py:27
  81.2 0.8 copy.53
  82.0 5.1 %all-to-all-start = ((bf16[2,4,32,1024]{3,2,0,1:T(8,128)(2,1)}), bf16[2,4,32,1024]{3,2,0,1:T(8,128)(2,1)S(1)}, u32[]{:S(2)}, u32[]{:S(2)}) async-start(bf16[2,4,32,1024]{3,2,0,1:T(8,128)(2,1)} %copy.53), calls=%async_computation | async-start | bytes 1048576 | tf_op jit(solution)/shard_map/all_to_all | solution.py:35
  87.2 2.5 copy.55
  89.6 9.2 %all-to-all-done = bf16[2,4,32,1024]{3,2,0,1:T(8,128)(2,1)S(1)} async-done(((bf16[2,4,32,1024]{3,2,0,1:T(8,128)(2,1)}), bf16[2,4,32,1024]{3,2,0,1:T(8,128)(2,1)S(1)}, u32[]{:S(2)}, u32[]{:S(2)}) %all-to-all-start) | async-done | bytes 524320 | tf_op jit(solution)/shard_map/all_to_all | solution.py:35
  98.9 7.5 %all-to-all-start.1 = ((bf16[2,4,32,2560]{3,2,0,1:T(8,128)(2,1)}), bf16[2,4,32,2560]{3,2,0,1:T(8,128)(2,1)}, u32[]{:S(2)}, u32[]{:S(2)}) async-start(bf16[2,4,32,2560]{3,2,0,1:T(8,128)(2,1)} %copy.55), calls=%async_computation.1 | async-start | bytes 2621440 | tf_op jit(solution)/shard_map/all_to_all | solution.py:33
  106.4 1.3 gather_fusion
  108.2 1.9 gather_fusion.2
  110.1 1.7 reshape.117
  111.8 1.7 copy.69
  113.5 2.8 bitcast_convert_fusion
  116.4 2.7 copy.85
  119.1 31.8 %all-to-all-done.1 = bf16[2,4,32,2560]{3,2,0,1:T(8,128)(2,1)} async-done(((bf16[2,4,32,2560]{3,2,0,1:T(8,128)(2,1)}), bf16[2,4,32,2560]{3,2,0,1:T(8,128)(2,1)}, u32[]{:S(2)}, u32[]{:S(2)}) %all-to-all-start.1) | async-done | bytes 1310752 | tf_op jit(solution)/shard_map/all_to_all | solution.py:33
  150.9 2.7 gather_fusion.1
  153.7 2.6 reshape.114
  156.2 2.4 copy.67
  158.6 2.2 fusion.24
  160.8 2.1 copy.98
  162.9 2.0 copy.99
  164.9 5.4 %fusion.25 = (f32[4,5,128]{2,1,0:T(8,128)S(1)}, f32[4,5,128,512]{2,3,1,0:T(8,128)}) fusion(pred[128,512]{0,1:T(8,128)(4,1)S(1)} %iota_compare_fusion, bf16[512,4,128,1]{0,2,3,1:T(8,128)(2,1)} %bitcast.136, bf16[128,4,5,128]{0,3,2,1:T(8,128)(2,1)} %copy.67), kind=kOutput, calls=%fused_computation.44 | convolution fusion | flops 340787712 | bytes 6498304 | tf_op jit(solution)/shard_map/sub | solution.py:61
  170.4 3.3 fusion.12
  173.7 1.9 convolution_bitcast_fusion.1
  176.4 2.8 fusion.4
  179.2 2.6 concatenate.9
  181.8 2.6 copy.72
  184.4 3.7 convolution_bitcast_fusion.2
  188.0 2.6 concatenate.8
  190.6 2.5 copy.71
  193.1 3.1 pad_maximum_fusion
  196.3 42.7 %reduce-scatter.6.cloned.1.call-done = f32[4,32,1024]{2,1,0:T(8,128)} async-done(((f32[4,128,1024]{2,1,0:T(8,128)}), f32[4,32,1024]{2,1,0:T(8,128)}) %reduce-scatter.6.cloned.1.call-update) | async-done | bytes 524304 | tf_op jit(solution)/shard_map/reduce_scatter | solution.py:88
  239.0 1.1 convert_element_type.36
  240.8 18.3 %all_to_all.75 = bf16[4,2,1,32,1024]{4,3,1,2,0:T(8,128)(2,1)S(1)} all-to-all(bf16[4,2,1,32,1024]{4,3,1,2,0:T(8,128)(2,1)S(1)} %bitcast.133), channel_id=1, replica_groups=mesh['dp'=8,'seq'=4] {'seq'}, dimensions={0} | all-to-all | bytes 1048576 | tf_op jit(solution)/shard_map/all_to_all | solution.py:103
  259.1 0.8 copy-done.6
  259.9 5.5 %convert_bitcast_fusion = bf16[5120,1024]{0,1:T(8,128)(2,1)} fusion(bf16[256,1024]{1,0:T(8,128)(2,1)S(1)} %bitcast.138, bf16[1,256,5120]{2,1,0:T(8,128)(2,1)S(1)} %copy-done), kind=kOutput, calls=%fused_computation.6 | convolution fusion | flops 2689597440 | bytes 13631488 | tf_op jit(solution)/shard_map/dot_general | solution.py:110
  265.4 14.4 %copy.96 = bf16[5120,1024]{1,0:T(8,128)(2,1)} copy(bf16[5120,1024]{0,1:T(8,128)(2,1)} %convert_bitcast_fusion) | data formatting | bytes 20971520
  279.9 82.0 %reduce-scatter.10.cloned.1.call-done = bf16[640,1024]{1,0:T(8,128)(2,1)} async-done(((bf16[5120,1024]{1,0:T(8,128)(2,1)}), bf16[640,1024]{1,0:T(8,128)(2,1)}) %reduce-scatter.10.cloned.1.call-update) | async-done | bytes 1310736
  361.9 2.4 copy.97
  364.3 3.2 convert_element_type.40
  367.6 1.6 fusion.18
  369.2 0.9 copy.64
  371.0 0.7 scatter_fusion
  371.7 68.0 %all_to_all.76 = bf16[4,2,1,32,2560]{4,3,1,2,0:T(8,128)(2,1)S(1)} all-to-all(bf16[4,2,1,32,2560]{4,3,1,2,0:T(8,128)(2,1)S(1)} %bitcast.130), channel_id=1, replica_groups=mesh['dp'=8,'seq'=4] {'seq'}, dimensions={0} | all-to-all | bytes 2621440 | tf_op jit(solution)/shard_map/all_to_all | solution.py:102
  439.8 1.1 copy.66
  440.9 12.5 %fusion.1 = bf16[1,256,5120]{2,1,0:T(8,128)(2,1)} fusion(bf16[256,1024]{1,0:T(8,128)(2,1)S(1)} %bitcast.139, bf16[5120,1024]{1,0:T(8,128)(2,1)} %all-gather.4.cloned.1.call-done), kind=kOutput, calls=%fused_computation.8 | convolution fusion | flops 2685665280 | bytes 13631488 | tf_op jit(solution)/shard_map/dot_general | solution.py:107
  453.4 2.2 copy.75
  (47 shorter events, 3.6 us)
Async XLA Ops:
  7.2 67.2 %copy-start = (bf16[1,256,5120]{2,1,0:T(8,128)(2,1)S(1)}, bf16[1,256,5120]{2,1,0:T(8,128)(2,1)}, u32[]{:S(2)}) copy-start(bf16[1,256,5120]{2,1,0:T(8,128)(2,1)} %param.5) | copy-start | bytes 7864324
  7.2 67.2 %all-gather.4.cloned.1.call-start = ((), (), s32[]{:S(2)}) async-start(), calls=%async_computation.8 | async-start | bytes 11796480 | tf_op jit(solution)/shard_map/all_gather | solution.py:25
  10.4 71.6 %all-to-all-start.2 = ((bf16[2,4,32,2560]{3,2,0,1:T(8,128)(2,1)}), bf16[2,4,32,2560]{3,2,0,1:T(8,128)(2,1)}, u32[]{:S(2)}, u32[]{:S(2)}) async-start(bf16[2,4,32,2560]{3,2,0,1:T(8,128)(2,1)} %copy.59), calls=%async_computation.2 | async-start | bytes 2621440 | tf_op jit(solution)/shard_map/all_to_all | solution.py:34
  82.0 16.8 %all-to-all-start = ((bf16[2,4,32,1024]{3,2,0,1:T(8,128)(2,1)}), bf16[2,4,32,1024]{3,2,0,1:T(8,128)(2,1)S(1)}, u32[]{:S(2)}, u32[]{:S(2)}) async-start(bf16[2,4,32,1024]{3,2,0,1:T(8,128)(2,1)} %copy.53), calls=%async_computation | async-start | bytes 1048576 | tf_op jit(solution)/shard_map/all_to_all | solution.py:35
  87.2 19.2 %copy-start.8 = (s32[1,4]{1,0:T(1,128)S(1)}, s32[1,4]{1,0:T(1,128)}, u32[]{:S(2)}) copy-start(s32[1,4]{1,0:T(1,128)} %param.9) | copy-start | bytes 52
  98.9 52.0 %all-to-all-start.1 = ((bf16[2,4,32,2560]{3,2,0,1:T(8,128)(2,1)}), bf16[2,4,32,2560]{3,2,0,1:T(8,128)(2,1)}, u32[]{:S(2)}, u32[]{:S(2)}) async-start(bf16[2,4,32,2560]{3,2,0,1:T(8,128)(2,1)} %copy.55), calls=%async_computation.1 | async-start | bytes 2621440 | tf_op jit(solution)/shard_map/all_to_all | solution.py:33
  106.4 52.2 %all-gather.6.cloned.1.call-start = ((), (), s32[]{:S(2)}) async-start(), calls=%async_computation.11 | async-start | bytes 1310720 | tf_op jit(solution)/shard_map/all_gather | solution.py:41
  107.7 131.3 %reduce-scatter.6.cloned.1.call-start = ((), (), s32[]{:S(2)}) async-start(), calls=%async_computation.9 | async-start | bytes 2621440 | tf_op jit(solution)/shard_map/reduce_scatter | solution.py:88
  170.4 6.0 %slice-start = ((s8[5242880]{0:T(1024)(128)(4,1)}), s8[4194304]{0:T(1024)(128)(4,1)S(1)}, s32[]{:S(2)}) async-start(s8[5242880]{0:T(1024)(128)(4,1)} %bitcast.131), calls=%async_computation.13 | async-start | bytes 8388608
  173.7 2.0 copy-start.3
  173.7 2.0 copy-start.5
  173.7 2.6 slice-start.1
  179.2 5.2 %copy-start.4 = (bf16[128,4,5,128]{0,3,2,1:T(8,128)(2,1)S(1)}, bf16[128,4,5,128]{0,3,2,1:T(8,128)(2,1)}, u32[]{:S(2)}) copy-start(bf16[128,4,5,128]{0,3,2,1:T(8,128)(2,1)} %copy.67) | copy-start | bytes 1966084
  196.2 165.7 %reduce-scatter.10.cloned.1.call-start = ((), (), s32[]{:S(2)}) async-start(), calls=%async_computation.12 | async-start | bytes 11796480
  259.1 0.8 copy-start.6
  279.9 173.6 %reduce-scatter.8.cloned.1.call-start = ((), (), s32[]{:S(2)}) async-start(), calls=%async_computation.10 | async-start | bytes 3276800 | tf_op jit(solution)/shard_map/reduce_scatter | solution.py:116
  364.3 3.2 copy-start.2
  371.7 69.2 %copy-start.7 = (bf16[4,2,1,32,1024]{4,3,0,1,2:T(8,128)(2,1)S(1)}, bf16[4,2,1,32,1024]{4,3,0,1,2:T(8,128)(2,1)}, u32[]{:S(2)}) copy-start(bf16[4,2,1,32,1024]{4,3,0,1,2:T(8,128)(2,1)} %copy-done.6) | copy-start | bytes 1572868
  440.9 14.7 %copy-start.1 = (bf16[1,256,5120]{2,1,0:T(8,128)(2,1)S(1)}, bf16[1,256,5120]{2,1,0:T(8,128)(2,1)}, u32[]{:S(2)}) copy-start(bf16[1,256,5120]{2,1,0:T(8,128)(2,1)} %param.5) | copy-start | bytes 7864324
Sparse Core Ops, SparseCore 0:
  9.9 64.4 all-gather.3
  108.8 43.2 all-gather.5
  196.4 42.5 reduce-scatter.5
  280.0 81.8 reduce-scatter.9
  367.7 79.3 reduce-scatter.7
where the time goes:
time: 467 us; the launch traced here: 462 us
  waiting for transfers between devices  225 us (48%)
  blocking collectives  86.4 us (19%)
  local copies, waits for them, and re-layouts  63.8 us (14%)
  matrix products  41 us (9%)
  starting transfers between devices  18.3 us (4%)
  between operations  14 us (3%)
  other arithmetic  13.6 us (3%)
    unnamed x6, waiting for transfers between devices  82.8 us
    all_to_all x1, blocking collectives, body(): lax.all_to_all(padded(query_grad), 'seq', split_axis=0, concat_axis=2, ti...  68 us
    all_gather x1, waiting for transfers between devices, body(): weight_full = lax.all_gather(kv_weight, 'dp', axis=0, tiled=True)  58.6 us
    reduce_scatter x1, waiting for transfers between devices, body(): lax.psum_scatter(kv_terms, 'seq', scatter_dimension=1, tiled=True)  42.7 us
    all_to_all x1, waiting for transfers between devices, body(): lax.all_to_all(spread(queries[0]), 'seq', split_axis=1, concat_axis=0, ti...  31.8 us
    unnamed x28, local copies, waits for them, and re-layouts  26.7 us
    all_to_all x1, blocking collectives, body(): lax.all_to_all(padded(kv_mine), 'seq', split_axis=0, concat_axis=2, tiled...  18.3 us
    dot_general x1, matrix products, body(): lax.dot_general(kv_back, weight_full, (((1,), (1,)), ((), ())), preferred...  12.5 us
  transfers between devices with their start and end apart: 8, of which 5 were waited for; matrix products, arithmetic and copies ran while one was open for 11% of the time, Pallas kernels for 0%

commit v1 on v0

v1 whole, which is shorter than its diff:
```python
import functools
import math

import jax
import jax.numpy as jnp
from jax import lax
from jax.experimental import pallas as pl
from jax.experimental.pallas import tpu as pltpu
from jax.sharding import PartitionSpec as P

HEAD_SIZE = 128
BLK = 128
CHUNKS = 2
VMEM_BYTES = 48 * 1024 * 1024
MASKED = -1e30


def params():
    return pltpu.CompilerParams(vmem_limit_bytes=VMEM_BYTES)


def vmem():
    return pl.BlockSpec(memory_space=pltpu.VMEM)


def smem():
    return pl.BlockSpec(memory_space=pltpu.SMEM)


def dot(left, right, left_dim, right_dim):
    return lax.dot_general(
        left, right, (((left_dim,), (right_dim,)), ((), ())), preferred_element_type=jnp.float32
    )


def exchange(value, axis, mask):
    count = lax.axis_size(axis)
    return lax.ppermute(value, axis, [(i, i ^ mask) for i in range(count)])


def moved(value, axis, step):
    count = lax.axis_size(axis)
    pairs = [(i, i + step) for i in range(count) if 0 <= i + step < count]
    return lax.ppermute(value, axis, pairs)


def half(piece, side):
    if len(piece) == 2:
        return piece[side]
    width = piece[0].shape[1] // 2
    return piece[0][:, side * width : (side + 1) * width]


def gather_pieces(own):
    count = lax.axis_size("dp")
    pieces = {0: (own,)}
    for mask in sorted(range(2, count, 2), key=lambda m: (m.bit_count(), m)):
        low, high = mask & -mask, 1 << (mask.bit_length() - 1)
        if low == high:
            pieces[mask] = (exchange(own, "dp", mask),)
        else:
            pieces[mask] = (
                exchange(half(pieces[mask ^ high], 0), "dp", high),
                exchange(half(pieces[mask ^ low], 1), "dp", low),
            )
    for mask in list(pieces):
        pieces[mask | 1] = tuple(exchange(part, "dp", 1) for part in pieces[mask])
    return [pieces[mask] for mask in range(count)]


def unflatten(lengths, refs):
    grouped, at = [], 0
    for length in lengths:
        grouped.append(refs[at : at + length])
        at += length
    return grouped


def side_of(piece, side):
    if len(piece) == 2:
        return piece[side][...]
    width = piece[0].shape[1] // 2
    return piece[0][:, side * width : (side + 1) * width]


def project_kernel(lengths, x_ref, *refs):
    out_ref = refs[-1]
    pieces = unflatten(lengths, refs[:-1])
    width = out_ref.shape[1] // 2
    for side in range(2):
        total = None
        for at, piece in enumerate(pieces):
            term = dot(x_ref[at], side_of(piece, side), 1, 0)
            total = term if total is None else total + term
        out_ref[:, side * width : (side + 1) * width] = total.astype(out_ref.dtype)


def project(x_blocks, pieces):
    lengths = [len(piece) for piece in pieces]
    flat = [part for piece in pieces for part in piece]
    tok_dev, width = x_blocks.shape[1], pieces[0][0].shape[1]
    return pl.pallas_call(
        functools.partial(project_kernel, lengths),
        out_shape=jax.ShapeDtypeStruct((tok_dev, width), jnp.bfloat16),
        in_specs=[vmem()] * (1 + len(flat)),
        out_specs=vmem(),
        compiler_params=params(),
        name="project",
    )(x_blocks, *flat)


def attend_kernel(sizes, info_ref, q_ref, g_ref, *refs):
    act_total, blocks_dev, seq_count, group, has_alias = sizes
    kv_refs = refs[: 2 * seq_count]
    refs = refs[2 * seq_count + (1 if has_alias else 0) :]
    dq_ref, own_ref = refs[0], refs[1]
    send_refs = refs[2 : 1 + seq_count]
    k_scr, v_scr, dk_scr, dv_scr = refs[1 + seq_count :]
    head = pl.program_id(0)
    width = own_ref.shape[1] // 2
    key_count = act_total * BLK
    scale = 1.0 / math.sqrt(HEAD_SIZE)
    columns = [pl.ds(pl.multiple_of(side * width + head * HEAD_SIZE, HEAD_SIZE), HEAD_SIZE) for side in range(2)]
    dk_scr[...] = jnp.zeros_like(dk_scr)
    dv_scr[...] = jnp.zeros_like(dv_scr)
    for slot in range(act_total):
        steps = info_ref[slot]
        row = pl.multiple_of(info_ref[act_total + slot] * BLK, BLK)
        rows = slice(slot * BLK, (slot + 1) * BLK)

        @pl.when(steps < 0)
        def _():
            k_scr[rows, :] = jnp.zeros((BLK, HEAD_SIZE), k_scr.dtype)
            v_scr[rows, :] = jnp.zeros((BLK, HEAD_SIZE), v_scr.dtype)

        for step in range(seq_count):

            @pl.when(steps == step)
            def _():
                k_scr[rows, :] = kv_refs[2 * step][pl.ds(row, BLK), :]
                v_scr[rows, :] = kv_refs[2 * step + 1][pl.ds(row, BLK), :]

    for block in range(blocks_dev):
        rank = info_ref[2 * act_total + block]
        rows = slice(block * BLK, (block + 1) * BLK)

        @pl.when(rank < 0)
        def _():
            dq_ref[rows, :] = jnp.zeros((BLK, group * HEAD_SIZE), dq_ref.dtype)

        @pl.when(rank >= 0)
        def _():
            keys, values = k_scr[...], v_scr[...]
            query = jnp.concatenate(
                [q_ref[rows, at * HEAD_SIZE : (at + 1) * HEAD_SIZE] for at in range(group)], axis=0
            )
            gradient = jnp.concatenate(
                [g_ref[rows, at * HEAD_SIZE : (at + 1) * HEAD_SIZE] for at in range(group)], axis=0
            )
            scores = dot(keys, query, 1, 1)
            shape = scores.shape
            key_pos = lax.broadcasted_iota(jnp.int32, shape, 0)
            query_pos = rank * BLK + (lax.broadcasted_iota(jnp.int32, shape, 1) & (BLK - 1))
            scores = jnp.where(key_pos <= query_pos, scores, MASKED)
            top = jnp.max(scores, axis=0, keepdims=True)
            exponent = jnp.exp((scores - top) * scale)
            probs = exponent * (1.0 / jnp.sum(exponent, axis=0, keepdims=True))
            probs_low = probs.astype(jnp.bfloat16)
            dprobs = dot(values, gradient, 1, 1)
            delta = jnp.sum(probs_low.astype(jnp.float32) * dprobs, axis=0, keepdims=True)
            dscores = (probs * (dprobs - delta) * scale).astype(jnp.bfloat16)
            dk_scr[...] += dot(dscores, query, 1, 0)
            dv_scr[...] += dot(probs_low, gradient, 1, 0)
            dquery = dot(keys, dscores, 0, 0).T.astype(dq_ref.dtype)
            for at in range(group):
                dq_ref[rows, at * HEAD_SIZE : (at + 1) * HEAD_SIZE] = dquery[at * BLK : (at + 1) * BLK]

    for target in (own_ref, *send_refs):
        for side in range(2):
            target[:, columns[side]] = jnp.zeros((target.shape[0], HEAD_SIZE), target.dtype)
    for slot in range(act_total):
        steps = info_ref[slot]
        row = pl.multiple_of(info_ref[act_total + slot] * BLK, BLK)
        rows = slice(slot * BLK, (slot + 1) * BLK)
        for step, target in enumerate((own_ref, *send_refs)):

            @pl.when(steps == step)
            def _():
                target[pl.ds(row, BLK), columns[0]] = dk_scr[rows, :].astype(target.dtype)
                target[pl.ds(row, BLK), columns[1]] = dv_scr[rows, :].astype(target.dtype)


def attend(info, queries, cotangent, kv_steps, chunk, heads, group, act_total, dq_so_far):
    seq_count = len(kv_steps)
    tok_dev, width = kv_steps[0].shape
    qwidth = queries.shape[2]
    group_width = group * HEAD_SIZE
    q_spec = pl.BlockSpec((None, tok_dev, group_width), lambda i: (0, 0, chunk * heads + i))
    kv_specs = [
        pl.BlockSpec((tok_dev, HEAD_SIZE), lambda i: (0, i)),
        pl.BlockSpec((tok_dev, HEAD_SIZE), lambda i: (0, heads + i)),
    ]
    whole_spec = pl.BlockSpec((tok_dev, width), lambda i: (0, 0))
    sizes = (act_total, tok_dev // BLK, seq_count, group, dq_so_far is not None)
    operands = [info, queries, cotangent, *[kv for kv in kv_steps for _ in range(2)]]
    in_specs = [smem(), q_spec, q_spec] + kv_specs * seq_count
    aliases = {}
    if dq_so_far is not None:
        aliases = {len(operands): 0}
        operands.append(dq_so_far)
        in_specs.append(pl.BlockSpec(memory_space=pl.ANY))
    outs = pl.pallas_call(
        functools.partial(attend_kernel, sizes),
        grid=(heads,),
        out_shape=[
            jax.ShapeDtypeStruct((1, tok_dev, qwidth), jnp.bfloat16),
            jax.ShapeDtypeStruct((tok_dev, width), jnp.float32),
            *[jax.ShapeDtypeStruct((tok_dev, width), jnp.bfloat16) for _ in range(seq_count - 1)],
        ],
        in_specs=in_specs,
        out_specs=[q_spec] + [whole_spec] * seq_count,
        scratch_shapes=[pltpu.VMEM((act_total * BLK, HEAD_SIZE), jnp.bfloat16)] * 2
        + [pltpu.VMEM((act_total * BLK, HEAD_SIZE), jnp.float32)] * 2,
        input_output_aliases=aliases,
        compiler_params=params(),
        name="attend",
    )(*operands)
    return outs[0], outs[1], outs[2:]


def token_kernel(lengths, chunk_count, *refs):
    out_ref = refs[-1]
    dkv_refs = refs[:chunk_count]
    per_chunk = sum(lengths)
    chunks = [
        unflatten(lengths, refs[chunk_count + at * per_chunk : chunk_count + (at + 1) * per_chunk])
        for at in range(chunk_count)
    ]
    width = dkv_refs[0].shape[1] // 2
    for at in range(len(lengths)):
        total = None
        for dkv_ref, pieces in zip(dkv_refs, chunks):
            for side in range(2):
                term = dot(dkv_ref[:, side * width : (side + 1) * width], side_of(pieces[at], side), 1, 1)
                total = term if total is None else total + term
        out_ref[at] = total.astype(out_ref.dtype)


def token_blocks(dkvs, weight_pieces):
    lengths = [len(piece) for piece in weight_pieces[0]]
    flat = [part for pieces in weight_pieces for piece in pieces for part in piece]
    rows = weight_pieces[0][0][0].shape[0]
    tok_dev = dkvs[0].shape[0]
    return pl.pallas_call(
        functools.partial(token_kernel, lengths, len(dkvs)),
        out_shape=jax.ShapeDtypeStruct((len(lengths), tok_dev, rows), jnp.bfloat16),
        in_specs=[vmem()] * (len(dkvs) + len(flat)),
        out_specs=vmem(),
        compiler_params=params(),
        name="token_grads",
    )(*dkvs, *flat)


def weight_kernel(lengths, dests, rank_ref, *refs):
    count = len(lengths)
    x_refs, refs = refs[:count], refs[count:]
    pieces = unflatten(lengths, refs[: sum(lengths)])
    own_ref, send_refs = refs[sum(lengths)], refs[sum(lengths) + 1 :]
    rank = rank_ref[0]
    column = own_ref.shape[1]
    totals = []
    for side in range(2):
        total = None
        for x_ref, piece in zip(x_refs, pieces):
            term = dot(x_ref[...], side_of(piece, side), 0, 0)
            total = term if total is None else total + term
        totals.append(total)
    own_ref[...] = jnp.zeros_like(own_ref)
    for dest, side, offset in dests:
        part = totals[side][:, offset : offset + column]

        @pl.when(rank == dest)
        def _():
            own_ref[...] = part

        for at, send_ref in enumerate(send_refs):

            @pl.when(rank ^ (at + 1) == dest)
            def _():
                send_ref[...] = part.astype(send_ref.dtype)


def weight_terms(rank, x_pieces, dkv_pieces, dests, column):
    lengths = [len(piece) for piece in dkv_pieces]
    flat = [part for piece in dkv_pieces for part in piece]
    seq_count = lax.axis_size("seq")
    rows = x_pieces[0].shape[1]
    outs = pl.pallas_call(
        functools.partial(weight_kernel, lengths, dests),
        out_shape=[jax.ShapeDtypeStruct((rows, column), jnp.float32)]
        + [jax.ShapeDtypeStruct((rows, column), jnp.bfloat16)] * (seq_count - 1),
        in_specs=[smem()] + [vmem()] * (len(x_pieces) + len(flat)),
        out_specs=[vmem()] * seq_count,
        compiler_params=params(),
        name="weight_grad",
    )(rank, *x_pieces, *flat)
    return outs[0], outs[1:]


def body(tokens, queries, cotangent, kv_weight, active):
    seq_count, dp_count = lax.axis_size("seq"), lax.axis_size("dp")
    seq_rank, dp_rank = lax.axis_index("seq"), lax.axis_index("dp")
    tok_dev, model = tokens.shape[1], tokens.shape[2]
    qwidth, kvwidth = queries.shape[2], kv_weight.shape[1]
    rows = kv_weight.shape[0]
    act_total = active.shape[1]
    kv_heads = kvwidth // (2 * HEAD_SIZE)
    group = qwidth // (HEAD_SIZE * kv_heads)
    heads = kv_heads // CHUNKS
    width = heads * HEAD_SIZE
    blocks_dev = tok_dev // BLK
    column = kvwidth // seq_count

    block_ids = active[0]
    local_ids = seq_rank * blocks_dev + jnp.arange(blocks_dev, dtype=jnp.int32)
    match = (block_ids[None, :] == local_ids[:, None]).astype(jnp.int32)
    slot_rank = jnp.sum(match * jnp.arange(1, act_total + 1, dtype=jnp.int32)[None, :], axis=1) - 1
    info = jnp.concatenate(
        [seq_rank - block_ids // blocks_dev, block_ids % blocks_dev, slot_rank]
    ).astype(jnp.int32)
    rank = seq_rank.astype(jnp.int32).reshape(1)

    others = dp_rank ^ jnp.arange(dp_count, dtype=jnp.int32)
    x_blocks = jnp.stack(
        [lax.dynamic_slice_in_dim(tokens[0], others[m] * rows, rows, axis=1) for m in range(dp_count)]
    )

    dq = None
    weight_pieces, owns = [], []
    dkvs, terms = [], []
    for chunk in range(CHUNKS):
        key_at, value_at = chunk * width, (kv_heads // CHUNKS * CHUNKS) * HEAD_SIZE + chunk * width
        shard = jnp.concatenate(
            [kv_weight[:, key_at : key_at + width], kv_weight[:, value_at : value_at + width]], axis=1
        )
        weight_pieces.append(gather_pieces(shard))
    x_pieces = [x_blocks[0]] + [exchange(x_blocks[m], "dp", m) for m in range(1, dp_count)]
    for chunk in range(CHUNKS):
        keyval = project(x_blocks, weight_pieces[chunk])
        kv_steps = [keyval] + [moved(keyval, "seq", step) for step in range(1, seq_count)]
        dq, own, sends = attend(
            info, queries, cotangent, kv_steps, chunk, heads, group, act_total, dq
        )
        total = own
        for step, send in enumerate(sends):
            total = total + moved(send, "seq", -(step + 1)).astype(jnp.float32)
        dkvs.append(total.astype(jnp.bfloat16))
    for chunk in range(CHUNKS):
        dkv_pieces = gather_pieces(dkvs[chunk])
        dests = []
        for side in range(2):
            start = side * (kvwidth // 2) + chunk * width
            for offset in range(0, width, column):
                dests.append(((start + offset) // column, side, offset))
        own, sends = weight_terms(rank, x_pieces, dkv_pieces, dests, column)
        terms.append(own)
        for at, send in enumerate(sends):
            pairs = [(dest ^ (at + 1), dest) for dest, _, _ in dests]
            terms.append(lax.ppermute(send, "seq", pairs).astype(jnp.float32))
    weight_grad = functools.reduce(lambda a, b: a + b, terms)
    blocks = token_blocks(dkvs, weight_pieces)
    token_grad = jnp.concatenate(
        [lax.dynamic_index_in_dim(blocks, others[m], axis=0, keepdims=False) for m in range(dp_count)], axis=1
    )
    return (dq, token_grad[None], weight_grad)


def solution(mesh):
    in_specs = (
        P("dp", "seq", None),
        P("dp", "seq", None),
        P("dp", "seq", None),
        P("dp", None),
        P("dp", None),
    )
    out_specs = (P("dp", "seq", None), P("dp", "seq", None), P("dp", "seq"))
    return jax.shard_map(body, mesh=mesh, in_specs=in_specs, out_specs=out_specs, check_vma=False)
```

time: 467 us -> 287 us (0.61)
  waiting for transfers between devices: 225 us -> 131 us
  blocking collectives: 86.4 us -> 0 us
  starting transfers between devices: 18.3 us -> 67.1 us
  matrix products: 41 us -> 0 us
  local copies, waits for them, and re-layouts: 63.8 us -> 29.3 us
  Pallas kernels: 0 us -> 29.6 us
  other arithmetic: 13.6 us -> 2.93 us
  between operations: 14 us -> 22.2 us
    ppermute x0 -> x61, waiting for transfers between devices: none -> 131 us  [the longest x12 64.8 us: moved(): return lax.ppermute(value, axis, pairs)]
    all_to_all x2 -> x0, blocking collectives: 86.4 us -> none  [the longest x1 68 us: body(): lax.all_to_all(padded(query_grad), 'seq', split_axis=0, concat_axis=2, ti...]
    unnamed x6 -> x0, waiting for transfers between devices: 82.8 us -> none
    ppermute x0 -> x61, starting transfers between devices: none -> 67.1 us  [the longest x12 28.3 us: moved(): return lax.ppermute(value, axis, pairs)]
    all_gather x2 -> x0, waiting for transfers between devices: 58.6 us -> none  [the longest x1 58.6 us: body(): weight_full = lax.all_gather(kv_weight, 'dp', axis=0, tiled=True)]
    reduce_scatter x2 -> x0, waiting for transfers between devices: 42.7 us -> none  [the longest x1 42.7 us: body(): lax.psum_scatter(kv_terms, 'seq', scatter_dimension=1, tiled=True)]
    all_to_all x3 -> x0, waiting for transfers between devices: 41 us -> none  [the longest x1 31.8 us: body(): lax.all_to_all(spread(queries[0]), 'seq', split_axis=1, concat_axis=0, ti...]
    dot_general x8 -> x0, matrix products: 35.5 us -> none  [the longest x1 12.5 us: body(): lax.dot_general(kv_back, weight_full, (((1,), (1,)), ((), ())), preferred...]
  transfers between devices with their start and end apart: 8 -> 61, of which waited for: 5 -> 19; matrix products, arithmetic and copies ran while one was open for 11% -> 6% of each run, Pallas kernels for 0% -> 10%
where the time goes in v1:
time: 287 us; the launch traced here: 283 us
  waiting for transfers between devices  131 us (46%)
  starting transfers between devices  67.1 us (23%)
  Pallas kernels  29.6 us (10%)
  local copies, waits for them, and re-layouts  29.3 us (10%)
  between operations  22.2 us (8%)
  other arithmetic  2.93 us (1%)
    ppermute x12, waiting for transfers between devices, moved(): return lax.ppermute(value, axis, pairs)  64.8 us
    ppermute x43, waiting for transfers between devices, exchange(): return lax.ppermute(value, axis, [(i, i ^ mask) for i in range(count)])  45.2 us
    ppermute x12, starting transfers between devices, moved(): return lax.ppermute(value, axis, pairs)  28.3 us
    ppermute x43, starting transfers between devices, exchange(): return lax.ppermute(value, axis, [(i, i ^ mask) for i in range(count)])  26.2 us
    ppermute x6, waiting for transfers between devices, body(): terms.append(lax.ppermute(send, 'seq', pairs).astype(jnp.float32))  21.4 us
    unnamed x97, local copies, waits for them, and re-layouts  16.1 us
    ppermute x6, starting transfers between devices, body(): terms.append(lax.ppermute(send, 'seq', pairs).astype(jnp.float32))  12.6 us
    pallas_call x2, Pallas kernels, project(): pl.pallas_call(functools.partial(project_kernel, lengths), out_shape=jax....  8.9 us
  transfers between devices with their start and end apart: 61, of which 19 were waited for; matrix products, arithmetic and copies ran while one was open for 6% of the time, Pallas kernels for 10%

profile of v1, /device:TPU:8, one launch (start us, length us, event | category | flops | bytes accessed | tf_op | source)
XLA Modules:
  0.0 282.6 jit_solution(1333638530445973679)
XLA Ops:
  2.1 1.6 collective-permute-start.1
  3.6 1.5 collective-permute-start.3
  6.3 13.4 %collective-permute-done.1.refs_2_.refs_14_ = bf16[640,512]{1,0:T(8,128)(2,1)S(1)} collective-permute-done((bf16[640,512]{1,0:T(8,128)(2,1)S(1)}, bf16[640,512]{1,0:T(8,128)(2,1)S(1)}, u32[]{:S(2)}, u32[]{:S(2)}) %collective-permute-start.1) | collective-permute-done | bytes 655392 | tf_op jit(solution)/shard_map/ppermute | solution.py:38
  20.6 1.5 collective-permute-start.5
  22.1 10.6 %collective-permute-done.13.refs_2_.refs_4_ = bf16[640,512]{1,0:T(8,128)(2,1)} collective-permute-done((bf16[640,512]{1,0:T(8,128)(2,1)S(1)}, bf16[640,512]{1,0:T(8,128)(2,1)}, u32[]{:S(2)}, u32[]{:S(2)}) %collective-permute-start.13) | collective-permute-done | bytes 655392 | tf_op jit(solution)/shard_map/ppermute | solution.py:38
  38.9 1.6 collective-permute-start.6
  41.5 1.6 collective-permute-start.17
  43.8 5.8 %collective-permute-done.6.refs_7_.refs_19_ = bf16[640,256]{1,0:T(8,128)(2,1)} collective-permute-done((bf16[640,256]{1,0:T(8,128)(2,1)S(1)}, bf16[640,256]{1,0:T(8,128)(2,1)}, u32[]{:S(2)}, u32[]{:S(2)}) %collective-permute-start.6) | collective-permute-done | bytes 327712 | tf_op jit(solution)/shard_map/ppermute | solution.py:38
  49.6 1.8 collective-permute-done.17.refs_6_.refs_8_
  51.4 4.7 %collective-permute-done.18.refs_7_.refs_9_ = bf16[640,256]{1,0:T(8,128)(2,1)S(1)} collective-permute-done((bf16[640,256]{1,0:T(8,128)(2,1)S(1)}, bf16[640,256]{1,0:T(8,128)(2,1)S(1)}, u32[]{:S(2)}, u32[]{:S(2)}) %collective-permute-start.18) | collective-permute-done | bytes 327712 | tf_op jit(solution)/shard_map/ppermute | solution.py:38
  56.9 1.5 copy-done.33
  60.4 3.4 %dynamic-slice_bitcast_fusion = (bf16[256,640]{1,0:T(8,128)(2,1)}, bf16[256,640]{1,0:T(8,128)(2,1)}, bf16[256,640]{1,0:T(8,128)(2,1)}, bf16[256,640]{1,0:T(8,128...) fusion(bf16[1,256,5120]{2,1,0:T(8,128)(2,1)} %param.5, ...), kind=kLoop, calls=%fused_computation.13 | loop fusion | bytes 5570592 | tf_op jit(solution)/shard_map/dynamic_slice | solution.py:335
  63.8 1.7 dynamic-slice_dynamic-update-slice_fusion.1
  66.0 1.7 dynamic-slice_dynamic-update-slice_fusion.x_ref
  67.8 4.2 %project.2.refs_0_.refs_1_ = bf16[256,512]{1,0:T(8,128)(2,1)S(1)} custom-call(bf16[8,256,640]{2,1,0:T(8,128)(2,1)} %dynamic-slice_dynamic-update-slice_fusion.x_ref, bf16[640,512]{1,0:T(8,128)(2,1)S(1)} %pad_maximum_fusion.refs_0_.refs_12_, bf16[640,512]{1,0:T(8,128)(2,1)S(1)} %collective-permute-done.refs_1_.refs_13_, ...), custom_call_target="tpu_custom_call" | custom-call | tf_op jit(solution)/shard_map/project/pallas_call | solution.py:102
  72.0 3.6 %collective-permute-start.9 = (bf16[256,512]{1,0:T(8,128)(2,1)S(1)}, bf16[256,512]{1,0:T(8,128)(2,1)S(1)}, u32[]{:S(2)}, u32[]{:S(2)}) collective-permute-start(bf16[256,512]{1,0:T(8,128)(2,1)S(1)} %project.2.refs_0_.refs_1_), channel_id=1, source_target_pairs={{0,1},{1,2},{2,3},{4,5},{5,6},{6,7},{8,9},{9,10},{10,11},{12,13},{... | collective-permute-start | bytes 786440 | tf_op jit(solution)/shard_map/ppermute | solution.py:44
  75.7 2.3 collective-permute-start.10
  78.1 4.7 %project.3.refs_0_.refs_1_ = bf16[256,512]{1,0:T(8,128)(2,1)S(1)} custom-call(bf16[8,256,640]{2,1,0:T(8,128)(2,1)} %dynamic-slice_dynamic-update-slice_fusion.x_ref, bf16[640,512]{1,0:T(8,128)(2,1)S(1)} %pad_maximum_fusion.1.refs_0_.refs_2_, bf16[640,512]{1,0:T(8,128)(2,1)} %collective-permute-done.12.refs_1_.refs_3_, ...), custom_call_target="tpu_custom_call" | custom-call | tf_op jit(solution)/shard_map/project/pallas_call | solution.py:102
  82.7 2.5 collective-permute-start.21
  88.2 19.3 %collective-permute-done.10.refs_4_.refs_5_ = bf16[256,512]{1,0:T(8,128)(2,1)S(1)} collective-permute-done((bf16[256,512]{1,0:T(8,128)(2,1)S(1)}, bf16[256,512]{1,0:T(8,128)(2,1)S(1)}, u32[]{:S(2)}, u32[]{:S(2)}) %collective-permute-start.10) | collective-permute-done | bytes 262176 | tf_op jit(solution)/shard_map/ppermute | solution.py:44
  108.2 1.5 collective-permute-start.31
  109.7 3.6 %collective-permute-done.21.refs_2_.refs_3_ = bf16[256,512]{1,0:T(8,128)(2,1)} collective-permute-done((bf16[256,512]{1,0:T(8,128)(2,1)S(1)}, bf16[256,512]{1,0:T(8,128)(2,1)}, u32[]{:S(2)}, u32[]{:S(2)}) %collective-permute-start.21) | collective-permute-done | bytes 262176 | tf_op jit(solution)/shard_map/ppermute | solution.py:44
  114.1 6.9 %collective-permute-done.22.refs_4_.refs_5_ = bf16[256,512]{1,0:T(8,128)(2,1)S(1)} collective-permute-done((bf16[256,512]{1,0:T(8,128)(2,1)S(1)}, bf16[256,512]{1,0:T(8,128)(2,1)S(1)}, u32[]{:S(2)}, u32[]{:S(2)}) %collective-permute-start.22) | collective-permute-done | bytes 262176 | tf_op jit(solution)/shard_map/ppermute | solution.py:44
  121.6 1.5 collective-permute-start.33
  124.6 2.6 attend.2
  127.2 2.3 attend.3
  131.5 11.1 %collective-permute-start.27 = (bf16[256,512]{1,0:T(8,128)(2,1)S(1)}, bf16[256,512]{1,0:T(8,128)(2,1)S(1)}, u32[]{:S(2)}, u32[]{:S(2)}) collective-permute-start(bf16[256,512]{1,0:T(8,128)(2,1)S(1)} %get-tuple-element.28), channel_id=1, source_target_pairs={{1,0},{2,1},{3,2},{5,4},{6,5},{7,6},{9,8},{10,9},{11,10},{13,12},{... | collective-permute-start | bytes 786440 | tf_op jit(solution)/shard_map/ppermute | solution.py:44
  143.5 4.9 %collective-permute-start.35 = (bf16[256,640]{1,0:T(8,128)(2,1)S(1)}, bf16[256,640]{1,0:T(8,128)(2,1)S(1)}, u32[]{:S(2)}, u32[]{:S(2)}) collective-permute-start(bf16[256,640]{1,0:T(8,128)(2,1)S(1)} %copy-done.38), channel_id=1, source_target_pairs={{0,24},{4,28},{8,16},{12,20},{16,8},{20,12},{24,0},{28,4},{1,25},{... | collective-permute-start | bytes 983048 | tf_op jit(solution)/shard_map/ppermute | solution.py:38
  149.1 11.2 %collective-permute-done.28 = bf16[256,512]{1,0:T(8,128)(2,1)S(1)} collective-permute-done((bf16[256,512]{1,0:T(8,128)(2,1)S(1)}, bf16[256,512]{1,0:T(8,128)(2,1)S(1)}, u32[]{:S(2)}, u32[]{:S(2)}) %collective-permute-start.28) | collective-permute-done | bytes 262176 | tf_op jit(solution)/shard_map/ppermute | solution.py:44
  161.6 15.4 %collective-permute-done.27 = bf16[256,512]{1,0:T(8,128)(2,1)S(1)} collective-permute-done((bf16[256,512]{1,0:T(8,128)(2,1)S(1)}, bf16[256,512]{1,0:T(8,128)(2,1)S(1)}, u32[]{:S(2)}, u32[]{:S(2)}) %collective-permute-start.27) | collective-permute-done | bytes 262176 | tf_op jit(solution)/shard_map/ppermute | solution.py:44
  177.0 2.1 collective-permute-start.24
  179.9 8.3 %collective-permute-done.24 = bf16[256,512]{1,0:T(8,128)(2,1)S(1)} collective-permute-done((bf16[256,512]{1,0:T(8,128)(2,1)S(1)}, bf16[256,512]{1,0:T(8,128)(2,1)S(1)}, u32[]{:S(2)}, u32[]{:S(2)}) %collective-permute-start.24) | collective-permute-done | bytes 262176 | tf_op jit(solution)/shard_map/ppermute | solution.py:44
  188.5 1.6 collective-permute-done.36.refs_7_
  190.6 2.4 collective-permute-done.50.refs_10_
  193.1 4.5 %collective-permute-done.52.refs_12_ = bf16[256,512]{1,0:T(8,128)(2,1)} collective-permute-done((bf16[256,512]{1,0:T(8,128)(2,1)S(1)}, bf16[256,512]{1,0:T(8,128)(2,1)}, u32[]{:S(2)}, u32[]{:S(2)}) %collective-permute-start.52) | collective-permute-done | bytes 262176 | tf_op jit(solution)/shard_map/ppermute | solution.py:38
  197.6 1.6 slice.94
  199.1 1.6 slice.95
  221.4 8.5 %token_grads.1 = bf16[8,256,640]{2,1,0:T(8,128)(2,1)} custom-call(bf16[256,512]{1,0:T(8,128)(2,1)S(1)} %add_convert_fusion.1.refs_0_.refs_8_, bf16[256,512]{1,0:T(8,128)(2,1)S(1)} %add_convert_fusion.refs_1_.refs_8_, bf16[640,512]{1,0:T(8,128)(2,1)S(1)} %pad_maximum_fusion.1.refs_0_.refs_2_, bf16[640,512]{1,0:T(8,128)(2,1)} %collective-permute-done.12.refs_1_.refs_3_, ...), custom_call_target="tpu_custom_call" | custom-call | tf_op jit(solution)/shard_map/token_grads/pallas_call | solution.py:254
  231.5 1.8 collective-permute-start.42
  233.3 1.9 collective-permute-start.43
  237.8 3.9 %weight_grad.3 = (f32[640,256]{1,0:T(8,128)}, bf16[640,256]{1,0:T(8,128)(2,1)S(1)}, bf16[640,256]{1,0:T(8,128)(2,1)S(1)}, bf16[640,256]{1,0:T(8,128)(2,1)S(1)}) custom-call(s32[1]{0:T(128)} %bitcast.18.rank_ref, bf16[256,640]{1,0:T(8,128)(2,1)S(1)} %copy-done.5, bf16[256,640]{1,0:T(8,128)(2,1)S(1)} %collective-permute-done.30.refs_1_, ...), custom_call_target="tpu_custom_call" | custom-call | tf_op jit(solution)/shard_map/weight_grad/pallas_call | solution.py:298
  243.7 1.9 collective-permute-start.59
  247.1 3.5 %weight_grad.2 = (f32[640,256]{1,0:T(8,128)}, bf16[640,256]{1,0:T(8,128)(2,1)S(1)}, bf16[640,256]{1,0:T(8,128)(2,1)S(1)}, bf16[640,256]{1,0:T(8,128)(2,1)S(1)}) custom-call(s32[1]{0:T(128)} %bitcast.18.rank_ref, bf16[256,640]{1,0:T(8,128)(2,1)S(1)} %copy-done.5, bf16[256,640]{1,0:T(8,128)(2,1)S(1)} %collective-permute-done.30.refs_1_, ...), custom_call_target="tpu_custom_call" | custom-call | tf_op jit(solution)/shard_map/weight_grad/pallas_call | solution.py:298
  250.6 6.0 %collective-permute-start.48 = (bf16[640,256]{1,0:T(8,128)(2,1)S(1)}, bf16[640,256]{1,0:T(8,128)(2,1)S(1)}, u32[]{:S(2)}, u32[]{:S(2)}) collective-permute-start(bf16[640,256]{1,0:T(8,128)(2,1)S(1)} %get-tuple-element.34), channel_id=1, source_target_pairs={{3,0},{1,2},{7,4},{5,6},{11,8},{9,10},{15,12},{13,14},{19,16},{17,... | collective-permute-start | bytes 983048 | tf_op jit(solution)/shard_map/ppermute | solution.py:369
  257.3 10.8 %collective-permute-done.60 = bf16[640,256]{1,0:T(8,128)(2,1)S(1)} collective-permute-done((bf16[640,256]{1,0:T(8,128)(2,1)S(1)}, bf16[640,256]{1,0:T(8,128)(2,1)S(1)}, u32[]{:S(2)}, u32[]{:S(2)}) %collective-permute-start.60) | collective-permute-done | bytes 327712 | tf_op jit(solution)/shard_map/ppermute | solution.py:369
  269.7 2.7 collective-permute-done.48
  272.4 7.9 %collective-permute-done.46 = bf16[640,256]{1,0:T(8,128)(2,1)S(1)} collective-permute-done((bf16[640,256]{1,0:T(8,128)(2,1)S(1)}, bf16[640,256]{1,0:T(8,128)(2,1)S(1)}, u32[]{:S(2)}, u32[]{:S(2)}) %collective-permute-start.46) | collective-permute-done | bytes 327712 | tf_op jit(solution)/shard_map/ppermute | solution.py:369
  280.3 2.3 convert_add_fusion
  (203 shorter events, 37.0 us)
Async XLA Ops:
  2.1 17.7 %collective-permute-start.1 = (bf16[640,512]{1,0:T(8,128)(2,1)S(1)}, bf16[640,512]{1,0:T(8,128)(2,1)S(1)}, u32[]{:S(2)}, u32[]{:S(2)}) collective-permute-start(bf16[640,512]{1,0:T(8,128)(2,1)S(1)} %pad_maximum_fusion.refs_0_.refs_12_), channel_id=1, source_target_pairs={{0,8},{4,12},{8,0},{12,4},{16,24},{20,28},{24,16},{28,20},{1,9},{5... | collective-permute-start | bytes 1966088 | tf_op jit(solution)/shard_map/ppermute | solution.py:38
  3.6 18.5 %collective-permute-start.3 = (bf16[640,512]{1,0:T(8,128)(2,1)S(1)}, bf16[640,512]{1,0:T(8,128)(2,1)S(1)}, u32[]{:S(2)}, u32[]{:S(2)}) collective-permute-start(bf16[640,512]{1,0:T(8,128)(2,1)S(1)} %pad_maximum_fusion.refs_0_.refs_12_), channel_id=1, source_target_pairs={{0,16},{4,20},{8,24},{12,28},{16,0},{20,4},{24,8},{28,12},{1,17},{... | collective-permute-start | bytes 1966088 | tf_op jit(solution)/shard_map/ppermute | solution.py:38
  5.2 27.6 %collective-permute-start.13 = (bf16[640,512]{1,0:T(8,128)(2,1)S(1)}, bf16[640,512]{1,0:T(8,128)(2,1)}, u32[]{:S(2)}, u32[]{:S(2)}) collective-permute-start(bf16[640,512]{1,0:T(8,128)(2,1)S(1)} %pad_maximum_fusion.1.refs_0_.refs_2_), channel_id=1, source_target_pairs={{0,8},{4,12},{8,0},{12,4},{16,24},{20,28},{24,16},{28,20},{1,9},{5... | collective-permute-start | bytes 1966088 | tf_op jit(solution)/shard_map/ppermute | solution.py:38
  5.8 33.1 %collective-permute-start.15 = (bf16[640,512]{1,0:T(8,128)(2,1)S(1)}, bf16[640,512]{1,0:T(8,128)(2,1)}, u32[]{:S(2)}, u32[]{:S(2)}) collective-permute-start(bf16[640,512]{1,0:T(8,128)(2,1)S(1)} %pad_maximum_fusion.1.refs_0_.refs_2_), channel_id=1, source_target_pairs={{0,16},{4,20},{8,24},{12,28},{16,0},{20,4},{24,8},{28,12},{1,17},{... | collective-permute-start | bytes 1966088 | tf_op jit(solution)/shard_map/ppermute | solution.py:38
  6.3 35.1 %collective-permute-start = (bf16[640,512]{1,0:T(8,128)(2,1)S(1)}, bf16[640,512]{1,0:T(8,128)(2,1)S(1)}, u32[]{:S(2)}, u32[]{:S(2)}) collective-permute-start(bf16[640,512]{1,0:T(8,128)(2,1)S(1)} %pad_maximum_fusion.refs_0_.refs_12_), channel_id=1, source_target_pairs={{0,4},{4,0},{8,12},{12,8},{16,20},{20,16},{24,28},{28,24},{1,5},{5... | collective-permute-start | bytes 1966088 | tf_op jit(solution)/shard_map/ppermute | solution.py:38
  20.6 22.5 %collective-permute-start.5 = (bf16[640,256]{1,0:T(8,128)(2,1)}, bf16[640,256]{1,0:T(8,128)(2,1)}, u32[]{:S(2)}, u32[]{:S(2)}) collective-permute-start(bf16[640,256]{1,0:T(8,128)(2,1)} %slice.88), channel_id=1, source_target_pairs={{0,16},{4,20},{8,24},{12,28},{16,0},{20,4},{24,8},{28,12},{1,17},{... | collective-permute-start | bytes 983048 | tf_op jit(solution)/shard_map/ppermute | solution.py:38
  22.1 34.0 %collective-permute-start.2 = (bf16[640,512]{1,0:T(8,128)(2,1)S(1)}, bf16[640,512]{1,0:T(8,128)(2,1)}, u32[]{:S(2)}, u32[]{:S(2)}) collective-permute-start(bf16[640,512]{1,0:T(8,128)(2,1)S(1)} %collective-permute-done.1.refs_2_.refs_14_), channel_id=1, source_target_pairs={{0,4},{4,0},{8,12},{12,8},{16,20},{20,16},{24,28},{28,24},{1,5},{5... | collective-permute-start | bytes 1966088 | tf_op jit(solution)/shard_map/ppermute | solution.py:38
  32.8 23.9 %collective-permute-start.4 = (bf16[640,512]{1,0:T(8,128)(2,1)S(1)}, bf16[640,512]{1,0:T(8,128)(2,1)}, u32[]{:S(2)}, u32[]{:S(2)}) collective-permute-start(bf16[640,512]{1,0:T(8,128)(2,1)S(1)} %collective-permute-done.3.refs_4_.refs_16_), channel_id=1, source_target_pairs={{0,4},{4,0},{8,12},{12,8},{16,20},{20,16},{24,28},{28,24},{1,5},{5... | collective-permute-start | bytes 1966088 | tf_op jit(solution)/shard_map/ppermute | solution.py:38
  43.1 13.0 %collective-permute-start.18 = (bf16[640,256]{1,0:T(8,128)(2,1)S(1)}, bf16[640,256]{1,0:T(8,128)(2,1)S(1)}, u32[]{:S(2)}, u32[]{:S(2)}) collective-permute-start(bf16[640,256]{1,0:T(8,128)(2,1)S(1)} %slice.91), channel_id=1, source_target_pairs={{0,8},{4,12},{8,0},{12,4},{16,24},{20,28},{24,16},{28,20},{1,9},{5... | collective-permute-start | bytes 983048 | tf_op jit(solution)/shard_map/ppermute | solution.py:38
  49.6 22.5 %collective-permute-start.12 = (bf16[640,512]{1,0:T(8,128)(2,1)S(1)}, bf16[640,512]{1,0:T(8,128)(2,1)}, u32[]{:S(2)}, u32[]{:S(2)}) collective-permute-start(bf16[640,512]{1,0:T(8,128)(2,1)S(1)} %pad_maximum_fusion.1.refs_0_.refs_2_), channel_id=1, source_target_pairs={{0,4},{4,0},{8,12},{12,8},{16,20},{20,16},{24,28},{28,24},{1,5},{5... | collective-permute-start | bytes 1966088 | tf_op jit(solution)/shard_map/ppermute | solution.py:38
  51.4 24.3 %collective-permute-start.14 = (bf16[640,512]{1,0:T(8,128)(2,1)}, bf16[640,512]{1,0:T(8,128)(2,1)}, u32[]{:S(2)}, u32[]{:S(2)}) collective-permute-start(bf16[640,512]{1,0:T(8,128)(2,1)} %collective-permute-done.13.refs_2_.refs_4_), channel_id=1, source_target_pairs={{0,4},{4,0},{8,12},{12,8},{16,20},{20,16},{24,28},{28,24},{1,5},{5... | collective-permute-start | bytes 1966088 | tf_op jit(solution)/shard_map/ppermute | solution.py:38
  56.1 21.9 %collective-permute-start.16 = (bf16[640,512]{1,0:T(8,128)(2,1)}, bf16[640,512]{1,0:T(8,128)(2,1)}, u32[]{:S(2)}, u32[]{:S(2)}) collective-permute-start(bf16[640,512]{1,0:T(8,128)(2,1)} %collective-permute-done.15.refs_4_.refs_6_), channel_id=1, source_target_pairs={{0,4},{4,0},{8,12},{12,8},{16,20},{20,16},{24,28},{28,24},{1,5},{5... | collective-permute-start | bytes 1966088 | tf_op jit(solution)/shard_map/ppermute | solution.py:38
  65.5 12.5 %collective-permute-start.19 = (bf16[640,256]{1,0:T(8,128)(2,1)S(1)}, bf16[640,256]{1,0:T(8,128)(2,1)S(1)}, u32[]{:S(2)}, u32[]{:S(2)}) collective-permute-start(bf16[640,256]{1,0:T(8,128)(2,1)S(1)} %copy-done.14), channel_id=1, source_target_pairs={{0,4},{4,0},{8,12},{12,8},{16,20},{20,16},{24,28},{28,24},{1,5},{5... | collective-permute-start | bytes 983048 | tf_op jit(solution)/shard_map/ppermute | solution.py:38
  65.8 12.2 %collective-permute-start.20 = (bf16[640,256]{1,0:T(8,128)(2,1)S(1)}, bf16[640,256]{1,0:T(8,128)(2,1)S(1)}, u32[]{:S(2)}, u32[]{:S(2)}) collective-permute-start(bf16[640,256]{1,0:T(8,128)(2,1)S(1)} %copy-done.17), channel_id=1, source_target_pairs={{0,4},{4,0},{8,12},{12,8},{16,20},{20,16},{24,28},{28,24},{1,5},{5... | collective-permute-start | bytes 983048 | tf_op jit(solution)/shard_map/ppermute | solution.py:38
  72.0 15.4 %collective-permute-start.9 = (bf16[256,512]{1,0:T(8,128)(2,1)S(1)}, bf16[256,512]{1,0:T(8,128)(2,1)S(1)}, u32[]{:S(2)}, u32[]{:S(2)}) collective-permute-start(bf16[256,512]{1,0:T(8,128)(2,1)S(1)} %project.2.refs_0_.refs_1_), channel_id=1, source_target_pairs={{0,1},{1,2},{2,3},{4,5},{5,6},{6,7},{8,9},{9,10},{10,11},{12,13},{... | collective-permute-start | bytes 786440 | tf_op jit(solution)/shard_map/ppermute | solution.py:44
  75.7 31.8 %collective-permute-start.10 = (bf16[256,512]{1,0:T(8,128)(2,1)S(1)}, bf16[256,512]{1,0:T(8,128)(2,1)S(1)}, u32[]{:S(2)}, u32[]{:S(2)}) collective-permute-start(bf16[256,512]{1,0:T(8,128)(2,1)S(1)} %project.2.refs_0_.refs_1_), channel_id=1, source_target_pairs={{0,2},{1,3},{4,6},{5,7},{8,10},{9,11},{12,14},{13,15},{16,18},{17,... | collective-permute-start | bytes 786440 | tf_op jit(solution)/shard_map/ppermute | solution.py:44
  82.7 30.5 %collective-permute-start.21 = (bf16[256,512]{1,0:T(8,128)(2,1)S(1)}, bf16[256,512]{1,0:T(8,128)(2,1)}, u32[]{:S(2)}, u32[]{:S(2)}) collective-permute-start(bf16[256,512]{1,0:T(8,128)(2,1)S(1)} %project.3.refs_0_.refs_1_), channel_id=1, source_target_pairs={{0,1},{1,2},{2,3},{4,5},{5,6},{6,7},{8,9},{9,10},{10,11},{12,13},{... | collective-permute-start | bytes 786440 | tf_op jit(solution)/shard_map/ppermute | solution.py:44
  85.2 35.8 %collective-permute-start.22 = (bf16[256,512]{1,0:T(8,128)(2,1)S(1)}, bf16[256,512]{1,0:T(8,128)(2,1)S(1)}, u32[]{:S(2)}, u32[]{:S(2)}) collective-permute-start(bf16[256,512]{1,0:T(8,128)(2,1)S(1)} %project.3.refs_0_.refs_1_), channel_id=1, source_target_pairs={{0,2},{1,3},{4,6},{5,7},{8,10},{9,11},{12,14},{13,15},{16,18},{17,... | collective-permute-start | bytes 786440 | tf_op jit(solution)/shard_map/ppermute | solution.py:44
  86.6 35.1 %collective-permute-start.23 = (bf16[256,512]{1,0:T(8,128)(2,1)S(1)}, bf16[256,512]{1,0:T(8,128)(2,1)S(1)}, u32[]{:S(2)}, u32[]{:S(2)}) collective-permute-start(bf16[256,512]{1,0:T(8,128)(2,1)S(1)} %project.3.refs_0_.refs_1_), channel_id=1, source_target_pairs={{0,3},{4,7},{8,11},{12,15},{16,19},{20,23},{24,27},{28,31}} | collective-permute-start | bytes 786440 | tf_op jit(solution)/shard_map/ppermute | solution.py:44
  88.2 42.0 %collective-permute-start.30 = (bf16[256,640]{1,0:T(8,128)(2,1)}, bf16[256,640]{1,0:T(8,128)(2,1)S(1)}, u32[]{:S(2)}, u32[]{:S(2)}) collective-permute-start(bf16[256,640]{1,0:T(8,128)(2,1)} %get-tuple-element.41), channel_id=1, source_target_pairs={{0,4},{4,0},{8,12},{12,8},{16,20},{20,16},{24,28},{28,24},{1,5},{5... | collective-permute-start | bytes 983048 | tf_op jit(solution)/shard_map/ppermute | solution.py:38
  108.2 23.3 %collective-permute-start.31 = (bf16[256,640]{1,0:T(8,128)(2,1)}, bf16[256,640]{1,0:T(8,128)(2,1)S(1)}, u32[]{:S(2)}, u32[]{:S(2)}) collective-permute-start(bf16[256,640]{1,0:T(8,128)(2,1)} %get-tuple-element.42), channel_id=1, source_target_pairs={{0,8},{4,12},{8,0},{12,4},{16,24},{20,28},{24,16},{28,20},{1,9},{5... | collective-permute-start | bytes 983048 | tf_op jit(solution)/shard_map/ppermute | solution.py:38
  113.2 13.9 %collective-permute-start.11 = (bf16[256,512]{1,0:T(8,128)(2,1)S(1)}, bf16[256,512]{1,0:T(8,128)(2,1)S(1)}, u32[]{:S(2)}, u32[]{:S(2)}) collective-permute-start(bf16[256,512]{1,0:T(8,128)(2,1)S(1)} %project.2.refs_0_.refs_1_), channel_id=1, source_target_pairs={{0,3},{4,7},{8,11},{12,15},{16,19},{20,23},{24,27},{28,31}} | collective-permute-start | bytes 786440 | tf_op jit(solution)/shard_map/ppermute | solution.py:44
  121.0 21.5 %collective-permute-start.32 = (bf16[256,640]{1,0:T(8,128)(2,1)}, bf16[256,640]{1,0:T(8,128)(2,1)S(1)}, u32[]{:S(2)}, u32[]{:S(2)}) collective-permute-start(bf16[256,640]{1,0:T(8,128)(2,1)} %get-tuple-element.43), channel_id=1, source_target_pairs={{0,12},{4,8},{8,4},{12,0},{16,28},{20,24},{24,20},{28,16},{1,13},{... | collective-permute-start | bytes 983048 | tf_op jit(solution)/shard_map/ppermute | solution.py:38
  121.6 21.8 %collective-permute-start.33 = (bf16[256,640]{1,0:T(8,128)(2,1)}, bf16[256,640]{1,0:T(8,128)(2,1)S(1)}, u32[]{:S(2)}, u32[]{:S(2)}) collective-permute-start(bf16[256,640]{1,0:T(8,128)(2,1)} %get-tuple-element.44), channel_id=1, source_target_pairs={{0,16},{4,20},{8,24},{12,28},{16,0},{20,4},{24,8},{28,12},{1,17},{... | collective-permute-start | bytes 983048 | tf_op jit(solution)/shard_map/ppermute | solution.py:38
  129.5 18.9 %collective-permute-start.29 = (bf16[256,512]{1,0:T(8,128)(2,1)S(1)}, bf16[256,512]{1,0:T(8,128)(2,1)S(1)}, u32[]{:S(2)}, u32[]{:S(2)}) collective-permute-start(bf16[256,512]{1,0:T(8,128)(2,1)S(1)} %get-tuple-element.30), channel_id=1, source_target_pairs={{3,0},{7,4},{11,8},{15,12},{19,16},{23,20},{27,24},{31,28}} | collective-permute-start | bytes 786440 | tf_op jit(solution)/shard_map/ppermute | solution.py:44
  130.2 30.1 %collective-permute-start.28 = (bf16[256,512]{1,0:T(8,128)(2,1)S(1)}, bf16[256,512]{1,0:T(8,128)(2,1)S(1)}, u32[]{:S(2)}, u32[]{:S(2)}) collective-permute-start(bf16[256,512]{1,0:T(8,128)(2,1)S(1)} %get-tuple-element.29), channel_id=1, source_target_pairs={{2,0},{3,1},{6,4},{7,5},{10,8},{11,9},{14,12},{15,13},{18,16},{19,... | collective-permute-start | bytes 786440 | tf_op jit(solution)/shard_map/ppermute | solution.py:44
  131.5 45.5 %collective-permute-start.27 = (bf16[256,512]{1,0:T(8,128)(2,1)S(1)}, bf16[256,512]{1,0:T(8,128)(2,1)S(1)}, u32[]{:S(2)}, u32[]{:S(2)}) collective-permute-start(bf16[256,512]{1,0:T(8,128)(2,1)S(1)} %get-tuple-element.28), channel_id=1, source_target_pairs={{1,0},{2,1},{3,2},{5,4},{6,5},{7,6},{9,8},{10,9},{11,10},{13,12},{... | collective-permute-start | bytes 786440 | tf_op jit(solution)/shard_map/ppermute | solution.py:44
  143.4 45.0 %collective-permute-start.34 = (bf16[256,640]{1,0:T(8,128)(2,1)S(1)}, bf16[256,640]{1,0:T(8,128)(2,1)S(1)}, u32[]{:S(2)}, u32[]{:S(2)}) collective-permute-start(bf16[256,640]{1,0:T(8,128)(2,1)S(1)} %copy-done.39), channel_id=1, source_target_pairs={{0,20},{4,16},{8,28},{12,24},{16,4},{20,0},{24,12},{28,8},{1,21},{... | collective-permute-start | bytes 983048 | tf_op jit(solution)/shard_map/ppermute | solution.py:38
  143.5 45.0 %collective-permute-start.35 = (bf16[256,640]{1,0:T(8,128)(2,1)S(1)}, bf16[256,640]{1,0:T(8,128)(2,1)S(1)}, u32[]{:S(2)}, u32[]{:S(2)}) collective-permute-start(bf16[256,640]{1,0:T(8,128)(2,1)S(1)} %copy-done.38), channel_id=1, source_target_pairs={{0,24},{4,28},{8,16},{12,20},{16,8},{20,12},{24,0},{28,4},{1,25},{... | collective-permute-start | bytes 983048 | tf_op jit(solution)/shard_map/ppermute | solution.py:38
  148.4 30.9 %collective-permute-start.26 = (bf16[256,512]{1,0:T(8,128)(2,1)S(1)}, bf16[256,512]{1,0:T(8,128)(2,1)S(1)}, u32[]{:S(2)}, u32[]{:S(2)}) collective-permute-start(bf16[256,512]{1,0:T(8,128)(2,1)S(1)} %get-tuple-element.26), channel_id=1, source_target_pairs={{3,0},{7,4},{11,8},{15,12},{19,16},{23,20},{27,24},{31,28}} | collective-permute-start | bytes 786440 | tf_op jit(solution)/shard_map/ppermute | solution.py:44
  160.3 19.1 %collective-permute-start.25 = (bf16[256,512]{1,0:T(8,128)(2,1)S(1)}, bf16[256,512]{1,0:T(8,128)(2,1)S(1)}, u32[]{:S(2)}, u32[]{:S(2)}) collective-permute-start(bf16[256,512]{1,0:T(8,128)(2,1)S(1)} %get-tuple-element.25), channel_id=1, source_target_pairs={{2,0},{3,1},{6,4},{7,5},{10,8},{11,9},{14,12},{15,13},{18,16},{19,... | collective-permute-start | bytes 786440 | tf_op jit(solution)/shard_map/ppermute | solution.py:44
  177.0 11.2 %collective-permute-start.24 = (bf16[256,512]{1,0:T(8,128)(2,1)S(1)}, bf16[256,512]{1,0:T(8,128)(2,1)S(1)}, u32[]{:S(2)}, u32[]{:S(2)}) collective-permute-start(bf16[256,512]{1,0:T(8,128)(2,1)S(1)} %get-tuple-element.24), channel_id=1, source_target_pairs={{1,0},{2,1},{3,2},{5,4},{6,5},{7,6},{9,8},{10,9},{11,10},{13,12},{... | collective-permute-start | bytes 786440 | tf_op jit(solution)/shard_map/ppermute | solution.py:44
  179.4 13.7 %collective-permute-start.50 = (bf16[256,512]{1,0:T(8,128)(2,1)S(1)}, bf16[256,512]{1,0:T(8,128)(2,1)}, u32[]{:S(2)}, u32[]{:S(2)}) collective-permute-start(bf16[256,512]{1,0:T(8,128)(2,1)S(1)} %add_convert_fusion.refs_1_.refs_8_), channel_id=1, source_target_pairs={{0,8},{4,12},{8,0},{12,4},{16,24},{20,28},{24,16},{28,20},{1,9},{5... | collective-permute-start | bytes 786440 | tf_op jit(solution)/shard_map/ppermute | solution.py:38
  188.4 12.3 %collective-permute-start.49 = (bf16[256,512]{1,0:T(8,128)(2,1)S(1)}, bf16[256,512]{1,0:T(8,128)(2,1)S(1)}, u32[]{:S(2)}, u32[]{:S(2)}) collective-permute-start(bf16[256,512]{1,0:T(8,128)(2,1)S(1)} %add_convert_fusion.refs_1_.refs_8_), channel_id=1, source_target_pairs={{0,4},{4,0},{8,12},{12,8},{16,20},{20,16},{24,28},{28,24},{1,5},{5... | collective-permute-start | bytes 786440 | tf_op jit(solution)/shard_map/ppermute | solution.py:38
  188.4 12.9 %collective-permute-start.38 = (bf16[256,512]{1,0:T(8,128)(2,1)S(1)}, bf16[256,512]{1,0:T(8,128)(2,1)S(1)}, u32[]{:S(2)}, u32[]{:S(2)}) collective-permute-start(bf16[256,512]{1,0:T(8,128)(2,1)S(1)} %add_convert_fusion.1.refs_0_.refs_8_), channel_id=1, source_target_pairs={{0,8},{4,12},{8,0},{12,4},{16,24},{20,28},{24,16},{28,20},{1,9},{5... | collective-permute-start | bytes 786440 | tf_op jit(solution)/shard_map/ppermute | solution.py:38
  190.1 11.4 %collective-permute-start.40 = (bf16[256,512]{1,0:T(8,128)(2,1)S(1)}, bf16[256,512]{1,0:T(8,128)(2,1)S(1)}, u32[]{:S(2)}, u32[]{:S(2)}) collective-permute-start(bf16[256,512]{1,0:T(8,128)(2,1)S(1)} %add_convert_fusion.1.refs_0_.refs_8_), channel_id=1, source_target_pairs={{0,16},{4,20},{8,24},{12,28},{16,0},{20,4},{24,8},{28,12},{1,17},{... | collective-permute-start | bytes 786440 | tf_op jit(solution)/shard_map/ppermute | solution.py:38
  193.1 38.5 %collective-permute-start.51 = (bf16[256,512]{1,0:T(8,128)(2,1)}, bf16[256,512]{1,0:T(8,128)(2,1)}, u32[]{:S(2)}, u32[]{:S(2)}) collective-permute-start(bf16[256,512]{1,0:T(8,128)(2,1)} %collective-permute-done.50.refs_10_), channel_id=1, source_target_pairs={{0,4},{4,0},{8,12},{12,8},{16,20},{20,16},{24,28},{28,24},{1,5},{5... | collective-permute-start | bytes 786440 | tf_op jit(solution)/shard_map/ppermute | solution.py:38
  197.6 35.8 %collective-permute-start.53 = (bf16[256,512]{1,0:T(8,128)(2,1)}, bf16[256,512]{1,0:T(8,128)(2,1)}, u32[]{:S(2)}, u32[]{:S(2)}) collective-permute-start(bf16[256,512]{1,0:T(8,128)(2,1)} %collective-permute-done.52.refs_12_), channel_id=1, source_target_pairs={{0,4},{4,0},{8,12},{12,8},{16,20},{20,16},{24,28},{28,24},{1,5},{5... | collective-permute-start | bytes 786440 | tf_op jit(solution)/shard_map/ppermute | solution.py:38
  201.4 28.5 %collective-permute-start.54 = (bf16[256,256]{1,0:T(8,128)(2,1)}, bf16[256,256]{1,0:T(8,128)(2,1)S(1)}, u32[]{:S(2)}, u32[]{:S(2)}) collective-permute-start(bf16[256,256]{1,0:T(8,128)(2,1)} %slice.94), channel_id=1, source_target_pairs={{0,16},{4,20},{8,24},{12,28},{16,0},{20,4},{24,8},{28,12},{1,17},{... | collective-permute-start | bytes 393224 | tf_op jit(solution)/shard_map/ppermute | solution.py:38
  201.4 28.6 %collective-permute-start.55 = (bf16[256,256]{1,0:T(8,128)(2,1)}, bf16[256,256]{1,0:T(8,128)(2,1)}, u32[]{:S(2)}, u32[]{:S(2)}) collective-permute-start(bf16[256,256]{1,0:T(8,128)(2,1)} %slice.95), channel_id=1, source_target_pairs={{0,8},{4,12},{8,0},{12,4},{16,24},{20,28},{24,16},{28,20},{1,9},{5... | collective-permute-start | bytes 393224 | tf_op jit(solution)/shard_map/ppermute | solution.py:38
  201.5 40.1 %collective-permute-start.37 = (bf16[256,512]{1,0:T(8,128)(2,1)S(1)}, bf16[256,512]{1,0:T(8,128)(2,1)}, u32[]{:S(2)}, u32[]{:S(2)}) collective-permute-start(bf16[256,512]{1,0:T(8,128)(2,1)S(1)} %add_convert_fusion.1.refs_0_.refs_8_), channel_id=1, source_target_pairs={{0,4},{4,0},{8,12},{12,8},{16,20},{20,16},{24,28},{28,24},{1,5},{5... | collective-permute-start | bytes 786440 | tf_op jit(solution)/shard_map/ppermute | solution.py:38
  231.5 11.5 %collective-permute-start.42 = (bf16[256,256]{1,0:T(8,128)(2,1)S(1)}, bf16[256,256]{1,0:T(8,128)(2,1)S(1)}, u32[]{:S(2)}, u32[]{:S(2)}) collective-permute-start(bf16[256,256]{1,0:T(8,128)(2,1)S(1)} %slice.92), channel_id=1, source_target_pairs={{0,16},{4,20},{8,24},{12,28},{16,0},{20,4},{24,8},{28,12},{1,17},{... | collective-permute-start | bytes 393224 | tf_op jit(solution)/shard_map/ppermute | solution.py:38
  241.6 26.5 %collective-permute-start.60 = (bf16[640,256]{1,0:T(8,128)(2,1)S(1)}, bf16[640,256]{1,0:T(8,128)(2,1)S(1)}, u32[]{:S(2)}, u32[]{:S(2)}) collective-permute-start(bf16[640,256]{1,0:T(8,128)(2,1)S(1)} %get-tuple-element.38), channel_id=1, source_target_pairs={{2,1},{0,3},{6,5},{4,7},{10,9},{8,11},{14,13},{12,15},{18,17},{16,... | collective-permute-start | bytes 983048 | tf_op jit(solution)/shard_map/ppermute | solution.py:369
  243.7 25.9 %collective-permute-start.59 = (bf16[640,256]{1,0:T(8,128)(2,1)S(1)}, bf16[640,256]{1,0:T(8,128)(2,1)S(1)}, u32[]{:S(2)}, u32[]{:S(2)}) collective-permute-start(bf16[640,256]{1,0:T(8,128)(2,1)S(1)} %get-tuple-element.37), channel_id=1, source_target_pairs={{3,1},{1,3},{7,5},{5,7},{11,9},{9,11},{15,13},{13,15},{19,17},{17,... | collective-permute-start | bytes 983048 | tf_op jit(solution)/shard_map/ppermute | solution.py:369
  245.7 24.0 %collective-permute-start.58 = (bf16[640,256]{1,0:T(8,128)(2,1)S(1)}, bf16[640,256]{1,0:T(8,128)(2,1)S(1)}, u32[]{:S(2)}, u32[]{:S(2)}) collective-permute-start(bf16[640,256]{1,0:T(8,128)(2,1)S(1)} %get-tuple-element.36), channel_id=1, source_target_pairs={{0,1},{2,3},{4,5},{6,7},{8,9},{10,11},{12,13},{14,15},{16,17},{18,... | collective-permute-start | bytes 983048 | tf_op jit(solution)/shard_map/ppermute | solution.py:369
  250.6 21.7 %collective-permute-start.48 = (bf16[640,256]{1,0:T(8,128)(2,1)S(1)}, bf16[640,256]{1,0:T(8,128)(2,1)S(1)}, u32[]{:S(2)}, u32[]{:S(2)}) collective-permute-start(bf16[640,256]{1,0:T(8,128)(2,1)S(1)} %get-tuple-element.34), channel_id=1, source_target_pairs={{3,0},{1,2},{7,4},{5,6},{11,8},{9,10},{15,12},{13,14},{19,16},{17,... | collective-permute-start | bytes 983048 | tf_op jit(solution)/shard_map/ppermute | solution.py:369
  256.7 15.7 %collective-permute-start.47 = (bf16[640,256]{1,0:T(8,128)(2,1)S(1)}, bf16[640,256]{1,0:T(8,128)(2,1)S(1)}, u32[]{:S(2)}, u32[]{:S(2)}) collective-permute-start(bf16[640,256]{1,0:T(8,128)(2,1)S(1)} %get-tuple-element.33), channel_id=1, source_target_pairs={{2,0},{0,2},{6,4},{4,6},{10,8},{8,10},{14,12},{12,14},{18,16},{16,... | collective-permute-start | bytes 983048 | tf_op jit(solution)/shard_map/ppermute | solution.py:369
  268.1 12.2 %collective-permute-start.46 = (bf16[640,256]{1,0:T(8,128)(2,1)S(1)}, bf16[640,256]{1,0:T(8,128)(2,1)S(1)}, u32[]{:S(2)}, u32[]{:S(2)}) collective-permute-start(bf16[640,256]{1,0:T(8,128)(2,1)S(1)} %get-tuple-element.32), channel_id=1, source_target_pairs={{1,0},{3,2},{5,4},{7,6},{9,8},{11,10},{13,12},{15,14},{17,16},{19,... | collective-permute-start | bytes 983048 | tf_op jit(solution)/shard_map/ppermute | solution.py:369
  (55 other events, 730.7 us)

commit v2 on v1

--- a/solution.py
+++ b/solution.py
@@ -11,12 +11,17 @@
 HEAD_SIZE = 128
 BLK = 128
 CHUNKS = 2
-VMEM_BYTES = 48 * 1024 * 1024
+PARTS = 1
+VMEM_BYTES = 56 * 1024 * 1024
 MASKED = -1e30
 
 
 def params():
     return pltpu.CompilerParams(vmem_limit_bytes=VMEM_BYTES)
+
+
+def lasting(microseconds):
+    return pl.CostEstimate(flops=4000000000 * microseconds, bytes_accessed=12000000 * microseconds, transcendentals=0)
 
 
 def vmem():
@@ -38,75 +43,156 @@
     return lax.ppermute(value, axis, [(i, i ^ mask) for i in range(count)])
 
 
-def moved(value, axis, step):
+def moved(value, axis, step, first=0):
     count = lax.axis_size(axis)
-    pairs = [(i, i + step) for i in range(count) if 0 <= i + step < count]
+    pairs = [(i, i + step) for i in range(first, count) if 0 <= i + step < count]
     return lax.ppermute(value, axis, pairs)
 
 
-def half(piece, side):
-    if len(piece) == 2:
-        return piece[side]
-    width = piece[0].shape[1] // 2
-    return piece[0][:, side * width : (side + 1) * width]
-
-
-def gather_pieces(own):
+def spread(value):
+    count = lax.axis_size("seq")
+    steps = [value] + [None] * (count - 1)
+    for step in range(2, count, 2):
+        steps[step] = moved(steps[step - 2], "seq", 2, step - 2)
+    for step in range(1, count, 2):
+        steps[step] = moved(steps[step - 1], "seq", 1, step - 1)
+    return steps
+
+
+def added(left, right):
+    return (left.astype(jnp.float32) + right.astype(jnp.float32)).astype(left.dtype)
+
+
+def collect(sends, gates, later):
+    count = lax.axis_size("seq")
+    sends = [None, *sends]
+    sends = [None] + [after(send, *gates) for send in sends[1:]]
+    arrived = []
+    for step in range(3, count, 2):
+        arrived.append(moved(sends[step], "seq", -1, step))
+        sends[step - 1] = added(sends[step - 1], arrived[-1])
+    if len(sends) > 2:
+        sends[2] = after(sends[2], *later)
+    for step in range((count - 1) // 2 * 2, 2, -2):
+        sends[step - 2] = added(sends[step - 2], moved(sends[step], "seq", -2, step))
+    return arrived, [moved(sends[step], "seq", -step, step) for step in (1, 2) if step < count]
+
+
+def gather_direct(own):
     count = lax.axis_size("dp")
-    pieces = {0: (own,)}
-    for mask in sorted(range(2, count, 2), key=lambda m: (m.bit_count(), m)):
-        low, high = mask & -mask, 1 << (mask.bit_length() - 1)
-        if low == high:
-            pieces[mask] = (exchange(own, "dp", mask),)
-        else:
-            pieces[mask] = (
-                exchange(half(pieces[mask ^ high], 0), "dp", high),
-                exchange(half(pieces[mask ^ low], 1), "dp", low),
-            )
-    for mask in list(pieces):
-        pieces[mask | 1] = tuple(exchange(part, "dp", 1) for part in pieces[mask])
-    return [pieces[mask] for mask in range(count)]
-
-
-def unflatten(lengths, refs):
-    grouped, at = [], 0
-    for length in lengths:
-        grouped.append(refs[at : at + length])
-        at += length
-    return grouped
-
-
-def side_of(piece, side):
-    if len(piece) == 2:
-        return piece[side][...]
-    width = piece[0].shape[1] // 2
-    return piece[0][:, side * width : (side + 1) * width]
-
-
-def project_kernel(lengths, x_ref, *refs):
-    out_ref = refs[-1]
-    pieces = unflatten(lengths, refs[:-1])
+    pieces = [own] + [None] * (count - 1)
+    for mask in range(2, count, 2):
+        pieces[mask] = exchange(own, "dp", mask)
+    for mask in range(0, count, 2):
+        pieces[mask + 1] = exchange(pieces[mask], "dp", 1)
+    return pieces
+
+
+def after(value, *others):
+    return lax.optimization_barrier((value, others))[0]
+
+
+def side_of(table, refs, at, side):
+    array, start, width = table[at][side]
+    return refs[array][:, start : start + width]
+
+
+def whole_table(count, width):
+    return tuple(((at, 0, width), (at, width, width)) for at in range(count))
+
+
+def gather_weights(shards, behind, use_first):
+    count = lax.axis_size("dp")
+    width = shards[0].shape[1] // 2
+    if count != 8 or len(shards) != 2:
+        result = []
+        for shard in shards:
+            pieces = gather_direct(shard)
+            result.append((pieces, whole_table(count, width)))
+        return result, [use_first(result[0])], pieces[-1:]
+    left, right = slice(0, width), slice(width, 2 * width)
+    first, second = shards
+    from_x, from_y = exchange(first, "dp", 2), exchange(first, "dp", 4)
+    here, there = after(from_x, *behind), after(from_y, *behind)
+    step_y = exchange(jnp.concatenate([here[:, left], second[:, left]], axis=1), "dp", 4)
+    step_x = exchange(jnp.concatenate([there[:, right], second[:, right]], axis=1), "dp", 2)
+    last_x = exchange(jnp.concatenate([step_y[:, right], second[:, left]], axis=1), "dp", 2)
+    last_y = exchange(jnp.concatenate([step_x[:, right], second[:, right]], axis=1), "dp", 4)
+    near = [first, from_x, from_y, step_y, step_x]
+    near_core = [exchange(part, "dp", 1) for part in near]
+    one = [((0, 0), (0, 1)), ((1, 0), (1, 1)), ((2, 0), (2, 1)), ((3, 0), (4, 0))]
+    two = [((0, 0), (0, 1)), ((1, 1), (4, 1)), ((3, 1), (2, 1)), ((1, 0), (2, 0))]
+    tables = []
+    for entries in (one, two):
+        table = []
+        for entry in entries:
+            for core in range(2):
+                table.append(tuple((array + core * 5, part * width, width) for array, part in entry))
+        tables.append(tuple(table))
+    pieces = [(near + near_core, tables[0])]
+    used = use_first(pieces[0])
+    last_x, last_y = after((last_x, last_y), used[min(2, len(used) - 1)])
+    far = [second, last_x, last_y]
+    far_core = [exchange(part, "dp", 1) for part in far]
+    pieces.append((far + [step_y, step_x] + far_core + near_core[3:], tables[1]))
+    return pieces, [used], (last_x, last_y)
+
+
+def split_kernel(x_ref, *out_refs):
+    for at, out_ref in enumerate(out_refs):
+        height = out_ref.shape[0]
+        out_ref[...] = x_ref[at * height : (at + 1) * height]
+
+
+def split_columns(tokens, count):
+    tok_dev, model = tokens.shape[1:]
+    rows, height = model // count, tok_dev // PARTS
+    if rows % 128:
+        return [
+            jnp.stack([tokens[0, part * height : (part + 1) * height, at * rows : (at + 1) * rows] for at in range(count)])
+            for part in range(PARTS)
+        ]
+    return pl.pallas_call(
+        split_kernel,
+        grid=(count,),
+        out_shape=[jax.ShapeDtypeStruct((count, height, rows), tokens.dtype)] * PARTS,
+        in_specs=[pl.BlockSpec((None, tok_dev, rows), lambda at: (0, 0, at))],
+        out_specs=[pl.BlockSpec((None, height, rows), lambda at: (at, 0, 0))] * PARTS,
+        compiler_params=params(),
+        cost_estimate=lasting(3),
+        name="split_columns",
+    )(tokens)
+
+
+def rows_of(x_refs, owner):
+    return jnp.concatenate([x_ref[owner] for x_ref in x_refs], axis=0)
+
+
+def project_kernel(table, rank_ref, *refs):
+    x_refs, refs, out_ref = refs[:PARTS], refs[PARTS:-1], refs[-1]
     width = out_ref.shape[1] // 2
+    totals = [None, None]
+    for at in range(len(table)):
+        rows = rows_of(x_refs, rank_ref[1] ^ at)
+        for side in range(2):
+            term = dot(rows, side_of(table, refs, at, side), 1, 0)
+            totals[side] = term if totals[side] is None else totals[side] + term
     for side in range(2):
-        total = None
-        for at, piece in enumerate(pieces):
-            term = dot(x_ref[at], side_of(piece, side), 1, 0)
-            total = term if total is None else total + term
-        out_ref[:, side * width : (side + 1) * width] = total.astype(out_ref.dtype)
-
-
-def project(x_blocks, pieces):
-    lengths = [len(piece) for piece in pieces]
-    flat = [part for piece in pieces for part in piece]
-    tok_dev, width = x_blocks.shape[1], pieces[0][0].shape[1]
+        out_ref[:, side * width : (side + 1) * width] = totals[side].astype(out_ref.dtype)
+
+
+def project(rank, x_by_owner, pieces):
+    arrays, table = pieces
+    tok_dev, width = x_by_owner[0].shape[1] * PARTS, table[0][0][2] * 2
     return pl.pallas_call(
-        functools.partial(project_kernel, lengths),
+        functools.partial(project_kernel, table),
         out_shape=jax.ShapeDtypeStruct((tok_dev, width), jnp.bfloat16),
-        in_specs=[vmem()] * (1 + len(flat)),
+        in_specs=[smem()] + [vmem()] * (PARTS + len(arrays)),
         out_specs=vmem(),
         compiler_params=params(),
+        cost_estimate=lasting(4),
         name="project",
-    )(x_blocks, *flat)
+    )(rank, *x_by_owner, *arrays)
 
 
 def attend_kernel(sizes, info_ref, q_ref, g_ref, *refs):
@@ -223,88 +309,98 @@
         + [pltpu.VMEM((act_total * BLK, HEAD_SIZE), jnp.float32)] * 2,
         input_output_aliases=aliases,
         compiler_params=params(),
+        cost_estimate=lasting(9),
         name="attend",
     )(*operands)
     return outs[0], outs[1], outs[2:]
 
 
-def token_kernel(lengths, chunk_count, *refs):
+def token_kernel(tables, indices, rank_ref, *refs):
     out_ref = refs[-1]
-    dkv_refs = refs[:chunk_count]
-    per_chunk = sum(lengths)
-    chunks = [
-        unflatten(lengths, refs[chunk_count + at * per_chunk : chunk_count + (at + 1) * per_chunk])
-        for at in range(chunk_count)
-    ]
+    dkv_refs, refs = refs[: len(tables)], refs[len(tables) : -1]
     width = dkv_refs[0].shape[1] // 2
-    for at in range(len(lengths)):
+    count = len(tables[0])
+    rows = out_ref.shape[-1] if len(out_ref.shape) == 3 else out_ref.shape[1] // count
+    for at in range(count):
+        owner = rank_ref[1] ^ at
         total = None
-        for dkv_ref, pieces in zip(dkv_refs, chunks):
+        for dkv_ref, table, index in zip(dkv_refs, tables, indices):
+            arrays = [refs[number] for number in index]
             for side in range(2):
-                term = dot(dkv_ref[:, side * width : (side + 1) * width], side_of(pieces[at], side), 1, 1)
+                term = dot(
+                    dkv_ref[:, side * width : (side + 1) * width], side_of(table, arrays, at, side), 1, 1
+                )
                 total = term if total is None else total + term
-        out_ref[at] = total.astype(out_ref.dtype)
-
-
-def token_blocks(dkvs, weight_pieces):
-    lengths = [len(piece) for piece in weight_pieces[0]]
-    flat = [part for pieces in weight_pieces for piece in pieces for part in piece]
-    rows = weight_pieces[0][0][0].shape[0]
+        if len(out_ref.shape) == 3:
+            out_ref[owner] = total.astype(out_ref.dtype)
+        else:
+            out_ref[:, pl.ds(pl.multiple_of(owner * rows, 128), rows)] = total.astype(out_ref.dtype)
+
+
+def token_grads(rank, dkvs, weight_pieces, rows):
+    flat, indices = [], []
+    for arrays, _ in weight_pieces:
+        index = []
+        for array in arrays:
+            known = [at for at, other in enumerate(flat) if other is array]
+            if not known:
+                known = [len(flat)]
+                flat.append(array)
+            index.append(known[0])
+        indices.append(tuple(index))
+    tables = tuple(table for _, table in weight_pieces)
+    count = lax.axis_size("dp")
     tok_dev = dkvs[0].shape[0]
-    return pl.pallas_call(
-        functools.partial(token_kernel, lengths, len(dkvs)),
-        out_shape=jax.ShapeDtypeStruct((len(lengths), tok_dev, rows), jnp.bfloat16),
-        in_specs=[vmem()] * (len(dkvs) + len(flat)),
+    flat_out = rows % 128 == 0
+    shape = (tok_dev, count * rows) if flat_out else (count, tok_dev, rows)
+    out = pl.pallas_call(
+        functools.partial(token_kernel, tables, tuple(indices)),
+        out_shape=jax.ShapeDtypeStruct(shape, jnp.bfloat16),
+        in_specs=[smem()] + [vmem()] * (len(dkvs) + len(flat)),
         out_specs=vmem(),
         compiler_params=params(),
+        cost_estimate=lasting(8),
         name="token_grads",
-    )(*dkvs, *flat)
-
-
-def weight_kernel(lengths, dests, rank_ref, *refs):
-    count = len(lengths)
-    x_refs, refs = refs[:count], refs[count:]
-    pieces = unflatten(lengths, refs[: sum(lengths)])
-    own_ref, send_refs = refs[sum(lengths)], refs[sum(lengths) + 1 :]
-    rank = rank_ref[0]
-    column = own_ref.shape[1]
-    totals = []
-    for side in range(2):
-        total = None
-        for x_ref, piece in zip(x_refs, pieces):
-            term = dot(x_ref[...], side_of(piece, side), 0, 0)
-            total = term if total is None else total + term
-        totals.append(total)
-    own_ref[...] = jnp.zeros_like(own_ref)
-    for dest, side, offset in dests:
-        part = totals[side][:, offset : offset + column]
-
-        @pl.when(rank == dest)
-        def _():
-            own_ref[...] = part
-
-        for at, send_ref in enumerate(send_refs):
-
-            @pl.when(rank ^ (at + 1) == dest)
+    )(rank, *dkvs, *flat)
+    return out if flat_out else jnp.concatenate(list(out), axis=1)
+
+
+def weight_kernel(dests, has_before, rank_ref, *refs):
+    x_refs, refs = refs[:PARTS], refs[PARTS:]
+    count = x_refs[0].shape[0]
+    pieces, refs = refs[:count], refs[count:]
+    out_refs = refs[len(refs) // 2 :] if has_before else refs
+    column, width = out_refs[0].shape[1], pieces[0].shape[1] // 2
+    totals = [None, None]
+    for at in range(count):
+        rows = rows_of(x_refs, rank_ref[1] ^ at)
+        for side in range(2):
+            term = dot(rows, pieces[at][:, side * width : (side + 1) * width], 0, 0)
+            totals[side] = term if totals[side] is None else totals[side] + term
+    for at, out_ref in enumerate(out_refs):
+        if has_before:
+            out_ref[...] = refs[at][...]
+        for dest, side, offset in dests:
+
+            @pl.when(rank_ref[0] ^ at == dest)
             def _():
-                send_ref[...] = part.astype(send_ref.dtype)
-
-
-def weight_terms(rank, x_pieces, dkv_pieces, dests, column):
-    lengths = [len(piece) for piece in dkv_pieces]
-    flat = [part for piece in dkv_pieces for part in piece]
+                out_ref[...] = totals[side][:, offset : offset + column].astype(out_ref.dtype)
+
+
+def weight_terms(rank, x_all, pieces, dests, column, before):
     seq_count = lax.axis_size("seq")
-    rows = x_pieces[0].shape[1]
-    outs = pl.pallas_call(
-        functools.partial(weight_kernel, lengths, dests),
+    rows = x_all[0].shape[2]
+    operands = [*x_all, *pieces, *before]
+    return pl.pallas_call(
+        functools.partial(weight_kernel, dests, bool(before)),
         out_shape=[jax.ShapeDtypeStruct((rows, column), jnp.float32)]
         + [jax.ShapeDtypeStruct((rows, column), jnp.bfloat16)] * (seq_count - 1),
-        in_specs=[smem()] + [vmem()] * (len(x_pieces) + len(flat)),
+        in_specs=[smem()] + [vmem()] * len(operands),
         out_specs=[vmem()] * seq_count,
         compiler_params=params(),
+        cost_estimate=lasting(4),
         name="weight_grad",
-    )(rank, *x_pieces, *flat)
-    return outs[0], outs[1:]
+    )(rank, *operands)
 
 
 def body(tokens, queries, cotangent, kv_weight, active):
@@ -328,50 +424,65 @@
     info = jnp.concatenate(
         [seq_rank - block_ids // blocks_dev, block_ids % blocks_dev, slot_rank]
     ).astype(jnp.int32)
-    rank = seq_rank.astype(jnp.int32).reshape(1)
-
-    others = dp_rank ^ jnp.arange(dp_count, dtype=jnp.int32)
-    x_blocks = jnp.stack(
-        [lax.dynamic_slice_in_dim(tokens[0], others[m] * rows, rows, axis=1) for m in range(dp_count)]
+    rank = jnp.stack([seq_rank, dp_rank]).astype(jnp.int32)
+
+    x_by_owner = split_columns(tokens, dp_count)
+
+    dq = None
+    dkvs, terms = [], []
+    shards = []
+    for chunk in range(CHUNKS):
+        key_at, value_at = chunk * width, kvwidth // 2 + chunk * width
+        shards.append(
+            jnp.concatenate(
+                [kv_weight[:, key_at : key_at + width], kv_weight[:, value_at : value_at + width]], axis=1
+            )
+        )
+    weight_pieces, keyvals, weight_gates = gather_weights(
+        shards, x_by_owner, lambda pieces: spread(project(rank, x_by_owner, pieces))
     )
-
-    dq = None
-    weight_pieces, owns = [], []
-    dkvs, terms = [], []
+    arrivals, keyvals = [steps[1:] for steps in keyvals], [steps[0] for steps in keyvals]
+    for chunk in range(1, CHUNKS):
+        waits = arrivals[-1][1:2]
+        keyvals.append(project(after(rank, *waits), x_by_owner, weight_pieces[chunk]))
+        arrivals.append(spread(keyvals[-1])[1:])
+    x_all, gates = [], weight_gates
+    for part in x_by_owner:
+        part = lax.all_to_all(after(part, *gates), "dp", split_axis=0, concat_axis=0, tiled=True)
+        x_all.append(part)
+        gates = (part,)
+
+    backs, owns = [], []
+    gates, waits, later = (keyvals[-1],), tuple(arrivals[-1][1:2]), tuple(x_all)
     for chunk in range(CHUNKS):
-        key_at, value_at = chunk * width, (kv_heads // CHUNKS * CHUNKS) * HEAD_SIZE + chunk * width
-        shard = jnp.concatenate(
-            [kv_weight[:, key_at : key_at + width], kv_weight[:, value_at : value_at + width]], axis=1
+        kv_steps = [keyvals[chunk]] + arrivals[chunk]
+        dq, own, sends = attend(
+            after(info, *gates), queries, cotangent, kv_steps, chunk, heads, group, act_total, dq
         )
-        weight_pieces.append(gather_pieces(shard))
-    x_pieces = [x_blocks[0]] + [exchange(x_blocks[m], "dp", m) for m in range(1, dp_count)]
+        arrived, back = collect(sends, waits, later)
+        backs.append(back)
+        owns.append(own)
+        gates, waits, later = tuple(arrived), tuple(back), ()
+    gates, sums = tuple(arrived), ()
     for chunk in range(CHUNKS):
-        keyval = project(x_blocks, weight_pieces[chunk])
-        kv_steps = [keyval] + [moved(keyval, "seq", step) for step in range(1, seq_count)]
-        dq, own, sends = attend(
-            info, queries, cotangent, kv_steps, chunk, heads, group, act_total, dq
-        )
-        total = own
-        for step, send in enumerate(sends):
-            total = total + moved(send, "seq", -(step + 1)).astype(jnp.float32)
+        total = after(owns[chunk], *gates)
+        for part in backs[chunk]:
+            total = total + part.astype(jnp.float32)
         dkvs.append(total.astype(jnp.bfloat16))
-    for chunk in range(CHUNKS):
-        dkv_pieces = gather_pieces(dkvs[chunk])
+        dkv_pieces = gather_direct(dkvs[chunk])
         dests = []
         for side in range(2):
             start = side * (kvwidth // 2) + chunk * width
             for offset in range(0, width, column):
                 dests.append(((start + offset) // column, side, offset))
-        own, sends = weight_terms(rank, x_pieces, dkv_pieces, dests, column)
-        terms.append(own)
-        for at, send in enumerate(sends):
-            pairs = [(dest ^ (at + 1), dest) for dest, _, _ in dests]
-            terms.append(lax.ppermute(send, "seq", pairs).astype(jnp.float32))
+        sums = weight_terms(rank, x_all, dkv_pieces, dests, column, sums)
+        gates = ()
+    gates = (sums[0],)
+    terms = [sums[0]]
+    for at, send in enumerate(sums[1:]):
+        terms.append(exchange(send, "seq", at + 1).astype(jnp.float32))
     weight_grad = functools.reduce(lambda a, b: a + b, terms)
-    blocks = token_blocks(dkvs, weight_pieces)
-    token_grad = jnp.concatenate(
-        [lax.dynamic_index_in_dim(blocks, others[m], axis=0, keepdims=False) for m in range(dp_count)], axis=1
-    )
+    token_grad = token_grads(after(rank, *gates), dkvs, weight_pieces, rows)
     return (dq, token_grad[None], weight_grad)
 
 

time: 287 us -> 207 us (0.72)
  waiting for transfers between devices: 131 us -> 83.2 us
  local copies, waits for them, and re-layouts: 29.3 us -> 7.5 us
  Pallas kernels: 29.6 us -> 51.4 us
  between operations: 22.2 us -> 1.16 us
  starting transfers between devices: 67.1 us -> 57 us
    ppermute x12, waiting for transfers between devices: 64.8 us -> 18 us  [moved(): return lax.ppermute(value, axis, pairs)]
    ppermute x6 -> x0, waiting for transfers between devices: 21.4 us -> none  [body(): terms.append(lax.ppermute(send, 'seq', pairs).astype(jnp.float32))]
    ppermute x43 -> x31, waiting for transfers between devices: 45.2 us -> 65.1 us  [exchange(): return lax.ppermute(value, axis, [(i, i ^ mask) for i in range(count)])]
    pallas_call x5 -> x6, Pallas kernels: 24.7 us -> 38.2 us  [the longest x2 12.2 us: project(): pl.pallas_call(functools.partial(project_kernel, table), out_shape=jax.Sh...]
    unnamed x97 -> x56, local copies, waits for them, and re-layouts: 16.1 us -> 3.12 us
    ppermute x6 -> x0, starting transfers between devices: 12.6 us -> none  [body(): terms.append(lax.ppermute(send, 'seq', pairs).astype(jnp.float32))]
    pallas_call x2, Pallas kernels: 4.91 us -> 13.2 us  [attend(): pl.pallas_call(functools.partial(attend_kernel, sizes), grid=(heads,), ou...]
    ppermute x43 -> x31, starting transfers between devices: 26.2 us -> 21.6 us  [exchange(): return lax.ppermute(value, axis, [(i, i ^ mask) for i in range(count)])]
  transfers between devices with their start and end apart: 61 -> 44, of which waited for: 19 -> 18; matrix products, arithmetic and copies ran while one was open for 6% -> 3% of each run, Pallas kernels for 10% -> 22%
where the time goes in v2:
time: 207 us; the launch traced here: 205 us
  waiting for transfers between devices  83.2 us (40%)
  starting transfers between devices  57 us (28%)
  Pallas kernels  51.4 us (25%)
  local copies, waits for them, and re-layouts  7.5 us (4%)
  other arithmetic  4.86 us (2%)
    ppermute x31, waiting for transfers between devices, exchange(): return lax.ppermute(value, axis, [(i, i ^ mask) for i in range(count)])  65.1 us
    ppermute x12, starting transfers between devices, moved(): return lax.ppermute(value, axis, pairs)  31.8 us
    ppermute x31, starting transfers between devices, exchange(): return lax.ppermute(value, axis, [(i, i ^ mask) for i in range(count)])  21.6 us
    ppermute x12, waiting for transfers between devices, moved(): return lax.ppermute(value, axis, pairs)  18 us
    pallas_call x2, Pallas kernels, attend(): pl.pallas_call(functools.partial(attend_kernel, sizes), grid=(heads,), ou...  13.2 us
    pallas_call x2, Pallas kernels, project(): pl.pallas_call(functools.partial(project_kernel, table), out_shape=jax.Sh...  12.2 us
    pallas_call x2, Pallas kernels, weight_terms(): pl.pallas_call(functools.partial(weight_kernel, dests, bool(before)), out...  10.8 us
    pallas_call x1, Pallas kernels, token_grads(): pl.pallas_call(functools.partial(token_kernel, tables, tuple(indices)), o...  9.28 us
  transfers between devices with their start and end apart: 44, of which 18 were waited for; matrix products, arithmetic and copies ran while one was open for 3% of the time, Pallas kernels for 22%

profile of v2, /device:TPU:8, one launch (start us, length us, event | category | flops | bytes accessed | tf_op | source)
XLA Modules:
  0.0 205.1 jit_solution(4141731892639488906)
XLA Ops:
  0.6 1.4 fusion.2
  2.1 1.6 collective-permute-start.1
  3.7 1.5 collective-permute-start
  5.1 5.9 %split_columns.1.refs_0_ = bf16[8,256,640]{2,1,0:T(8,128)(2,1)} custom-call(bf16[1,256,5120]{2,1,0:T(8,128)(2,1)} %x_ref.1), custom_call_target="tpu_custom_call" | custom-call | flops 12000000000 | bytes 36000000 | tf_op jit(solution)/shard_map/split_columns/pallas_call | solution.py:155
  11.0 7.6 %collective-permute-done.1.refs_3_.refs_4_ = bf16[640,512]{1,0:T(8,128)(2,1)S(1)} collective-permute-done((bf16[640,512]{1,0:T(8,128)(2,1)S(1)}, bf16[640,512]{1,0:T(8,128)(2,1)S(1)}, u32[]{:S(2)}, u32[]{:S(2)}) %collective-permute-start.1) | collective-permute-done | bytes 655392 | tf_op jit(solution)/shard_map/ppermute | solution.py:43
  18.6 1.3 collective-permute-done.refs_2_.refs_3_
  20.0 1.0 slice.26
  21.0 1.6 collective-permute-start.3
  23.8 12.7 %collective-permute-done.3.refs_5_.refs_6_ = bf16[640,512]{1,0:T(8,128)(2,1)} collective-permute-done((bf16[640,512]{1,0:T(8,128)(2,1)S(1)}, bf16[640,512]{1,0:T(8,128)(2,1)}, u32[]{:S(2)}, u32[]{:S(2)}) %collective-permute-start.3) | collective-permute-done | bytes 655392 | tf_op jit(solution)/shard_map/ppermute | solution.py:43
  36.5 1.3 collective-permute-done.2.refs_4_.refs_5_
  38.4 1.0 slice.33
  39.4 1.0 slice.32
  40.4 1.0 pad_maximum_fusion
  43.0 6.1 %project.2.refs_0_.refs_1_ = bf16[256,512]{1,0:T(8,128)(2,1)} custom-call(s32[2]{0:T(128)} %pad_add_fusion.1.rank_ref, bf16[8,256,640]{2,1,0:T(8,128)(2,1)} %split_columns.1.refs_0_, bf16[640,512]{1,0:T(8,128)(2,1)} %copy-done.1, bf16[640,512]{1,0:T(8,128)(2,1)} %collective-permute-done.refs_2_.refs_3_, bf16[640,512]{1,0:T(8,128)(2,1)} %copy-done.8, ...), custom_call_target="tpu_custom_call" | custom-call | flops 16000000000 | bytes 48000000 | tf_op jit(solution)/shard_map/project/pallas_call | solution.py:187
  49.0 4.5 %collective-permute-start.9 = (bf16[256,512]{1,0:T(8,128)(2,1)}, bf16[256,512]{1,0:T(8,128)(2,1)S(1)}, u32[]{:S(2)}, u32[]{:S(2)}) collective-permute-start(bf16[256,512]{1,0:T(8,128)(2,1)} %project.2.refs_0_.refs_1_), channel_id=1, source_target_pairs={{0,2},{1,3},{4,6},{5,7},{8,10},{9,11},{12,14},{13,15},{16,18},{17,... | collective-permute-start | bytes 786440 | tf_op jit(solution)/shard_map/ppermute | solution.py:49
  53.6 4.9 %collective-permute-done.11.refs_3_.refs_14_ = bf16[640,512]{1,0:T(8,128)(2,1)S(1)} collective-permute-done((bf16[640,512]{1,0:T(8,128)(2,1)S(1)}, bf16[640,512]{1,0:T(8,128)(2,1)S(1)}, u32[]{:S(2)}, u32[]{:S(2)}) %collective-permute-start.11) | collective-permute-done | bytes 655392 | tf_op jit(solution)/shard_map/ppermute | solution.py:43
  59.2 5.6 %collective-permute-done.9.refs_4_.refs_5_ = bf16[256,512]{1,0:T(8,128)(2,1)S(1)} collective-permute-done((bf16[256,512]{1,0:T(8,128)(2,1)}, bf16[256,512]{1,0:T(8,128)(2,1)S(1)}, u32[]{:S(2)}, u32[]{:S(2)}) %collective-permute-start.9) | collective-permute-done | bytes 262176 | tf_op jit(solution)/shard_map/ppermute | solution.py:49
  66.2 1.9 collective-permute-start.15
  68.1 3.6 %all-to-all-start = ((bf16[8,256,640]{2,1,0:T(8,128)(2,1)}), bf16[8,256,640]{2,1,0:T(8,128)(2,1)S(1)}, u32[]{:S(2)}, u32[]{:S(2)}) async-start(bf16[8,256,640]{2,1,0:T(8,128)(2,1)} %split_columns.1.refs_0_), calls=%async_computation | async-start | bytes 5242880 | tf_op jit(solution)/shard_map/all_to_all | solution.py:451
  72.5 6.1 %project.3.refs_0_.refs_1_ = bf16[256,512]{1,0:T(8,128)(2,1)} custom-call(s32[2]{0:T(128)} %pad_add_fusion.1.rank_ref, bf16[8,256,640]{2,1,0:T(8,128)(2,1)} %split_columns.1.refs_0_, bf16[640,512]{1,0:T(8,128)(2,1)} %get-tuple-element.78.refs_1_.refs_12_, bf16[640,512]{1,0:T(8,128)(2,1)} %collective-permute-done.10.refs_2_.refs_13_, ...), custom_call_target="tpu_custom_call" | custom-call | flops 16000000000 | bytes 48000000 | tf_op jit(solution)/shard_map/project/pallas_call | solution.py:187
  78.6 5.9 %collective-permute-start.17 = (bf16[256,512]{1,0:T(8,128)(2,1)}, bf16[256,512]{1,0:T(8,128)(2,1)}, u32[]{:S(2)}, u32[]{:S(2)}) collective-permute-start(bf16[256,512]{1,0:T(8,128)(2,1)} %project.3.refs_0_.refs_1_), channel_id=1, source_target_pairs={{0,2},{1,3},{4,6},{5,7},{8,10},{9,11},{12,14},{13,15},{16,18},{17,... | collective-permute-start | bytes 786440 | tf_op jit(solution)/shard_map/ppermute | solution.py:49
  85.2 6.6 %attend.2 = (bf16[1,256,2560]{2,1,0:T(8,128)(2,1)}, f32[256,512]{1,0:T(8,128)}, bf16[256,512]{1,0:T(8,128)(2,1)}, bf16[256,512]{1,0:T(8,128)(2,1)}, bf16[256,512]{1,0:T(8,128)(2,1)}) custom-call(s32[10]{0:T(128)} %pad_add_fusion.info_ref, bf16[1,256,2560]{2,1,0:T(8,128)(2,1)} %q_ref.3, bf16[1,256,2560]{2,1,0:T(8,128)(2,1)} %g_ref.3, ...), custom_call_target="tpu_custom_call" | custom-call | flops 35999997952 | bytes 108000000 | tf_op jit(solution)/shard_map/attend/pallas_call | solution.py:298
  91.8 4.0 %collective-permute-done.17.refs_4_.refs_5_ = bf16[256,512]{1,0:T(8,128)(2,1)} collective-permute-done((bf16[256,512]{1,0:T(8,128)(2,1)}, bf16[256,512]{1,0:T(8,128)(2,1)}, u32[]{:S(2)}, u32[]{:S(2)}) %collective-permute-start.17) | collective-permute-done | bytes 262176 | tf_op jit(solution)/shard_map/ppermute | solution.py:49
  96.5 1.9 collective-permute-start.19
  98.4 1.4 collective-permute-start.20
  99.8 3.9 %collective-permute-start.21 = (bf16[256,512]{1,0:T(8,128)(2,1)}, bf16[256,512]{1,0:T(8,128)(2,1)S(1)}, u32[]{:S(2)}, u32[]{:S(2)}) collective-permute-start(bf16[256,512]{1,0:T(8,128)(2,1)} %get-tuple-element.53), channel_id=1, source_target_pairs={{1,0},{2,1},{3,2},{5,4},{6,5},{7,6},{9,8},{10,9},{11,10},{13,12},{... | collective-permute-start | bytes 786440 | tf_op jit(solution)/shard_map/ppermute | solution.py:49
  103.8 1.0 add_convert_fusion.3
  104.8 1.5 collective-permute-start.22
  107.1 6.7 %attend.3 = (bf16[1,256,2560]{2,1,0:T(8,128)(2,1)}, f32[256,512]{1,0:T(8,128)}, bf16[256,512]{1,0:T(8,128)(2,1)}, bf16[256,512]{1,0:T(8,128)(2,1)}, bf16[256,512]{1,0:T(8,128)(2,1)}) custom-call(s32[10]{0:T(128)} %pad_add_fusion.info_ref, bf16[1,256,2560]{2,1,0:T(8,128)(2,1)} %q_ref.3, ...), custom_call_target="tpu_custom_call", output_to_operand_aliasing={{0}: (11, {})} | custom-call | flops 35999997952 | bytes 108000000 | tf_op jit(solution)/shard_map/attend/pallas_call | solution.py:298
  113.8 6.2 %collective-permute-done.21 = bf16[256,512]{1,0:T(8,128)(2,1)S(1)} collective-permute-done((bf16[256,512]{1,0:T(8,128)(2,1)}, bf16[256,512]{1,0:T(8,128)(2,1)S(1)}, u32[]{:S(2)}, u32[]{:S(2)}) %collective-permute-start.21) | collective-permute-done | bytes 262176 | tf_op jit(solution)/shard_map/ppermute | solution.py:49
  120.6 7.5 %collective-permute-start.23 = (bf16[256,512]{1,0:T(8,128)(2,1)}, bf16[256,512]{1,0:T(8,128)(2,1)S(1)}, u32[]{:S(2)}, u32[]{:S(2)}) collective-permute-start(bf16[256,512]{1,0:T(8,128)(2,1)} %get-tuple-element.57), channel_id=1, source_target_pairs={{1,0},{2,1},{3,2},{5,4},{6,5},{7,6},{9,8},{10,9},{11,10},{13,12},{... | collective-permute-start | bytes 786440 | tf_op jit(solution)/shard_map/ppermute | solution.py:49
  128.3 2.4 %collective-permute-start.38 = (bf16[256,512]{1,0:T(8,128)(2,1)S(1)}, bf16[256,512]{1,0:T(8,128)(2,1)S(1)}, u32[]{:S(2)}, u32[]{:S(2)}) collective-permute-start(bf16[256,512]{1,0:T(8,128)(2,1)S(1)} %add_convert_fusion.refs_1_.refs_0_), channel_id=1, source_target_pairs={{0,24},{4,28},{8,16},{12,20},{16,8},{20,12},{24,0},{28,4},{1,25},{... | collective-permute-start | bytes 786440 | tf_op jit(solution)/shard_map/ppermute | solution.py:43
  131.3 1.3 collective-permute-start.25
  133.3 4.7 %collective-permute-done.38.refs_7_ = bf16[256,512]{1,0:T(8,128)(2,1)S(1)} collective-permute-done((bf16[256,512]{1,0:T(8,128)(2,1)S(1)}, bf16[256,512]{1,0:T(8,128)(2,1)S(1)}, u32[]{:S(2)}, u32[]{:S(2)}) %collective-permute-start.38) | collective-permute-done | bytes 262176 | tf_op jit(solution)/shard_map/ppermute | solution.py:43
  138.0 3.4 %collective-permute-done.36.refs_5_ = bf16[256,512]{1,0:T(8,128)(2,1)S(1)} collective-permute-done((bf16[256,512]{1,0:T(8,128)(2,1)S(1)}, bf16[256,512]{1,0:T(8,128)(2,1)S(1)}, u32[]{:S(2)}, u32[]{:S(2)}) %collective-permute-start.36) | collective-permute-done | bytes 262176 | tf_op jit(solution)/shard_map/ppermute | solution.py:43
  141.5 2.1 %collective-permute-done.25 = bf16[256,512]{1,0:T(8,128)(2,1)S(1)} collective-permute-done((bf16[256,512]{1,0:T(8,128)(2,1)S(1)}, bf16[256,512]{1,0:T(8,128)(2,1)S(1)}, u32[]{:S(2)}, u32[]{:S(2)}) %collective-permute-start.25) | collective-permute-done | bytes 262176 | tf_op jit(solution)/shard_map/ppermute | solution.py:49
  143.7 2.0 collective-permute-start.31
  145.7 1.4 collective-permute-start.29
  147.8 6.1 %collective-permute-done.31.refs_7_ = bf16[256,512]{1,0:T(8,128)(2,1)S(1)} collective-permute-done((bf16[256,512]{1,0:T(8,128)(2,1)S(1)}, bf16[256,512]{1,0:T(8,128)(2,1)S(1)}, u32[]{:S(2)}, u32[]{:S(2)}) %collective-permute-start.31) | collective-permute-done | bytes 262176 | tf_op jit(solution)/shard_map/ppermute | solution.py:43
  153.9 3.0 %collective-permute-done.29.refs_5_ = bf16[256,512]{1,0:T(8,128)(2,1)S(1)} collective-permute-done((bf16[256,512]{1,0:T(8,128)(2,1)S(1)}, bf16[256,512]{1,0:T(8,128)(2,1)S(1)}, u32[]{:S(2)}, u32[]{:S(2)}) %collective-permute-start.29) | collective-permute-done | bytes 262176 | tf_op jit(solution)/shard_map/ppermute | solution.py:43
  158.2 5.1 %weight_grad.2 = (f32[640,256]{1,0:T(8,128)}, bf16[640,256]{1,0:T(8,128)(2,1)}, bf16[640,256]{1,0:T(8,128)(2,1)}, bf16[640,256]{1,0:T(8,128)(2,1)}) custom-call(s32[2]{0:T(128)} %pad_add_fusion.1.rank_ref, bf16[8,256,640]{2,1,0:T(8,128)(2,1)} %copy-done, bf16[256,512]{1,0:T(8,128)(2,1)} %copy-done.5, bf16[256,512]{1,0:T(8,128)(2,1)} %copy-done.14, ...), custom_call_target="tpu_custom_call" | custom-call | flops 16000000000 | bytes 48000000 | tf_op jit(solution)/shard_map/weight_grad/pallas_call | solution.py:394
  164.3 5.7 %weight_grad.3 = (f32[640,256]{1,0:T(8,128)}, bf16[640,256]{1,0:T(8,128)(2,1)}, bf16[640,256]{1,0:T(8,128)(2,1)}, bf16[640,256]{1,0:T(8,128)(2,1)}) custom-call(s32[2]{0:T(128)} %pad_add_fusion.1.rank_ref, bf16[8,256,640]{2,1,0:T(8,128)(2,1)} %copy-done, bf16[256,512]{1,0:T(8,128)(2,1)} %copy-done.6, bf16[256,512]{1,0:T(8,128)(2,1)} %copy-done.21, ...), custom_call_target="tpu_custom_call" | custom-call | flops 16000000000 | bytes 48000000 | tf_op jit(solution)/shard_map/weight_grad/pallas_call | solution.py:394
  170.0 2.8 %collective-permute-start.40 = (bf16[640,256]{1,0:T(8,128)(2,1)}, bf16[640,256]{1,0:T(8,128)(2,1)S(1)}, u32[]{:S(2)}, u32[]{:S(2)}) collective-permute-start(bf16[640,256]{1,0:T(8,128)(2,1)} %get-tuple-element.70), channel_id=1, source_target_pairs={{0,1},{1,0},{2,3},{3,2},{4,5},{5,4},{6,7},{7,6},{8,9},{9,8},{10,11... | collective-permute-start | bytes 983048 | tf_op jit(solution)/shard_map/ppermute | solution.py:43
  172.9 2.7 %collective-permute-start.41 = (bf16[640,256]{1,0:T(8,128)(2,1)}, bf16[640,256]{1,0:T(8,128)(2,1)S(1)}, u32[]{:S(2)}, u32[]{:S(2)}) collective-permute-start(bf16[640,256]{1,0:T(8,128)(2,1)} %get-tuple-element.71), channel_id=1, source_target_pairs={{0,2},{1,3},{2,0},{3,1},{4,6},{5,7},{6,4},{7,5},{8,10},{9,11},{10,... | collective-permute-start | bytes 983048 | tf_op jit(solution)/shard_map/ppermute | solution.py:43
  175.6 9.3 %token_grads.1 = bf16[256,5120]{1,0:T(8,128)(2,1)} custom-call(s32[2]{0:T(128)} %pad_add_fusion.1.rank_ref, bf16[256,512]{1,0:T(8,128)(2,1)} %copy-done.5, bf16[256,512]{1,0:T(8,128)(2,1)} %copy-done.6, bf16[640,512]{1,0:T(8,128)(2,1)} %copy-done.1, bf16[640,512]{1,0:T(8,128)(2,1)} %collective-permute-done.refs_2_.refs_3_, bf16[640,512]{1,0:T(8,128)(2,1)} %copy-done.8, ...), custom_call_target="tpu_custom_call" | custom-call | flops 32000000000 | bytes 96000000 | tf_op jit(solution)/shard_map/token_grads/pallas_call | solution.py:356
  184.8 2.6 %collective-permute-done.40 = bf16[640,256]{1,0:T(8,128)(2,1)S(1)} collective-permute-done((bf16[640,256]{1,0:T(8,128)(2,1)}, bf16[640,256]{1,0:T(8,128)(2,1)S(1)}, u32[]{:S(2)}, u32[]{:S(2)}) %collective-permute-start.40) | collective-permute-done | bytes 327712 | tf_op jit(solution)/shard_map/ppermute | solution.py:43
  187.4 10.6 %collective-permute-done.41 = bf16[640,256]{1,0:T(8,128)(2,1)S(1)} collective-permute-done((bf16[640,256]{1,0:T(8,128)(2,1)}, bf16[640,256]{1,0:T(8,128)(2,1)S(1)}, u32[]{:S(2)}, u32[]{:S(2)}) %collective-permute-start.41) | collective-permute-done | bytes 327712 | tf_op jit(solution)/shard_map/ppermute | solution.py:43
  198.1 6.1 %collective-permute-done.42 = bf16[640,256]{1,0:T(8,128)(2,1)S(1)} collective-permute-done((bf16[640,256]{1,0:T(8,128)(2,1)}, bf16[640,256]{1,0:T(8,128)(2,1)S(1)}, u32[]{:S(2)}, u32[]{:S(2)}) %collective-permute-start.42) | collective-permute-done | bytes 327712 | tf_op jit(solution)/shard_map/ppermute | solution.py:43
  (125 shorter events, 14.4 us)
Async XLA Ops:
  2.1 16.5 %collective-permute-start.1 = (bf16[640,512]{1,0:T(8,128)(2,1)S(1)}, bf16[640,512]{1,0:T(8,128)(2,1)S(1)}, u32[]{:S(2)}, u32[]{:S(2)}) collective-permute-start(bf16[640,512]{1,0:T(8,128)(2,1)S(1)} %pad_maximum_fusion.5.refs_1_.refs_2_), channel_id=1, source_target_pairs={{0,16},{4,20},{8,24},{12,28},{16,0},{20,4},{24,8},{28,12},{1,17},{... | collective-permute-start | bytes 1966088 | tf_op jit(solution)/shard_map/ppermute | solution.py:43
  3.7 16.3 %collective-permute-start = (bf16[640,512]{1,0:T(8,128)(2,1)S(1)}, bf16[640,512]{1,0:T(8,128)(2,1)}, u32[]{:S(2)}, u32[]{:S(2)}) collective-permute-start(bf16[640,512]{1,0:T(8,128)(2,1)S(1)} %pad_maximum_fusion.5.refs_1_.refs_2_), channel_id=1, source_target_pairs={{0,8},{4,12},{8,0},{12,4},{16,24},{20,28},{24,16},{28,20},{1,9},{5... | collective-permute-start | bytes 1966088 | tf_op jit(solution)/shard_map/ppermute | solution.py:43
  21.0 15.5 %collective-permute-start.3 = (bf16[640,512]{1,0:T(8,128)(2,1)S(1)}, bf16[640,512]{1,0:T(8,128)(2,1)}, u32[]{:S(2)}, u32[]{:S(2)}) collective-permute-start(bf16[640,512]{1,0:T(8,128)(2,1)S(1)} %pad_maximum_fusion.2), channel_id=1, source_target_pairs={{0,8},{4,12},{8,0},{12,4},{16,24},{20,28},{24,16},{28,20},{1,9},{5... | collective-permute-start | bytes 1966088 | tf_op jit(solution)/shard_map/ppermute | solution.py:43
  22.6 15.2 %collective-permute-start.2 = (bf16[640,512]{1,0:T(8,128)(2,1)S(1)}, bf16[640,512]{1,0:T(8,128)(2,1)}, u32[]{:S(2)}, u32[]{:S(2)}) collective-permute-start(bf16[640,512]{1,0:T(8,128)(2,1)S(1)} %pad_maximum_fusion.4), channel_id=1, source_target_pairs={{0,16},{4,20},{8,24},{12,28},{16,0},{20,4},{24,8},{28,12},{1,17},{... | collective-permute-start | bytes 1966088 | tf_op jit(solution)/shard_map/ppermute | solution.py:43
  23.2 18.2 %collective-permute-start.4 = (bf16[640,512]{1,0:T(8,128)(2,1)S(1)}, bf16[640,512]{1,0:T(8,128)(2,1)}, u32[]{:S(2)}, u32[]{:S(2)}) collective-permute-start(bf16[640,512]{1,0:T(8,128)(2,1)S(1)} %pad_maximum_fusion.5.refs_1_.refs_2_), channel_id=1, source_target_pairs={{0,4},{4,0},{8,12},{12,8},{16,20},{20,16},{24,28},{28,24},{1,5},{5... | collective-permute-start | bytes 1966088 | tf_op jit(solution)/shard_map/ppermute | solution.py:43
  23.2 19.0 %collective-permute-start.6 = (bf16[640,512]{1,0:T(8,128)(2,1)S(1)}, bf16[640,512]{1,0:T(8,128)(2,1)}, u32[]{:S(2)}, u32[]{:S(2)}) collective-permute-start(bf16[640,512]{1,0:T(8,128)(2,1)S(1)} %collective-permute-done.1.refs_3_.refs_4_), channel_id=1, source_target_pairs={{0,4},{4,0},{8,12},{12,8},{16,20},{20,16},{24,28},{28,24},{1,5},{5... | collective-permute-start | bytes 1966088 | tf_op jit(solution)/shard_map/ppermute | solution.py:43
  23.7 19.2 %collective-permute-start.5 = (bf16[640,512]{1,0:T(8,128)(2,1)}, bf16[640,512]{1,0:T(8,128)(2,1)}, u32[]{:S(2)}, u32[]{:S(2)}) collective-permute-start(bf16[640,512]{1,0:T(8,128)(2,1)} %collective-permute-done.refs_2_.refs_3_), channel_id=1, source_target_pairs={{0,4},{4,0},{8,12},{12,8},{16,20},{20,16},{24,28},{28,24},{1,5},{5... | collective-permute-start | bytes 1966088 | tf_op jit(solution)/shard_map/ppermute | solution.py:43
  36.5 6.5 %collective-permute-start.8 = (bf16[640,512]{1,0:T(8,128)(2,1)}, bf16[640,512]{1,0:T(8,128)(2,1)}, u32[]{:S(2)}, u32[]{:S(2)}) collective-permute-start(bf16[640,512]{1,0:T(8,128)(2,1)} %collective-permute-done.3.refs_5_.refs_6_), channel_id=1, source_target_pairs={{0,4},{4,0},{8,12},{12,8},{16,20},{20,16},{24,28},{28,24},{1,5},{5... | collective-permute-start | bytes 1966088 | tf_op jit(solution)/shard_map/ppermute | solution.py:43
  37.8 5.1 %collective-permute-start.7 = (bf16[640,512]{1,0:T(8,128)(2,1)}, bf16[640,512]{1,0:T(8,128)(2,1)}, u32[]{:S(2)}, u32[]{:S(2)}) collective-permute-start(bf16[640,512]{1,0:T(8,128)(2,1)} %collective-permute-done.2.refs_4_.refs_5_), channel_id=1, source_target_pairs={{0,4},{4,0},{8,12},{12,8},{16,20},{20,16},{24,28},{28,24},{1,5},{5... | collective-permute-start | bytes 1966088 | tf_op jit(solution)/shard_map/ppermute | solution.py:43
  41.4 17.1 %collective-permute-start.11 = (bf16[640,512]{1,0:T(8,128)(2,1)S(1)}, bf16[640,512]{1,0:T(8,128)(2,1)S(1)}, u32[]{:S(2)}, u32[]{:S(2)}) collective-permute-start(bf16[640,512]{1,0:T(8,128)(2,1)S(1)} %get-tuple-element.77), channel_id=1, source_target_pairs={{0,16},{4,20},{8,24},{12,28},{16,0},{20,4},{24,8},{28,12},{1,17},{... | collective-permute-start | bytes 1966088 | tf_op jit(solution)/shard_map/ppermute | solution.py:43
  42.3 23.1 %copy-start.9 = (s32[1,4]{1,0:T(1,128)S(1)}, s32[1,4]{1,0:T(1,128)}, u32[]{:S(2)}) copy-start(s32[1,4]{1,0:T(1,128)} %param.9) | copy-start | bytes 52
  42.3 17.0 %collective-permute-start.10 = (bf16[640,512]{1,0:T(8,128)(2,1)S(1)}, bf16[640,512]{1,0:T(8,128)(2,1)}, u32[]{:S(2)}, u32[]{:S(2)}) collective-permute-start(bf16[640,512]{1,0:T(8,128)(2,1)S(1)} %get-tuple-element.79), channel_id=1, source_target_pairs={{0,8},{4,12},{8,0},{12,4},{16,24},{20,28},{24,16},{28,20},{1,9},{5... | collective-permute-start | bytes 1966088 | tf_op jit(solution)/shard_map/ppermute | solution.py:43
  49.0 15.8 %collective-permute-start.9 = (bf16[256,512]{1,0:T(8,128)(2,1)}, bf16[256,512]{1,0:T(8,128)(2,1)S(1)}, u32[]{:S(2)}, u32[]{:S(2)}) collective-permute-start(bf16[256,512]{1,0:T(8,128)(2,1)} %project.2.refs_0_.refs_1_), channel_id=1, source_target_pairs={{0,2},{1,3},{4,6},{5,7},{8,10},{9,11},{12,14},{13,15},{16,18},{17,... | collective-permute-start | bytes 786440 | tf_op jit(solution)/shard_map/ppermute | solution.py:49
  53.6 18.9 %collective-permute-start.12 = (bf16[640,512]{1,0:T(8,128)(2,1)}, bf16[640,512]{1,0:T(8,128)(2,1)}, u32[]{:S(2)}, u32[]{:S(2)}) collective-permute-start(bf16[640,512]{1,0:T(8,128)(2,1)} %get-tuple-element.78.refs_1_.refs_12_), channel_id=1, source_target_pairs={{0,4},{4,0},{8,12},{12,8},{16,20},{20,16},{24,28},{28,24},{1,5},{5... | collective-permute-start | bytes 1966088 | tf_op jit(solution)/shard_map/ppermute | solution.py:43
  64.9 7.6 %collective-permute-start.13 = (bf16[640,512]{1,0:T(8,128)(2,1)}, bf16[640,512]{1,0:T(8,128)(2,1)}, u32[]{:S(2)}, u32[]{:S(2)}) collective-permute-start(bf16[640,512]{1,0:T(8,128)(2,1)} %collective-permute-done.10.refs_2_.refs_13_), channel_id=1, source_target_pairs={{0,4},{4,0},{8,12},{12,8},{16,20},{20,16},{24,28},{28,24},{1,5},{5... | collective-permute-start | bytes 1966088 | tf_op jit(solution)/shard_map/ppermute | solution.py:43
  64.9 7.6 %collective-permute-start.14 = (bf16[640,512]{1,0:T(8,128)(2,1)S(1)}, bf16[640,512]{1,0:T(8,128)(2,1)}, u32[]{:S(2)}, u32[]{:S(2)}) collective-permute-start(bf16[640,512]{1,0:T(8,128)(2,1)S(1)} %collective-permute-done.11.refs_3_.refs_14_), channel_id=1, source_target_pairs={{0,4},{4,0},{8,12},{12,8},{16,20},{20,16},{24,28},{28,24},{1,5},{5... | collective-permute-start | bytes 1966088 | tf_op jit(solution)/shard_map/ppermute | solution.py:43
  66.2 18.3 %collective-permute-start.15 = (bf16[256,512]{1,0:T(8,128)(2,1)}, bf16[256,512]{1,0:T(8,128)(2,1)}, u32[]{:S(2)}, u32[]{:S(2)}) collective-permute-start(bf16[256,512]{1,0:T(8,128)(2,1)} %project.2.refs_0_.refs_1_), channel_id=1, source_target_pairs={{0,1},{1,2},{2,3},{4,5},{5,6},{6,7},{8,9},{9,10},{10,11},{12,13},{... | collective-permute-start | bytes 786440 | tf_op jit(solution)/shard_map/ppermute | solution.py:49
  68.1 36.6 %all-to-all-start = ((bf16[8,256,640]{2,1,0:T(8,128)(2,1)}), bf16[8,256,640]{2,1,0:T(8,128)(2,1)S(1)}, u32[]{:S(2)}, u32[]{:S(2)}) async-start(bf16[8,256,640]{2,1,0:T(8,128)(2,1)} %split_columns.1.refs_0_), calls=%async_computation | async-start | bytes 5242880 | tf_op jit(solution)/shard_map/all_to_all | solution.py:451
  71.8 12.7 %collective-permute-start.16 = (bf16[256,512]{1,0:T(8,128)(2,1)S(1)}, bf16[256,512]{1,0:T(8,128)(2,1)S(1)}, u32[]{:S(2)}, u32[]{:S(2)}) collective-permute-start(bf16[256,512]{1,0:T(8,128)(2,1)S(1)} %collective-permute-done.9.refs_4_.refs_5_), channel_id=1, source_target_pairs={{2,3},{6,7},{10,11},{14,15},{18,19},{22,23},{26,27},{30,31}} | collective-permute-start | bytes 786440 | tf_op jit(solution)/shard_map/ppermute | solution.py:49
  78.6 17.2 %collective-permute-start.17 = (bf16[256,512]{1,0:T(8,128)(2,1)}, bf16[256,512]{1,0:T(8,128)(2,1)}, u32[]{:S(2)}, u32[]{:S(2)}) collective-permute-start(bf16[256,512]{1,0:T(8,128)(2,1)} %project.3.refs_0_.refs_1_), channel_id=1, source_target_pairs={{0,2},{1,3},{4,6},{5,7},{8,10},{9,11},{12,14},{13,15},{16,18},{17,... | collective-permute-start | bytes 786440 | tf_op jit(solution)/shard_map/ppermute | solution.py:49
  95.8 7.9 %collective-permute-start.18 = (bf16[256,512]{1,0:T(8,128)(2,1)}, bf16[256,512]{1,0:T(8,128)(2,1)S(1)}, u32[]{:S(2)}, u32[]{:S(2)}) collective-permute-start(bf16[256,512]{1,0:T(8,128)(2,1)} %get-tuple-element.45), channel_id=1, source_target_pairs={{3,2},{7,6},{11,10},{15,14},{19,18},{23,22},{27,26},{31,30}} | collective-permute-start | bytes 786440 | tf_op jit(solution)/shard_map/ppermute | solution.py:49
  96.5 9.9 %collective-permute-start.19 = (bf16[256,512]{1,0:T(8,128)(2,1)}, bf16[256,512]{1,0:T(8,128)(2,1)S(1)}, u32[]{:S(2)}, u32[]{:S(2)}) collective-permute-start(bf16[256,512]{1,0:T(8,128)(2,1)} %project.3.refs_0_.refs_1_), channel_id=1, source_target_pairs={{0,1},{1,2},{2,3},{4,5},{5,6},{6,7},{8,9},{9,10},{10,11},{12,13},{... | collective-permute-start | bytes 786440 | tf_op jit(solution)/shard_map/ppermute | solution.py:49
  98.4 8.0 %collective-permute-start.20 = (bf16[256,512]{1,0:T(8,128)(2,1)}, bf16[256,512]{1,0:T(8,128)(2,1)}, u32[]{:S(2)}, u32[]{:S(2)}) collective-permute-start(bf16[256,512]{1,0:T(8,128)(2,1)} %collective-permute-done.17.refs_4_.refs_5_), channel_id=1, source_target_pairs={{2,3},{6,7},{10,11},{14,15},{18,19},{22,23},{26,27},{30,31}} | collective-permute-start | bytes 786440 | tf_op jit(solution)/shard_map/ppermute | solution.py:49
  99.8 20.1 %collective-permute-start.21 = (bf16[256,512]{1,0:T(8,128)(2,1)}, bf16[256,512]{1,0:T(8,128)(2,1)S(1)}, u32[]{:S(2)}, u32[]{:S(2)}) collective-permute-start(bf16[256,512]{1,0:T(8,128)(2,1)} %get-tuple-element.53), channel_id=1, source_target_pairs={{1,0},{2,1},{3,2},{5,4},{6,5},{7,6},{9,8},{10,9},{11,10},{13,12},{... | collective-permute-start | bytes 786440 | tf_op jit(solution)/shard_map/ppermute | solution.py:49
  104.8 15.1 %collective-permute-start.22 = (bf16[256,512]{1,0:T(8,128)(2,1)S(1)}, bf16[256,512]{1,0:T(8,128)(2,1)S(1)}, u32[]{:S(2)}, u32[]{:S(2)}) collective-permute-start(bf16[256,512]{1,0:T(8,128)(2,1)S(1)} %add_convert_fusion.3), channel_id=1, source_target_pairs={{2,0},{3,1},{6,4},{7,5},{10,8},{11,9},{14,12},{15,13},{18,16},{19,... | collective-permute-start | bytes 786440 | tf_op jit(solution)/shard_map/ppermute | solution.py:49
  113.8 29.8 %copy-start.4 = (f32[256,512]{1,0:T(8,128)S(1)}, f32[256,512]{1,0:T(8,128)}, u32[]{:S(2)}) copy-start(f32[256,512]{1,0:T(8,128)} %get-tuple-element.50) | copy-start | bytes 1572868
  119.9 8.2 %collective-permute-start.24 = (bf16[256,512]{1,0:T(8,128)(2,1)}, bf16[256,512]{1,0:T(8,128)(2,1)S(1)}, u32[]{:S(2)}, u32[]{:S(2)}) collective-permute-start(bf16[256,512]{1,0:T(8,128)(2,1)} %get-tuple-element.61), channel_id=1, source_target_pairs={{3,2},{7,6},{11,10},{15,14},{19,18},{23,22},{27,26},{31,30}} | collective-permute-start | bytes 786440 | tf_op jit(solution)/shard_map/ppermute | solution.py:49
  120.6 12.7 %collective-permute-start.23 = (bf16[256,512]{1,0:T(8,128)(2,1)}, bf16[256,512]{1,0:T(8,128)(2,1)S(1)}, u32[]{:S(2)}, u32[]{:S(2)}) collective-permute-start(bf16[256,512]{1,0:T(8,128)(2,1)} %get-tuple-element.57), channel_id=1, source_target_pairs={{1,0},{2,1},{3,2},{5,4},{6,5},{7,6},{9,8},{10,9},{11,10},{13,12},{... | collective-permute-start | bytes 786440 | tf_op jit(solution)/shard_map/ppermute | solution.py:49
  128.3 29.1 %copy-start.5 = (bf16[256,512]{1,0:T(8,128)(2,1)}, bf16[256,512]{1,0:T(8,128)(2,1)S(1)}, u32[]{:S(2)}) copy-start(bf16[256,512]{1,0:T(8,128)(2,1)S(1)} %add_convert_fusion.refs_1_.refs_0_) | copy-start | bytes 786436
  128.3 9.7 %collective-permute-start.38 = (bf16[256,512]{1,0:T(8,128)(2,1)S(1)}, bf16[256,512]{1,0:T(8,128)(2,1)S(1)}, u32[]{:S(2)}, u32[]{:S(2)}) collective-permute-start(bf16[256,512]{1,0:T(8,128)(2,1)S(1)} %add_convert_fusion.refs_1_.refs_0_), channel_id=1, source_target_pairs={{0,24},{4,28},{8,16},{12,20},{16,8},{20,12},{24,0},{28,4},{1,25},{... | collective-permute-start | bytes 786440 | tf_op jit(solution)/shard_map/ppermute | solution.py:43
  130.7 10.7 %collective-permute-start.36 = (bf16[256,512]{1,0:T(8,128)(2,1)S(1)}, bf16[256,512]{1,0:T(8,128)(2,1)S(1)}, u32[]{:S(2)}, u32[]{:S(2)}) collective-permute-start(bf16[256,512]{1,0:T(8,128)(2,1)S(1)} %add_convert_fusion.refs_1_.refs_0_), channel_id=1, source_target_pairs={{0,16},{4,20},{8,24},{12,28},{16,0},{20,4},{24,8},{28,12},{1,17},{... | collective-permute-start | bytes 786440 | tf_op jit(solution)/shard_map/ppermute | solution.py:43
  131.3 12.2 %collective-permute-start.25 = (bf16[256,512]{1,0:T(8,128)(2,1)S(1)}, bf16[256,512]{1,0:T(8,128)(2,1)S(1)}, u32[]{:S(2)}, u32[]{:S(2)}) collective-permute-start(bf16[256,512]{1,0:T(8,128)(2,1)S(1)} %add_convert_fusion.2), channel_id=1, source_target_pairs={{2,0},{3,1},{6,4},{7,5},{10,8},{11,9},{14,12},{15,13},{18,16},{19,... | collective-permute-start | bytes 786440 | tf_op jit(solution)/shard_map/ppermute | solution.py:49
  132.6 13.0 %collective-permute-start.34 = (bf16[256,512]{1,0:T(8,128)(2,1)S(1)}, bf16[256,512]{1,0:T(8,128)(2,1)S(1)}, u32[]{:S(2)}, u32[]{:S(2)}) collective-permute-start(bf16[256,512]{1,0:T(8,128)(2,1)S(1)} %add_convert_fusion.refs_1_.refs_0_), channel_id=1, source_target_pairs={{0,8},{4,12},{8,0},{12,4},{16,24},{20,28},{24,16},{28,20},{1,9},{5... | collective-permute-start | bytes 786440 | tf_op jit(solution)/shard_map/ppermute | solution.py:43
  133.3 13.8 %collective-permute-start.33 = (bf16[256,512]{1,0:T(8,128)(2,1)S(1)}, bf16[256,512]{1,0:T(8,128)(2,1)S(1)}, u32[]{:S(2)}, u32[]{:S(2)}) collective-permute-start(bf16[256,512]{1,0:T(8,128)(2,1)S(1)} %add_convert_fusion.refs_1_.refs_0_), channel_id=1, source_target_pairs={{0,4},{4,0},{8,12},{12,8},{16,20},{20,16},{24,28},{28,24},{1,5},{5... | collective-permute-start | bytes 786440 | tf_op jit(solution)/shard_map/ppermute | solution.py:43
  138.0 9.2 %collective-permute-start.39 = (bf16[256,512]{1,0:T(8,128)(2,1)S(1)}, bf16[256,512]{1,0:T(8,128)(2,1)S(1)}, u32[]{:S(2)}, u32[]{:S(2)}) collective-permute-start(bf16[256,512]{1,0:T(8,128)(2,1)S(1)} %collective-permute-done.38.refs_7_), channel_id=1, source_target_pairs={{0,4},{4,0},{8,12},{12,8},{16,20},{20,16},{24,28},{28,24},{1,5},{5... | collective-permute-start | bytes 786440 | tf_op jit(solution)/shard_map/ppermute | solution.py:43
  141.4 5.8 %collective-permute-start.37 = (bf16[256,512]{1,0:T(8,128)(2,1)S(1)}, bf16[256,512]{1,0:T(8,128)(2,1)S(1)}, u32[]{:S(2)}, u32[]{:S(2)}) collective-permute-start(bf16[256,512]{1,0:T(8,128)(2,1)S(1)} %collective-permute-done.36.refs_5_), channel_id=1, source_target_pairs={{0,4},{4,0},{8,12},{12,8},{16,20},{20,16},{24,28},{28,24},{1,5},{5... | collective-permute-start | bytes 786440 | tf_op jit(solution)/shard_map/ppermute | solution.py:43
  143.7 10.2 %collective-permute-start.31 = (bf16[256,512]{1,0:T(8,128)(2,1)S(1)}, bf16[256,512]{1,0:T(8,128)(2,1)S(1)}, u32[]{:S(2)}, u32[]{:S(2)}) collective-permute-start(bf16[256,512]{1,0:T(8,128)(2,1)S(1)} %add_convert_fusion.1.refs_1_), channel_id=1, source_target_pairs={{0,24},{4,28},{8,16},{12,20},{16,8},{20,12},{24,0},{28,4},{1,25},{... | collective-permute-start | bytes 786440 | tf_op jit(solution)/shard_map/ppermute | solution.py:43
  145.7 11.2 %collective-permute-start.29 = (bf16[256,512]{1,0:T(8,128)(2,1)S(1)}, bf16[256,512]{1,0:T(8,128)(2,1)S(1)}, u32[]{:S(2)}, u32[]{:S(2)}) collective-permute-start(bf16[256,512]{1,0:T(8,128)(2,1)S(1)} %add_convert_fusion.1.refs_1_), channel_id=1, source_target_pairs={{0,16},{4,20},{8,24},{12,28},{16,0},{20,4},{24,8},{28,12},{1,17},{... | collective-permute-start | bytes 786440 | tf_op jit(solution)/shard_map/ppermute | solution.py:43
  147.1 9.8 %collective-permute-start.27 = (bf16[256,512]{1,0:T(8,128)(2,1)S(1)}, bf16[256,512]{1,0:T(8,128)(2,1)S(1)}, u32[]{:S(2)}, u32[]{:S(2)}) collective-permute-start(bf16[256,512]{1,0:T(8,128)(2,1)S(1)} %add_convert_fusion.1.refs_1_), channel_id=1, source_target_pairs={{0,8},{4,12},{8,0},{12,4},{16,24},{20,28},{24,16},{28,20},{1,9},{5... | collective-permute-start | bytes 786440 | tf_op jit(solution)/shard_map/ppermute | solution.py:43
  147.2 10.2 %collective-permute-start.35 = (bf16[256,512]{1,0:T(8,128)(2,1)S(1)}, bf16[256,512]{1,0:T(8,128)(2,1)S(1)}, u32[]{:S(2)}, u32[]{:S(2)}) collective-permute-start(bf16[256,512]{1,0:T(8,128)(2,1)S(1)} %collective-permute-done.34.refs_3_), channel_id=1, source_target_pairs={{0,4},{4,0},{8,12},{12,8},{16,20},{20,16},{24,28},{28,24},{1,5},{5... | collective-permute-start | bytes 786440 | tf_op jit(solution)/shard_map/ppermute | solution.py:43
  147.3 16.0 %collective-permute-start.26 = (bf16[256,512]{1,0:T(8,128)(2,1)S(1)}, bf16[256,512]{1,0:T(8,128)(2,1)S(1)}, u32[]{:S(2)}, u32[]{:S(2)}) collective-permute-start(bf16[256,512]{1,0:T(8,128)(2,1)S(1)} %add_convert_fusion.1.refs_1_), channel_id=1, source_target_pairs={{0,4},{4,0},{8,12},{12,8},{16,20},{20,16},{24,28},{28,24},{1,5},{5... | collective-permute-start | bytes 786440 | tf_op jit(solution)/shard_map/ppermute | solution.py:43
  153.9 9.5 %collective-permute-start.32 = (bf16[256,512]{1,0:T(8,128)(2,1)S(1)}, bf16[256,512]{1,0:T(8,128)(2,1)S(1)}, u32[]{:S(2)}, u32[]{:S(2)}) collective-permute-start(bf16[256,512]{1,0:T(8,128)(2,1)S(1)} %collective-permute-done.31.refs_7_), channel_id=1, source_target_pairs={{0,4},{4,0},{8,12},{12,8},{16,20},{20,16},{24,28},{28,24},{1,5},{5... | collective-permute-start | bytes 786440 | tf_op jit(solution)/shard_map/ppermute | solution.py:43
  156.9 6.5 %collective-permute-start.30 = (bf16[256,512]{1,0:T(8,128)(2,1)S(1)}, bf16[256,512]{1,0:T(8,128)(2,1)S(1)}, u32[]{:S(2)}, u32[]{:S(2)}) collective-permute-start(bf16[256,512]{1,0:T(8,128)(2,1)S(1)} %collective-permute-done.29.refs_5_), channel_id=1, source_target_pairs={{0,4},{4,0},{8,12},{12,8},{16,20},{20,16},{24,28},{28,24},{1,5},{5... | collective-permute-start | bytes 786440 | tf_op jit(solution)/shard_map/ppermute | solution.py:43
  156.9 6.5 %collective-permute-start.28 = (bf16[256,512]{1,0:T(8,128)(2,1)S(1)}, bf16[256,512]{1,0:T(8,128)(2,1)S(1)}, u32[]{:S(2)}, u32[]{:S(2)}) collective-permute-start(bf16[256,512]{1,0:T(8,128)(2,1)S(1)} %collective-permute-done.27.refs_3_), channel_id=1, source_target_pairs={{0,4},{4,0},{8,12},{12,8},{16,20},{20,16},{24,28},{28,24},{1,5},{5... | collective-permute-start | bytes 786440 | tf_op jit(solution)/shard_map/ppermute | solution.py:43
  170.0 17.4 %collective-permute-start.40 = (bf16[640,256]{1,0:T(8,128)(2,1)}, bf16[640,256]{1,0:T(8,128)(2,1)S(1)}, u32[]{:S(2)}, u32[]{:S(2)}) collective-permute-start(bf16[640,256]{1,0:T(8,128)(2,1)} %get-tuple-element.70), channel_id=1, source_target_pairs={{0,1},{1,0},{2,3},{3,2},{4,5},{5,4},{6,7},{7,6},{8,9},{9,8},{10,11... | collective-permute-start | bytes 983048 | tf_op jit(solution)/shard_map/ppermute | solution.py:43
  172.9 25.2 %collective-permute-start.41 = (bf16[640,256]{1,0:T(8,128)(2,1)}, bf16[640,256]{1,0:T(8,128)(2,1)S(1)}, u32[]{:S(2)}, u32[]{:S(2)}) collective-permute-start(bf16[640,256]{1,0:T(8,128)(2,1)} %get-tuple-element.71), channel_id=1, source_target_pairs={{0,2},{1,3},{2,0},{3,1},{4,6},{5,7},{6,4},{7,5},{8,10},{9,11},{10,... | collective-permute-start | bytes 983048 | tf_op jit(solution)/shard_map/ppermute | solution.py:43
  175.6 28.6 %copy-start.2 = (f32[640,256]{1,0:T(8,128)S(1)}, f32[640,256]{1,0:T(8,128)}, u32[]{:S(2)}) copy-start(f32[640,256]{1,0:T(8,128)} %get-tuple-element.68) | copy-start | bytes 1966084
  175.6 28.6 %collective-permute-start.42 = (bf16[640,256]{1,0:T(8,128)(2,1)}, bf16[640,256]{1,0:T(8,128)(2,1)S(1)}, u32[]{:S(2)}, u32[]{:S(2)}) collective-permute-start(bf16[640,256]{1,0:T(8,128)(2,1)} %get-tuple-element.72), channel_id=1, source_target_pairs={{0,3},{1,2},{2,1},{3,0},{4,7},{5,6},{6,5},{7,4},{8,11},{9,10},{10,... | collective-permute-start | bytes 983048 | tf_op jit(solution)/shard_map/ppermute | solution.py:43
  (24 other events, 215.0 us)

commit v3 on v2

--- a/solution.py
+++ b/solution.py
@@ -12,7 +12,7 @@
 BLK = 128
 CHUNKS = 2
 PARTS = 1
-VMEM_BYTES = 56 * 1024 * 1024
+VMEM_BYTES = 24 * 1024 * 1024
 MASKED = -1e30
 
 
@@ -54,8 +54,25 @@
     steps = [value] + [None] * (count - 1)
     for step in range(2, count, 2):
         steps[step] = moved(steps[step - 2], "seq", 2, step - 2)
-    for step in range(1, count, 2):
-        steps[step] = moved(steps[step - 1], "seq", 1, step - 1)
+    if count > 1:
+        steps[1] = moved(value, "seq", 1)
+    return steps
+
+
+def relay(value):
+    steps = [value]
+    for step in range(1, lax.axis_size("seq") - 1):
+        steps.append(moved(steps[-1], "seq", 1, step - 1))
+    return steps
+
+
+def finish_relay(steps, *gates):
+    return [*steps, moved(after(steps[-1], *gates), "seq", 1, len(steps) - 1)]
+
+
+def finish(steps, *gates):
+    for step in range(3, len(steps), 2):
+        steps[step] = moved(after(steps[step - 1], *gates), "seq", 1, step - 1)
     return steps
 
 
@@ -78,14 +95,24 @@
     return arrived, [moved(sends[step], "seq", -step, step) for step in (1, 2) if step < count]
 
 
-def gather_direct(own):
+def gather_direct(own, *gates):
     count = lax.axis_size("dp")
     pieces = [own] + [None] * (count - 1)
     for mask in range(2, count, 2):
         pieces[mask] = exchange(own, "dp", mask)
     for mask in range(0, count, 2):
-        pieces[mask + 1] = exchange(pieces[mask], "dp", 1)
+        pieces[mask + 1] = exchange(after(pieces[mask], *gates), "dp", 1)
     return pieces
+
+
+def gather_doubling(own, second, last):
+    bit, stack = 2, own
+    while bit < lax.axis_size("dp"):
+        stack = jnp.concatenate([stack, exchange(stack, "dp", bit)], axis=0)
+        if bit == 2:
+            stack = after(stack, *second)
+        bit *= 2
+    return [stack, exchange(after(stack, *last), "dp", 1)]
 
 
 def after(value, *others):
@@ -99,6 +126,27 @@
 
 def whole_table(count, width):
     return tuple(((at, 0, width), (at, width, width)) for at in range(count))
+
+
+def pack_kernel(near_ref, far_ref, own_ref, left_ref, right_ref, *, near_start, far_start):
+    width = own_ref.shape[1] // 2
+    left_ref[:, :width] = near_ref[:, near_start : near_start + width]
+    left_ref[:, width:] = own_ref[:, :width]
+    right_ref[:, :width] = far_ref[:, far_start : far_start + width]
+    right_ref[:, width:] = own_ref[:, width:]
+
+
+def pack(near, far, own, near_start, far_start):
+    shape = jax.ShapeDtypeStruct(own.shape, own.dtype)
+    return pl.pallas_call(
+        functools.partial(pack_kernel, near_start=near_start, far_start=far_start),
+        out_shape=[shape, shape],
+        in_specs=[vmem()] * 3,
+        out_specs=[vmem()] * 2,
+        compiler_params=params(),
+        cost_estimate=lasting(1),
+        name="pack",
+    )(near, far, own)
 
 
 def gather_weights(shards, behind, use_first):
@@ -110,14 +158,13 @@
             pieces = gather_direct(shard)
             result.append((pieces, whole_table(count, width)))
         return result, [use_first(result[0])], pieces[-1:]
-    left, right = slice(0, width), slice(width, 2 * width)
     first, second = shards
     from_x, from_y = exchange(first, "dp", 2), exchange(first, "dp", 4)
     here, there = after(from_x, *behind), after(from_y, *behind)
-    step_y = exchange(jnp.concatenate([here[:, left], second[:, left]], axis=1), "dp", 4)
-    step_x = exchange(jnp.concatenate([there[:, right], second[:, right]], axis=1), "dp", 2)
-    last_x = exchange(jnp.concatenate([step_y[:, right], second[:, left]], axis=1), "dp", 2)
-    last_y = exchange(jnp.concatenate([step_x[:, right], second[:, right]], axis=1), "dp", 4)
+    to_y, to_x = pack(here, there, second, 0, width)
+    step_y, step_x = exchange(to_y, "dp", 4), exchange(to_x, "dp", 2)
+    to_x, to_y = pack(step_y, step_x, second, width, width)
+    last_x, last_y = exchange(to_x, "dp", 2), exchange(to_y, "dp", 4)
     near = [first, from_x, from_y, step_y, step_x]
     near_core = [exchange(part, "dp", 1) for part in near]
     one = [((0, 0), (0, 1)), ((1, 0), (1, 1)), ((2, 0), (2, 1)), ((3, 0), (4, 0))]
@@ -131,11 +178,11 @@
         tables.append(tuple(table))
     pieces = [(near + near_core, tables[0])]
     used = use_first(pieces[0])
-    last_x, last_y = after((last_x, last_y), used[min(2, len(used) - 1)])
+    last_x, last_y = after((last_x, last_y), used[min(1, len(used) - 1)])
     far = [second, last_x, last_y]
     far_core = [exchange(part, "dp", 1) for part in far]
     pieces.append((far + [step_y, step_x] + far_core + near_core[3:], tables[1]))
-    return pieces, [used], (last_x, last_y)
+    return pieces, [used], used[1:2]
 
 
 def split_kernel(x_ref, *out_refs):
@@ -308,7 +355,7 @@
         scratch_shapes=[pltpu.VMEM((act_total * BLK, HEAD_SIZE), jnp.bfloat16)] * 2
         + [pltpu.VMEM((act_total * BLK, HEAD_SIZE), jnp.float32)] * 2,
         input_output_aliases=aliases,
-        compiler_params=params(),
+        compiler_params=pltpu.CompilerParams(vmem_limit_bytes=60 * 1024 * 1024),
         cost_estimate=lasting(9),
         name="attend",
     )(*operands)
@@ -365,17 +412,22 @@
     return out if flat_out else jnp.concatenate(list(out), axis=1)
 
 
-def weight_kernel(dests, has_before, rank_ref, *refs):
+def weight_kernel(dests, pieces_total, has_before, rank_ref, *refs):
     x_refs, refs = refs[:PARTS], refs[PARTS:]
     count = x_refs[0].shape[0]
-    pieces, refs = refs[:count], refs[count:]
+    height = x_refs[0].shape[1] * PARTS
+    pieces, refs = refs[:pieces_total], refs[pieces_total:]
     out_refs = refs[len(refs) // 2 :] if has_before else refs
     column, width = out_refs[0].shape[1], pieces[0].shape[1] // 2
     totals = [None, None]
     for at in range(count):
         rows = rows_of(x_refs, rank_ref[1] ^ at)
         for side in range(2):
-            term = dot(rows, pieces[at][:, side * width : (side + 1) * width], 0, 0)
+            if pieces_total == count:
+                piece, start = pieces[at], 0
+            else:
+                piece, start = pieces[at % 2], at // 2 * height
+            term = dot(rows, piece[start : start + height, side * width : (side + 1) * width], 0, 0)
             totals[side] = term if totals[side] is None else totals[side] + term
     for at, out_ref in enumerate(out_refs):
         if has_before:
@@ -392,7 +444,7 @@
     rows = x_all[0].shape[2]
     operands = [*x_all, *pieces, *before]
     return pl.pallas_call(
-        functools.partial(weight_kernel, dests, bool(before)),
+        functools.partial(weight_kernel, dests, len(pieces), bool(before)),
         out_shape=[jax.ShapeDtypeStruct((rows, column), jnp.float32)]
         + [jax.ShapeDtypeStruct((rows, column), jnp.bfloat16)] * (seq_count - 1),
         in_specs=[smem()] + [vmem()] * len(operands),
@@ -439,13 +491,14 @@
             )
         )
     weight_pieces, keyvals, weight_gates = gather_weights(
-        shards, x_by_owner, lambda pieces: spread(project(rank, x_by_owner, pieces))
+        shards, x_by_owner, lambda pieces: relay(project(rank, x_by_owner, pieces))
     )
-    arrivals, keyvals = [steps[1:] for steps in keyvals], [steps[0] for steps in keyvals]
+    arrivals, keyvals = keyvals, [steps[0] for steps in keyvals]
     for chunk in range(1, CHUNKS):
-        waits = arrivals[-1][1:2]
-        keyvals.append(project(after(rank, *waits), x_by_owner, weight_pieces[chunk]))
-        arrivals.append(spread(keyvals[-1])[1:])
+        keyvals.append(project(rank, x_by_owner, weight_pieces[chunk]))
+        arrivals[-1] = (finish_relay if chunk == 1 else finish)(arrivals[-1], keyvals[-1])
+        arrivals.append(spread(keyvals[-1]))
+    arrivals = [steps[1:] for steps in [*arrivals[:-1], finish(arrivals[-1])]]
     x_all, gates = [], weight_gates
     for part in x_by_owner:
         part = lax.all_to_all(after(part, *gates), "dp", split_axis=0, concat_axis=0, tiled=True)
@@ -453,23 +506,30 @@
         gates = (part,)
 
     backs, owns = [], []
-    gates, waits, later = (keyvals[-1],), tuple(arrivals[-1][1:2]), tuple(x_all)
+    gates, waits, later = (keyvals[-1],), tuple(arrivals[-1][1:2]), ()
     for chunk in range(CHUNKS):
         kv_steps = [keyvals[chunk]] + arrivals[chunk]
         dq, own, sends = attend(
             after(info, *gates), queries, cotangent, kv_steps, chunk, heads, group, act_total, dq
         )
-        arrived, back = collect(sends, waits, later)
+        if chunk < CHUNKS - 1 or seq_count > 4:
+            arrived, back = collect(sends, waits, later)
+        else:
+            back = [moved(after(sends[step - 1], *waits), "seq", -step) for step in range(seq_count - 1, 0, -1)]
+            arrived = ()
         backs.append(back)
         owns.append(own)
-        gates, waits, later = tuple(arrived), tuple(back), ()
-    gates, sums = tuple(arrived), ()
+        gates, waits, later = (*arrived, *x_all), tuple(back), ()
+    gates, sums = (owns[-1],), ()
     for chunk in range(CHUNKS):
         total = after(owns[chunk], *gates)
         for part in backs[chunk]:
             total = total + part.astype(jnp.float32)
         dkvs.append(total.astype(jnp.bfloat16))
-        dkv_pieces = gather_direct(dkvs[chunk])
+        if chunk < CHUNKS - 1 or lax.axis_size("dp") > 8:
+            dkv_pieces = gather_doubling(dkvs[chunk], backs[-1][:1], backs[-1][1:])
+        else:
+            dkv_pieces = gather_direct(dkvs[chunk], *sums[:1])
         dests = []
         for side in range(2):
             start = side * (kvwidth // 2) + chunk * width

time: 207 us -> 201 us (0.971)
  Pallas kernels: 51.4 us -> 33.3 us
  waiting for transfers between devices: 83.2 us -> 95 us
  starting transfers between devices: 57 us -> 64.2 us
  local copies, waits for them, and re-layouts: 7.5 us -> 2.22 us
    ppermute x12, starting transfers between devices: 31.8 us -> 39.6 us  [moved(): return lax.ppermute(value, axis, pairs)]
    pallas_call x2, Pallas kernels: 13.2 us -> 6.64 us  [attend(): pl.pallas_call(functools.partial(attend_kernel, sizes), grid=(heads,), ou...]
    ppermute x12, waiting for transfers between devices: 18 us -> 23.5 us  [moved(): return lax.ppermute(value, axis, pairs)]
    pallas_call x2 -> x4, Pallas kernels: 10.8 us -> 5.76 us  [the longest x2 4.51 us: weight_terms(): pl.pallas_call(functools.partial(weight_kernel, dests, len(pieces), bool(...]
    all_to_all x1, waiting for transfers between devices: 0.01 us -> 3.88 us  [body(): lax.all_to_all(after(part, *gates), 'dp', split_axis=0, concat_axis=0, ti...]
    slice x5 -> x1, local copies, waits for them, and re-layouts: 4.38 us -> 1.37 us  [body(): kv_weight[:, key_at:key_at + width]]
    pallas_call x1, Pallas kernels: 5.88 us -> 3.39 us  [split_columns(): pl.pallas_call(split_kernel, grid=(count,), out_shape=[jax.ShapeDtypeStru...]
    pallas_call x2, Pallas kernels: 12.2 us -> 9.73 us  [project(): pl.pallas_call(functools.partial(project_kernel, table), out_shape=jax.Sh...]
  transfers between devices with their start and end apart: 44 -> 40, of which waited for: 18 -> 21; matrix products, arithmetic and copies ran while one was open for 3% -> 1% of each run, Pallas kernels for 22% -> 15%
where the time goes in v3:
time: 201 us
  waiting for transfers between devices  95 us (47%)
  starting transfers between devices  64.2 us (32%)
  Pallas kernels  33.3 us (17%)
  other arithmetic  5.05 us (3%)
  local copies, waits for them, and re-layouts  2.22 us (1%)
    ppermute x27, waiting for transfers between devices, exchange(): return lax.ppermute(value, axis, [(i, i ^ mask) for i in range(count)])  67.6 us
    ppermute x12, starting transfers between devices, moved(): return lax.ppermute(value, axis, pairs)  39.6 us
    ppermute x12, waiting for transfers between devices, moved(): return lax.ppermute(value, axis, pairs)  23.5 us
    ppermute x27, starting transfers between devices, exchange(): return lax.ppermute(value, axis, [(i, i ^ mask) for i in range(count)])  20.8 us
    pallas_call x2, Pallas kernels, project(): pl.pallas_call(functools.partial(project_kernel, table), out_shape=jax.Sh...  9.73 us
    pallas_call x1, Pallas kernels, token_grads(): pl.pallas_call(functools.partial(token_kernel, tables, tuple(indices)), o...  7.79 us
    pallas_call x2, Pallas kernels, attend(): pl.pallas_call(functools.partial(attend_kernel, sizes), grid=(heads,), ou...  6.64 us
    pallas_call x2, Pallas kernels, weight_terms(): pl.pallas_call(functools.partial(weight_kernel, dests, len(pieces), bool(...  4.51 us
  transfers between devices with their start and end apart: 40, of which 21 were waited for; matrix products, arithmetic and copies ran while one was open for 1% of the time, Pallas kernels for 15%

profile of v3, /device:TPU:8, one launch (start us, length us, event | category | flops | bytes accessed | tf_op | source)
XLA Modules:
  0.0 200.8 jit_solution(10385182526449739116)
XLA Ops:
  0.6 1.4 fusion.2
  2.1 1.6 collective-permute-start.1
  3.7 1.5 collective-permute-start
  5.2 3.4 %split_columns.1.refs_0_ = bf16[8,256,640]{2,1,0:T(8,128)(2,1)} custom-call(bf16[1,256,5120]{2,1,0:T(8,128)(2,1)S(1)} %copy-done.2), custom_call_target="tpu_custom_call" | custom-call | flops 12000000000 | bytes 36000000 | tf_op jit(solution)/shard_map/split_columns/pallas_call | solution.py:202
  8.6 10.0 %collective-permute-done.1.far_ref.refs_3_.refs_4_ = bf16[640,512]{1,0:T(8,128)(2,1)S(1)} collective-permute-done((bf16[640,512]{1,0:T(8,128)(2,1)S(1)}, bf16[640,512]{1,0:T(8,128)(2,1)S(1)}, u32[]{:S(2)}, u32[]{:S(2)}) %collective-permute-start.1) | collective-permute-done | bytes 655392 | tf_op jit(solution)/shard_map/ppermute | solution.py:43
  18.6 1.2 collective-permute-done.near_ref.refs_2_.refs_3_
  20.5 1.5 collective-permute-start.3
  22.5 12.8 %collective-permute-done.2.near_ref.refs_4_.refs_5_ = bf16[640,512]{1,0:T(8,128)(2,1)S(1)} collective-permute-done((bf16[640,512]{1,0:T(8,128)(2,1)S(1)}, bf16[640,512]{1,0:T(8,128)(2,1)S(1)}, u32[]{:S(2)}, u32[]{:S(2)}) %collective-permute-start.2) | collective-permute-done | bytes 655392 | tf_op jit(solution)/shard_map/ppermute | solution.py:43
  35.9 1.2 pack.3
  37.1 1.6 collective-permute-start.4
  38.6 1.3 collective-permute-start.5
  40.0 4.6 %project.2.refs_0_.refs_1_ = bf16[256,512]{1,0:T(8,128)(2,1)S(1)} custom-call(s32[2]{0:T(128)S(1)} %pad_add_fusion.1.rank_ref, bf16[8,256,640]{2,1,0:T(8,128)(2,1)} %split_columns.1.refs_0_, bf16[640,512]{1,0:T(8,128)(2,1)S(1)} %pad_maximum_fusion.1.refs_1_.refs_2_, bf16[640,512]{1,0:T(8,128)(2,1)S(1)} %collective-permute-done.near_ref.refs_2_.refs_3_, ...), custom_call_target="tpu_custom_call" | custom-call | flops 16000000000 | bytes 48000000 | tf_op jit(solution)/shard_map/project/pallas_call | solution.py:234
  44.7 3.5 %collective-permute-start.11 = (bf16[256,512]{1,0:T(8,128)(2,1)S(1)}, bf16[256,512]{1,0:T(8,128)(2,1)}, u32[]{:S(2)}, u32[]{:S(2)}) collective-permute-start(bf16[256,512]{1,0:T(8,128)(2,1)S(1)} %project.2.refs_0_.refs_1_), channel_id=1, source_target_pairs={{0,1},{1,2},{2,3},{4,5},{5,6},{6,7},{8,9},{9,10},{10,11},{12,13},{... | collective-permute-start | bytes 786440 | tf_op jit(solution)/shard_map/ppermute | solution.py:49
  48.2 6.1 %collective-permute-done.4.refs_2_.refs_13_ = bf16[640,512]{1,0:T(8,128)(2,1)} collective-permute-done((bf16[640,512]{1,0:T(8,128)(2,1)S(1)}, bf16[640,512]{1,0:T(8,128)(2,1)}, u32[]{:S(2)}, u32[]{:S(2)}) %collective-permute-start.4) | collective-permute-done | bytes 655392 | tf_op jit(solution)/shard_map/ppermute | solution.py:43
  54.3 1.2 collective-permute-done.5.refs_3_.refs_14_
  56.3 4.2 %collective-permute-start.15 = (bf16[256,512]{1,0:T(8,128)(2,1)}, bf16[256,512]{1,0:T(8,128)(2,1)}, u32[]{:S(2)}, u32[]{:S(2)}) collective-permute-start(bf16[256,512]{1,0:T(8,128)(2,1)} %collective-permute-done.11.refs_2_.refs_3_), channel_id=1, source_target_pairs={{1,2},{2,3},{5,6},{6,7},{9,10},{10,11},{13,14},{14,15},{17,18},{18... | collective-permute-start | bytes 786440 | tf_op jit(solution)/shard_map/ppermute | solution.py:49
  60.5 5.1 %project.3.refs_0_.refs_1_ = bf16[256,512]{1,0:T(8,128)(2,1)S(1)} custom-call(s32[2]{0:T(128)S(1)} %pad_add_fusion.1.rank_ref, bf16[8,256,640]{2,1,0:T(8,128)(2,1)} %split_columns.1.refs_0_, bf16[640,512]{1,0:T(8,128)(2,1)S(1)} %pad_maximum_fusion.own_ref.refs_1_.refs_12_, bf16[640,512]{1,0:T(8,128)(2,1)} %collective-permute-done.4.refs_2_.refs_13_, ...), custom_call_target="tpu_custom_call" | custom-call | flops 16000000000 | bytes 48000000 | tf_op jit(solution)/shard_map/project/pallas_call | solution.py:234
  66.3 1.4 collective-permute-start.16
  68.4 3.8 %all-to-all-start = ((bf16[8,256,640]{2,1,0:T(8,128)(2,1)}), bf16[8,256,640]{2,1,0:T(8,128)(2,1)S(1)}, u32[]{:S(2)}, u32[]{:S(2)}) async-start(bf16[8,256,640]{2,1,0:T(8,128)(2,1)} %split_columns.1.refs_0_), calls=%async_computation | async-start | bytes 5242880 | tf_op jit(solution)/shard_map/all_to_all | solution.py:504
  72.1 5.5 %collective-permute-start.17 = (bf16[256,512]{1,0:T(8,128)(2,1)S(1)}, bf16[256,512]{1,0:T(8,128)(2,1)}, u32[]{:S(2)}, u32[]{:S(2)}) collective-permute-start(bf16[256,512]{1,0:T(8,128)(2,1)S(1)} %copy-done.15), channel_id=1, source_target_pairs={{0,2},{1,3},{4,6},{5,7},{8,10},{9,11},{12,14},{13,15},{16,18},{17,... | collective-permute-start | bytes 786440 | tf_op jit(solution)/shard_map/ppermute | solution.py:49
  77.7 3.3 %attend.2 = (bf16[1,256,2560]{2,1,0:T(8,128)(2,1)}, f32[256,512]{1,0:T(8,128)}, bf16[256,512]{1,0:T(8,128)(2,1)}, bf16[256,512]{1,0:T(8,128)(2,1)}, bf16[256,512]{1,0:T(8,128)(2,1)}) custom-call(s32[10]{0:T(128)} %pad_add_fusion.info_ref, bf16[1,256,2560]{2,1,0:T(8,128)(2,1)} %q_ref.3, bf16[1,256,2560]{2,1,0:T(8,128)(2,1)} %g_ref.3, ...), custom_call_target="tpu_custom_call" | custom-call | flops 35999997952 | bytes 108000000 | tf_op jit(solution)/shard_map/attend/pallas_call | solution.py:345
  80.9 7.7 %collective-permute-done.17.refs_4_.refs_5_ = bf16[256,512]{1,0:T(8,128)(2,1)} collective-permute-done((bf16[256,512]{1,0:T(8,128)(2,1)S(1)}, bf16[256,512]{1,0:T(8,128)(2,1)}, u32[]{:S(2)}, u32[]{:S(2)}) %collective-permute-start.17) | collective-permute-done | bytes 262176 | tf_op jit(solution)/shard_map/ppermute | solution.py:49
  89.3 2.4 %collective-permute-start.19 = (bf16[256,512]{1,0:T(8,128)(2,1)S(1)}, bf16[256,512]{1,0:T(8,128)(2,1)}, u32[]{:S(2)}, u32[]{:S(2)}) collective-permute-start(bf16[256,512]{1,0:T(8,128)(2,1)S(1)} %copy-done.15), channel_id=1, source_target_pairs={{0,1},{1,2},{2,3},{4,5},{5,6},{6,7},{8,9},{9,10},{10,11},{12,13},{... | collective-permute-start | bytes 786440 | tf_op jit(solution)/shard_map/ppermute | solution.py:49
  91.7 1.4 collective-permute-start.20
  93.1 4.1 %collective-permute-start.21 = (bf16[256,512]{1,0:T(8,128)(2,1)}, bf16[256,512]{1,0:T(8,128)(2,1)}, u32[]{:S(2)}, u32[]{:S(2)}) collective-permute-start(bf16[256,512]{1,0:T(8,128)(2,1)} %get-tuple-element.66), channel_id=1, source_target_pairs={{1,0},{2,1},{3,2},{5,4},{6,5},{7,6},{9,8},{10,9},{11,10},{13,12},{... | collective-permute-start | bytes 786440 | tf_op jit(solution)/shard_map/ppermute | solution.py:49
  97.2 1.7 add_convert_fusion.2
  99.0 1.5 collective-permute-start.22
  100.4 3.9 %all-to-all-done.refs_0_ = bf16[8,256,640]{2,1,0:T(8,128)(2,1)S(1)} async-done(((bf16[8,256,640]{2,1,0:T(8,128)(2,1)}), bf16[8,256,640]{2,1,0:T(8,128)(2,1)S(1)}, u32[]{:S(2)}, u32[]{:S(2)}) %all-to-all-start) | async-done | bytes 2621472 | tf_op jit(solution)/shard_map/all_to_all | solution.py:504
  104.3 3.4 %attend.3 = (bf16[1,256,2560]{2,1,0:T(8,128)(2,1)}, f32[256,512]{1,0:T(8,128)}, bf16[256,512]{1,0:T(8,128)(2,1)}, bf16[256,512]{1,0:T(8,128)(2,1)}, bf16[256,512]{1,0:T(8,128)(2,1)}) custom-call(s32[10]{0:T(128)} %pad_add_fusion.info_ref, bf16[1,256,2560]{2,1,0:T(8,128)(2,1)} %q_ref.3, ...), custom_call_target="tpu_custom_call", output_to_operand_aliasing={{0}: (11, {})} | custom-call | flops 35999997952 | bytes 108000000 | tf_op jit(solution)/shard_map/attend/pallas_call | solution.py:345
  107.7 5.2 %collective-permute-done.21 = bf16[256,512]{1,0:T(8,128)(2,1)} collective-permute-done((bf16[256,512]{1,0:T(8,128)(2,1)}, bf16[256,512]{1,0:T(8,128)(2,1)}, u32[]{:S(2)}, u32[]{:S(2)}) %collective-permute-start.21) | collective-permute-done | bytes 262176 | tf_op jit(solution)/shard_map/ppermute | solution.py:49
  112.9 1.1 add_convert_fusion.refs_0_
  114.1 1.7 collective-permute-start.26
  116.5 4.0 %collective-permute-done.26 = bf16[256,512]{1,0:T(8,128)(2,1)S(1)} collective-permute-done((bf16[256,512]{1,0:T(8,128)(2,1)S(1)}, bf16[256,512]{1,0:T(8,128)(2,1)S(1)}, u32[]{:S(2)}, u32[]{:S(2)}) %collective-permute-start.26) | collective-permute-done | bytes 262176 | tf_op jit(solution)/shard_map/ppermute | solution.py:43
  120.6 1.8 collective-permute-start.27
  122.3 1.3 collective-permute-start.24
  123.6 13.1 %collective-permute-start.25 = (bf16[256,512]{1,0:T(8,128)(2,1)S(1)}, bf16[256,512]{1,0:T(8,128)(2,1)S(1)}, u32[]{:S(2)}, u32[]{:S(2)}) collective-permute-start(bf16[256,512]{1,0:T(8,128)(2,1)S(1)} %copy-done.19), channel_id=1, source_target_pairs={{1,0},{2,1},{3,2},{5,4},{6,5},{7,6},{9,8},{10,9},{11,10},{13,12},{... | collective-permute-start | bytes 786440 | tf_op jit(solution)/shard_map/ppermute | solution.py:49
  136.8 1.1 collective-permute-done.24
  137.9 9.5 %collective-permute-done.25 = bf16[256,512]{1,0:T(8,128)(2,1)S(1)} collective-permute-done((bf16[256,512]{1,0:T(8,128)(2,1)S(1)}, bf16[256,512]{1,0:T(8,128)(2,1)S(1)}, u32[]{:S(2)}, u32[]{:S(2)}) %collective-permute-start.25) | collective-permute-done | bytes 262176 | tf_op jit(solution)/shard_map/ppermute | solution.py:49
  147.5 1.2 collective-permute-start.34
  149.6 1.5 collective-permute-start.30
  151.1 2.2 %weight_grad.2 = (f32[640,256]{1,0:T(8,128)S(1)}, bf16[640,256]{1,0:T(8,128)(2,1)S(1)}, bf16[640,256]{1,0:T(8,128)(2,1)S(1)}, bf16[640,256]{1,0:T(8,128)(2,1)S(1)}) custom-call(s32[2]{0:T(128)S(1)} %pad_add_fusion.1.rank_ref, bf16[8,256,640]{2,1,0:T(8,128)(2,1)S(1)} %all-to-all-done.refs_0_, bf16[1024,512]{1,0:T(8,128)(2,1)S(1)} %constant_dynamic-update-slice_fusion.refs_1_, ...), custom_call_target="tpu_custom_call" | custom-call | flops 16000000000 | bytes 48000000 | tf_op jit(solution)/shard_map/weight_grad/pallas_call | solution.py:446
  153.3 4.3 %collective-permute-done.34.refs_7_ = bf16[256,512]{1,0:T(8,128)(2,1)S(1)} collective-permute-done((bf16[256,512]{1,0:T(8,128)(2,1)S(1)}, bf16[256,512]{1,0:T(8,128)(2,1)S(1)}, u32[]{:S(2)}, u32[]{:S(2)}) %collective-permute-start.34) | collective-permute-done | bytes 262176 | tf_op jit(solution)/shard_map/ppermute | solution.py:43
  157.7 5.1 %collective-permute-done.32.refs_5_ = bf16[256,512]{1,0:T(8,128)(2,1)S(1)} collective-permute-done((bf16[256,512]{1,0:T(8,128)(2,1)S(1)}, bf16[256,512]{1,0:T(8,128)(2,1)S(1)}, u32[]{:S(2)}, u32[]{:S(2)}) %collective-permute-start.32) | collective-permute-done | bytes 262176 | tf_op jit(solution)/shard_map/ppermute | solution.py:43
  165.5 2.3 %weight_grad.3 = (f32[640,256]{1,0:T(8,128)S(1)}, bf16[640,256]{1,0:T(8,128)(2,1)S(1)}, bf16[640,256]{1,0:T(8,128)(2,1)S(1)}, bf16[640,256]{1,0:T(8,128)(2,1)S(1)}) custom-call(s32[2]{0:T(128)S(1)} %pad_add_fusion.1.rank_ref, bf16[8,256,640]{2,1,0:T(8,128)(2,1)S(1)} %all-to-all-done.refs_0_, bf16[256,512]{1,0:T(8,128)(2,1)S(1)} %add_convert_fusion.1.refs_1_, ...), custom_call_target="tpu_custom_call" | custom-call | flops 16000000000 | bytes 48000000 | tf_op jit(solution)/shard_map/weight_grad/pallas_call | solution.py:446
  168.8 2.5 %collective-permute-start.38 = (bf16[640,256]{1,0:T(8,128)(2,1)S(1)}, bf16[640,256]{1,0:T(8,128)(2,1)S(1)}, u32[]{:S(2)}, u32[]{:S(2)}) collective-permute-start(bf16[640,256]{1,0:T(8,128)(2,1)S(1)} %get-tuple-element.90), channel_id=1, source_target_pairs={{0,3},{1,2},{2,1},{3,0},{4,7},{5,6},{6,5},{7,4},{8,11},{9,10},{10,... | collective-permute-start | bytes 983048 | tf_op jit(solution)/shard_map/ppermute | solution.py:43
  171.4 7.8 %token_grads.1 = bf16[256,5120]{1,0:T(8,128)(2,1)} custom-call(s32[2]{0:T(128)S(1)} %pad_add_fusion.1.rank_ref, bf16[256,512]{1,0:T(8,128)(2,1)S(1)} %add_convert_fusion.refs_0_, bf16[256,512]{1,0:T(8,128)(2,1)S(1)} %add_convert_fusion.1.refs_1_, bf16[640,512]{1,0:T(8,128)(2,1)S(1)} %pad_maximum_fusion.1.refs_1_.refs_2_, bf16[640,512]{1,0:T(8,128)(2,1)S(1)} %copy-done.6, ...), custom_call_target="tpu_custom_call" | custom-call | flops 32000000000 | bytes 96000000 | tf_op jit(solution)/shard_map/token_grads/pallas_call | solution.py:403
  180.2 4.2 %collective-permute-done.37 = bf16[640,256]{1,0:T(8,128)(2,1)S(1)} collective-permute-done((bf16[640,256]{1,0:T(8,128)(2,1)S(1)}, bf16[640,256]{1,0:T(8,128)(2,1)S(1)}, u32[]{:S(2)}, u32[]{:S(2)}) %collective-permute-start.37) | collective-permute-done | bytes 327712 | tf_op jit(solution)/shard_map/ppermute | solution.py:43
  184.5 15.4 %collective-permute-done.38 = bf16[640,256]{1,0:T(8,128)(2,1)S(1)} collective-permute-done((bf16[640,256]{1,0:T(8,128)(2,1)S(1)}, bf16[640,256]{1,0:T(8,128)(2,1)S(1)}, u32[]{:S(2)}, u32[]{:S(2)}) %collective-permute-start.38) | collective-permute-done | bytes 327712 | tf_op jit(solution)/shard_map/ppermute | solution.py:43
  (103 shorter events, 12.4 us)
Async XLA Ops:
  2.1 16.5 %collective-permute-start.1 = (bf16[640,512]{1,0:T(8,128)(2,1)S(1)}, bf16[640,512]{1,0:T(8,128)(2,1)S(1)}, u32[]{:S(2)}, u32[]{:S(2)}) collective-permute-start(bf16[640,512]{1,0:T(8,128)(2,1)S(1)} %pad_maximum_fusion.1.refs_1_.refs_2_), channel_id=1, source_target_pairs={{0,16},{4,20},{8,24},{12,28},{16,0},{20,4},{24,8},{28,12},{1,17},{... | collective-permute-start | bytes 1966088 | tf_op jit(solution)/shard_map/ppermute | solution.py:43
  3.7 16.2 %collective-permute-start = (bf16[640,512]{1,0:T(8,128)(2,1)S(1)}, bf16[640,512]{1,0:T(8,128)(2,1)S(1)}, u32[]{:S(2)}, u32[]{:S(2)}) collective-permute-start(bf16[640,512]{1,0:T(8,128)(2,1)S(1)} %pad_maximum_fusion.1.refs_1_.refs_2_), channel_id=1, source_target_pairs={{0,8},{4,12},{8,0},{12,4},{16,24},{20,28},{24,16},{28,20},{1,9},{5... | collective-permute-start | bytes 1966088 | tf_op jit(solution)/shard_map/ppermute | solution.py:43
  5.2 55.3 %copy-start = (bf16[640,512]{1,0:T(8,128)(2,1)}, bf16[640,512]{1,0:T(8,128)(2,1)S(1)}, u32[]{:S(2)}) copy-start(bf16[640,512]{1,0:T(8,128)(2,1)S(1)} %pad_maximum_fusion.own_ref.refs_1_.refs_12_) | copy-start | bytes 1966084
  18.6 21.4 %copy-start.3 = (bf16[640,512]{1,0:T(8,128)(2,1)}, bf16[640,512]{1,0:T(8,128)(2,1)S(1)}, u32[]{:S(2)}) copy-start(bf16[640,512]{1,0:T(8,128)(2,1)S(1)} %collective-permute-done.1.far_ref.refs_3_.refs_4_) | copy-start | bytes 1966084
  19.8 20.1 %copy-start.5 = (bf16[640,512]{1,0:T(8,128)(2,1)}, bf16[640,512]{1,0:T(8,128)(2,1)S(1)}, u32[]{:S(2)}) copy-start(bf16[640,512]{1,0:T(8,128)(2,1)S(1)} %collective-permute-done.near_ref.refs_2_.refs_3_) | copy-start | bytes 1966084
  19.9 15.3 %collective-permute-start.2 = (bf16[640,512]{1,0:T(8,128)(2,1)S(1)}, bf16[640,512]{1,0:T(8,128)(2,1)S(1)}, u32[]{:S(2)}, u32[]{:S(2)}) collective-permute-start(bf16[640,512]{1,0:T(8,128)(2,1)S(1)} %get-tuple-element.49), channel_id=1, source_target_pairs={{0,16},{4,20},{8,24},{12,28},{16,0},{20,4},{24,8},{28,12},{1,17},{... | collective-permute-start | bytes 1966088 | tf_op jit(solution)/shard_map/ppermute | solution.py:43
  20.5 15.2 %collective-permute-start.3 = (bf16[640,512]{1,0:T(8,128)(2,1)S(1)}, bf16[640,512]{1,0:T(8,128)(2,1)}, u32[]{:S(2)}, u32[]{:S(2)}) collective-permute-start(bf16[640,512]{1,0:T(8,128)(2,1)S(1)} %get-tuple-element.50), channel_id=1, source_target_pairs={{0,8},{4,12},{8,0},{12,4},{16,24},{20,28},{24,16},{28,20},{1,9},{5... | collective-permute-start | bytes 1966088 | tf_op jit(solution)/shard_map/ppermute | solution.py:43
  22.0 15.1 %collective-permute-start.6 = (bf16[640,512]{1,0:T(8,128)(2,1)S(1)}, bf16[640,512]{1,0:T(8,128)(2,1)}, u32[]{:S(2)}, u32[]{:S(2)}) collective-permute-start(bf16[640,512]{1,0:T(8,128)(2,1)S(1)} %pad_maximum_fusion.1.refs_1_.refs_2_), channel_id=1, source_target_pairs={{0,4},{4,0},{8,12},{12,8},{16,20},{20,16},{24,28},{28,24},{1,5},{5... | collective-permute-start | bytes 1966088 | tf_op jit(solution)/shard_map/ppermute | solution.py:43
  22.0 16.6 %collective-permute-start.8 = (bf16[640,512]{1,0:T(8,128)(2,1)S(1)}, bf16[640,512]{1,0:T(8,128)(2,1)}, u32[]{:S(2)}, u32[]{:S(2)}) collective-permute-start(bf16[640,512]{1,0:T(8,128)(2,1)S(1)} %collective-permute-done.1.far_ref.refs_3_.refs_4_), channel_id=1, source_target_pairs={{0,4},{4,0},{8,12},{12,8},{16,20},{20,16},{24,28},{28,24},{1,5},{5... | collective-permute-start | bytes 1966088 | tf_op jit(solution)/shard_map/ppermute | solution.py:43
  22.5 17.5 %collective-permute-start.7 = (bf16[640,512]{1,0:T(8,128)(2,1)S(1)}, bf16[640,512]{1,0:T(8,128)(2,1)}, u32[]{:S(2)}, u32[]{:S(2)}) collective-permute-start(bf16[640,512]{1,0:T(8,128)(2,1)S(1)} %collective-permute-done.near_ref.refs_2_.refs_3_), channel_id=1, source_target_pairs={{0,4},{4,0},{8,12},{12,8},{16,20},{20,16},{24,28},{28,24},{1,5},{5... | collective-permute-start | bytes 1966088 | tf_op jit(solution)/shard_map/ppermute | solution.py:43
  35.3 25.2 %copy-start.7 = (bf16[640,512]{1,0:T(8,128)(2,1)}, bf16[640,512]{1,0:T(8,128)(2,1)S(1)}, u32[]{:S(2)}) copy-start(bf16[640,512]{1,0:T(8,128)(2,1)S(1)} %collective-permute-done.2.near_ref.refs_4_.refs_5_) | copy-start | bytes 1966084
  35.3 4.7 %collective-permute-start.9 = (bf16[640,512]{1,0:T(8,128)(2,1)S(1)}, bf16[640,512]{1,0:T(8,128)(2,1)}, u32[]{:S(2)}, u32[]{:S(2)}) collective-permute-start(bf16[640,512]{1,0:T(8,128)(2,1)S(1)} %collective-permute-done.2.near_ref.refs_4_.refs_5_), channel_id=1, source_target_pairs={{0,4},{4,0},{8,12},{12,8},{16,20},{20,16},{24,28},{28,24},{1,5},{5... | collective-permute-start | bytes 1966088 | tf_op jit(solution)/shard_map/ppermute | solution.py:43
  35.7 4.3 %collective-permute-start.10 = (bf16[640,512]{1,0:T(8,128)(2,1)}, bf16[640,512]{1,0:T(8,128)(2,1)}, u32[]{:S(2)}, u32[]{:S(2)}) collective-permute-start(bf16[640,512]{1,0:T(8,128)(2,1)} %collective-permute-done.3.far_ref.refs_5_.refs_6_), channel_id=1, source_target_pairs={{0,4},{4,0},{8,12},{12,8},{16,20},{20,16},{24,28},{28,24},{1,5},{5... | collective-permute-start | bytes 1966088 | tf_op jit(solution)/shard_map/ppermute | solution.py:43
  37.1 17.2 %collective-permute-start.4 = (bf16[640,512]{1,0:T(8,128)(2,1)S(1)}, bf16[640,512]{1,0:T(8,128)(2,1)}, u32[]{:S(2)}, u32[]{:S(2)}) collective-permute-start(bf16[640,512]{1,0:T(8,128)(2,1)S(1)} %get-tuple-element.51), channel_id=1, source_target_pairs={{0,8},{4,12},{8,0},{12,4},{16,24},{20,28},{24,16},{28,20},{1,9},{5... | collective-permute-start | bytes 1966088 | tf_op jit(solution)/shard_map/ppermute | solution.py:43
  38.6 17.4 %copy-start.18 = (s32[1,4]{1,0:T(1,128)S(1)}, s32[1,4]{1,0:T(1,128)}, u32[]{:S(2)}) copy-start(s32[1,4]{1,0:T(1,128)} %param.9) | copy-start | bytes 52
  38.6 16.9 %collective-permute-start.5 = (bf16[640,512]{1,0:T(8,128)(2,1)S(1)}, bf16[640,512]{1,0:T(8,128)(2,1)}, u32[]{:S(2)}, u32[]{:S(2)}) collective-permute-start(bf16[640,512]{1,0:T(8,128)(2,1)S(1)} %get-tuple-element.52), channel_id=1, source_target_pairs={{0,16},{4,20},{8,24},{12,28},{16,0},{20,4},{24,8},{28,12},{1,17},{... | collective-permute-start | bytes 1966088 | tf_op jit(solution)/shard_map/ppermute | solution.py:43
  44.7 20.9 %copy-start.13 = (bf16[256,512]{1,0:T(8,128)(2,1)}, bf16[256,512]{1,0:T(8,128)(2,1)S(1)}, u32[]{:S(2)}) copy-start(bf16[256,512]{1,0:T(8,128)(2,1)S(1)} %project.2.refs_0_.refs_1_) | copy-start | bytes 786436
  44.7 10.9 %collective-permute-start.11 = (bf16[256,512]{1,0:T(8,128)(2,1)S(1)}, bf16[256,512]{1,0:T(8,128)(2,1)}, u32[]{:S(2)}, u32[]{:S(2)}) collective-permute-start(bf16[256,512]{1,0:T(8,128)(2,1)S(1)} %project.2.refs_0_.refs_1_), channel_id=1, source_target_pairs={{0,1},{1,2},{2,3},{4,5},{5,6},{6,7},{8,9},{9,10},{10,11},{12,13},{... | collective-permute-start | bytes 786440 | tf_op jit(solution)/shard_map/ppermute | solution.py:49
  48.2 12.3 %collective-permute-start.12 = (bf16[640,512]{1,0:T(8,128)(2,1)S(1)}, bf16[640,512]{1,0:T(8,128)(2,1)S(1)}, u32[]{:S(2)}, u32[]{:S(2)}) collective-permute-start(bf16[640,512]{1,0:T(8,128)(2,1)S(1)} %pad_maximum_fusion.own_ref.refs_1_.refs_12_), channel_id=1, source_target_pairs={{0,4},{4,0},{8,12},{12,8},{16,20},{20,16},{24,28},{28,24},{1,5},{5... | collective-permute-start | bytes 1966088 | tf_op jit(solution)/shard_map/ppermute | solution.py:43
  55.5 4.9 %collective-permute-start.13 = (bf16[640,512]{1,0:T(8,128)(2,1)}, bf16[640,512]{1,0:T(8,128)(2,1)S(1)}, u32[]{:S(2)}, u32[]{:S(2)}) collective-permute-start(bf16[640,512]{1,0:T(8,128)(2,1)} %collective-permute-done.4.refs_2_.refs_13_), channel_id=1, source_target_pairs={{0,4},{4,0},{8,12},{12,8},{16,20},{20,16},{24,28},{28,24},{1,5},{5... | collective-permute-start | bytes 1966088 | tf_op jit(solution)/shard_map/ppermute | solution.py:43
  55.5 4.9 %collective-permute-start.14 = (bf16[640,512]{1,0:T(8,128)(2,1)}, bf16[640,512]{1,0:T(8,128)(2,1)}, u32[]{:S(2)}, u32[]{:S(2)}) collective-permute-start(bf16[640,512]{1,0:T(8,128)(2,1)} %collective-permute-done.5.refs_3_.refs_14_), channel_id=1, source_target_pairs={{0,4},{4,0},{8,12},{12,8},{16,20},{20,16},{24,28},{28,24},{1,5},{5... | collective-permute-start | bytes 1966088 | tf_op jit(solution)/shard_map/ppermute | solution.py:43
  56.3 10.1 %collective-permute-start.15 = (bf16[256,512]{1,0:T(8,128)(2,1)}, bf16[256,512]{1,0:T(8,128)(2,1)}, u32[]{:S(2)}, u32[]{:S(2)}) collective-permute-start(bf16[256,512]{1,0:T(8,128)(2,1)} %collective-permute-done.11.refs_2_.refs_3_), channel_id=1, source_target_pairs={{1,2},{2,3},{5,6},{6,7},{9,10},{10,11},{13,14},{14,15},{17,18},{18... | collective-permute-start | bytes 786440 | tf_op jit(solution)/shard_map/ppermute | solution.py:49
  66.3 11.3 %collective-permute-start.16 = (bf16[256,512]{1,0:T(8,128)(2,1)}, bf16[256,512]{1,0:T(8,128)(2,1)}, u32[]{:S(2)}, u32[]{:S(2)}) collective-permute-start(bf16[256,512]{1,0:T(8,128)(2,1)} %collective-permute-done.15.refs_4_.refs_5_), channel_id=1, source_target_pairs={{2,3},{6,7},{10,11},{14,15},{18,19},{22,23},{26,27},{30,31}} | collective-permute-start | bytes 786440 | tf_op jit(solution)/shard_map/ppermute | solution.py:49
  68.4 36.0 %all-to-all-start = ((bf16[8,256,640]{2,1,0:T(8,128)(2,1)}), bf16[8,256,640]{2,1,0:T(8,128)(2,1)S(1)}, u32[]{:S(2)}, u32[]{:S(2)}) async-start(bf16[8,256,640]{2,1,0:T(8,128)(2,1)} %split_columns.1.refs_0_), calls=%async_computation | async-start | bytes 5242880 | tf_op jit(solution)/shard_map/all_to_all | solution.py:504
  72.1 16.5 %collective-permute-start.17 = (bf16[256,512]{1,0:T(8,128)(2,1)S(1)}, bf16[256,512]{1,0:T(8,128)(2,1)}, u32[]{:S(2)}, u32[]{:S(2)}) collective-permute-start(bf16[256,512]{1,0:T(8,128)(2,1)S(1)} %copy-done.15), channel_id=1, source_target_pairs={{0,2},{1,3},{4,6},{5,7},{8,10},{9,11},{12,14},{13,15},{16,18},{17,... | collective-permute-start | bytes 786440 | tf_op jit(solution)/shard_map/ppermute | solution.py:49
  88.6 8.6 %collective-permute-start.18 = (bf16[256,512]{1,0:T(8,128)(2,1)}, bf16[256,512]{1,0:T(8,128)(2,1)S(1)}, u32[]{:S(2)}, u32[]{:S(2)}) collective-permute-start(bf16[256,512]{1,0:T(8,128)(2,1)} %get-tuple-element.58), channel_id=1, source_target_pairs={{3,2},{7,6},{11,10},{15,14},{19,18},{23,22},{27,26},{31,30}} | collective-permute-start | bytes 786440 | tf_op jit(solution)/shard_map/ppermute | solution.py:49
  89.3 15.0 %collective-permute-start.19 = (bf16[256,512]{1,0:T(8,128)(2,1)S(1)}, bf16[256,512]{1,0:T(8,128)(2,1)}, u32[]{:S(2)}, u32[]{:S(2)}) collective-permute-start(bf16[256,512]{1,0:T(8,128)(2,1)S(1)} %copy-done.15), channel_id=1, source_target_pairs={{0,1},{1,2},{2,3},{4,5},{5,6},{6,7},{8,9},{9,10},{10,11},{12,13},{... | collective-permute-start | bytes 786440 | tf_op jit(solution)/shard_map/ppermute | solution.py:49
  91.7 12.6 %collective-permute-start.20 = (bf16[256,512]{1,0:T(8,128)(2,1)}, bf16[256,512]{1,0:T(8,128)(2,1)}, u32[]{:S(2)}, u32[]{:S(2)}) collective-permute-start(bf16[256,512]{1,0:T(8,128)(2,1)} %collective-permute-done.17.refs_4_.refs_5_), channel_id=1, source_target_pairs={{2,3},{6,7},{10,11},{14,15},{18,19},{22,23},{26,27},{30,31}} | collective-permute-start | bytes 786440 | tf_op jit(solution)/shard_map/ppermute | solution.py:49
  93.1 19.9 %collective-permute-start.21 = (bf16[256,512]{1,0:T(8,128)(2,1)}, bf16[256,512]{1,0:T(8,128)(2,1)}, u32[]{:S(2)}, u32[]{:S(2)}) collective-permute-start(bf16[256,512]{1,0:T(8,128)(2,1)} %get-tuple-element.66), channel_id=1, source_target_pairs={{1,0},{2,1},{3,2},{5,4},{6,5},{7,6},{9,8},{10,9},{11,10},{13,12},{... | collective-permute-start | bytes 786440 | tf_op jit(solution)/shard_map/ppermute | solution.py:49
  99.0 14.0 %collective-permute-start.22 = (bf16[256,512]{1,0:T(8,128)(2,1)}, bf16[256,512]{1,0:T(8,128)(2,1)}, u32[]{:S(2)}, u32[]{:S(2)}) collective-permute-start(bf16[256,512]{1,0:T(8,128)(2,1)} %add_convert_fusion.2), channel_id=1, source_target_pairs={{2,0},{3,1},{6,4},{7,5},{10,8},{11,9},{14,12},{15,13},{18,16},{19,... | collective-permute-start | bytes 786440 | tf_op jit(solution)/shard_map/ppermute | solution.py:49
  107.7 15.9 %copy-start.19 = (bf16[256,512]{1,0:T(8,128)(2,1)S(1)}, bf16[256,512]{1,0:T(8,128)(2,1)}, u32[]{:S(2)}) copy-start(bf16[256,512]{1,0:T(8,128)(2,1)} %get-tuple-element.73) | copy-start | bytes 786436
  114.1 6.4 %collective-permute-start.26 = (bf16[256,512]{1,0:T(8,128)(2,1)S(1)}, bf16[256,512]{1,0:T(8,128)(2,1)S(1)}, u32[]{:S(2)}, u32[]{:S(2)}) collective-permute-start(bf16[256,512]{1,0:T(8,128)(2,1)S(1)} %add_convert_fusion.refs_0_), channel_id=1, source_target_pairs={{0,8},{4,12},{8,0},{12,4},{16,24},{20,28},{24,16},{28,20},{1,9},{5... | collective-permute-start | bytes 786440 | tf_op jit(solution)/shard_map/ppermute | solution.py:43
  115.8 4.7 %collective-permute-start.23 = (bf16[256,512]{1,0:T(8,128)(2,1)S(1)}, bf16[256,512]{1,0:T(8,128)(2,1)S(1)}, u32[]{:S(2)}, u32[]{:S(2)}) collective-permute-start(bf16[256,512]{1,0:T(8,128)(2,1)S(1)} %copy-done.21), channel_id=1, source_target_pairs={{3,0},{7,4},{11,8},{15,12},{19,16},{23,20},{27,24},{31,28}} | collective-permute-start | bytes 786440 | tf_op jit(solution)/shard_map/ppermute | solution.py:49
  120.6 26.8 %copy-start.16 = (f32[256,512]{1,0:T(8,128)S(1)}, f32[256,512]{1,0:T(8,128)}, u32[]{:S(2)}) copy-start(f32[256,512]{1,0:T(8,128)} %get-tuple-element.63) | copy-start | bytes 1572868
  120.6 16.2 %collective-permute-start.27 = (bf16[512,512]{1,0:T(8,128)(2,1)S(1)}, bf16[512,512]{1,0:T(8,128)(2,1)S(1)}, u32[]{:S(2)}, u32[]{:S(2)}) collective-permute-start(bf16[512,512]{1,0:T(8,128)(2,1)S(1)} %pad_maximum_fusion.2), channel_id=1, source_target_pairs={{0,16},{4,20},{8,24},{12,28},{16,0},{20,4},{24,8},{28,12},{1,17},{... | collective-permute-start | bytes 1572872 | tf_op jit(solution)/shard_map/ppermute | solution.py:43
  122.3 15.6 %collective-permute-start.24 = (bf16[256,512]{1,0:T(8,128)(2,1)S(1)}, bf16[256,512]{1,0:T(8,128)(2,1)S(1)}, u32[]{:S(2)}, u32[]{:S(2)}) collective-permute-start(bf16[256,512]{1,0:T(8,128)(2,1)S(1)} %copy-done.20), channel_id=1, source_target_pairs={{2,0},{3,1},{6,4},{7,5},{10,8},{11,9},{14,12},{15,13},{18,16},{19,... | collective-permute-start | bytes 786440 | tf_op jit(solution)/shard_map/ppermute | solution.py:49
  123.6 23.7 %collective-permute-start.25 = (bf16[256,512]{1,0:T(8,128)(2,1)S(1)}, bf16[256,512]{1,0:T(8,128)(2,1)S(1)}, u32[]{:S(2)}, u32[]{:S(2)}) collective-permute-start(bf16[256,512]{1,0:T(8,128)(2,1)S(1)} %copy-done.19), channel_id=1, source_target_pairs={{1,0},{2,1},{3,2},{5,4},{6,5},{7,6},{9,8},{10,9},{11,10},{13,12},{... | collective-permute-start | bytes 786440 | tf_op jit(solution)/shard_map/ppermute | solution.py:49
  147.4 3.7 %collective-permute-start.28 = (bf16[1024,512]{1,0:T(8,128)(2,1)S(1)}, bf16[1024,512]{1,0:T(8,128)(2,1)S(1)}, u32[]{:S(2)}, u32[]{:S(2)}) collective-permute-start(bf16[1024,512]{1,0:T(8,128)(2,1)S(1)} %constant_dynamic-update-slice_fusion.refs_1_), channel_id=1, source_target_pairs={{0,4},{4,0},{8,12},{12,8},{16,20},{20,16},{24,28},{28,24},{1,5},{5... | collective-permute-start | bytes 3145736 | tf_op jit(solution)/shard_map/ppermute | solution.py:43
  147.5 10.1 %collective-permute-start.34 = (bf16[256,512]{1,0:T(8,128)(2,1)S(1)}, bf16[256,512]{1,0:T(8,128)(2,1)S(1)}, u32[]{:S(2)}, u32[]{:S(2)}) collective-permute-start(bf16[256,512]{1,0:T(8,128)(2,1)S(1)} %add_convert_fusion.1.refs_1_), channel_id=1, source_target_pairs={{0,24},{4,28},{8,16},{12,20},{16,8},{20,12},{24,0},{28,4},{1,25},{... | collective-permute-start | bytes 786440 | tf_op jit(solution)/shard_map/ppermute | solution.py:43
  148.7 14.1 %collective-permute-start.32 = (bf16[256,512]{1,0:T(8,128)(2,1)S(1)}, bf16[256,512]{1,0:T(8,128)(2,1)S(1)}, u32[]{:S(2)}, u32[]{:S(2)}) collective-permute-start(bf16[256,512]{1,0:T(8,128)(2,1)S(1)} %add_convert_fusion.1.refs_1_), channel_id=1, source_target_pairs={{0,16},{4,20},{8,24},{12,28},{16,0},{20,4},{24,8},{28,12},{1,17},{... | collective-permute-start | bytes 786440 | tf_op jit(solution)/shard_map/ppermute | solution.py:43
  149.6 13.2 %collective-permute-start.30 = (bf16[256,512]{1,0:T(8,128)(2,1)S(1)}, bf16[256,512]{1,0:T(8,128)(2,1)S(1)}, u32[]{:S(2)}, u32[]{:S(2)}) collective-permute-start(bf16[256,512]{1,0:T(8,128)(2,1)S(1)} %add_convert_fusion.1.refs_1_), channel_id=1, source_target_pairs={{0,8},{4,12},{8,0},{12,4},{16,24},{20,28},{24,16},{28,20},{1,9},{5... | collective-permute-start | bytes 786440 | tf_op jit(solution)/shard_map/ppermute | solution.py:43
  162.8 1.5 collective-permute-start.29
  162.8 1.9 collective-permute-start.31
  163.3 1.8 collective-permute-start.33
  163.3 2.1 %collective-permute-start.35 = (bf16[256,512]{1,0:T(8,128)(2,1)S(1)}, bf16[256,512]{1,0:T(8,128)(2,1)S(1)}, u32[]{:S(2)}, u32[]{:S(2)}) collective-permute-start(bf16[256,512]{1,0:T(8,128)(2,1)S(1)} %collective-permute-done.34.refs_7_), channel_id=1, source_target_pairs={{0,4},{4,0},{8,12},{12,8},{16,20},{20,16},{24,28},{28,24},{1,5},{5... | collective-permute-start | bytes 786440 | tf_op jit(solution)/shard_map/ppermute | solution.py:43
  167.8 12.5 %collective-permute-start.36 = (bf16[640,256]{1,0:T(8,128)(2,1)S(1)}, bf16[640,256]{1,0:T(8,128)(2,1)S(1)}, u32[]{:S(2)}, u32[]{:S(2)}) collective-permute-start(bf16[640,256]{1,0:T(8,128)(2,1)S(1)} %get-tuple-element.88), channel_id=1, source_target_pairs={{0,1},{1,0},{2,3},{3,2},{4,5},{5,4},{6,7},{7,6},{8,9},{9,8},{10,11... | collective-permute-start | bytes 983048 | tf_op jit(solution)/shard_map/ppermute | solution.py:43
  167.8 16.6 %collective-permute-start.37 = (bf16[640,256]{1,0:T(8,128)(2,1)S(1)}, bf16[640,256]{1,0:T(8,128)(2,1)S(1)}, u32[]{:S(2)}, u32[]{:S(2)}) collective-permute-start(bf16[640,256]{1,0:T(8,128)(2,1)S(1)} %get-tuple-element.89), channel_id=1, source_target_pairs={{0,2},{1,3},{2,0},{3,1},{4,6},{5,7},{6,4},{7,5},{8,10},{9,11},{10,... | collective-permute-start | bytes 983048 | tf_op jit(solution)/shard_map/ppermute | solution.py:43
  168.8 31.1 %collective-permute-start.38 = (bf16[640,256]{1,0:T(8,128)(2,1)S(1)}, bf16[640,256]{1,0:T(8,128)(2,1)S(1)}, u32[]{:S(2)}, u32[]{:S(2)}) collective-permute-start(bf16[640,256]{1,0:T(8,128)(2,1)S(1)} %get-tuple-element.90), channel_id=1, source_target_pairs={{0,3},{1,2},{2,1},{3,0},{4,7},{5,6},{6,5},{7,4},{8,11},{9,10},{10,... | collective-permute-start | bytes 983048 | tf_op jit(solution)/shard_map/ppermute | solution.py:43
  (14 other events, 84.7 us)

commit v4 on v3

--- a/solution.py
+++ b/solution.py
@@ -61,13 +61,9 @@
 
 def relay(value):
     steps = [value]
-    for step in range(1, lax.axis_size("seq") - 1):
+    for step in range(1, lax.axis_size("seq")):
         steps.append(moved(steps[-1], "seq", 1, step - 1))
     return steps
-
-
-def finish_relay(steps, *gates):
-    return [*steps, moved(after(steps[-1], *gates), "seq", 1, len(steps) - 1)]
 
 
 def finish(steps, *gates):
@@ -128,25 +124,23 @@
     return tuple(((at, 0, width), (at, width, width)) for at in range(count))
 
 
-def pack_kernel(near_ref, far_ref, own_ref, left_ref, right_ref, *, near_start, far_start):
-    width = own_ref.shape[1] // 2
-    left_ref[:, :width] = near_ref[:, near_start : near_start + width]
-    left_ref[:, width:] = own_ref[:, :width]
-    right_ref[:, :width] = far_ref[:, far_start : far_start + width]
-    right_ref[:, width:] = own_ref[:, width:]
-
-
-def pack(near, far, own, near_start, far_start):
-    shape = jax.ShapeDtypeStruct(own.shape, own.dtype)
+def halves_kernel(near_ref, far_ref, left_ref, right_ref, *, near_start, far_start):
+    width = left_ref.shape[1]
+    left_ref[...] = near_ref[:, near_start : near_start + width]
+    right_ref[...] = far_ref[:, far_start : far_start + width]
+
+
+def halves(near, far, near_start, far_start):
+    shape = jax.ShapeDtypeStruct((near.shape[0], near.shape[1] // 2), near.dtype)
     return pl.pallas_call(
-        functools.partial(pack_kernel, near_start=near_start, far_start=far_start),
+        functools.partial(halves_kernel, near_start=near_start, far_start=far_start),
         out_shape=[shape, shape],
-        in_specs=[vmem()] * 3,
+        in_specs=[vmem()] * 2,
         out_specs=[vmem()] * 2,
         compiler_params=params(),
         cost_estimate=lasting(1),
-        name="pack",
-    )(near, far, own)
+        name="halves",
+    )(near, far)
 
 
 def gather_weights(shards, behind, use_first):
@@ -159,30 +153,29 @@
             result.append((pieces, whole_table(count, width)))
         return result, [use_first(result[0])], pieces[-1:]
     first, second = shards
-    from_x, from_y = exchange(first, "dp", 2), exchange(first, "dp", 4)
-    here, there = after(from_x, *behind), after(from_y, *behind)
-    to_y, to_x = pack(here, there, second, 0, width)
-    step_y, step_x = exchange(to_y, "dp", 4), exchange(to_x, "dp", 2)
-    to_x, to_y = pack(step_y, step_x, second, width, width)
-    last_x, last_y = exchange(to_x, "dp", 2), exchange(to_y, "dp", 4)
-    near = [first, from_x, from_y, step_y, step_x]
-    near_core = [exchange(part, "dp", 1) for part in near]
-    one = [((0, 0), (0, 1)), ((1, 0), (1, 1)), ((2, 0), (2, 1)), ((3, 0), (4, 0))]
-    two = [((0, 0), (0, 1)), ((1, 1), (4, 1)), ((3, 1), (2, 1)), ((1, 0), (2, 0))]
-    tables = []
-    for entries in (one, two):
-        table = []
-        for entry in entries:
-            for core in range(2):
-                table.append(tuple((array + core * 5, part * width, width) for array, part in entry))
-        tables.append(tuple(table))
-    pieces = [(near + near_core, tables[0])]
+    table = []
+    for entry in [((0, 0), (0, 1)), ((1, 0), (1, 1)), ((2, 0), (2, 1)), ((3, 0), (4, 0))]:
+        for core in range(2):
+            table.append(tuple((array + core * 5, part * width, width) for array, part in entry))
+    table = tuple(table)
+
+    def near_of(own, *gates):
+        from_x, from_y = after((exchange(own, "dp", 2), exchange(own, "dp", 4)), *gates)
+        to_y, to_x = halves(from_x, from_y, 0, width)
+        return [from_x, from_y, exchange(to_y, "dp", 4), exchange(to_x, "dp", 2)]
+
+    def with_core(own, own_core, others):
+        cores = [exchange(part, "dp", 1) for part in others]
+        return [own, *others, own_core, *cores], table
+
+    others = near_of(first, *behind, second)
+    pieces = [with_core(first, exchange(first, "dp", 1), others)]
     used = use_first(pieces[0])
-    last_x, last_y = after((last_x, last_y), used[min(1, len(used) - 1)])
-    far = [second, last_x, last_y]
-    far_core = [exchange(part, "dp", 1) for part in far]
-    pieces.append((far + [step_y, step_x] + far_core + near_core[3:], tables[1]))
-    return pieces, [used], used[1:2]
+    hops = list(used[1:]) + [used[0]] * 3
+    second_core = exchange(after(second, used[0]), "dp", 1)
+    others = near_of(after(second, *others[2:]), hops[0], second_core)
+    pieces.append(with_core(second, second_core, others))
+    return pieces, [used], hops[1:2]
 
 
 def split_kernel(x_ref, *out_refs):
@@ -251,7 +244,6 @@
     k_scr, v_scr, dk_scr, dv_scr = refs[1 + seq_count :]
     head = pl.program_id(0)
     width = own_ref.shape[1] // 2
-    key_count = act_total * BLK
     scale = 1.0 / math.sqrt(HEAD_SIZE)
     columns = [pl.ds(pl.multiple_of(side * width + head * HEAD_SIZE, HEAD_SIZE), HEAD_SIZE) for side in range(2)]
     dk_scr[...] = jnp.zeros_like(dk_scr)
@@ -273,40 +265,45 @@
                 k_scr[rows, :] = kv_refs[2 * step][pl.ds(row, BLK), :]
                 v_scr[rows, :] = kv_refs[2 * step + 1][pl.ds(row, BLK), :]
 
-    for block in range(blocks_dev):
+    def attend_block(rows, slots):
+        span = slots * BLK
+        keys, values = k_scr[:span, :], v_scr[:span, :]
+        query, gradient = (
+            jnp.concatenate([ref[rows, at * HEAD_SIZE : (at + 1) * HEAD_SIZE] for at in range(group)], axis=0)
+            for ref in (q_ref, g_ref)
+        )
+        scores = dot(keys, query, 1, 1)
+        last = scores[span - BLK :]
+        key_pos = lax.broadcasted_iota(jnp.int32, last.shape, 0)
+        query_pos = lax.broadcasted_iota(jnp.int32, last.shape, 1) & (BLK - 1)
+        last = jnp.where(key_pos <= query_pos, last, MASKED)
+        scores = last if slots == 1 else jnp.concatenate([scores[: span - BLK], last], axis=0)
+        top = jnp.max(scores, axis=0, keepdims=True)
+        exponent = jnp.exp2((scores - top) * (scale * math.log2(math.e)))
+        probs = exponent * (1.0 / jnp.sum(exponent, axis=0, keepdims=True))
+        dprobs = dot(values, gradient, 1, 1)
+        delta = jnp.sum(probs * dprobs, axis=0, keepdims=True)
+        dscores = (probs * (dprobs - delta)).astype(jnp.bfloat16)
+        dk_scr[:span, :] += dot(dscores, query, 1, 0)
+        dv_scr[:span, :] += dot(probs.astype(jnp.bfloat16), gradient, 1, 0)
+        dquery = (dot(keys, dscores, 0, 0) * scale).T.astype(dq_ref.dtype)
+        for at in range(group):
+            dq_ref[rows, at * HEAD_SIZE : (at + 1) * HEAD_SIZE] = dquery[at * BLK : (at + 1) * BLK]
+
+    @pl.loop(0, blocks_dev)
+    def _(block):
         rank = info_ref[2 * act_total + block]
-        rows = slice(block * BLK, (block + 1) * BLK)
+        rows = pl.ds(pl.multiple_of(block * BLK, BLK), BLK)
 
         @pl.when(rank < 0)
         def _():
             dq_ref[rows, :] = jnp.zeros((BLK, group * HEAD_SIZE), dq_ref.dtype)
 
-        @pl.when(rank >= 0)
-        def _():
-            keys, values = k_scr[...], v_scr[...]
-            query = jnp.concatenate(
-                [q_ref[rows, at * HEAD_SIZE : (at + 1) * HEAD_SIZE] for at in range(group)], axis=0
-            )
-            gradient = jnp.concatenate(
-                [g_ref[rows, at * HEAD_SIZE : (at + 1) * HEAD_SIZE] for at in range(group)], axis=0
-            )
-            scores = dot(keys, query, 1, 1)
-            shape = scores.shape
-            key_pos = lax.broadcasted_iota(jnp.int32, shape, 0)
-            query_pos = rank * BLK + (lax.broadcasted_iota(jnp.int32, shape, 1) & (BLK - 1))
-            scores = jnp.where(key_pos <= query_pos, scores, MASKED)
-            top = jnp.max(scores, axis=0, keepdims=True)
-            exponent = jnp.exp((scores - top) * scale)
-            probs = exponent * (1.0 / jnp.sum(exponent, axis=0, keepdims=True))
-            probs_low = probs.astype(jnp.bfloat16)
-            dprobs = dot(values, gradient, 1, 1)
-            delta = jnp.sum(probs_low.astype(jnp.float32) * dprobs, axis=0, keepdims=True)
-            dscores = (probs * (dprobs - delta) * scale).astype(jnp.bfloat16)
-            dk_scr[...] += dot(dscores, query, 1, 0)
-            dv_scr[...] += dot(probs_low, gradient, 1, 0)
-            dquery = dot(keys, dscores, 0, 0).T.astype(dq_ref.dtype)
-            for at in range(group):
-                dq_ref[rows, at * HEAD_SIZE : (at + 1) * HEAD_SIZE] = dquery[at * BLK : (at + 1) * BLK]
+        for slots in range(1, act_total + 1):
+
+            @pl.when(rank == slots - 1)
+            def _():
+                attend_block(rows, slots)
 
     for target in (own_ref, *send_refs):
         for side in range(2):
@@ -319,7 +316,7 @@
 
             @pl.when(steps == step)
             def _():
-                target[pl.ds(row, BLK), columns[0]] = dk_scr[rows, :].astype(target.dtype)
+                target[pl.ds(row, BLK), columns[0]] = (dk_scr[rows, :] * scale).astype(target.dtype)
                 target[pl.ds(row, BLK), columns[1]] = dv_scr[rows, :].astype(target.dtype)
 
 
@@ -356,7 +353,7 @@
         + [pltpu.VMEM((act_total * BLK, HEAD_SIZE), jnp.float32)] * 2,
         input_output_aliases=aliases,
         compiler_params=pltpu.CompilerParams(vmem_limit_bytes=60 * 1024 * 1024),
-        cost_estimate=lasting(9),
+        cost_estimate=lasting(2 if chunk == 1 else 9),
         name="attend",
     )(*operands)
     return outs[0], outs[1], outs[2:]
@@ -496,10 +493,10 @@
     arrivals, keyvals = keyvals, [steps[0] for steps in keyvals]
     for chunk in range(1, CHUNKS):
         keyvals.append(project(rank, x_by_owner, weight_pieces[chunk]))
-        arrivals[-1] = (finish_relay if chunk == 1 else finish)(arrivals[-1], keyvals[-1])
+        arrivals[-1] = arrivals[-1] if chunk == 1 else finish(arrivals[-1], keyvals[-1])
         arrivals.append(spread(keyvals[-1]))
     arrivals = [steps[1:] for steps in [*arrivals[:-1], finish(arrivals[-1])]]
-    x_all, gates = [], weight_gates
+    x_all, gates = [], (keyvals[-1],)
     for part in x_by_owner:
         part = lax.all_to_all(after(part, *gates), "dp", split_axis=0, concat_axis=0, tiled=True)
         x_all.append(part)
@@ -519,7 +516,7 @@
             arrived = ()
         backs.append(back)
         owns.append(own)
-        gates, waits, later = (*arrived, *x_all), tuple(back), ()
+        gates, waits, later = tuple(arrived), (*back, *x_all), ()
     gates, sums = (owns[-1],), ()
     for chunk in range(CHUNKS):
         total = after(owns[chunk], *gates)

time: 201 us -> 200 us (level)
  waiting for transfers between devices: 95 us -> 88.4 us
  Pallas kernels: 33.3 us -> 35.9 us
    ppermute x27 -> x31, waiting for transfers between devices: 67.6 us -> 60.7 us  [exchange(): return lax.ppermute(value, axis, [(i, i ^ mask) for i in range(count)])]
    ppermute x12, waiting for transfers between devices: 23.5 us -> 27.7 us  [moved(): return lax.ppermute(value, axis, pairs)]
    all_to_all x1, waiting for transfers between devices: 3.88 us -> 0.01 us  [body(): lax.all_to_all(after(part, *gates), 'dp', split_axis=0, concat_axis=0, ti...]
    pallas_call x2, Pallas kernels: 6.64 us -> 10.5 us  [attend(): pl.pallas_call(functools.partial(attend_kernel, sizes), grid=(heads,), ou...]
    ppermute x27 -> x31, starting transfers between devices: 20.8 us -> 24 us  [exchange(): return lax.ppermute(value, axis, [(i, i ^ mask) for i in range(count)])]
    ppermute x12, starting transfers between devices: 39.6 us -> 37.3 us  [moved(): return lax.ppermute(value, axis, pairs)]
  transfers between devices with their start and end apart: 40 -> 44, of which waited for: 21 -> 25; matrix products, arithmetic and copies ran while one was open for 1% -> 3% of each run, Pallas kernels for 15% -> 17%
where the time goes in v4:
time: 200 us; the launch traced here: 199 us
  waiting for transfers between devices  88.4 us (44%)
  starting transfers between devices  64.9 us (32%)
  Pallas kernels  35.9 us (18%)
  other arithmetic  5.99 us (3%)
  local copies, waits for them, and re-layouts  2.94 us (1%)
    ppermute x31, waiting for transfers between devices, exchange(): return lax.ppermute(value, axis, [(i, i ^ mask) for i in range(count)])  60.7 us
    ppermute x12, starting transfers between devices, moved(): return lax.ppermute(value, axis, pairs)  37.3 us
    ppermute x12, waiting for transfers between devices, moved(): return lax.ppermute(value, axis, pairs)  27.7 us
    ppermute x31, starting transfers between devices, exchange(): return lax.ppermute(value, axis, [(i, i ^ mask) for i in range(count)])  24 us
    pallas_call x2, Pallas kernels, attend(): pl.pallas_call(functools.partial(attend_kernel, sizes), grid=(heads,), ou...  10.5 us
    pallas_call x2, Pallas kernels, project(): pl.pallas_call(functools.partial(project_kernel, table), out_shape=jax.Sh...  8.78 us
    pallas_call x1, Pallas kernels, token_grads(): pl.pallas_call(functools.partial(token_kernel, tables, tuple(indices)), o...  7.21 us
    pallas_call x2, Pallas kernels, weight_terms(): pl.pallas_call(functools.partial(weight_kernel, dests, len(pieces), bool(...  4.48 us
  transfers between devices with their start and end apart: 44, of which 25 were waited for; matrix products, arithmetic and copies ran while one was open for 3% of the time, Pallas kernels for 17%

profile of v4, /device:TPU:8, one launch (start us, length us, event | category | flops | bytes accessed | tf_op | source)
XLA Modules:
  0.0 199.4 jit_solution(5058634336875989618)
XLA Ops:
  0.6 1.4 fusion.2
  2.1 1.6 collective-permute-start.1
  3.7 1.5 collective-permute-start
  5.3 3.4 %split_columns.1.refs_0_ = bf16[8,256,640]{2,1,0:T(8,128)(2,1)} custom-call(bf16[1,256,5120]{2,1,0:T(8,128)(2,1)S(1)} %copy-done.2), custom_call_target="tpu_custom_call" | custom-call | flops 12000000000 | bytes 36000000 | tf_op jit(solution)/shard_map/split_columns/pallas_call | solution.py:195
  8.7 10.6 %collective-permute-done.1.far_ref.refs_3_.refs_4_ = bf16[640,512]{1,0:T(8,128)(2,1)S(1)} collective-permute-done((bf16[640,512]{1,0:T(8,128)(2,1)S(1)}, bf16[640,512]{1,0:T(8,128)(2,1)S(1)}, u32[]{:S(2)}, u32[]{:S(2)}) %collective-permute-start.1) | collective-permute-done | bytes 655392 | tf_op jit(solution)/shard_map/ppermute | solution.py:43
  19.3 1.2 collective-permute-done.near_ref.refs_2_.refs_3_
  21.2 1.5 collective-permute-start.3
  23.2 6.5 %collective-permute-done.2.refs_4_.refs_5_ = bf16[640,256]{1,0:T(8,128)(2,1)} collective-permute-done((bf16[640,256]{1,0:T(8,128)(2,1)S(1)}, bf16[640,256]{1,0:T(8,128)(2,1)}, u32[]{:S(2)}, u32[]{:S(2)}) %collective-permute-start.2) | collective-permute-done | bytes 327712 | tf_op jit(solution)/shard_map/ppermute | solution.py:43
  30.3 1.3 collective-permute-start.5
  31.7 1.5 collective-permute-start.4
  33.2 4.3 %project.2.refs_0_.refs_1_ = bf16[256,512]{1,0:T(8,128)(2,1)S(1)} custom-call(s32[2]{0:T(128)S(1)} %pad_add_fusion.1.rank_ref, bf16[8,256,640]{2,1,0:T(8,128)(2,1)} %split_columns.1.refs_0_, bf16[640,512]{1,0:T(8,128)(2,1)S(1)} %pad_maximum_fusion.1.refs_1_.refs_2_, bf16[640,512]{1,0:T(8,128)(2,1)S(1)} %collective-permute-done.near_ref.refs_2_.refs_3_, ...), custom_call_target="tpu_custom_call" | custom-call | flops 16000000000 | bytes 48000000 | tf_op jit(solution)/shard_map/project/pallas_call | solution.py:227
  37.6 3.5 %collective-permute-start.11 = (bf16[256,512]{1,0:T(8,128)(2,1)S(1)}, bf16[256,512]{1,0:T(8,128)(2,1)}, u32[]{:S(2)}, u32[]{:S(2)}) collective-permute-start(bf16[256,512]{1,0:T(8,128)(2,1)S(1)} %project.2.refs_0_.refs_1_), channel_id=1, source_target_pairs={{0,1},{1,2},{2,3},{4,5},{5,6},{6,7},{8,9},{9,10},{10,11},{12,13},{... | collective-permute-start | bytes 786440 | tf_op jit(solution)/shard_map/ppermute | solution.py:49
  41.1 7.2 %collective-permute-done.11.refs_2_.refs_3_ = bf16[256,512]{1,0:T(8,128)(2,1)} collective-permute-done((bf16[256,512]{1,0:T(8,128)(2,1)S(1)}, bf16[256,512]{1,0:T(8,128)(2,1)}, u32[]{:S(2)}, u32[]{:S(2)}) %collective-permute-start.11) | collective-permute-done | bytes 262176 | tf_op jit(solution)/shard_map/ppermute | solution.py:49
  48.6 1.6 halves.3
  51.1 1.5 collective-permute-start.14
  52.8 4.2 %collective-permute-start.19 = (bf16[256,512]{1,0:T(8,128)(2,1)}, bf16[256,512]{1,0:T(8,128)(2,1)}, u32[]{:S(2)}, u32[]{:S(2)}) collective-permute-start(bf16[256,512]{1,0:T(8,128)(2,1)} %collective-permute-done.11.refs_2_.refs_3_), channel_id=1, source_target_pairs={{1,2},{2,3},{5,6},{6,7},{9,10},{10,11},{13,14},{14,15},{17,18},{18... | collective-permute-start | bytes 786440 | tf_op jit(solution)/shard_map/ppermute | solution.py:49
  57.0 3.4 %collective-permute-done.13.refs_4_.refs_15_ = bf16[640,256]{1,0:T(8,128)(2,1)S(1)} collective-permute-done((bf16[640,256]{1,0:T(8,128)(2,1)S(1)}, bf16[640,256]{1,0:T(8,128)(2,1)S(1)}, u32[]{:S(2)}, u32[]{:S(2)}) %collective-permute-start.13) | collective-permute-done | bytes 327712 | tf_op jit(solution)/shard_map/ppermute | solution.py:43
  62.0 1.4 collective-permute-start.20
  63.4 4.5 %project.3.refs_0_.refs_1_ = bf16[256,512]{1,0:T(8,128)(2,1)S(1)} custom-call(s32[2]{0:T(128)S(1)} %pad_add_fusion.1.rank_ref, bf16[8,256,640]{2,1,0:T(8,128)(2,1)} %split_columns.1.refs_0_, bf16[640,512]{1,0:T(8,128)(2,1)S(1)} %pad_maximum_fusion.refs_1_.refs_12_, bf16[640,512]{1,0:T(8,128)(2,1)} %collective-permute-done.4.near_ref.refs_2_.refs_13_, ...), custom_call_target="tpu_custom_call" | custom-call | flops 16000000000 | bytes 48000000 | tf_op jit(solution)/shard_map/project/pallas_call | solution.py:227
  68.0 6.0 %collective-permute-start.21 = (bf16[256,512]{1,0:T(8,128)(2,1)S(1)}, bf16[256,512]{1,0:T(8,128)(2,1)}, u32[]{:S(2)}, u32[]{:S(2)}) collective-permute-start(bf16[256,512]{1,0:T(8,128)(2,1)S(1)} %project.3.refs_0_.refs_1_), channel_id=1, source_target_pairs={{0,2},{1,3},{4,6},{5,7},{8,10},{9,11},{12,14},{13,15},{16,18},{17,... | collective-permute-start | bytes 786440 | tf_op jit(solution)/shard_map/ppermute | solution.py:49
  74.1 3.6 %all-to-all-start = ((bf16[8,256,640]{2,1,0:T(8,128)(2,1)}), bf16[8,256,640]{2,1,0:T(8,128)(2,1)S(1)}, u32[]{:S(2)}, u32[]{:S(2)}) async-start(bf16[8,256,640]{2,1,0:T(8,128)(2,1)} %split_columns.1.refs_0_), calls=%async_computation | async-start | bytes 5242880 | tf_op jit(solution)/shard_map/all_to_all | solution.py:501
  77.7 5.2 %attend.2 = (bf16[1,256,2560]{2,1,0:T(8,128)(2,1)}, f32[256,512]{1,0:T(8,128)}, bf16[256,512]{1,0:T(8,128)(2,1)}, bf16[256,512]{1,0:T(8,128)(2,1)}, bf16[256,512]{1,0:T(8,128)(2,1)}) custom-call(s32[10]{0:T(128)} %pad_add_fusion.info_ref, bf16[1,256,2560]{2,1,0:T(8,128)(2,1)} %q_ref.3, bf16[1,256,2560]{2,1,0:T(8,128)(2,1)} %g_ref.3, ...), custom_call_target="tpu_custom_call" | custom-call | flops 35999997952 | bytes 108000000 | tf_op jit(solution)/shard_map/attend/pallas_call | solution.py:342
  84.3 2.1 %collective-permute-start.23 = (bf16[256,512]{1,0:T(8,128)(2,1)S(1)}, bf16[256,512]{1,0:T(8,128)(2,1)S(1)}, u32[]{:S(2)}, u32[]{:S(2)}) collective-permute-start(bf16[256,512]{1,0:T(8,128)(2,1)S(1)} %project.3.refs_0_.refs_1_), channel_id=1, source_target_pairs={{0,1},{1,2},{2,3},{4,5},{5,6},{6,7},{8,9},{9,10},{10,11},{12,13},{... | collective-permute-start | bytes 786440 | tf_op jit(solution)/shard_map/ppermute | solution.py:49
  87.1 3.8 %collective-permute-start.25 = (bf16[256,512]{1,0:T(8,128)(2,1)}, bf16[256,512]{1,0:T(8,128)(2,1)}, u32[]{:S(2)}, u32[]{:S(2)}) collective-permute-start(bf16[256,512]{1,0:T(8,128)(2,1)} %get-tuple-element.68), channel_id=1, source_target_pairs={{1,0},{2,1},{3,2},{5,4},{6,5},{7,6},{9,8},{10,9},{11,10},{13,12},{... | collective-permute-start | bytes 786440 | tf_op jit(solution)/shard_map/ppermute | solution.py:49
  90.9 1.7 add_convert_fusion.2
  92.6 1.5 collective-permute-start.26
  95.9 5.3 %attend.3 = (bf16[1,256,2560]{2,1,0:T(8,128)(2,1)}, f32[256,512]{1,0:T(8,128)}, bf16[256,512]{1,0:T(8,128)(2,1)}, bf16[256,512]{1,0:T(8,128)(2,1)}, bf16[256,512]{1,0:T(8,128)(2,1)}) custom-call(s32[10]{0:T(128)} %pad_add_fusion.info_ref, bf16[1,256,2560]{2,1,0:T(8,128)(2,1)} %q_ref.3, ...), custom_call_target="tpu_custom_call", output_to_operand_aliasing={{0}: (11, {})} | custom-call | flops 8000000000 | bytes 24000000 | tf_op jit(solution)/shard_map/attend/pallas_call | solution.py:342
  101.2 6.1 %collective-permute-done.25 = bf16[256,512]{1,0:T(8,128)(2,1)} collective-permute-done((bf16[256,512]{1,0:T(8,128)(2,1)}, bf16[256,512]{1,0:T(8,128)(2,1)}, u32[]{:S(2)}, u32[]{:S(2)}) %collective-permute-start.25) | collective-permute-done | bytes 262176 | tf_op jit(solution)/shard_map/ppermute | solution.py:49
  107.3 1.1 add_convert_fusion.refs_0_
  108.5 2.9 %collective-permute-start.30 = (bf16[256,512]{1,0:T(8,128)(2,1)S(1)}, bf16[256,512]{1,0:T(8,128)(2,1)}, u32[]{:S(2)}, u32[]{:S(2)}) collective-permute-start(bf16[256,512]{1,0:T(8,128)(2,1)S(1)} %add_convert_fusion.refs_0_), channel_id=1, source_target_pairs={{0,8},{4,12},{8,0},{12,4},{16,24},{20,28},{24,16},{28,20},{1,9},{5... | collective-permute-start | bytes 786440 | tf_op jit(solution)/shard_map/ppermute | solution.py:43
  112.0 5.8 %collective-permute-done.30 = bf16[256,512]{1,0:T(8,128)(2,1)} collective-permute-done((bf16[256,512]{1,0:T(8,128)(2,1)S(1)}, bf16[256,512]{1,0:T(8,128)(2,1)}, u32[]{:S(2)}, u32[]{:S(2)}) %collective-permute-start.30) | collective-permute-done | bytes 262176 | tf_op jit(solution)/shard_map/ppermute | solution.py:43
  118.9 1.6 collective-permute-start.31
  120.5 1.3 collective-permute-start.28
  121.8 11.6 %collective-permute-start.29 = (bf16[256,512]{1,0:T(8,128)(2,1)}, bf16[256,512]{1,0:T(8,128)(2,1)S(1)}, u32[]{:S(2)}, u32[]{:S(2)}) collective-permute-start(bf16[256,512]{1,0:T(8,128)(2,1)} %get-tuple-element.75), channel_id=1, source_target_pairs={{1,0},{2,1},{3,2},{5,4},{6,5},{7,6},{9,8},{10,9},{11,10},{13,12},{... | collective-permute-start | bytes 786440 | tf_op jit(solution)/shard_map/ppermute | solution.py:49
  133.5 1.6 collective-permute-done.28
  135.1 11.2 %collective-permute-done.29 = bf16[256,512]{1,0:T(8,128)(2,1)S(1)} collective-permute-done((bf16[256,512]{1,0:T(8,128)(2,1)}, bf16[256,512]{1,0:T(8,128)(2,1)S(1)}, u32[]{:S(2)}, u32[]{:S(2)}) %collective-permute-start.29) | collective-permute-done | bytes 262176 | tf_op jit(solution)/shard_map/ppermute | solution.py:49
  147.3 1.3 collective-permute-start.36
  148.6 1.4 collective-permute-start.34
  150.0 2.2 %weight_grad.2 = (f32[640,256]{1,0:T(8,128)S(1)}, bf16[640,256]{1,0:T(8,128)(2,1)S(1)}, bf16[640,256]{1,0:T(8,128)(2,1)S(1)}, bf16[640,256]{1,0:T(8,128)(2,1)S(1)}) custom-call(s32[2]{0:T(128)S(1)} %pad_add_fusion.1.rank_ref, bf16[8,256,640]{2,1,0:T(8,128)(2,1)S(1)} %all-to-all-done.refs_0_, bf16[1024,512]{1,0:T(8,128)(2,1)S(1)} %constant_dynamic-update-slice_fusion.refs_1_, ...), custom_call_target="tpu_custom_call" | custom-call | flops 16000000000 | bytes 48000000 | tf_op jit(solution)/shard_map/weight_grad/pallas_call | solution.py:443
  152.2 4.3 %collective-permute-done.38.refs_7_ = bf16[256,512]{1,0:T(8,128)(2,1)S(1)} collective-permute-done((bf16[256,512]{1,0:T(8,128)(2,1)S(1)}, bf16[256,512]{1,0:T(8,128)(2,1)S(1)}, u32[]{:S(2)}, u32[]{:S(2)}) %collective-permute-start.38) | collective-permute-done | bytes 262176 | tf_op jit(solution)/shard_map/ppermute | solution.py:43
  156.5 4.8 %collective-permute-done.36.refs_5_ = bf16[256,512]{1,0:T(8,128)(2,1)S(1)} collective-permute-done((bf16[256,512]{1,0:T(8,128)(2,1)S(1)}, bf16[256,512]{1,0:T(8,128)(2,1)S(1)}, u32[]{:S(2)}, u32[]{:S(2)}) %collective-permute-start.36) | collective-permute-done | bytes 262176 | tf_op jit(solution)/shard_map/ppermute | solution.py:43
  164.0 2.3 %weight_grad.3 = (f32[640,256]{1,0:T(8,128)S(1)}, bf16[640,256]{1,0:T(8,128)(2,1)S(1)}, bf16[640,256]{1,0:T(8,128)(2,1)S(1)}, bf16[640,256]{1,0:T(8,128)(2,1)S(1)}) custom-call(s32[2]{0:T(128)S(1)} %pad_add_fusion.1.rank_ref, bf16[8,256,640]{2,1,0:T(8,128)(2,1)S(1)} %all-to-all-done.refs_0_, bf16[256,512]{1,0:T(8,128)(2,1)S(1)} %add_convert_fusion.1.refs_1_, ...), custom_call_target="tpu_custom_call" | custom-call | flops 16000000000 | bytes 48000000 | tf_op jit(solution)/shard_map/weight_grad/pallas_call | solution.py:443
  166.4 1.1 collective-permute-start.41
  167.5 2.4 %collective-permute-start.42 = (bf16[640,256]{1,0:T(8,128)(2,1)S(1)}, bf16[640,256]{1,0:T(8,128)(2,1)S(1)}, u32[]{:S(2)}, u32[]{:S(2)}) collective-permute-start(bf16[640,256]{1,0:T(8,128)(2,1)S(1)} %get-tuple-element.92), channel_id=1, source_target_pairs={{0,3},{1,2},{2,1},{3,0},{4,7},{5,6},{6,5},{7,4},{8,11},{9,10},{10,... | collective-permute-start | bytes 983048 | tf_op jit(solution)/shard_map/ppermute | solution.py:43
  170.0 7.2 %token_grads.1 = bf16[256,5120]{1,0:T(8,128)(2,1)} custom-call(s32[2]{0:T(128)S(1)} %pad_add_fusion.1.rank_ref, bf16[256,512]{1,0:T(8,128)(2,1)S(1)} %add_convert_fusion.refs_0_, bf16[256,512]{1,0:T(8,128)(2,1)S(1)} %add_convert_fusion.1.refs_1_, bf16[640,512]{1,0:T(8,128)(2,1)S(1)} %pad_maximum_fusion.1.refs_1_.refs_2_, bf16[640,512]{1,0:T(8,128)(2,1)S(1)} %copy-done.8, ...), custom_call_target="tpu_custom_call" | custom-call | flops 32000000000 | bytes 96000000 | tf_op jit(solution)/shard_map/token_grads/pallas_call | solution.py:400
  177.2 1.7 collective-permute-done.40
  178.9 10.6 %collective-permute-done.41 = bf16[640,256]{1,0:T(8,128)(2,1)S(1)} collective-permute-done((bf16[640,256]{1,0:T(8,128)(2,1)S(1)}, bf16[640,256]{1,0:T(8,128)(2,1)S(1)}, u32[]{:S(2)}, u32[]{:S(2)}) %collective-permute-start.41) | collective-permute-done | bytes 327712 | tf_op jit(solution)/shard_map/ppermute | solution.py:43
  189.5 8.9 %collective-permute-done.42 = bf16[640,256]{1,0:T(8,128)(2,1)S(1)} collective-permute-done((bf16[640,256]{1,0:T(8,128)(2,1)S(1)}, bf16[640,256]{1,0:T(8,128)(2,1)S(1)}, u32[]{:S(2)}, u32[]{:S(2)}) %collective-permute-start.42) | collective-permute-done | bytes 327712 | tf_op jit(solution)/shard_map/ppermute | solution.py:43
  (127 shorter events, 15.6 us)
Async XLA Ops:
  2.1 28.2 %collective-permute-start.6 = (bf16[640,512]{1,0:T(8,128)(2,1)S(1)}, bf16[640,512]{1,0:T(8,128)(2,1)S(1)}, u32[]{:S(2)}, u32[]{:S(2)}) collective-permute-start(bf16[640,512]{1,0:T(8,128)(2,1)S(1)} %pad_maximum_fusion.1.refs_1_.refs_2_), channel_id=1, source_target_pairs={{0,4},{4,0},{8,12},{12,8},{16,20},{20,16},{24,28},{28,24},{1,5},{5... | collective-permute-start | bytes 1966088 | tf_op jit(solution)/shard_map/ppermute | solution.py:43
  2.1 17.1 %collective-permute-start.1 = (bf16[640,512]{1,0:T(8,128)(2,1)S(1)}, bf16[640,512]{1,0:T(8,128)(2,1)S(1)}, u32[]{:S(2)}, u32[]{:S(2)}) collective-permute-start(bf16[640,512]{1,0:T(8,128)(2,1)S(1)} %pad_maximum_fusion.1.refs_1_.refs_2_), channel_id=1, source_target_pairs={{0,16},{4,20},{8,24},{12,28},{16,0},{20,4},{24,8},{28,12},{1,17},{... | collective-permute-start | bytes 1966088 | tf_op jit(solution)/shard_map/ppermute | solution.py:43
  3.7 16.8 %collective-permute-start = (bf16[640,512]{1,0:T(8,128)(2,1)S(1)}, bf16[640,512]{1,0:T(8,128)(2,1)S(1)}, u32[]{:S(2)}, u32[]{:S(2)}) collective-permute-start(bf16[640,512]{1,0:T(8,128)(2,1)S(1)} %pad_maximum_fusion.1.refs_1_.refs_2_), channel_id=1, source_target_pairs={{0,8},{4,12},{8,0},{12,4},{16,24},{20,28},{24,16},{28,20},{1,9},{5... | collective-permute-start | bytes 1966088 | tf_op jit(solution)/shard_map/ppermute | solution.py:43
  5.3 58.1 %copy-start = (bf16[640,512]{1,0:T(8,128)(2,1)}, bf16[640,512]{1,0:T(8,128)(2,1)S(1)}, u32[]{:S(2)}) copy-start(bf16[640,512]{1,0:T(8,128)(2,1)S(1)} %pad_maximum_fusion.refs_1_.refs_12_) | copy-start | bytes 1966084
  20.6 9.1 %collective-permute-start.2 = (bf16[640,256]{1,0:T(8,128)(2,1)S(1)}, bf16[640,256]{1,0:T(8,128)(2,1)}, u32[]{:S(2)}, u32[]{:S(2)}) collective-permute-start(bf16[640,256]{1,0:T(8,128)(2,1)S(1)} %get-tuple-element.50), channel_id=1, source_target_pairs={{0,16},{4,20},{8,24},{12,28},{16,0},{20,4},{24,8},{28,12},{1,17},{... | collective-permute-start | bytes 983048 | tf_op jit(solution)/shard_map/ppermute | solution.py:43
  21.2 8.9 %collective-permute-start.3 = (bf16[640,256]{1,0:T(8,128)(2,1)S(1)}, bf16[640,256]{1,0:T(8,128)(2,1)}, u32[]{:S(2)}, u32[]{:S(2)}) collective-permute-start(bf16[640,256]{1,0:T(8,128)(2,1)S(1)} %get-tuple-element.51), channel_id=1, source_target_pairs={{0,8},{4,12},{8,0},{12,4},{16,24},{20,28},{24,16},{28,20},{1,9},{5... | collective-permute-start | bytes 983048 | tf_op jit(solution)/shard_map/ppermute | solution.py:43
  22.7 10.5 %collective-permute-start.7 = (bf16[640,512]{1,0:T(8,128)(2,1)S(1)}, bf16[640,512]{1,0:T(8,128)(2,1)}, u32[]{:S(2)}, u32[]{:S(2)}) collective-permute-start(bf16[640,512]{1,0:T(8,128)(2,1)S(1)} %collective-permute-done.near_ref.refs_2_.refs_3_), channel_id=1, source_target_pairs={{0,4},{4,0},{8,12},{12,8},{16,20},{20,16},{24,28},{28,24},{1,5},{5... | collective-permute-start | bytes 1966088 | tf_op jit(solution)/shard_map/ppermute | solution.py:43
  22.7 10.5 %collective-permute-start.8 = (bf16[640,512]{1,0:T(8,128)(2,1)S(1)}, bf16[640,512]{1,0:T(8,128)(2,1)}, u32[]{:S(2)}, u32[]{:S(2)}) collective-permute-start(bf16[640,512]{1,0:T(8,128)(2,1)S(1)} %collective-permute-done.1.far_ref.refs_3_.refs_4_), channel_id=1, source_target_pairs={{0,4},{4,0},{8,12},{12,8},{16,20},{20,16},{24,28},{28,24},{1,5},{5... | collective-permute-start | bytes 1966088 | tf_op jit(solution)/shard_map/ppermute | solution.py:43
  29.7 2.0 collective-permute-start.9
  30.0 3.1 %collective-permute-start.10 = (bf16[640,256]{1,0:T(8,128)(2,1)}, bf16[640,256]{1,0:T(8,128)(2,1)}, u32[]{:S(2)}, u32[]{:S(2)}) collective-permute-start(bf16[640,256]{1,0:T(8,128)(2,1)} %collective-permute-done.3.refs_5_.refs_6_), channel_id=1, source_target_pairs={{0,4},{4,0},{8,12},{12,8},{16,20},{20,16},{24,28},{28,24},{1,5},{5... | collective-permute-start | bytes 983048 | tf_op jit(solution)/shard_map/ppermute | solution.py:43
  30.3 18.0 %collective-permute-start.5 = (bf16[640,512]{1,0:T(8,128)(2,1)S(1)}, bf16[640,512]{1,0:T(8,128)(2,1)}, u32[]{:S(2)}, u32[]{:S(2)}) collective-permute-start(bf16[640,512]{1,0:T(8,128)(2,1)S(1)} %pad_maximum_fusion.refs_1_.refs_12_), channel_id=1, source_target_pairs={{0,16},{4,20},{8,24},{12,28},{16,0},{20,4},{24,8},{28,12},{1,17},{... | collective-permute-start | bytes 1966088 | tf_op jit(solution)/shard_map/ppermute | solution.py:43
  31.7 16.9 %collective-permute-start.4 = (bf16[640,512]{1,0:T(8,128)(2,1)S(1)}, bf16[640,512]{1,0:T(8,128)(2,1)}, u32[]{:S(2)}, u32[]{:S(2)}) collective-permute-start(bf16[640,512]{1,0:T(8,128)(2,1)S(1)} %pad_maximum_fusion.refs_1_.refs_12_), channel_id=1, source_target_pairs={{0,8},{4,12},{8,0},{12,4},{16,24},{20,28},{24,16},{28,20},{1,9},{5... | collective-permute-start | bytes 1966088 | tf_op jit(solution)/shard_map/ppermute | solution.py:43
  37.5 11.1 %collective-permute-start.12 = (bf16[640,512]{1,0:T(8,128)(2,1)S(1)}, bf16[640,512]{1,0:T(8,128)(2,1)S(1)}, u32[]{:S(2)}, u32[]{:S(2)}) collective-permute-start(bf16[640,512]{1,0:T(8,128)(2,1)S(1)} %pad_maximum_fusion.refs_1_.refs_12_), channel_id=1, source_target_pairs={{0,4},{4,0},{8,12},{12,8},{16,20},{20,16},{24,28},{28,24},{1,5},{5... | collective-permute-start | bytes 1966088 | tf_op jit(solution)/shard_map/ppermute | solution.py:43
  37.6 10.7 %collective-permute-start.11 = (bf16[256,512]{1,0:T(8,128)(2,1)S(1)}, bf16[256,512]{1,0:T(8,128)(2,1)}, u32[]{:S(2)}, u32[]{:S(2)}) collective-permute-start(bf16[256,512]{1,0:T(8,128)(2,1)S(1)} %project.2.refs_0_.refs_1_), channel_id=1, source_target_pairs={{0,1},{1,2},{2,3},{4,5},{5,6},{6,7},{8,9},{9,10},{10,11},{12,13},{... | collective-permute-start | bytes 786440 | tf_op jit(solution)/shard_map/ppermute | solution.py:49
  48.6 14.8 %copy-start.9 = (bf16[640,512]{1,0:T(8,128)(2,1)}, bf16[640,512]{1,0:T(8,128)(2,1)S(1)}, u32[]{:S(2)}) copy-start(bf16[640,512]{1,0:T(8,128)(2,1)S(1)} %collective-permute-done.12.refs_6_.refs_17_) | copy-start | bytes 1966084
  48.6 14.8 %collective-permute-start.15 = (bf16[640,512]{1,0:T(8,128)(2,1)}, bf16[640,512]{1,0:T(8,128)(2,1)S(1)}, u32[]{:S(2)}, u32[]{:S(2)}) collective-permute-start(bf16[640,512]{1,0:T(8,128)(2,1)} %collective-permute-done.4.near_ref.refs_2_.refs_13_), channel_id=1, source_target_pairs={{0,4},{4,0},{8,12},{12,8},{16,20},{20,16},{24,28},{28,24},{1,5},{5... | collective-permute-start | bytes 1966088 | tf_op jit(solution)/shard_map/ppermute | solution.py:43
  50.2 13.2 %collective-permute-start.16 = (bf16[640,512]{1,0:T(8,128)(2,1)}, bf16[640,512]{1,0:T(8,128)(2,1)S(1)}, u32[]{:S(2)}, u32[]{:S(2)}) collective-permute-start(bf16[640,512]{1,0:T(8,128)(2,1)} %collective-permute-done.5.far_ref.refs_3_.refs_14_), channel_id=1, source_target_pairs={{0,4},{4,0},{8,12},{12,8},{16,20},{20,16},{24,28},{28,24},{1,5},{5... | collective-permute-start | bytes 1966088 | tf_op jit(solution)/shard_map/ppermute | solution.py:43
  50.5 9.9 %collective-permute-start.13 = (bf16[640,256]{1,0:T(8,128)(2,1)S(1)}, bf16[640,256]{1,0:T(8,128)(2,1)S(1)}, u32[]{:S(2)}, u32[]{:S(2)}) collective-permute-start(bf16[640,256]{1,0:T(8,128)(2,1)S(1)} %get-tuple-element.56), channel_id=1, source_target_pairs={{0,16},{4,20},{8,24},{12,28},{16,0},{20,4},{24,8},{28,12},{1,17},{... | collective-permute-start | bytes 983048 | tf_op jit(solution)/shard_map/ppermute | solution.py:43
  51.1 9.6 %collective-permute-start.14 = (bf16[640,256]{1,0:T(8,128)(2,1)S(1)}, bf16[640,256]{1,0:T(8,128)(2,1)S(1)}, u32[]{:S(2)}, u32[]{:S(2)}) collective-permute-start(bf16[640,256]{1,0:T(8,128)(2,1)S(1)} %get-tuple-element.57), channel_id=1, source_target_pairs={{0,8},{4,12},{8,0},{12,4},{16,24},{20,28},{24,16},{28,20},{1,9},{5... | collective-permute-start | bytes 983048 | tf_op jit(solution)/shard_map/ppermute | solution.py:43
  52.8 9.2 %collective-permute-start.19 = (bf16[256,512]{1,0:T(8,128)(2,1)}, bf16[256,512]{1,0:T(8,128)(2,1)}, u32[]{:S(2)}, u32[]{:S(2)}) collective-permute-start(bf16[256,512]{1,0:T(8,128)(2,1)} %collective-permute-done.11.refs_2_.refs_3_), channel_id=1, source_target_pairs={{1,2},{2,3},{5,6},{6,7},{9,10},{10,11},{13,14},{14,15},{17,18},{18... | collective-permute-start | bytes 786440 | tf_op jit(solution)/shard_map/ppermute | solution.py:49
  60.3 3.0 %collective-permute-start.17 = (bf16[640,256]{1,0:T(8,128)(2,1)S(1)}, bf16[640,256]{1,0:T(8,128)(2,1)S(1)}, u32[]{:S(2)}, u32[]{:S(2)}) collective-permute-start(bf16[640,256]{1,0:T(8,128)(2,1)S(1)} %collective-permute-done.13.refs_4_.refs_15_), channel_id=1, source_target_pairs={{0,4},{4,0},{8,12},{12,8},{16,20},{20,16},{24,28},{28,24},{1,5},{5... | collective-permute-start | bytes 983048 | tf_op jit(solution)/shard_map/ppermute | solution.py:43
  60.7 2.7 %collective-permute-start.18 = (bf16[640,256]{1,0:T(8,128)(2,1)S(1)}, bf16[640,256]{1,0:T(8,128)(2,1)S(1)}, u32[]{:S(2)}, u32[]{:S(2)}) collective-permute-start(bf16[640,256]{1,0:T(8,128)(2,1)S(1)} %collective-permute-done.14.refs_5_.refs_16_), channel_id=1, source_target_pairs={{0,4},{4,0},{8,12},{12,8},{16,20},{20,16},{24,28},{28,24},{1,5},{5... | collective-permute-start | bytes 983048 | tf_op jit(solution)/shard_map/ppermute | solution.py:43
  62.0 15.7 %collective-permute-start.20 = (bf16[256,512]{1,0:T(8,128)(2,1)}, bf16[256,512]{1,0:T(8,128)(2,1)}, u32[]{:S(2)}, u32[]{:S(2)}) collective-permute-start(bf16[256,512]{1,0:T(8,128)(2,1)} %collective-permute-done.19.refs_4_.refs_5_), channel_id=1, source_target_pairs={{2,3},{6,7},{10,11},{14,15},{18,19},{22,23},{26,27},{30,31}} | collective-permute-start | bytes 786440 | tf_op jit(solution)/shard_map/ppermute | solution.py:49
  68.0 16.3 %copy-start.24 = (bf16[256,512]{1,0:T(8,128)(2,1)}, bf16[256,512]{1,0:T(8,128)(2,1)S(1)}, u32[]{:S(2)}) copy-start(bf16[256,512]{1,0:T(8,128)(2,1)S(1)} %project.3.refs_0_.refs_1_) | copy-start | bytes 786436
  68.0 15.6 %collective-permute-start.21 = (bf16[256,512]{1,0:T(8,128)(2,1)S(1)}, bf16[256,512]{1,0:T(8,128)(2,1)}, u32[]{:S(2)}, u32[]{:S(2)}) collective-permute-start(bf16[256,512]{1,0:T(8,128)(2,1)S(1)} %project.3.refs_0_.refs_1_), channel_id=1, source_target_pairs={{0,2},{1,3},{4,6},{5,7},{8,10},{9,11},{12,14},{13,15},{16,18},{17,... | collective-permute-start | bytes 786440 | tf_op jit(solution)/shard_map/ppermute | solution.py:49
  74.1 37.3 %all-to-all-start = ((bf16[8,256,640]{2,1,0:T(8,128)(2,1)}), bf16[8,256,640]{2,1,0:T(8,128)(2,1)S(1)}, u32[]{:S(2)}, u32[]{:S(2)}) async-start(bf16[8,256,640]{2,1,0:T(8,128)(2,1)} %split_columns.1.refs_0_), calls=%async_computation | async-start | bytes 5242880 | tf_op jit(solution)/shard_map/all_to_all | solution.py:501
  83.7 7.2 %collective-permute-start.22 = (bf16[256,512]{1,0:T(8,128)(2,1)}, bf16[256,512]{1,0:T(8,128)(2,1)S(1)}, u32[]{:S(2)}, u32[]{:S(2)}) collective-permute-start(bf16[256,512]{1,0:T(8,128)(2,1)} %get-tuple-element.60), channel_id=1, source_target_pairs={{3,2},{7,6},{11,10},{15,14},{19,18},{23,22},{27,26},{31,30}} | collective-permute-start | bytes 786440 | tf_op jit(solution)/shard_map/ppermute | solution.py:49
  84.3 10.2 %collective-permute-start.23 = (bf16[256,512]{1,0:T(8,128)(2,1)S(1)}, bf16[256,512]{1,0:T(8,128)(2,1)S(1)}, u32[]{:S(2)}, u32[]{:S(2)}) collective-permute-start(bf16[256,512]{1,0:T(8,128)(2,1)S(1)} %project.3.refs_0_.refs_1_), channel_id=1, source_target_pairs={{0,1},{1,2},{2,3},{4,5},{5,6},{6,7},{8,9},{9,10},{10,11},{12,13},{... | collective-permute-start | bytes 786440 | tf_op jit(solution)/shard_map/ppermute | solution.py:49
  86.4 8.1 %collective-permute-start.24 = (bf16[256,512]{1,0:T(8,128)(2,1)}, bf16[256,512]{1,0:T(8,128)(2,1)S(1)}, u32[]{:S(2)}, u32[]{:S(2)}) collective-permute-start(bf16[256,512]{1,0:T(8,128)(2,1)} %collective-permute-done.21.refs_4_.refs_5_), channel_id=1, source_target_pairs={{2,3},{6,7},{10,11},{14,15},{18,19},{22,23},{26,27},{30,31}} | collective-permute-start | bytes 786440 | tf_op jit(solution)/shard_map/ppermute | solution.py:49
  87.1 20.2 %collective-permute-start.25 = (bf16[256,512]{1,0:T(8,128)(2,1)}, bf16[256,512]{1,0:T(8,128)(2,1)}, u32[]{:S(2)}, u32[]{:S(2)}) collective-permute-start(bf16[256,512]{1,0:T(8,128)(2,1)} %get-tuple-element.68), channel_id=1, source_target_pairs={{1,0},{2,1},{3,2},{5,4},{6,5},{7,6},{9,8},{10,9},{11,10},{13,12},{... | collective-permute-start | bytes 786440 | tf_op jit(solution)/shard_map/ppermute | solution.py:49
  92.6 14.7 %collective-permute-start.26 = (bf16[256,512]{1,0:T(8,128)(2,1)}, bf16[256,512]{1,0:T(8,128)(2,1)}, u32[]{:S(2)}, u32[]{:S(2)}) collective-permute-start(bf16[256,512]{1,0:T(8,128)(2,1)} %add_convert_fusion.2), channel_id=1, source_target_pairs={{2,0},{3,1},{6,4},{7,5},{10,8},{11,9},{14,12},{15,13},{18,16},{19,... | collective-permute-start | bytes 786440 | tf_op jit(solution)/shard_map/ppermute | solution.py:49
  108.5 9.4 %collective-permute-start.30 = (bf16[256,512]{1,0:T(8,128)(2,1)S(1)}, bf16[256,512]{1,0:T(8,128)(2,1)}, u32[]{:S(2)}, u32[]{:S(2)}) collective-permute-start(bf16[256,512]{1,0:T(8,128)(2,1)S(1)} %add_convert_fusion.refs_0_), channel_id=1, source_target_pairs={{0,8},{4,12},{8,0},{12,4},{16,24},{20,28},{24,16},{28,20},{1,9},{5... | collective-permute-start | bytes 786440 | tf_op jit(solution)/shard_map/ppermute | solution.py:43
  111.4 7.5 %collective-permute-start.27 = (bf16[256,512]{1,0:T(8,128)(2,1)}, bf16[256,512]{1,0:T(8,128)(2,1)S(1)}, u32[]{:S(2)}, u32[]{:S(2)}) collective-permute-start(bf16[256,512]{1,0:T(8,128)(2,1)} %get-tuple-element.71), channel_id=1, source_target_pairs={{3,0},{7,4},{11,8},{15,12},{19,16},{23,20},{27,24},{31,28}} | collective-permute-start | bytes 786440 | tf_op jit(solution)/shard_map/ppermute | solution.py:49
  118.8 27.4 %copy-start.25 = (f32[256,512]{1,0:T(8,128)S(1)}, f32[256,512]{1,0:T(8,128)}, u32[]{:S(2)}) copy-start(f32[256,512]{1,0:T(8,128)} %get-tuple-element.65) | copy-start | bytes 1572868
  118.9 14.6 %collective-permute-start.31 = (bf16[512,512]{1,0:T(8,128)(2,1)S(1)}, bf16[512,512]{1,0:T(8,128)(2,1)S(1)}, u32[]{:S(2)}, u32[]{:S(2)}) collective-permute-start(bf16[512,512]{1,0:T(8,128)(2,1)S(1)} %pad_maximum_fusion.2), channel_id=1, source_target_pairs={{0,16},{4,20},{8,24},{12,28},{16,0},{20,4},{24,8},{28,12},{1,17},{... | collective-permute-start | bytes 1572872 | tf_op jit(solution)/shard_map/ppermute | solution.py:43
  120.5 14.6 %collective-permute-start.28 = (bf16[256,512]{1,0:T(8,128)(2,1)}, bf16[256,512]{1,0:T(8,128)(2,1)S(1)}, u32[]{:S(2)}, u32[]{:S(2)}) collective-permute-start(bf16[256,512]{1,0:T(8,128)(2,1)} %get-tuple-element.73), channel_id=1, source_target_pairs={{2,0},{3,1},{6,4},{7,5},{10,8},{11,9},{14,12},{15,13},{18,16},{19,... | collective-permute-start | bytes 786440 | tf_op jit(solution)/shard_map/ppermute | solution.py:49
  121.8 24.5 %collective-permute-start.29 = (bf16[256,512]{1,0:T(8,128)(2,1)}, bf16[256,512]{1,0:T(8,128)(2,1)S(1)}, u32[]{:S(2)}, u32[]{:S(2)}) collective-permute-start(bf16[256,512]{1,0:T(8,128)(2,1)} %get-tuple-element.75), channel_id=1, source_target_pairs={{1,0},{2,1},{3,2},{5,4},{6,5},{7,6},{9,8},{10,9},{11,10},{13,12},{... | collective-permute-start | bytes 786440 | tf_op jit(solution)/shard_map/ppermute | solution.py:49
  146.3 3.7 %collective-permute-start.32 = (bf16[1024,512]{1,0:T(8,128)(2,1)S(1)}, bf16[1024,512]{1,0:T(8,128)(2,1)S(1)}, u32[]{:S(2)}, u32[]{:S(2)}) collective-permute-start(bf16[1024,512]{1,0:T(8,128)(2,1)S(1)} %constant_dynamic-update-slice_fusion.refs_1_), channel_id=1, source_target_pairs={{0,4},{4,0},{8,12},{12,8},{16,20},{20,16},{24,28},{28,24},{1,5},{5... | collective-permute-start | bytes 3145736 | tf_op jit(solution)/shard_map/ppermute | solution.py:43
  146.4 10.1 %collective-permute-start.38 = (bf16[256,512]{1,0:T(8,128)(2,1)S(1)}, bf16[256,512]{1,0:T(8,128)(2,1)S(1)}, u32[]{:S(2)}, u32[]{:S(2)}) collective-permute-start(bf16[256,512]{1,0:T(8,128)(2,1)S(1)} %add_convert_fusion.1.refs_1_), channel_id=1, source_target_pairs={{0,24},{4,28},{8,16},{12,20},{16,8},{20,12},{24,0},{28,4},{1,25},{... | collective-permute-start | bytes 786440 | tf_op jit(solution)/shard_map/ppermute | solution.py:43
  147.3 14.0 %collective-permute-start.36 = (bf16[256,512]{1,0:T(8,128)(2,1)S(1)}, bf16[256,512]{1,0:T(8,128)(2,1)S(1)}, u32[]{:S(2)}, u32[]{:S(2)}) collective-permute-start(bf16[256,512]{1,0:T(8,128)(2,1)S(1)} %add_convert_fusion.1.refs_1_), channel_id=1, source_target_pairs={{0,16},{4,20},{8,24},{12,28},{16,0},{20,4},{24,8},{28,12},{1,17},{... | collective-permute-start | bytes 786440 | tf_op jit(solution)/shard_map/ppermute | solution.py:43
  148.6 12.7 %collective-permute-start.34 = (bf16[256,512]{1,0:T(8,128)(2,1)S(1)}, bf16[256,512]{1,0:T(8,128)(2,1)S(1)}, u32[]{:S(2)}, u32[]{:S(2)}) collective-permute-start(bf16[256,512]{1,0:T(8,128)(2,1)S(1)} %add_convert_fusion.1.refs_1_), channel_id=1, source_target_pairs={{0,8},{4,12},{8,0},{12,4},{16,24},{20,28},{24,16},{28,20},{1,9},{5... | collective-permute-start | bytes 786440 | tf_op jit(solution)/shard_map/ppermute | solution.py:43
  161.3 1.5 collective-permute-start.33
  161.3 1.9 collective-permute-start.35
  161.8 1.8 collective-permute-start.37
  161.8 2.1 %collective-permute-start.39 = (bf16[256,512]{1,0:T(8,128)(2,1)S(1)}, bf16[256,512]{1,0:T(8,128)(2,1)S(1)}, u32[]{:S(2)}, u32[]{:S(2)}) collective-permute-start(bf16[256,512]{1,0:T(8,128)(2,1)S(1)} %collective-permute-done.38.refs_7_), channel_id=1, source_target_pairs={{0,4},{4,0},{8,12},{12,8},{16,20},{20,16},{24,28},{28,24},{1,5},{5... | collective-permute-start | bytes 786440 | tf_op jit(solution)/shard_map/ppermute | solution.py:43
  166.3 12.6 %collective-permute-start.40 = (bf16[640,256]{1,0:T(8,128)(2,1)S(1)}, bf16[640,256]{1,0:T(8,128)(2,1)S(1)}, u32[]{:S(2)}, u32[]{:S(2)}) collective-permute-start(bf16[640,256]{1,0:T(8,128)(2,1)S(1)} %get-tuple-element.90), channel_id=1, source_target_pairs={{0,1},{1,0},{2,3},{3,2},{4,5},{5,4},{6,7},{7,6},{8,9},{9,8},{10,11... | collective-permute-start | bytes 983048 | tf_op jit(solution)/shard_map/ppermute | solution.py:43
  166.4 23.1 %collective-permute-start.41 = (bf16[640,256]{1,0:T(8,128)(2,1)S(1)}, bf16[640,256]{1,0:T(8,128)(2,1)S(1)}, u32[]{:S(2)}, u32[]{:S(2)}) collective-permute-start(bf16[640,256]{1,0:T(8,128)(2,1)S(1)} %get-tuple-element.91), channel_id=1, source_target_pairs={{0,2},{1,3},{2,0},{3,1},{4,6},{5,7},{6,4},{7,5},{8,10},{9,11},{10,... | collective-permute-start | bytes 983048 | tf_op jit(solution)/shard_map/ppermute | solution.py:43
  167.5 30.9 %collective-permute-start.42 = (bf16[640,256]{1,0:T(8,128)(2,1)S(1)}, bf16[640,256]{1,0:T(8,128)(2,1)S(1)}, u32[]{:S(2)}, u32[]{:S(2)}) collective-permute-start(bf16[640,256]{1,0:T(8,128)(2,1)S(1)} %get-tuple-element.92), channel_id=1, source_target_pairs={{0,3},{1,2},{2,1},{3,0},{4,7},{5,6},{6,5},{7,4},{8,11},{9,10},{10,... | collective-permute-start | bytes 983048 | tf_op jit(solution)/shard_map/ppermute | solution.py:43
  (26 other events, 172.5 us)

commit v5 on v4

--- a/solution.py
+++ b/solution.py
@@ -174,7 +174,7 @@
     hops = list(used[1:]) + [used[0]] * 3
     second_core = exchange(after(second, used[0]), "dp", 1)
     others = near_of(after(second, *others[2:]), hops[0], second_core)
-    pieces.append(with_core(second, second_core, others))
+    pieces.append(with_core(second, second_core, [*others[:2], *after(tuple(others[2:]), hops[1])]))
     return pieces, [used], hops[1:2]
 
 
@@ -536,8 +536,8 @@
         gates = ()
     gates = (sums[0],)
     terms = [sums[0]]
-    for at, send in enumerate(sums[1:]):
-        terms.append(exchange(send, "seq", at + 1).astype(jnp.float32))
+    for mask in (*range(2, seq_count), 1):
+        terms.append(exchange(sums[mask], "seq", mask).astype(jnp.float32))
     weight_grad = functools.reduce(lambda a, b: a + b, terms)
     token_grad = token_grads(after(rank, *gates), dkvs, weight_pieces, rows)
     return (dq, token_grad[None], weight_grad)

time: 200 us -> 194 us (0.970)
  waiting for transfers between devices: 88.4 us -> 82.5 us
  starting transfers between devices: 64.9 us -> 59.1 us
  Pallas kernels: 35.9 us -> 40.6 us
    pallas_call x2, Pallas kernels: 10.5 us -> 15.2 us  [attend(): pl.pallas_call(functools.partial(attend_kernel, sizes), grid=(heads,), ou...]
    ppermute x12, starting transfers between devices: 37.3 us -> 32.5 us  [moved(): return lax.ppermute(value, axis, pairs)]
    ppermute x12, waiting for transfers between devices: 27.7 us -> 23.4 us  [moved(): return lax.ppermute(value, axis, pairs)]
  transfers between devices with their start and end apart: 44 -> 44, of which waited for: 25 -> 21; matrix products, arithmetic and copies ran while one was open for 3% -> 3% of each run, Pallas kernels for 17% -> 20%
where the time goes in v5:
time: 194 us; the launch traced here: 193 us
  waiting for transfers between devices  82.5 us (43%)
  starting transfers between devices  59.1 us (30%)
  Pallas kernels  40.6 us (21%)
  other arithmetic  5.99 us (3%)
  local copies, waits for them, and re-layouts  2.93 us (2%)
    ppermute x31, waiting for transfers between devices, exchange(): return lax.ppermute(value, axis, [(i, i ^ mask) for i in range(count)])  59.2 us
    ppermute x12, starting transfers between devices, moved(): return lax.ppermute(value, axis, pairs)  32.5 us
    ppermute x12, waiting for transfers between devices, moved(): return lax.ppermute(value, axis, pairs)  23.4 us
    ppermute x31, starting transfers between devices, exchange(): return lax.ppermute(value, axis, [(i, i ^ mask) for i in range(count)])  23 us
    pallas_call x2, Pallas kernels, attend(): pl.pallas_call(functools.partial(attend_kernel, sizes), grid=(heads,), ou...  15.2 us
    pallas_call x2, Pallas kernels, project(): pl.pallas_call(functools.partial(project_kernel, table), out_shape=jax.Sh...  8.77 us
    pallas_call x1, Pallas kernels, token_grads(): pl.pallas_call(functools.partial(token_kernel, tables, tuple(indices)), o...  7.22 us
    pallas_call x2, Pallas kernels, weight_terms(): pl.pallas_call(functools.partial(weight_kernel, dests, len(pieces), bool(...  4.48 us
  transfers between devices with their start and end apart: 44, of which 21 were waited for; matrix products, arithmetic and copies ran while one was open for 3% of the time, Pallas kernels for 20%

profile of v5, /device:TPU:8, one launch (start us, length us, event | category | flops | bytes accessed | tf_op | source)
XLA Modules:
  0.0 192.5 jit_solution(8043837064791559686)
XLA Ops:
  0.6 1.4 fusion.2
  2.1 1.6 collective-permute-start.1
  3.7 1.5 collective-permute-start
  5.3 3.4 %split_columns.1.refs_0_ = bf16[8,256,640]{2,1,0:T(8,128)(2,1)} custom-call(bf16[1,256,5120]{2,1,0:T(8,128)(2,1)S(1)} %copy-done.2), custom_call_target="tpu_custom_call" | custom-call | flops 12000000000 | bytes 36000000 | tf_op jit(solution)/shard_map/split_columns/pallas_call | solution.py:195
  8.7 10.6 %collective-permute-done.1.far_ref.refs_3_.refs_4_ = bf16[640,512]{1,0:T(8,128)(2,1)S(1)} collective-permute-done((bf16[640,512]{1,0:T(8,128)(2,1)S(1)}, bf16[640,512]{1,0:T(8,128)(2,1)S(1)}, u32[]{:S(2)}, u32[]{:S(2)}) %collective-permute-start.1) | collective-permute-done | bytes 655392 | tf_op jit(solution)/shard_map/ppermute | solution.py:43
  19.3 1.2 collective-permute-done.near_ref.refs_2_.refs_3_
  21.2 1.5 collective-permute-start.3
  23.2 6.5 %collective-permute-done.2.refs_4_.refs_5_ = bf16[640,256]{1,0:T(8,128)(2,1)} collective-permute-done((bf16[640,256]{1,0:T(8,128)(2,1)S(1)}, bf16[640,256]{1,0:T(8,128)(2,1)}, u32[]{:S(2)}, u32[]{:S(2)}) %collective-permute-start.2) | collective-permute-done | bytes 327712 | tf_op jit(solution)/shard_map/ppermute | solution.py:43
  30.3 1.3 collective-permute-start.5
  31.7 1.5 collective-permute-start.4
  33.2 4.3 %project.2.refs_0_.refs_1_ = bf16[256,512]{1,0:T(8,128)(2,1)S(1)} custom-call(s32[2]{0:T(128)S(1)} %pad_add_fusion.1.rank_ref, bf16[8,256,640]{2,1,0:T(8,128)(2,1)} %split_columns.1.refs_0_, bf16[640,512]{1,0:T(8,128)(2,1)S(1)} %pad_maximum_fusion.1.refs_1_.refs_2_, bf16[640,512]{1,0:T(8,128)(2,1)S(1)} %collective-permute-done.near_ref.refs_2_.refs_3_, ...), custom_call_target="tpu_custom_call" | custom-call | flops 16000000000 | bytes 48000000 | tf_op jit(solution)/shard_map/project/pallas_call | solution.py:227
  37.6 3.5 %collective-permute-start.11 = (bf16[256,512]{1,0:T(8,128)(2,1)S(1)}, bf16[256,512]{1,0:T(8,128)(2,1)}, u32[]{:S(2)}, u32[]{:S(2)}) collective-permute-start(bf16[256,512]{1,0:T(8,128)(2,1)S(1)} %project.2.refs_0_.refs_1_), channel_id=1, source_target_pairs={{0,1},{1,2},{2,3},{4,5},{5,6},{6,7},{8,9},{9,10},{10,11},{12,13},{... | collective-permute-start | bytes 786440 | tf_op jit(solution)/shard_map/ppermute | solution.py:49
  41.1 7.2 %collective-permute-done.11.refs_2_.refs_3_ = bf16[256,512]{1,0:T(8,128)(2,1)} collective-permute-done((bf16[256,512]{1,0:T(8,128)(2,1)S(1)}, bf16[256,512]{1,0:T(8,128)(2,1)}, u32[]{:S(2)}, u32[]{:S(2)}) %collective-permute-start.11) | collective-permute-done | bytes 262176 | tf_op jit(solution)/shard_map/ppermute | solution.py:49
  48.3 4.2 %collective-permute-start.15 = (bf16[256,512]{1,0:T(8,128)(2,1)}, bf16[256,512]{1,0:T(8,128)(2,1)}, u32[]{:S(2)}, u32[]{:S(2)}) collective-permute-start(bf16[256,512]{1,0:T(8,128)(2,1)} %collective-permute-done.11.refs_2_.refs_3_), channel_id=1, source_target_pairs={{1,2},{2,3},{5,6},{6,7},{9,10},{10,11},{13,14},{14,15},{17,18},{18... | collective-permute-start | bytes 786440 | tf_op jit(solution)/shard_map/ppermute | solution.py:49
  52.6 1.5 halves.3
  55.1 1.1 collective-permute-start.14
  56.4 1.1 collective-permute-done.15.refs_4_.refs_5_
  57.5 6.8 %collective-permute-done.13.refs_4_.refs_15_ = bf16[640,256]{1,0:T(8,128)(2,1)S(1)} collective-permute-done((bf16[640,256]{1,0:T(8,128)(2,1)S(1)}, bf16[640,256]{1,0:T(8,128)(2,1)S(1)}, u32[]{:S(2)}, u32[]{:S(2)}) %collective-permute-start.13) | collective-permute-done | bytes 327712 | tf_op jit(solution)/shard_map/ppermute | solution.py:43
  65.8 1.4 collective-permute-start.20
  67.3 4.5 %project.3.refs_0_.refs_1_ = bf16[256,512]{1,0:T(8,128)(2,1)S(1)} custom-call(s32[2]{0:T(128)S(1)} %pad_add_fusion.1.rank_ref, bf16[8,256,640]{2,1,0:T(8,128)(2,1)} %split_columns.1.refs_0_, bf16[640,512]{1,0:T(8,128)(2,1)S(1)} %pad_maximum_fusion.refs_1_.refs_12_, bf16[640,512]{1,0:T(8,128)(2,1)} %collective-permute-done.4.near_ref.refs_2_.refs_13_, ...), custom_call_target="tpu_custom_call" | custom-call | flops 16000000000 | bytes 48000000 | tf_op jit(solution)/shard_map/project/pallas_call | solution.py:227
  71.9 2.3 %collective-permute-start.21 = (bf16[256,512]{1,0:T(8,128)(2,1)S(1)}, bf16[256,512]{1,0:T(8,128)(2,1)}, u32[]{:S(2)}, u32[]{:S(2)}) collective-permute-start(bf16[256,512]{1,0:T(8,128)(2,1)S(1)} %project.3.refs_0_.refs_1_), channel_id=1, source_target_pairs={{0,2},{1,3},{4,6},{5,7},{8,10},{9,11},{12,14},{13,15},{16,18},{17,... | collective-permute-start | bytes 786440 | tf_op jit(solution)/shard_map/ppermute | solution.py:49
  74.1 3.6 %all-to-all-start = ((bf16[8,256,640]{2,1,0:T(8,128)(2,1)}), bf16[8,256,640]{2,1,0:T(8,128)(2,1)S(1)}, u32[]{:S(2)}, u32[]{:S(2)}) async-start(bf16[8,256,640]{2,1,0:T(8,128)(2,1)} %split_columns.1.refs_0_), calls=%async_computation | async-start | bytes 5242880 | tf_op jit(solution)/shard_map/all_to_all | solution.py:501
  77.8 7.6 %attend.2 = (bf16[1,256,2560]{2,1,0:T(8,128)(2,1)}, f32[256,512]{1,0:T(8,128)}, bf16[256,512]{1,0:T(8,128)(2,1)}, bf16[256,512]{1,0:T(8,128)(2,1)}, bf16[256,512]{1,0:T(8,128)(2,1)}) custom-call(s32[10]{0:T(128)} %pad_add_fusion.info_ref, bf16[1,256,2560]{2,1,0:T(8,128)(2,1)} %q_ref.3, bf16[1,256,2560]{2,1,0:T(8,128)(2,1)} %g_ref.3, ...), custom_call_target="tpu_custom_call" | custom-call | flops 35999997952 | bytes 108000000 | tf_op jit(solution)/shard_map/attend/pallas_call | solution.py:342
  86.1 1.9 collective-permute-start.23
  88.7 3.9 %collective-permute-start.25 = (bf16[256,512]{1,0:T(8,128)(2,1)}, bf16[256,512]{1,0:T(8,128)(2,1)}, u32[]{:S(2)}, u32[]{:S(2)}) collective-permute-start(bf16[256,512]{1,0:T(8,128)(2,1)} %get-tuple-element.72), channel_id=1, source_target_pairs={{1,0},{2,1},{3,2},{5,4},{6,5},{7,6},{9,8},{10,9},{11,10},{13,12},{... | collective-permute-start | bytes 786440 | tf_op jit(solution)/shard_map/ppermute | solution.py:49
  92.6 1.7 add_convert_fusion.2
  94.3 1.5 collective-permute-start.26
  97.2 7.7 %attend.3 = (bf16[1,256,2560]{2,1,0:T(8,128)(2,1)}, f32[256,512]{1,0:T(8,128)}, bf16[256,512]{1,0:T(8,128)(2,1)}, bf16[256,512]{1,0:T(8,128)(2,1)}, bf16[256,512]{1,0:T(8,128)(2,1)}) custom-call(s32[10]{0:T(128)} %pad_add_fusion.info_ref, bf16[1,256,2560]{2,1,0:T(8,128)(2,1)} %q_ref.3, ...), custom_call_target="tpu_custom_call", output_to_operand_aliasing={{0}: (11, {})} | custom-call | flops 8000000000 | bytes 24000000 | tf_op jit(solution)/shard_map/attend/pallas_call | solution.py:342
  104.9 3.6 %collective-permute-done.25 = bf16[256,512]{1,0:T(8,128)(2,1)} collective-permute-done((bf16[256,512]{1,0:T(8,128)(2,1)}, bf16[256,512]{1,0:T(8,128)(2,1)}, u32[]{:S(2)}, u32[]{:S(2)}) %collective-permute-start.25) | collective-permute-done | bytes 262176 | tf_op jit(solution)/shard_map/ppermute | solution.py:49
  108.4 1.1 add_convert_fusion.refs_0_
  109.6 1.1 collective-permute-start.30
  111.4 4.7 %collective-permute-done.30 = bf16[256,512]{1,0:T(8,128)(2,1)} collective-permute-done((bf16[256,512]{1,0:T(8,128)(2,1)S(1)}, bf16[256,512]{1,0:T(8,128)(2,1)}, u32[]{:S(2)}, u32[]{:S(2)}) %collective-permute-start.30) | collective-permute-done | bytes 262176 | tf_op jit(solution)/shard_map/ppermute | solution.py:43
  116.1 1.0 pad_maximum_fusion.2
  117.1 1.4 collective-permute-start.31
  118.6 1.3 collective-permute-start.28
  119.8 10.6 %collective-permute-start.29 = (bf16[256,512]{1,0:T(8,128)(2,1)}, bf16[256,512]{1,0:T(8,128)(2,1)S(1)}, u32[]{:S(2)}, u32[]{:S(2)}) collective-permute-start(bf16[256,512]{1,0:T(8,128)(2,1)} %get-tuple-element.79), channel_id=1, source_target_pairs={{1,0},{2,1},{3,2},{5,4},{6,5},{7,6},{9,8},{10,9},{11,10},{13,12},{... | collective-permute-start | bytes 786440 | tf_op jit(solution)/shard_map/ppermute | solution.py:49
  131.4 10.7 %collective-permute-done.29 = bf16[256,512]{1,0:T(8,128)(2,1)S(1)} collective-permute-done((bf16[256,512]{1,0:T(8,128)(2,1)}, bf16[256,512]{1,0:T(8,128)(2,1)S(1)}, u32[]{:S(2)}, u32[]{:S(2)}) %collective-permute-start.29) | collective-permute-done | bytes 262176 | tf_op jit(solution)/shard_map/ppermute | solution.py:49
  142.2 1.4 collective-permute-start.38
  143.6 1.3 collective-permute-start.36
  145.8 2.2 %weight_grad.2 = (f32[640,256]{1,0:T(8,128)S(1)}, bf16[640,256]{1,0:T(8,128)(2,1)S(1)}, bf16[640,256]{1,0:T(8,128)(2,1)S(1)}, bf16[640,256]{1,0:T(8,128)(2,1)S(1)}) custom-call(s32[2]{0:T(128)S(1)} %pad_add_fusion.1.rank_ref, bf16[8,256,640]{2,1,0:T(8,128)(2,1)S(1)} %all-to-all-done.refs_0_, bf16[1024,512]{1,0:T(8,128)(2,1)S(1)} %constant_dynamic-update-slice_fusion.refs_1_, ...), custom_call_target="tpu_custom_call" | custom-call | flops 16000000000 | bytes 48000000 | tf_op jit(solution)/shard_map/weight_grad/pallas_call | solution.py:443
  148.0 4.3 %collective-permute-done.38.refs_7_ = bf16[256,512]{1,0:T(8,128)(2,1)S(1)} collective-permute-done((bf16[256,512]{1,0:T(8,128)(2,1)S(1)}, bf16[256,512]{1,0:T(8,128)(2,1)S(1)}, u32[]{:S(2)}, u32[]{:S(2)}) %collective-permute-start.38) | collective-permute-done | bytes 262176 | tf_op jit(solution)/shard_map/ppermute | solution.py:43
  152.4 5.2 %collective-permute-done.36.refs_5_ = bf16[256,512]{1,0:T(8,128)(2,1)S(1)} collective-permute-done((bf16[256,512]{1,0:T(8,128)(2,1)S(1)}, bf16[256,512]{1,0:T(8,128)(2,1)S(1)}, u32[]{:S(2)}, u32[]{:S(2)}) %collective-permute-start.36) | collective-permute-done | bytes 262176 | tf_op jit(solution)/shard_map/ppermute | solution.py:43
  160.3 2.3 %weight_grad.3 = (f32[640,256]{1,0:T(8,128)S(1)}, bf16[640,256]{1,0:T(8,128)(2,1)S(1)}, bf16[640,256]{1,0:T(8,128)(2,1)S(1)}, bf16[640,256]{1,0:T(8,128)(2,1)S(1)}) custom-call(s32[2]{0:T(128)S(1)} %pad_add_fusion.1.rank_ref, bf16[8,256,640]{2,1,0:T(8,128)(2,1)S(1)} %all-to-all-done.refs_0_, bf16[256,512]{1,0:T(8,128)(2,1)S(1)} %add_convert_fusion.1.refs_1_, ...), custom_call_target="tpu_custom_call" | custom-call | flops 16000000000 | bytes 48000000 | tf_op jit(solution)/shard_map/weight_grad/pallas_call | solution.py:443
  162.7 4.3 %collective-permute-start.42 = (bf16[640,256]{1,0:T(8,128)(2,1)S(1)}, bf16[640,256]{1,0:T(8,128)(2,1)S(1)}, u32[]{:S(2)}, u32[]{:S(2)}) collective-permute-start(bf16[640,256]{1,0:T(8,128)(2,1)S(1)} %get-tuple-element.96), channel_id=1, source_target_pairs={{0,1},{1,0},{2,3},{3,2},{4,5},{5,4},{6,7},{7,6},{8,9},{9,8},{10,11... | collective-permute-start | bytes 983048 | tf_op jit(solution)/shard_map/ppermute | solution.py:43
  167.1 7.2 %token_grads.1 = bf16[256,5120]{1,0:T(8,128)(2,1)} custom-call(s32[2]{0:T(128)S(1)} %pad_add_fusion.1.rank_ref, bf16[256,512]{1,0:T(8,128)(2,1)S(1)} %add_convert_fusion.refs_0_, bf16[256,512]{1,0:T(8,128)(2,1)S(1)} %add_convert_fusion.1.refs_1_, bf16[640,512]{1,0:T(8,128)(2,1)S(1)} %pad_maximum_fusion.1.refs_1_.refs_2_, bf16[640,512]{1,0:T(8,128)(2,1)S(1)} %copy-done.8, ...), custom_call_target="tpu_custom_call" | custom-call | flops 32000000000 | bytes 96000000 | tf_op jit(solution)/shard_map/token_grads/pallas_call | solution.py:400
  174.3 10.2 %collective-permute-done.40 = bf16[640,256]{1,0:T(8,128)(2,1)S(1)} collective-permute-done((bf16[640,256]{1,0:T(8,128)(2,1)S(1)}, bf16[640,256]{1,0:T(8,128)(2,1)S(1)}, u32[]{:S(2)}, u32[]{:S(2)}) %collective-permute-start.40) | collective-permute-done | bytes 327712 | tf_op jit(solution)/shard_map/ppermute | solution.py:43
  184.6 7.0 %collective-permute-done.41 = bf16[640,256]{1,0:T(8,128)(2,1)S(1)} collective-permute-done((bf16[640,256]{1,0:T(8,128)(2,1)S(1)}, bf16[640,256]{1,0:T(8,128)(2,1)S(1)}, u32[]{:S(2)}, u32[]{:S(2)}) %collective-permute-start.41) | collective-permute-done | bytes 327712 | tf_op jit(solution)/shard_map/ppermute | solution.py:43
  191.5 1.0 convert_add_fusion
  (127 shorter events, 13.3 us)
Async XLA Ops:
  2.1 28.2 %collective-permute-start.6 = (bf16[640,512]{1,0:T(8,128)(2,1)S(1)}, bf16[640,512]{1,0:T(8,128)(2,1)S(1)}, u32[]{:S(2)}, u32[]{:S(2)}) collective-permute-start(bf16[640,512]{1,0:T(8,128)(2,1)S(1)} %pad_maximum_fusion.1.refs_1_.refs_2_), channel_id=1, source_target_pairs={{0,4},{4,0},{8,12},{12,8},{16,20},{20,16},{24,28},{28,24},{1,5},{5... | collective-permute-start | bytes 1966088 | tf_op jit(solution)/shard_map/ppermute | solution.py:43
  2.1 17.1 %collective-permute-start.1 = (bf16[640,512]{1,0:T(8,128)(2,1)S(1)}, bf16[640,512]{1,0:T(8,128)(2,1)S(1)}, u32[]{:S(2)}, u32[]{:S(2)}) collective-permute-start(bf16[640,512]{1,0:T(8,128)(2,1)S(1)} %pad_maximum_fusion.1.refs_1_.refs_2_), channel_id=1, source_target_pairs={{0,16},{4,20},{8,24},{12,28},{16,0},{20,4},{24,8},{28,12},{1,17},{... | collective-permute-start | bytes 1966088 | tf_op jit(solution)/shard_map/ppermute | solution.py:43
  3.7 16.8 %collective-permute-start = (bf16[640,512]{1,0:T(8,128)(2,1)S(1)}, bf16[640,512]{1,0:T(8,128)(2,1)S(1)}, u32[]{:S(2)}, u32[]{:S(2)}) collective-permute-start(bf16[640,512]{1,0:T(8,128)(2,1)S(1)} %pad_maximum_fusion.1.refs_1_.refs_2_), channel_id=1, source_target_pairs={{0,8},{4,12},{8,0},{12,4},{16,24},{20,28},{24,16},{28,20},{1,9},{5... | collective-permute-start | bytes 1966088 | tf_op jit(solution)/shard_map/ppermute | solution.py:43
  5.3 61.9 %copy-start = (bf16[640,512]{1,0:T(8,128)(2,1)}, bf16[640,512]{1,0:T(8,128)(2,1)S(1)}, u32[]{:S(2)}) copy-start(bf16[640,512]{1,0:T(8,128)(2,1)S(1)} %pad_maximum_fusion.refs_1_.refs_12_) | copy-start | bytes 1966084
  20.6 9.1 %collective-permute-start.2 = (bf16[640,256]{1,0:T(8,128)(2,1)S(1)}, bf16[640,256]{1,0:T(8,128)(2,1)}, u32[]{:S(2)}, u32[]{:S(2)}) collective-permute-start(bf16[640,256]{1,0:T(8,128)(2,1)S(1)} %get-tuple-element.52), channel_id=1, source_target_pairs={{0,16},{4,20},{8,24},{12,28},{16,0},{20,4},{24,8},{28,12},{1,17},{... | collective-permute-start | bytes 983048 | tf_op jit(solution)/shard_map/ppermute | solution.py:43
  21.2 8.9 %collective-permute-start.3 = (bf16[640,256]{1,0:T(8,128)(2,1)S(1)}, bf16[640,256]{1,0:T(8,128)(2,1)}, u32[]{:S(2)}, u32[]{:S(2)}) collective-permute-start(bf16[640,256]{1,0:T(8,128)(2,1)S(1)} %get-tuple-element.53), channel_id=1, source_target_pairs={{0,8},{4,12},{8,0},{12,4},{16,24},{20,28},{24,16},{28,20},{1,9},{5... | collective-permute-start | bytes 983048 | tf_op jit(solution)/shard_map/ppermute | solution.py:43
  22.7 10.5 %collective-permute-start.7 = (bf16[640,512]{1,0:T(8,128)(2,1)S(1)}, bf16[640,512]{1,0:T(8,128)(2,1)}, u32[]{:S(2)}, u32[]{:S(2)}) collective-permute-start(bf16[640,512]{1,0:T(8,128)(2,1)S(1)} %collective-permute-done.near_ref.refs_2_.refs_3_), channel_id=1, source_target_pairs={{0,4},{4,0},{8,12},{12,8},{16,20},{20,16},{24,28},{28,24},{1,5},{5... | collective-permute-start | bytes 1966088 | tf_op jit(solution)/shard_map/ppermute | solution.py:43
  22.7 10.5 %collective-permute-start.8 = (bf16[640,512]{1,0:T(8,128)(2,1)S(1)}, bf16[640,512]{1,0:T(8,128)(2,1)}, u32[]{:S(2)}, u32[]{:S(2)}) collective-permute-start(bf16[640,512]{1,0:T(8,128)(2,1)S(1)} %collective-permute-done.1.far_ref.refs_3_.refs_4_), channel_id=1, source_target_pairs={{0,4},{4,0},{8,12},{12,8},{16,20},{20,16},{24,28},{28,24},{1,5},{5... | collective-permute-start | bytes 1966088 | tf_op jit(solution)/shard_map/ppermute | solution.py:43
  29.7 2.0 %collective-permute-start.9 = (bf16[640,256]{1,0:T(8,128)(2,1)}, bf16[640,256]{1,0:T(8,128)(2,1)}, u32[]{:S(2)}, u32[]{:S(2)}) collective-permute-start(bf16[640,256]{1,0:T(8,128)(2,1)} %collective-permute-done.2.refs_4_.refs_5_), channel_id=1, source_target_pairs={{0,4},{4,0},{8,12},{12,8},{16,20},{20,16},{24,28},{28,24},{1,5},{5... | collective-permute-start | bytes 983048 | tf_op jit(solution)/shard_map/ppermute | solution.py:43
  30.0 3.1 %collective-permute-start.10 = (bf16[640,256]{1,0:T(8,128)(2,1)}, bf16[640,256]{1,0:T(8,128)(2,1)}, u32[]{:S(2)}, u32[]{:S(2)}) collective-permute-start(bf16[640,256]{1,0:T(8,128)(2,1)} %collective-permute-done.3.refs_5_.refs_6_), channel_id=1, source_target_pairs={{0,4},{4,0},{8,12},{12,8},{16,20},{20,16},{24,28},{28,24},{1,5},{5... | collective-permute-start | bytes 983048 | tf_op jit(solution)/shard_map/ppermute | solution.py:43
  30.3 22.2 %collective-permute-start.5 = (bf16[640,512]{1,0:T(8,128)(2,1)S(1)}, bf16[640,512]{1,0:T(8,128)(2,1)}, u32[]{:S(2)}, u32[]{:S(2)}) collective-permute-start(bf16[640,512]{1,0:T(8,128)(2,1)S(1)} %pad_maximum_fusion.refs_1_.refs_12_), channel_id=1, source_target_pairs={{0,16},{4,20},{8,24},{12,28},{16,0},{20,4},{24,8},{28,12},{1,17},{... | collective-permute-start | bytes 1966088 | tf_op jit(solution)/shard_map/ppermute | solution.py:43
  31.7 20.8 %collective-permute-start.4 = (bf16[640,512]{1,0:T(8,128)(2,1)S(1)}, bf16[640,512]{1,0:T(8,128)(2,1)}, u32[]{:S(2)}, u32[]{:S(2)}) collective-permute-start(bf16[640,512]{1,0:T(8,128)(2,1)S(1)} %pad_maximum_fusion.refs_1_.refs_12_), channel_id=1, source_target_pairs={{0,8},{4,12},{8,0},{12,4},{16,24},{20,28},{24,16},{28,20},{1,9},{5... | collective-permute-start | bytes 1966088 | tf_op jit(solution)/shard_map/ppermute | solution.py:43
  37.5 16.6 %copy-start.23 = (bf16[256,512]{1,0:T(8,128)(2,1)}, bf16[256,512]{1,0:T(8,128)(2,1)S(1)}, u32[]{:S(2)}) copy-start(bf16[256,512]{1,0:T(8,128)(2,1)S(1)} %project.2.refs_0_.refs_1_) | copy-start | bytes 786436
  37.5 15.0 %collective-permute-start.12 = (bf16[640,512]{1,0:T(8,128)(2,1)S(1)}, bf16[640,512]{1,0:T(8,128)(2,1)S(1)}, u32[]{:S(2)}, u32[]{:S(2)}) collective-permute-start(bf16[640,512]{1,0:T(8,128)(2,1)S(1)} %pad_maximum_fusion.refs_1_.refs_12_), channel_id=1, source_target_pairs={{0,4},{4,0},{8,12},{12,8},{16,20},{20,16},{24,28},{28,24},{1,5},{5... | collective-permute-start | bytes 1966088 | tf_op jit(solution)/shard_map/ppermute | solution.py:43
  37.6 10.7 %collective-permute-start.11 = (bf16[256,512]{1,0:T(8,128)(2,1)S(1)}, bf16[256,512]{1,0:T(8,128)(2,1)}, u32[]{:S(2)}, u32[]{:S(2)}) collective-permute-start(bf16[256,512]{1,0:T(8,128)(2,1)S(1)} %project.2.refs_0_.refs_1_), channel_id=1, source_target_pairs={{0,1},{1,2},{2,3},{4,5},{5,6},{6,7},{8,9},{9,10},{10,11},{12,13},{... | collective-permute-start | bytes 786440 | tf_op jit(solution)/shard_map/ppermute | solution.py:49
  41.1 15.1 %copy-start.27 = (s32[1,4]{1,0:T(1,128)S(1)}, s32[1,4]{1,0:T(1,128)}, u32[]{:S(2)}) copy-start(s32[1,4]{1,0:T(1,128)} %param.9) | copy-start | bytes 52
  48.3 9.2 %collective-permute-start.15 = (bf16[256,512]{1,0:T(8,128)(2,1)}, bf16[256,512]{1,0:T(8,128)(2,1)}, u32[]{:S(2)}, u32[]{:S(2)}) collective-permute-start(bf16[256,512]{1,0:T(8,128)(2,1)} %collective-permute-done.11.refs_2_.refs_3_), channel_id=1, source_target_pairs={{1,2},{2,3},{5,6},{6,7},{9,10},{10,11},{13,14},{14,15},{17,18},{18... | collective-permute-start | bytes 786440 | tf_op jit(solution)/shard_map/ppermute | solution.py:49
  52.5 14.7 %collective-permute-start.16 = (bf16[640,512]{1,0:T(8,128)(2,1)}, bf16[640,512]{1,0:T(8,128)(2,1)S(1)}, u32[]{:S(2)}, u32[]{:S(2)}) collective-permute-start(bf16[640,512]{1,0:T(8,128)(2,1)} %collective-permute-done.4.near_ref.refs_2_.refs_13_), channel_id=1, source_target_pairs={{0,4},{4,0},{8,12},{12,8},{16,20},{20,16},{24,28},{28,24},{1,5},{5... | collective-permute-start | bytes 1966088 | tf_op jit(solution)/shard_map/ppermute | solution.py:43
  54.1 13.2 %collective-permute-start.17 = (bf16[640,512]{1,0:T(8,128)(2,1)}, bf16[640,512]{1,0:T(8,128)(2,1)S(1)}, u32[]{:S(2)}, u32[]{:S(2)}) collective-permute-start(bf16[640,512]{1,0:T(8,128)(2,1)} %collective-permute-done.5.far_ref.refs_3_.refs_14_), channel_id=1, source_target_pairs={{0,4},{4,0},{8,12},{12,8},{16,20},{20,16},{24,28},{28,24},{1,5},{5... | collective-permute-start | bytes 1966088 | tf_op jit(solution)/shard_map/ppermute | solution.py:43
  54.5 9.8 %collective-permute-start.13 = (bf16[640,256]{1,0:T(8,128)(2,1)S(1)}, bf16[640,256]{1,0:T(8,128)(2,1)S(1)}, u32[]{:S(2)}, u32[]{:S(2)}) collective-permute-start(bf16[640,256]{1,0:T(8,128)(2,1)S(1)} %get-tuple-element.58), channel_id=1, source_target_pairs={{0,16},{4,20},{8,24},{12,28},{16,0},{20,4},{24,8},{28,12},{1,17},{... | collective-permute-start | bytes 983048 | tf_op jit(solution)/shard_map/ppermute | solution.py:43
  55.1 9.5 %collective-permute-start.14 = (bf16[640,256]{1,0:T(8,128)(2,1)S(1)}, bf16[640,256]{1,0:T(8,128)(2,1)S(1)}, u32[]{:S(2)}, u32[]{:S(2)}) collective-permute-start(bf16[640,256]{1,0:T(8,128)(2,1)S(1)} %get-tuple-element.59), channel_id=1, source_target_pairs={{0,8},{4,12},{8,0},{12,4},{16,24},{20,28},{24,16},{28,20},{1,9},{5... | collective-permute-start | bytes 983048 | tf_op jit(solution)/shard_map/ppermute | solution.py:43
  64.6 2.5 %collective-permute-start.18 = (bf16[640,256]{1,0:T(8,128)(2,1)S(1)}, bf16[640,256]{1,0:T(8,128)(2,1)S(1)}, u32[]{:S(2)}, u32[]{:S(2)}) collective-permute-start(bf16[640,256]{1,0:T(8,128)(2,1)S(1)} %collective-permute-done.13.refs_4_.refs_15_), channel_id=1, source_target_pairs={{0,4},{4,0},{8,12},{12,8},{16,20},{20,16},{24,28},{28,24},{1,5},{5... | collective-permute-start | bytes 983048 | tf_op jit(solution)/shard_map/ppermute | solution.py:43
  64.6 2.6 %collective-permute-start.19 = (bf16[640,256]{1,0:T(8,128)(2,1)S(1)}, bf16[640,256]{1,0:T(8,128)(2,1)S(1)}, u32[]{:S(2)}, u32[]{:S(2)}) collective-permute-start(bf16[640,256]{1,0:T(8,128)(2,1)S(1)} %collective-permute-done.14.refs_5_.refs_16_), channel_id=1, source_target_pairs={{0,4},{4,0},{8,12},{12,8},{16,20},{20,16},{24,28},{28,24},{1,5},{5... | collective-permute-start | bytes 983048 | tf_op jit(solution)/shard_map/ppermute | solution.py:43
  65.8 11.9 %collective-permute-start.20 = (bf16[256,512]{1,0:T(8,128)(2,1)}, bf16[256,512]{1,0:T(8,128)(2,1)}, u32[]{:S(2)}, u32[]{:S(2)}) collective-permute-start(bf16[256,512]{1,0:T(8,128)(2,1)} %collective-permute-done.15.refs_4_.refs_5_), channel_id=1, source_target_pairs={{2,3},{6,7},{10,11},{14,15},{18,19},{22,23},{26,27},{30,31}} | collective-permute-start | bytes 786440 | tf_op jit(solution)/shard_map/ppermute | solution.py:49
  71.9 13.5 %collective-permute-start.21 = (bf16[256,512]{1,0:T(8,128)(2,1)S(1)}, bf16[256,512]{1,0:T(8,128)(2,1)}, u32[]{:S(2)}, u32[]{:S(2)}) collective-permute-start(bf16[256,512]{1,0:T(8,128)(2,1)S(1)} %project.3.refs_0_.refs_1_), channel_id=1, source_target_pairs={{0,2},{1,3},{4,6},{5,7},{8,10},{9,11},{12,14},{13,15},{16,18},{17,... | collective-permute-start | bytes 786440 | tf_op jit(solution)/shard_map/ppermute | solution.py:49
  74.1 36.6 %all-to-all-start = ((bf16[8,256,640]{2,1,0:T(8,128)(2,1)}), bf16[8,256,640]{2,1,0:T(8,128)(2,1)S(1)}, u32[]{:S(2)}, u32[]{:S(2)}) async-start(bf16[8,256,640]{2,1,0:T(8,128)(2,1)} %split_columns.1.refs_0_), calls=%async_computation | async-start | bytes 5242880 | tf_op jit(solution)/shard_map/all_to_all | solution.py:501
  85.4 7.3 %collective-permute-start.22 = (bf16[256,512]{1,0:T(8,128)(2,1)}, bf16[256,512]{1,0:T(8,128)(2,1)S(1)}, u32[]{:S(2)}, u32[]{:S(2)}) collective-permute-start(bf16[256,512]{1,0:T(8,128)(2,1)} %get-tuple-element.64), channel_id=1, source_target_pairs={{3,2},{7,6},{11,10},{15,14},{19,18},{23,22},{27,26},{31,30}} | collective-permute-start | bytes 786440 | tf_op jit(solution)/shard_map/ppermute | solution.py:49
  86.1 9.8 %collective-permute-start.23 = (bf16[256,512]{1,0:T(8,128)(2,1)S(1)}, bf16[256,512]{1,0:T(8,128)(2,1)S(1)}, u32[]{:S(2)}, u32[]{:S(2)}) collective-permute-start(bf16[256,512]{1,0:T(8,128)(2,1)S(1)} %project.3.refs_0_.refs_1_), channel_id=1, source_target_pairs={{0,1},{1,2},{2,3},{4,5},{5,6},{6,7},{8,9},{9,10},{10,11},{12,13},{... | collective-permute-start | bytes 786440 | tf_op jit(solution)/shard_map/ppermute | solution.py:49
  88.0 7.8 %collective-permute-start.24 = (bf16[256,512]{1,0:T(8,128)(2,1)}, bf16[256,512]{1,0:T(8,128)(2,1)S(1)}, u32[]{:S(2)}, u32[]{:S(2)}) collective-permute-start(bf16[256,512]{1,0:T(8,128)(2,1)} %collective-permute-done.21.refs_4_.refs_5_), channel_id=1, source_target_pairs={{2,3},{6,7},{10,11},{14,15},{18,19},{22,23},{26,27},{30,31}} | collective-permute-start | bytes 786440 | tf_op jit(solution)/shard_map/ppermute | solution.py:49
  88.7 19.7 %collective-permute-start.25 = (bf16[256,512]{1,0:T(8,128)(2,1)}, bf16[256,512]{1,0:T(8,128)(2,1)}, u32[]{:S(2)}, u32[]{:S(2)}) collective-permute-start(bf16[256,512]{1,0:T(8,128)(2,1)} %get-tuple-element.72), channel_id=1, source_target_pairs={{1,0},{2,1},{3,2},{5,4},{6,5},{7,6},{9,8},{10,9},{11,10},{13,12},{... | collective-permute-start | bytes 786440 | tf_op jit(solution)/shard_map/ppermute | solution.py:49
  94.3 14.1 %collective-permute-start.26 = (bf16[256,512]{1,0:T(8,128)(2,1)}, bf16[256,512]{1,0:T(8,128)(2,1)}, u32[]{:S(2)}, u32[]{:S(2)}) collective-permute-start(bf16[256,512]{1,0:T(8,128)(2,1)} %add_convert_fusion.2), channel_id=1, source_target_pairs={{2,0},{3,1},{6,4},{7,5},{10,8},{11,9},{14,12},{15,13},{18,16},{19,... | collective-permute-start | bytes 786440 | tf_op jit(solution)/shard_map/ppermute | solution.py:49
  109.6 6.5 %collective-permute-start.30 = (bf16[256,512]{1,0:T(8,128)(2,1)S(1)}, bf16[256,512]{1,0:T(8,128)(2,1)}, u32[]{:S(2)}, u32[]{:S(2)}) collective-permute-start(bf16[256,512]{1,0:T(8,128)(2,1)S(1)} %add_convert_fusion.refs_0_), channel_id=1, source_target_pairs={{0,8},{4,12},{8,0},{12,4},{16,24},{20,28},{24,16},{28,20},{1,9},{5... | collective-permute-start | bytes 786440 | tf_op jit(solution)/shard_map/ppermute | solution.py:43
  110.7 6.4 %collective-permute-start.27 = (bf16[256,512]{1,0:T(8,128)(2,1)}, bf16[256,512]{1,0:T(8,128)(2,1)S(1)}, u32[]{:S(2)}, u32[]{:S(2)}) collective-permute-start(bf16[256,512]{1,0:T(8,128)(2,1)} %get-tuple-element.75), channel_id=1, source_target_pairs={{3,0},{7,4},{11,8},{15,12},{19,16},{23,20},{27,24},{31,28}} | collective-permute-start | bytes 786440 | tf_op jit(solution)/shard_map/ppermute | solution.py:49
  117.1 25.0 %copy-start.25 = (f32[256,512]{1,0:T(8,128)S(1)}, f32[256,512]{1,0:T(8,128)}, u32[]{:S(2)}) copy-start(f32[256,512]{1,0:T(8,128)} %get-tuple-element.69) | copy-start | bytes 1572868
  117.1 13.4 %collective-permute-start.31 = (bf16[512,512]{1,0:T(8,128)(2,1)S(1)}, bf16[512,512]{1,0:T(8,128)(2,1)S(1)}, u32[]{:S(2)}, u32[]{:S(2)}) collective-permute-start(bf16[512,512]{1,0:T(8,128)(2,1)S(1)} %pad_maximum_fusion.2), channel_id=1, source_target_pairs={{0,16},{4,20},{8,24},{12,28},{16,0},{20,4},{24,8},{28,12},{1,17},{... | collective-permute-start | bytes 1572872 | tf_op jit(solution)/shard_map/ppermute | solution.py:43
  118.6 12.8 %collective-permute-start.28 = (bf16[256,512]{1,0:T(8,128)(2,1)}, bf16[256,512]{1,0:T(8,128)(2,1)S(1)}, u32[]{:S(2)}, u32[]{:S(2)}) collective-permute-start(bf16[256,512]{1,0:T(8,128)(2,1)} %get-tuple-element.77), channel_id=1, source_target_pairs={{2,0},{3,1},{6,4},{7,5},{10,8},{11,9},{14,12},{15,13},{18,16},{19,... | collective-permute-start | bytes 786440 | tf_op jit(solution)/shard_map/ppermute | solution.py:49
  119.8 22.3 %collective-permute-start.29 = (bf16[256,512]{1,0:T(8,128)(2,1)}, bf16[256,512]{1,0:T(8,128)(2,1)S(1)}, u32[]{:S(2)}, u32[]{:S(2)}) collective-permute-start(bf16[256,512]{1,0:T(8,128)(2,1)} %get-tuple-element.79), channel_id=1, source_target_pairs={{1,0},{2,1},{3,2},{5,4},{6,5},{7,6},{9,8},{10,9},{11,10},{13,12},{... | collective-permute-start | bytes 786440 | tf_op jit(solution)/shard_map/ppermute | solution.py:49
  142.1 3.7 %collective-permute-start.32 = (bf16[1024,512]{1,0:T(8,128)(2,1)S(1)}, bf16[1024,512]{1,0:T(8,128)(2,1)S(1)}, u32[]{:S(2)}, u32[]{:S(2)}) collective-permute-start(bf16[1024,512]{1,0:T(8,128)(2,1)S(1)} %constant_dynamic-update-slice_fusion.refs_1_), channel_id=1, source_target_pairs={{0,4},{4,0},{8,12},{12,8},{16,20},{20,16},{24,28},{28,24},{1,5},{5... | collective-permute-start | bytes 3145736 | tf_op jit(solution)/shard_map/ppermute | solution.py:43
  142.2 10.1 %collective-permute-start.38 = (bf16[256,512]{1,0:T(8,128)(2,1)S(1)}, bf16[256,512]{1,0:T(8,128)(2,1)S(1)}, u32[]{:S(2)}, u32[]{:S(2)}) collective-permute-start(bf16[256,512]{1,0:T(8,128)(2,1)S(1)} %add_convert_fusion.1.refs_1_), channel_id=1, source_target_pairs={{0,24},{4,28},{8,16},{12,20},{16,8},{20,12},{24,0},{28,4},{1,25},{... | collective-permute-start | bytes 786440 | tf_op jit(solution)/shard_map/ppermute | solution.py:43
  143.6 13.9 %collective-permute-start.36 = (bf16[256,512]{1,0:T(8,128)(2,1)S(1)}, bf16[256,512]{1,0:T(8,128)(2,1)S(1)}, u32[]{:S(2)}, u32[]{:S(2)}) collective-permute-start(bf16[256,512]{1,0:T(8,128)(2,1)S(1)} %add_convert_fusion.1.refs_1_), channel_id=1, source_target_pairs={{0,16},{4,20},{8,24},{12,28},{16,0},{20,4},{24,8},{28,12},{1,17},{... | collective-permute-start | bytes 786440 | tf_op jit(solution)/shard_map/ppermute | solution.py:43
  144.9 12.6 %collective-permute-start.34 = (bf16[256,512]{1,0:T(8,128)(2,1)S(1)}, bf16[256,512]{1,0:T(8,128)(2,1)S(1)}, u32[]{:S(2)}, u32[]{:S(2)}) collective-permute-start(bf16[256,512]{1,0:T(8,128)(2,1)S(1)} %add_convert_fusion.1.refs_1_), channel_id=1, source_target_pairs={{0,8},{4,12},{8,0},{12,4},{16,24},{20,28},{24,16},{28,20},{1,9},{5... | collective-permute-start | bytes 786440 | tf_op jit(solution)/shard_map/ppermute | solution.py:43
  157.5 1.5 collective-permute-start.33
  157.6 1.9 collective-permute-start.35
  158.1 1.8 collective-permute-start.37
  158.1 2.1 %collective-permute-start.39 = (bf16[256,512]{1,0:T(8,128)(2,1)S(1)}, bf16[256,512]{1,0:T(8,128)(2,1)S(1)}, u32[]{:S(2)}, u32[]{:S(2)}) collective-permute-start(bf16[256,512]{1,0:T(8,128)(2,1)S(1)} %collective-permute-done.38.refs_7_), channel_id=1, source_target_pairs={{0,4},{4,0},{8,12},{12,8},{16,20},{20,16},{24,28},{28,24},{1,5},{5... | collective-permute-start | bytes 786440 | tf_op jit(solution)/shard_map/ppermute | solution.py:43
  162.6 22.0 %collective-permute-start.40 = (bf16[640,256]{1,0:T(8,128)(2,1)S(1)}, bf16[640,256]{1,0:T(8,128)(2,1)S(1)}, u32[]{:S(2)}, u32[]{:S(2)}) collective-permute-start(bf16[640,256]{1,0:T(8,128)(2,1)S(1)} %get-tuple-element.94), channel_id=1, source_target_pairs={{0,2},{1,3},{2,0},{3,1},{4,6},{5,7},{6,4},{7,5},{8,10},{9,11},{10,... | collective-permute-start | bytes 983048 | tf_op jit(solution)/shard_map/ppermute | solution.py:43
  162.7 28.9 %collective-permute-start.41 = (bf16[640,256]{1,0:T(8,128)(2,1)S(1)}, bf16[640,256]{1,0:T(8,128)(2,1)S(1)}, u32[]{:S(2)}, u32[]{:S(2)}) collective-permute-start(bf16[640,256]{1,0:T(8,128)(2,1)S(1)} %get-tuple-element.95), channel_id=1, source_target_pairs={{0,3},{1,2},{2,1},{3,0},{4,7},{5,6},{6,5},{7,4},{8,11},{9,10},{10,... | collective-permute-start | bytes 983048 | tf_op jit(solution)/shard_map/ppermute | solution.py:43
  162.7 28.8 %collective-permute-start.42 = (bf16[640,256]{1,0:T(8,128)(2,1)S(1)}, bf16[640,256]{1,0:T(8,128)(2,1)S(1)}, u32[]{:S(2)}, u32[]{:S(2)}) collective-permute-start(bf16[640,256]{1,0:T(8,128)(2,1)S(1)} %get-tuple-element.96), channel_id=1, source_target_pairs={{0,1},{1,0},{2,3},{3,2},{4,5},{5,4},{6,7},{7,6},{8,9},{9,8},{10,11... | collective-permute-start | bytes 983048 | tf_op jit(solution)/shard_map/ppermute | solution.py:43
  (26 other events, 186.8 us)

commit v6 on v5

--- a/solution.py
+++ b/solution.py
@@ -91,13 +91,13 @@
     return arrived, [moved(sends[step], "seq", -step, step) for step in (1, 2) if step < count]
 
 
-def gather_direct(own, *gates):
+def gather_direct(own):
     count = lax.axis_size("dp")
     pieces = [own] + [None] * (count - 1)
     for mask in range(2, count, 2):
         pieces[mask] = exchange(own, "dp", mask)
     for mask in range(0, count, 2):
-        pieces[mask + 1] = exchange(after(pieces[mask], *gates), "dp", 1)
+        pieces[mask + 1] = exchange(pieces[mask], "dp", 1)
     return pieces
 
 
@@ -509,11 +509,7 @@
         dq, own, sends = attend(
             after(info, *gates), queries, cotangent, kv_steps, chunk, heads, group, act_total, dq
         )
-        if chunk < CHUNKS - 1 or seq_count > 4:
-            arrived, back = collect(sends, waits, later)
-        else:
-            back = [moved(after(sends[step - 1], *waits), "seq", -step) for step in range(seq_count - 1, 0, -1)]
-            arrived = ()
+        arrived, back = collect(sends, waits, later)
         backs.append(back)
         owns.append(own)
         gates, waits, later = tuple(arrived), (*back, *x_all), ()
@@ -526,7 +522,7 @@
         if chunk < CHUNKS - 1 or lax.axis_size("dp") > 8:
             dkv_pieces = gather_doubling(dkvs[chunk], backs[-1][:1], backs[-1][1:])
         else:
-            dkv_pieces = gather_direct(dkvs[chunk], *sums[:1])
+            dkv_pieces = gather_direct(dkvs[chunk])
         dests = []
         for side in range(2):
             start = side * (kvwidth // 2) + chunk * width

time: 194 us -> 187 us (0.964)
  Pallas kernels: 40.6 us -> 32.2 us
    pallas_call x2, Pallas kernels: 15.2 us -> 6.82 us  [attend(): pl.pallas_call(functools.partial(attend_kernel, sizes), grid=(heads,), ou...]
    ppermute x12, starting transfers between devices: 32.5 us -> 29 us  [moved(): return lax.ppermute(value, axis, pairs)]
    ppermute x31, starting transfers between devices: 23 us -> 26 us  [exchange(): return lax.ppermute(value, axis, [(i, i ^ mask) for i in range(count)])]
  transfers between devices with their start and end apart: 44 -> 44, of which waited for: 21 -> 19; matrix products, arithmetic and copies ran while one was open for 3% -> 3% of each run, Pallas kernels for 20% -> 16%
where the time goes in v6:
time: 187 us; the launch traced here: 186 us
  waiting for transfers between devices  83.6 us (45%)
  starting transfers between devices  58.7 us (31%)
  Pallas kernels  32.2 us (17%)
  other arithmetic  7.05 us (4%)
  local copies, waits for them, and re-layouts  2.95 us (2%)
    ppermute x31, waiting for transfers between devices, exchange(): return lax.ppermute(value, axis, [(i, i ^ mask) for i in range(count)])  59.6 us
    ppermute x12, starting transfers between devices, moved(): return lax.ppermute(value, axis, pairs)  29 us
    ppermute x31, starting transfers between devices, exchange(): return lax.ppermute(value, axis, [(i, i ^ mask) for i in range(count)])  26 us
    ppermute x12, waiting for transfers between devices, moved(): return lax.ppermute(value, axis, pairs)  23.9 us
    pallas_call x2, Pallas kernels, project(): pl.pallas_call(functools.partial(project_kernel, table), out_shape=jax.Sh...  8.77 us
    pallas_call x1, Pallas kernels, token_grads(): pl.pallas_call(functools.partial(token_kernel, tables, tuple(indices)), o...  7.21 us
    pallas_call x2, Pallas kernels, attend(): pl.pallas_call(functools.partial(attend_kernel, sizes), grid=(heads,), ou...  6.82 us
    pallas_call x2, Pallas kernels, weight_terms(): pl.pallas_call(functools.partial(weight_kernel, dests, len(pieces), bool(...  4.48 us
  transfers between devices with their start and end apart: 44, of which 19 were waited for; matrix products, arithmetic and copies ran while one was open for 3% of the time, Pallas kernels for 16%

profile of v6, /device:TPU:8, one launch (start us, length us, event | category | flops | bytes accessed | tf_op | source)
XLA Modules:
  0.0 185.8 jit_solution(2864346007157099583)
XLA Ops:
  0.6 1.4 fusion.2
  2.1 1.6 collective-permute-start
  3.6 1.5 collective-permute-start.1
  5.2 3.4 %split_columns.1.refs_0_ = bf16[8,256,640]{2,1,0:T(8,128)(2,1)} custom-call(bf16[1,256,5120]{2,1,0:T(8,128)(2,1)S(1)} %copy-done.2), custom_call_target="tpu_custom_call" | custom-call | flops 12000000000 | bytes 36000000 | tf_op jit(solution)/shard_map/split_columns/pallas_call | solution.py:195
  8.6 10.0 %collective-permute-done.near_ref.refs_2_.refs_3_ = bf16[640,512]{1,0:T(8,128)(2,1)S(1)} collective-permute-done((bf16[640,512]{1,0:T(8,128)(2,1)S(1)}, bf16[640,512]{1,0:T(8,128)(2,1)S(1)}, u32[]{:S(2)}, u32[]{:S(2)}) %collective-permute-start) | collective-permute-done | bytes 655392 | tf_op jit(solution)/shard_map/ppermute | solution.py:43
  18.6 1.2 collective-permute-done.1.far_ref.refs_3_.refs_4_
  20.5 1.5 collective-permute-start.2
  22.5 5.8 %collective-permute-done.3.refs_5_.refs_6_ = bf16[640,256]{1,0:T(8,128)(2,1)} collective-permute-done((bf16[640,256]{1,0:T(8,128)(2,1)S(1)}, bf16[640,256]{1,0:T(8,128)(2,1)}, u32[]{:S(2)}, u32[]{:S(2)}) %collective-permute-start.3) | collective-permute-done | bytes 327712 | tf_op jit(solution)/shard_map/ppermute | solution.py:43
  28.9 1.3 collective-permute-start.4
  30.3 1.5 collective-permute-start.5
  31.8 4.3 %project.2.refs_0_.refs_1_ = bf16[256,512]{1,0:T(8,128)(2,1)S(1)} custom-call(s32[2]{0:T(128)S(1)} %pad_add_fusion.1.rank_ref, bf16[8,256,640]{2,1,0:T(8,128)(2,1)} %split_columns.1.refs_0_, bf16[640,512]{1,0:T(8,128)(2,1)S(1)} %pad_maximum_fusion.1.refs_1_.refs_2_, bf16[640,512]{1,0:T(8,128)(2,1)S(1)} %collective-permute-done.near_ref.refs_2_.refs_3_, ...), custom_call_target="tpu_custom_call" | custom-call | flops 16000000000 | bytes 48000000 | tf_op jit(solution)/shard_map/project/pallas_call | solution.py:227
  36.2 3.5 %collective-permute-start.11 = (bf16[256,512]{1,0:T(8,128)(2,1)S(1)}, bf16[256,512]{1,0:T(8,128)(2,1)}, u32[]{:S(2)}, u32[]{:S(2)}) collective-permute-start(bf16[256,512]{1,0:T(8,128)(2,1)S(1)} %project.2.refs_0_.refs_1_), channel_id=1, source_target_pairs={{0,1},{1,2},{2,3},{4,5},{5,6},{6,7},{8,9},{9,10},{10,11},{12,13},{... | collective-permute-start | bytes 786440 | tf_op jit(solution)/shard_map/ppermute | solution.py:49
  39.7 7.2 %collective-permute-done.11.refs_2_.refs_3_ = bf16[256,512]{1,0:T(8,128)(2,1)} collective-permute-done((bf16[256,512]{1,0:T(8,128)(2,1)S(1)}, bf16[256,512]{1,0:T(8,128)(2,1)}, u32[]{:S(2)}, u32[]{:S(2)}) %collective-permute-start.11) | collective-permute-done | bytes 262176 | tf_op jit(solution)/shard_map/ppermute | solution.py:49
  46.9 4.2 %collective-permute-start.15 = (bf16[256,512]{1,0:T(8,128)(2,1)}, bf16[256,512]{1,0:T(8,128)(2,1)}, u32[]{:S(2)}, u32[]{:S(2)}) collective-permute-start(bf16[256,512]{1,0:T(8,128)(2,1)} %collective-permute-done.11.refs_2_.refs_3_), channel_id=1, source_target_pairs={{1,2},{2,3},{5,6},{6,7},{9,10},{10,11},{13,14},{14,15},{17,18},{18... | collective-permute-start | bytes 786440 | tf_op jit(solution)/shard_map/ppermute | solution.py:49
  51.2 1.5 halves.3
  53.6 1.2 collective-permute-start.14
  56.1 6.8 %collective-permute-done.13.refs_4_.refs_15_ = bf16[640,256]{1,0:T(8,128)(2,1)S(1)} collective-permute-done((bf16[640,256]{1,0:T(8,128)(2,1)S(1)}, bf16[640,256]{1,0:T(8,128)(2,1)S(1)}, u32[]{:S(2)}, u32[]{:S(2)}) %collective-permute-start.13) | collective-permute-done | bytes 327712 | tf_op jit(solution)/shard_map/ppermute | solution.py:43
  64.3 1.4 collective-permute-start.20
  65.7 4.5 %project.3.refs_0_.refs_1_ = bf16[256,512]{1,0:T(8,128)(2,1)S(1)} custom-call(s32[2]{0:T(128)S(1)} %pad_add_fusion.1.rank_ref, bf16[8,256,640]{2,1,0:T(8,128)(2,1)} %split_columns.1.refs_0_, bf16[640,512]{1,0:T(8,128)(2,1)S(1)} %pad_maximum_fusion.refs_1_.refs_12_, bf16[640,512]{1,0:T(8,128)(2,1)} %collective-permute-done.4.near_ref.refs_2_.refs_13_, ...), custom_call_target="tpu_custom_call" | custom-call | flops 16000000000 | bytes 48000000 | tf_op jit(solution)/shard_map/project/pallas_call | solution.py:227
  70.3 2.3 %collective-permute-start.21 = (bf16[256,512]{1,0:T(8,128)(2,1)S(1)}, bf16[256,512]{1,0:T(8,128)(2,1)}, u32[]{:S(2)}, u32[]{:S(2)}) collective-permute-start(bf16[256,512]{1,0:T(8,128)(2,1)S(1)} %project.3.refs_0_.refs_1_), channel_id=1, source_target_pairs={{0,2},{1,3},{4,6},{5,7},{8,10},{9,11},{12,14},{13,15},{16,18},{17,... | collective-permute-start | bytes 786440 | tf_op jit(solution)/shard_map/ppermute | solution.py:49
  72.6 3.6 %all-to-all-start = ((bf16[8,256,640]{2,1,0:T(8,128)(2,1)}), bf16[8,256,640]{2,1,0:T(8,128)(2,1)S(1)}, u32[]{:S(2)}, u32[]{:S(2)}) async-start(bf16[8,256,640]{2,1,0:T(8,128)(2,1)} %split_columns.1.refs_0_), calls=%async_computation | async-start | bytes 5242880 | tf_op jit(solution)/shard_map/all_to_all | solution.py:501
  76.2 3.4 %attend.2 = (bf16[1,256,2560]{2,1,0:T(8,128)(2,1)}, f32[256,512]{1,0:T(8,128)}, bf16[256,512]{1,0:T(8,128)(2,1)}, bf16[256,512]{1,0:T(8,128)(2,1)}, bf16[256,512]{1,0:T(8,128)(2,1)}) custom-call(s32[10]{0:T(128)} %pad_add_fusion.info_ref, bf16[1,256,2560]{2,1,0:T(8,128)(2,1)} %q_ref.3, bf16[1,256,2560]{2,1,0:T(8,128)(2,1)} %g_ref.3, ...), custom_call_target="tpu_custom_call" | custom-call | flops 35999997952 | bytes 108000000 | tf_op jit(solution)/shard_map/attend/pallas_call | solution.py:342
  79.6 3.6 %collective-permute-done.21.refs_4_.refs_5_ = bf16[256,512]{1,0:T(8,128)(2,1)} collective-permute-done((bf16[256,512]{1,0:T(8,128)(2,1)S(1)}, bf16[256,512]{1,0:T(8,128)(2,1)}, u32[]{:S(2)}, u32[]{:S(2)}) %collective-permute-start.21) | collective-permute-done | bytes 262176 | tf_op jit(solution)/shard_map/ppermute | solution.py:49
  83.9 3.7 %collective-permute-start.23 = (bf16[256,512]{1,0:T(8,128)(2,1)S(1)}, bf16[256,512]{1,0:T(8,128)(2,1)S(1)}, u32[]{:S(2)}, u32[]{:S(2)}) collective-permute-start(bf16[256,512]{1,0:T(8,128)(2,1)S(1)} %project.3.refs_0_.refs_1_), channel_id=1, source_target_pairs={{0,1},{1,2},{2,3},{4,5},{5,6},{6,7},{8,9},{9,10},{10,11},{12,13},{... | collective-permute-start | bytes 786440 | tf_op jit(solution)/shard_map/ppermute | solution.py:49
  88.3 2.1 %collective-permute-start.25 = (bf16[256,512]{1,0:T(8,128)(2,1)}, bf16[256,512]{1,0:T(8,128)(2,1)}, u32[]{:S(2)}, u32[]{:S(2)}) collective-permute-start(bf16[256,512]{1,0:T(8,128)(2,1)} %get-tuple-element.68), channel_id=1, source_target_pairs={{1,0},{2,1},{3,2},{5,4},{6,5},{7,6},{9,8},{10,9},{11,10},{13,12},{... | collective-permute-start | bytes 786440 | tf_op jit(solution)/shard_map/ppermute | solution.py:49
  90.5 1.7 add_convert_fusion.3
  92.2 1.5 collective-permute-start.26
  93.7 1.2 collective-permute-done.23.refs_2_.refs_3_
  96.3 3.4 %attend.3 = (bf16[1,256,2560]{2,1,0:T(8,128)(2,1)}, f32[256,512]{1,0:T(8,128)}, bf16[256,512]{1,0:T(8,128)(2,1)}, bf16[256,512]{1,0:T(8,128)(2,1)}, bf16[256,512]{1,0:T(8,128)(2,1)}) custom-call(s32[10]{0:T(128)} %pad_add_fusion.info_ref, bf16[1,256,2560]{2,1,0:T(8,128)(2,1)} %q_ref.3, ...), custom_call_target="tpu_custom_call", output_to_operand_aliasing={{0}: (11, {})} | custom-call | flops 8000000000 | bytes 24000000 | tf_op jit(solution)/shard_map/attend/pallas_call | solution.py:342
  99.7 7.2 %collective-permute-done.25 = bf16[256,512]{1,0:T(8,128)(2,1)} collective-permute-done((bf16[256,512]{1,0:T(8,128)(2,1)}, bf16[256,512]{1,0:T(8,128)(2,1)}, u32[]{:S(2)}, u32[]{:S(2)}) %collective-permute-start.25) | collective-permute-done | bytes 262176 | tf_op jit(solution)/shard_map/ppermute | solution.py:49
  106.9 1.1 add_convert_fusion.refs_0_
  108.0 1.3 collective-permute-start.37
  109.3 7.1 %collective-permute-start.27 = (bf16[256,512]{1,0:T(8,128)(2,1)}, bf16[256,512]{1,0:T(8,128)(2,1)S(1)}, u32[]{:S(2)}, u32[]{:S(2)}) collective-permute-start(bf16[256,512]{1,0:T(8,128)(2,1)} %get-tuple-element.71), channel_id=1, source_target_pairs={{1,0},{2,1},{3,2},{5,4},{6,5},{7,6},{9,8},{10,9},{11,10},{13,12},{... | collective-permute-start | bytes 786440 | tf_op jit(solution)/shard_map/ppermute | solution.py:49
  118.2 2.5 %collective-permute-done.27 = bf16[256,512]{1,0:T(8,128)(2,1)S(1)} collective-permute-done((bf16[256,512]{1,0:T(8,128)(2,1)}, bf16[256,512]{1,0:T(8,128)(2,1)S(1)}, u32[]{:S(2)}, u32[]{:S(2)}) %collective-permute-start.27) | collective-permute-done | bytes 262176 | tf_op jit(solution)/shard_map/ppermute | solution.py:49
  122.7 1.3 collective-permute-start.29
  124.0 7.6 %collective-permute-done.38 = bf16[512,512]{1,0:T(8,128)(2,1)S(1)} collective-permute-done((bf16[512,512]{1,0:T(8,128)(2,1)S(1)}, bf16[512,512]{1,0:T(8,128)(2,1)S(1)}, u32[]{:S(2)}, u32[]{:S(2)}) %collective-permute-start.38) | collective-permute-done | bytes 524320 | tf_op jit(solution)/shard_map/ppermute | solution.py:43
  131.7 1.1 collective-permute-done.29
  133.8 1.4 collective-permute-start.33
  135.2 1.3 collective-permute-start.35
  136.5 5.6 %collective-permute-done.31.refs_3_ = bf16[256,512]{1,0:T(8,128)(2,1)S(1)} collective-permute-done((bf16[256,512]{1,0:T(8,128)(2,1)S(1)}, bf16[256,512]{1,0:T(8,128)(2,1)S(1)}, u32[]{:S(2)}, u32[]{:S(2)}) %collective-permute-start.31) | collective-permute-done | bytes 262176 | tf_op jit(solution)/shard_map/ppermute | solution.py:43
  142.1 5.7 %collective-permute-done.33.refs_5_ = bf16[256,512]{1,0:T(8,128)(2,1)S(1)} collective-permute-done((bf16[256,512]{1,0:T(8,128)(2,1)S(1)}, bf16[256,512]{1,0:T(8,128)(2,1)S(1)}, u32[]{:S(2)}, u32[]{:S(2)}) %collective-permute-start.33) | collective-permute-done | bytes 262176 | tf_op jit(solution)/shard_map/ppermute | solution.py:43
  148.4 2.2 %weight_grad.2 = (f32[640,256]{1,0:T(8,128)S(1)}, bf16[640,256]{1,0:T(8,128)(2,1)S(1)}, bf16[640,256]{1,0:T(8,128)(2,1)S(1)}, bf16[640,256]{1,0:T(8,128)(2,1)S(1)}) custom-call(s32[2]{0:T(128)S(1)} %pad_add_fusion.1.rank_ref, bf16[8,256,640]{2,1,0:T(8,128)(2,1)S(1)} %all-to-all-done.refs_0_, bf16[1024,512]{1,0:T(8,128)(2,1)S(1)} %constant_dynamic-update-slice_fusion.refs_1_, ...), custom_call_target="tpu_custom_call" | custom-call | flops 16000000000 | bytes 48000000 | tf_op jit(solution)/shard_map/weight_grad/pallas_call | solution.py:443
  150.7 2.3 %weight_grad.3 = (f32[640,256]{1,0:T(8,128)S(1)}, bf16[640,256]{1,0:T(8,128)(2,1)S(1)}, bf16[640,256]{1,0:T(8,128)(2,1)S(1)}, bf16[640,256]{1,0:T(8,128)(2,1)S(1)}) custom-call(s32[2]{0:T(128)S(1)} %pad_add_fusion.1.rank_ref, bf16[8,256,640]{2,1,0:T(8,128)(2,1)S(1)} %all-to-all-done.refs_0_, bf16[256,512]{1,0:T(8,128)(2,1)S(1)} %add_convert_fusion.1.refs_1_, ...), custom_call_target="tpu_custom_call" | custom-call | flops 16000000000 | bytes 48000000 | tf_op jit(solution)/shard_map/weight_grad/pallas_call | solution.py:443
  153.0 2.8 %collective-permute-start.40 = (bf16[640,256]{1,0:T(8,128)(2,1)S(1)}, bf16[640,256]{1,0:T(8,128)(2,1)S(1)}, u32[]{:S(2)}, u32[]{:S(2)}) collective-permute-start(bf16[640,256]{1,0:T(8,128)(2,1)S(1)} %get-tuple-element.86), channel_id=1, source_target_pairs={{0,2},{1,3},{2,0},{3,1},{4,6},{5,7},{6,4},{7,5},{8,10},{9,11},{10,... | collective-permute-start | bytes 983048 | tf_op jit(solution)/shard_map/ppermute | solution.py:43
  155.8 5.5 %collective-permute-start.41 = (bf16[640,256]{1,0:T(8,128)(2,1)S(1)}, bf16[640,256]{1,0:T(8,128)(2,1)S(1)}, u32[]{:S(2)}, u32[]{:S(2)}) collective-permute-start(bf16[640,256]{1,0:T(8,128)(2,1)S(1)} %get-tuple-element.87), channel_id=1, source_target_pairs={{0,3},{1,2},{2,1},{3,0},{4,7},{5,6},{6,5},{7,4},{8,11},{9,10},{10,... | collective-permute-start | bytes 983048 | tf_op jit(solution)/shard_map/ppermute | solution.py:43
  161.4 7.2 %token_grads.1 = bf16[256,5120]{1,0:T(8,128)(2,1)} custom-call(s32[2]{0:T(128)S(1)} %pad_add_fusion.1.rank_ref, bf16[256,512]{1,0:T(8,128)(2,1)S(1)} %add_convert_fusion.refs_0_, bf16[256,512]{1,0:T(8,128)(2,1)S(1)} %add_convert_fusion.1.refs_1_, bf16[640,512]{1,0:T(8,128)(2,1)S(1)} %pad_maximum_fusion.1.refs_1_.refs_2_, bf16[640,512]{1,0:T(8,128)(2,1)S(1)} %copy-done.4, ...), custom_call_target="tpu_custom_call" | custom-call | flops 32000000000 | bytes 96000000 | tf_op jit(solution)/shard_map/token_grads/pallas_call | solution.py:400
  168.6 9.4 %collective-permute-done.40 = bf16[640,256]{1,0:T(8,128)(2,1)S(1)} collective-permute-done((bf16[640,256]{1,0:T(8,128)(2,1)S(1)}, bf16[640,256]{1,0:T(8,128)(2,1)S(1)}, u32[]{:S(2)}, u32[]{:S(2)}) %collective-permute-start.40) | collective-permute-done | bytes 327712 | tf_op jit(solution)/shard_map/ppermute | solution.py:43
  178.0 6.8 %collective-permute-done.41 = bf16[640,256]{1,0:T(8,128)(2,1)S(1)} collective-permute-done((bf16[640,256]{1,0:T(8,128)(2,1)S(1)}, bf16[640,256]{1,0:T(8,128)(2,1)S(1)}, u32[]{:S(2)}, u32[]{:S(2)}) %collective-permute-start.41) | collective-permute-done | bytes 327712 | tf_op jit(solution)/shard_map/ppermute | solution.py:43
  (128 shorter events, 14.9 us)
Async XLA Ops:
  2.1 16.5 %collective-permute-start = (bf16[640,512]{1,0:T(8,128)(2,1)S(1)}, bf16[640,512]{1,0:T(8,128)(2,1)S(1)}, u32[]{:S(2)}, u32[]{:S(2)}) collective-permute-start(bf16[640,512]{1,0:T(8,128)(2,1)S(1)} %pad_maximum_fusion.1.refs_1_.refs_2_), channel_id=1, source_target_pairs={{0,8},{4,12},{8,0},{12,4},{16,24},{20,28},{24,16},{28,20},{1,9},{5... | collective-permute-start | bytes 1966088 | tf_op jit(solution)/shard_map/ppermute | solution.py:43
  3.6 16.2 %collective-permute-start.1 = (bf16[640,512]{1,0:T(8,128)(2,1)S(1)}, bf16[640,512]{1,0:T(8,128)(2,1)S(1)}, u32[]{:S(2)}, u32[]{:S(2)}) collective-permute-start(bf16[640,512]{1,0:T(8,128)(2,1)S(1)} %pad_maximum_fusion.1.refs_1_.refs_2_), channel_id=1, source_target_pairs={{0,16},{4,20},{8,24},{12,28},{16,0},{20,4},{24,8},{28,12},{1,17},{... | collective-permute-start | bytes 1966088 | tf_op jit(solution)/shard_map/ppermute | solution.py:43
  5.1 23.7 %collective-permute-start.6 = (bf16[640,512]{1,0:T(8,128)(2,1)S(1)}, bf16[640,512]{1,0:T(8,128)(2,1)S(1)}, u32[]{:S(2)}, u32[]{:S(2)}) collective-permute-start(bf16[640,512]{1,0:T(8,128)(2,1)S(1)} %pad_maximum_fusion.1.refs_1_.refs_2_), channel_id=1, source_target_pairs={{0,4},{4,0},{8,12},{12,8},{16,20},{20,16},{24,28},{28,24},{1,5},{5... | collective-permute-start | bytes 1966088 | tf_op jit(solution)/shard_map/ppermute | solution.py:43
  5.2 60.5 %copy-start = (bf16[640,512]{1,0:T(8,128)(2,1)}, bf16[640,512]{1,0:T(8,128)(2,1)S(1)}, u32[]{:S(2)}) copy-start(bf16[640,512]{1,0:T(8,128)(2,1)S(1)} %pad_maximum_fusion.refs_1_.refs_12_) | copy-start | bytes 1966084
  19.9 8.4 %collective-permute-start.3 = (bf16[640,256]{1,0:T(8,128)(2,1)S(1)}, bf16[640,256]{1,0:T(8,128)(2,1)}, u32[]{:S(2)}, u32[]{:S(2)}) collective-permute-start(bf16[640,256]{1,0:T(8,128)(2,1)S(1)} %get-tuple-element.49), channel_id=1, source_target_pairs={{0,8},{4,12},{8,0},{12,4},{16,24},{20,28},{24,16},{28,20},{1,9},{5... | collective-permute-start | bytes 983048 | tf_op jit(solution)/shard_map/ppermute | solution.py:43
  20.5 8.2 %collective-permute-start.2 = (bf16[640,256]{1,0:T(8,128)(2,1)S(1)}, bf16[640,256]{1,0:T(8,128)(2,1)}, u32[]{:S(2)}, u32[]{:S(2)}) collective-permute-start(bf16[640,256]{1,0:T(8,128)(2,1)S(1)} %get-tuple-element.48), channel_id=1, source_target_pairs={{0,16},{4,20},{8,24},{12,28},{16,0},{20,4},{24,8},{28,12},{1,17},{... | collective-permute-start | bytes 983048 | tf_op jit(solution)/shard_map/ppermute | solution.py:43
  22.0 9.8 %collective-permute-start.7 = (bf16[640,512]{1,0:T(8,128)(2,1)S(1)}, bf16[640,512]{1,0:T(8,128)(2,1)}, u32[]{:S(2)}, u32[]{:S(2)}) collective-permute-start(bf16[640,512]{1,0:T(8,128)(2,1)S(1)} %collective-permute-done.near_ref.refs_2_.refs_3_), channel_id=1, source_target_pairs={{0,4},{4,0},{8,12},{12,8},{16,20},{20,16},{24,28},{28,24},{1,5},{5... | collective-permute-start | bytes 1966088 | tf_op jit(solution)/shard_map/ppermute | solution.py:43
  22.0 9.8 %collective-permute-start.8 = (bf16[640,512]{1,0:T(8,128)(2,1)S(1)}, bf16[640,512]{1,0:T(8,128)(2,1)}, u32[]{:S(2)}, u32[]{:S(2)}) collective-permute-start(bf16[640,512]{1,0:T(8,128)(2,1)S(1)} %collective-permute-done.1.far_ref.refs_3_.refs_4_), channel_id=1, source_target_pairs={{0,4},{4,0},{8,12},{12,8},{16,20},{20,16},{24,28},{28,24},{1,5},{5... | collective-permute-start | bytes 1966088 | tf_op jit(solution)/shard_map/ppermute | solution.py:43
  28.3 2.0 %collective-permute-start.10 = (bf16[640,256]{1,0:T(8,128)(2,1)}, bf16[640,256]{1,0:T(8,128)(2,1)}, u32[]{:S(2)}, u32[]{:S(2)}) collective-permute-start(bf16[640,256]{1,0:T(8,128)(2,1)} %collective-permute-done.3.refs_5_.refs_6_), channel_id=1, source_target_pairs={{0,4},{4,0},{8,12},{12,8},{16,20},{20,16},{24,28},{28,24},{1,5},{5... | collective-permute-start | bytes 983048 | tf_op jit(solution)/shard_map/ppermute | solution.py:43
  28.6 3.2 %collective-permute-start.9 = (bf16[640,256]{1,0:T(8,128)(2,1)}, bf16[640,256]{1,0:T(8,128)(2,1)}, u32[]{:S(2)}, u32[]{:S(2)}) collective-permute-start(bf16[640,256]{1,0:T(8,128)(2,1)} %collective-permute-done.2.refs_4_.refs_5_), channel_id=1, source_target_pairs={{0,4},{4,0},{8,12},{12,8},{16,20},{20,16},{24,28},{28,24},{1,5},{5... | collective-permute-start | bytes 983048 | tf_op jit(solution)/shard_map/ppermute | solution.py:43
  28.9 22.2 %collective-permute-start.4 = (bf16[640,512]{1,0:T(8,128)(2,1)S(1)}, bf16[640,512]{1,0:T(8,128)(2,1)}, u32[]{:S(2)}, u32[]{:S(2)}) collective-permute-start(bf16[640,512]{1,0:T(8,128)(2,1)S(1)} %pad_maximum_fusion.refs_1_.refs_12_), channel_id=1, source_target_pairs={{0,8},{4,12},{8,0},{12,4},{16,24},{20,28},{24,16},{28,20},{1,9},{5... | collective-permute-start | bytes 1966088 | tf_op jit(solution)/shard_map/ppermute | solution.py:43
  30.3 20.8 %collective-permute-start.5 = (bf16[640,512]{1,0:T(8,128)(2,1)S(1)}, bf16[640,512]{1,0:T(8,128)(2,1)}, u32[]{:S(2)}, u32[]{:S(2)}) collective-permute-start(bf16[640,512]{1,0:T(8,128)(2,1)S(1)} %pad_maximum_fusion.refs_1_.refs_12_), channel_id=1, source_target_pairs={{0,16},{4,20},{8,24},{12,28},{16,0},{20,4},{24,8},{28,12},{1,17},{... | collective-permute-start | bytes 1966088 | tf_op jit(solution)/shard_map/ppermute | solution.py:43
  36.1 16.6 %copy-start.23 = (bf16[256,512]{1,0:T(8,128)(2,1)}, bf16[256,512]{1,0:T(8,128)(2,1)S(1)}, u32[]{:S(2)}) copy-start(bf16[256,512]{1,0:T(8,128)(2,1)S(1)} %project.2.refs_0_.refs_1_) | copy-start | bytes 786436
  36.1 15.0 %collective-permute-start.12 = (bf16[640,512]{1,0:T(8,128)(2,1)S(1)}, bf16[640,512]{1,0:T(8,128)(2,1)S(1)}, u32[]{:S(2)}, u32[]{:S(2)}) collective-permute-start(bf16[640,512]{1,0:T(8,128)(2,1)S(1)} %pad_maximum_fusion.refs_1_.refs_12_), channel_id=1, source_target_pairs={{0,4},{4,0},{8,12},{12,8},{16,20},{20,16},{24,28},{28,24},{1,5},{5... | collective-permute-start | bytes 1966088 | tf_op jit(solution)/shard_map/ppermute | solution.py:43
  36.2 10.7 %collective-permute-start.11 = (bf16[256,512]{1,0:T(8,128)(2,1)S(1)}, bf16[256,512]{1,0:T(8,128)(2,1)}, u32[]{:S(2)}, u32[]{:S(2)}) collective-permute-start(bf16[256,512]{1,0:T(8,128)(2,1)S(1)} %project.2.refs_0_.refs_1_), channel_id=1, source_target_pairs={{0,1},{1,2},{2,3},{4,5},{5,6},{6,7},{8,9},{9,10},{10,11},{12,13},{... | collective-permute-start | bytes 786440 | tf_op jit(solution)/shard_map/ppermute | solution.py:49
  39.7 15.1 %copy-start.27 = (s32[1,4]{1,0:T(1,128)S(1)}, s32[1,4]{1,0:T(1,128)}, u32[]{:S(2)}) copy-start(s32[1,4]{1,0:T(1,128)} %param.9) | copy-start | bytes 52
  46.9 9.2 %collective-permute-start.15 = (bf16[256,512]{1,0:T(8,128)(2,1)}, bf16[256,512]{1,0:T(8,128)(2,1)}, u32[]{:S(2)}, u32[]{:S(2)}) collective-permute-start(bf16[256,512]{1,0:T(8,128)(2,1)} %collective-permute-done.11.refs_2_.refs_3_), channel_id=1, source_target_pairs={{1,2},{2,3},{5,6},{6,7},{9,10},{10,11},{13,14},{14,15},{17,18},{18... | collective-permute-start | bytes 786440 | tf_op jit(solution)/shard_map/ppermute | solution.py:49
  51.1 14.6 %copy-start.9 = (bf16[640,512]{1,0:T(8,128)(2,1)}, bf16[640,512]{1,0:T(8,128)(2,1)S(1)}, u32[]{:S(2)}) copy-start(bf16[640,512]{1,0:T(8,128)(2,1)S(1)} %collective-permute-done.12.refs_6_.refs_17_) | copy-start | bytes 1966084
  51.1 14.6 %collective-permute-start.16 = (bf16[640,512]{1,0:T(8,128)(2,1)}, bf16[640,512]{1,0:T(8,128)(2,1)S(1)}, u32[]{:S(2)}, u32[]{:S(2)}) collective-permute-start(bf16[640,512]{1,0:T(8,128)(2,1)} %collective-permute-done.4.near_ref.refs_2_.refs_13_), channel_id=1, source_target_pairs={{0,4},{4,0},{8,12},{12,8},{16,20},{20,16},{24,28},{28,24},{1,5},{5... | collective-permute-start | bytes 1966088 | tf_op jit(solution)/shard_map/ppermute | solution.py:43
  52.7 13.0 %collective-permute-start.17 = (bf16[640,512]{1,0:T(8,128)(2,1)}, bf16[640,512]{1,0:T(8,128)(2,1)S(1)}, u32[]{:S(2)}, u32[]{:S(2)}) collective-permute-start(bf16[640,512]{1,0:T(8,128)(2,1)} %collective-permute-done.5.far_ref.refs_3_.refs_14_), channel_id=1, source_target_pairs={{0,4},{4,0},{8,12},{12,8},{16,20},{20,16},{24,28},{28,24},{1,5},{5... | collective-permute-start | bytes 1966088 | tf_op jit(solution)/shard_map/ppermute | solution.py:43
  53.1 9.8 %collective-permute-start.13 = (bf16[640,256]{1,0:T(8,128)(2,1)S(1)}, bf16[640,256]{1,0:T(8,128)(2,1)S(1)}, u32[]{:S(2)}, u32[]{:S(2)}) collective-permute-start(bf16[640,256]{1,0:T(8,128)(2,1)S(1)} %get-tuple-element.54), channel_id=1, source_target_pairs={{0,16},{4,20},{8,24},{12,28},{16,0},{20,4},{24,8},{28,12},{1,17},{... | collective-permute-start | bytes 983048 | tf_op jit(solution)/shard_map/ppermute | solution.py:43
  53.6 9.5 %collective-permute-start.14 = (bf16[640,256]{1,0:T(8,128)(2,1)S(1)}, bf16[640,256]{1,0:T(8,128)(2,1)S(1)}, u32[]{:S(2)}, u32[]{:S(2)}) collective-permute-start(bf16[640,256]{1,0:T(8,128)(2,1)S(1)} %get-tuple-element.55), channel_id=1, source_target_pairs={{0,8},{4,12},{8,0},{12,4},{16,24},{20,28},{24,16},{28,20},{1,9},{5... | collective-permute-start | bytes 983048 | tf_op jit(solution)/shard_map/ppermute | solution.py:43
  63.1 2.5 %collective-permute-start.18 = (bf16[640,256]{1,0:T(8,128)(2,1)S(1)}, bf16[640,256]{1,0:T(8,128)(2,1)S(1)}, u32[]{:S(2)}, u32[]{:S(2)}) collective-permute-start(bf16[640,256]{1,0:T(8,128)(2,1)S(1)} %collective-permute-done.13.refs_4_.refs_15_), channel_id=1, source_target_pairs={{0,4},{4,0},{8,12},{12,8},{16,20},{20,16},{24,28},{28,24},{1,5},{5... | collective-permute-start | bytes 983048 | tf_op jit(solution)/shard_map/ppermute | solution.py:43
  63.1 2.6 %collective-permute-start.19 = (bf16[640,256]{1,0:T(8,128)(2,1)S(1)}, bf16[640,256]{1,0:T(8,128)(2,1)S(1)}, u32[]{:S(2)}, u32[]{:S(2)}) collective-permute-start(bf16[640,256]{1,0:T(8,128)(2,1)S(1)} %collective-permute-done.14.refs_5_.refs_16_), channel_id=1, source_target_pairs={{0,4},{4,0},{8,12},{12,8},{16,20},{20,16},{24,28},{28,24},{1,5},{5... | collective-permute-start | bytes 983048 | tf_op jit(solution)/shard_map/ppermute | solution.py:43
  64.3 11.9 %collective-permute-start.20 = (bf16[256,512]{1,0:T(8,128)(2,1)}, bf16[256,512]{1,0:T(8,128)(2,1)}, u32[]{:S(2)}, u32[]{:S(2)}) collective-permute-start(bf16[256,512]{1,0:T(8,128)(2,1)} %collective-permute-done.15.refs_4_.refs_5_), channel_id=1, source_target_pairs={{2,3},{6,7},{10,11},{14,15},{18,19},{22,23},{26,27},{30,31}} | collective-permute-start | bytes 786440 | tf_op jit(solution)/shard_map/ppermute | solution.py:49
  70.3 12.9 %collective-permute-start.21 = (bf16[256,512]{1,0:T(8,128)(2,1)S(1)}, bf16[256,512]{1,0:T(8,128)(2,1)}, u32[]{:S(2)}, u32[]{:S(2)}) collective-permute-start(bf16[256,512]{1,0:T(8,128)(2,1)S(1)} %project.3.refs_0_.refs_1_), channel_id=1, source_target_pairs={{0,2},{1,3},{4,6},{5,7},{8,10},{9,11},{12,14},{13,15},{16,18},{17,... | collective-permute-start | bytes 786440 | tf_op jit(solution)/shard_map/ppermute | solution.py:49
  72.6 36.7 %all-to-all-start = ((bf16[8,256,640]{2,1,0:T(8,128)(2,1)}), bf16[8,256,640]{2,1,0:T(8,128)(2,1)S(1)}, u32[]{:S(2)}, u32[]{:S(2)}) async-start(bf16[8,256,640]{2,1,0:T(8,128)(2,1)} %split_columns.1.refs_0_), calls=%async_computation | async-start | bytes 5242880 | tf_op jit(solution)/shard_map/all_to_all | solution.py:501
  83.2 7.2 %collective-permute-start.22 = (bf16[256,512]{1,0:T(8,128)(2,1)}, bf16[256,512]{1,0:T(8,128)(2,1)S(1)}, u32[]{:S(2)}, u32[]{:S(2)}) collective-permute-start(bf16[256,512]{1,0:T(8,128)(2,1)} %get-tuple-element.60), channel_id=1, source_target_pairs={{3,2},{7,6},{11,10},{15,14},{19,18},{23,22},{27,26},{31,30}} | collective-permute-start | bytes 786440 | tf_op jit(solution)/shard_map/ppermute | solution.py:49
  83.9 11.0 %collective-permute-start.23 = (bf16[256,512]{1,0:T(8,128)(2,1)S(1)}, bf16[256,512]{1,0:T(8,128)(2,1)S(1)}, u32[]{:S(2)}, u32[]{:S(2)}) collective-permute-start(bf16[256,512]{1,0:T(8,128)(2,1)S(1)} %project.3.refs_0_.refs_1_), channel_id=1, source_target_pairs={{0,1},{1,2},{2,3},{4,5},{5,6},{6,7},{8,9},{9,10},{10,11},{12,13},{... | collective-permute-start | bytes 786440 | tf_op jit(solution)/shard_map/ppermute | solution.py:49
  87.6 7.3 %collective-permute-start.24 = (bf16[256,512]{1,0:T(8,128)(2,1)}, bf16[256,512]{1,0:T(8,128)(2,1)S(1)}, u32[]{:S(2)}, u32[]{:S(2)}) collective-permute-start(bf16[256,512]{1,0:T(8,128)(2,1)} %collective-permute-done.21.refs_4_.refs_5_), channel_id=1, source_target_pairs={{2,3},{6,7},{10,11},{14,15},{18,19},{22,23},{26,27},{30,31}} | collective-permute-start | bytes 786440 | tf_op jit(solution)/shard_map/ppermute | solution.py:49
  88.3 18.6 %collective-permute-start.25 = (bf16[256,512]{1,0:T(8,128)(2,1)}, bf16[256,512]{1,0:T(8,128)(2,1)}, u32[]{:S(2)}, u32[]{:S(2)}) collective-permute-start(bf16[256,512]{1,0:T(8,128)(2,1)} %get-tuple-element.68), channel_id=1, source_target_pairs={{1,0},{2,1},{3,2},{5,4},{6,5},{7,6},{9,8},{10,9},{11,10},{13,12},{... | collective-permute-start | bytes 786440 | tf_op jit(solution)/shard_map/ppermute | solution.py:49
  92.2 14.7 %collective-permute-start.26 = (bf16[256,512]{1,0:T(8,128)(2,1)}, bf16[256,512]{1,0:T(8,128)(2,1)}, u32[]{:S(2)}, u32[]{:S(2)}) collective-permute-start(bf16[256,512]{1,0:T(8,128)(2,1)} %add_convert_fusion.3), channel_id=1, source_target_pairs={{2,0},{3,1},{6,4},{7,5},{10,8},{11,9},{14,12},{15,13},{18,16},{19,... | collective-permute-start | bytes 786440 | tf_op jit(solution)/shard_map/ppermute | solution.py:49
  108.0 9.1 %collective-permute-start.37 = (bf16[256,512]{1,0:T(8,128)(2,1)S(1)}, bf16[256,512]{1,0:T(8,128)(2,1)}, u32[]{:S(2)}, u32[]{:S(2)}) collective-permute-start(bf16[256,512]{1,0:T(8,128)(2,1)S(1)} %add_convert_fusion.refs_0_), channel_id=1, source_target_pairs={{0,8},{4,12},{8,0},{12,4},{16,24},{20,28},{24,16},{28,20},{1,9},{5... | collective-permute-start | bytes 786440 | tf_op jit(solution)/shard_map/ppermute | solution.py:43
  109.3 11.3 %collective-permute-start.27 = (bf16[256,512]{1,0:T(8,128)(2,1)}, bf16[256,512]{1,0:T(8,128)(2,1)S(1)}, u32[]{:S(2)}, u32[]{:S(2)}) collective-permute-start(bf16[256,512]{1,0:T(8,128)(2,1)} %get-tuple-element.71), channel_id=1, source_target_pairs={{1,0},{2,1},{3,2},{5,4},{6,5},{7,6},{9,8},{10,9},{11,10},{13,12},{... | collective-permute-start | bytes 786440 | tf_op jit(solution)/shard_map/ppermute | solution.py:49
  116.5 5.1 %collective-permute-start.28 = (bf16[256,512]{1,0:T(8,128)(2,1)}, bf16[256,512]{1,0:T(8,128)(2,1)S(1)}, u32[]{:S(2)}, u32[]{:S(2)}) collective-permute-start(bf16[256,512]{1,0:T(8,128)(2,1)} %get-tuple-element.75), channel_id=1, source_target_pairs={{3,2},{7,6},{11,10},{15,14},{19,18},{23,22},{27,26},{31,30}} | collective-permute-start | bytes 786440 | tf_op jit(solution)/shard_map/ppermute | solution.py:49
  120.7 11.0 %collective-permute-start.38 = (bf16[512,512]{1,0:T(8,128)(2,1)S(1)}, bf16[512,512]{1,0:T(8,128)(2,1)S(1)}, u32[]{:S(2)}, u32[]{:S(2)}) collective-permute-start(bf16[512,512]{1,0:T(8,128)(2,1)S(1)} %pad_maximum_fusion.2), channel_id=1, source_target_pairs={{0,16},{4,20},{8,24},{12,28},{16,0},{20,4},{24,8},{28,12},{1,17},{... | collective-permute-start | bytes 1572872 | tf_op jit(solution)/shard_map/ppermute | solution.py:43
  122.7 10.1 %collective-permute-start.29 = (bf16[256,512]{1,0:T(8,128)(2,1)S(1)}, bf16[256,512]{1,0:T(8,128)(2,1)S(1)}, u32[]{:S(2)}, u32[]{:S(2)}) collective-permute-start(bf16[256,512]{1,0:T(8,128)(2,1)S(1)} %add_convert_fusion.2), channel_id=1, source_target_pairs={{2,0},{3,1},{6,4},{7,5},{10,8},{11,9},{14,12},{15,13},{18,16},{19,... | collective-permute-start | bytes 786440 | tf_op jit(solution)/shard_map/ppermute | solution.py:49
  132.8 15.6 %collective-permute-start.39 = (bf16[1024,512]{1,0:T(8,128)(2,1)S(1)}, bf16[1024,512]{1,0:T(8,128)(2,1)S(1)}, u32[]{:S(2)}, u32[]{:S(2)}) collective-permute-start(bf16[1024,512]{1,0:T(8,128)(2,1)S(1)} %constant_dynamic-update-slice_fusion.refs_1_), channel_id=1, source_target_pairs={{0,4},{4,0},{8,12},{12,8},{16,20},{20,16},{24,28},{28,24},{1,5},{5... | collective-permute-start | bytes 3145736 | tf_op jit(solution)/shard_map/ppermute | solution.py:43
  132.9 9.2 %collective-permute-start.31 = (bf16[256,512]{1,0:T(8,128)(2,1)S(1)}, bf16[256,512]{1,0:T(8,128)(2,1)S(1)}, u32[]{:S(2)}, u32[]{:S(2)}) collective-permute-start(bf16[256,512]{1,0:T(8,128)(2,1)S(1)} %add_convert_fusion.1.refs_1_), channel_id=1, source_target_pairs={{0,8},{4,12},{8,0},{12,4},{16,24},{20,28},{24,16},{28,20},{1,9},{5... | collective-permute-start | bytes 786440 | tf_op jit(solution)/shard_map/ppermute | solution.py:43
  133.8 14.1 %collective-permute-start.33 = (bf16[256,512]{1,0:T(8,128)(2,1)S(1)}, bf16[256,512]{1,0:T(8,128)(2,1)S(1)}, u32[]{:S(2)}, u32[]{:S(2)}) collective-permute-start(bf16[256,512]{1,0:T(8,128)(2,1)S(1)} %add_convert_fusion.1.refs_1_), channel_id=1, source_target_pairs={{0,16},{4,20},{8,24},{12,28},{16,0},{20,4},{24,8},{28,12},{1,17},{... | collective-permute-start | bytes 786440 | tf_op jit(solution)/shard_map/ppermute | solution.py:43
  135.2 12.7 %collective-permute-start.35 = (bf16[256,512]{1,0:T(8,128)(2,1)S(1)}, bf16[256,512]{1,0:T(8,128)(2,1)S(1)}, u32[]{:S(2)}, u32[]{:S(2)}) collective-permute-start(bf16[256,512]{1,0:T(8,128)(2,1)S(1)} %add_convert_fusion.1.refs_1_), channel_id=1, source_target_pairs={{0,24},{4,28},{8,16},{12,20},{16,8},{20,12},{24,0},{28,4},{1,25},{... | collective-permute-start | bytes 786440 | tf_op jit(solution)/shard_map/ppermute | solution.py:43
  136.5 14.1 %collective-permute-start.30 = (bf16[256,512]{1,0:T(8,128)(2,1)S(1)}, bf16[256,512]{1,0:T(8,128)(2,1)S(1)}, u32[]{:S(2)}, u32[]{:S(2)}) collective-permute-start(bf16[256,512]{1,0:T(8,128)(2,1)S(1)} %add_convert_fusion.1.refs_1_), channel_id=1, source_target_pairs={{0,4},{4,0},{8,12},{12,8},{16,20},{20,16},{24,28},{28,24},{1,5},{5... | collective-permute-start | bytes 786440 | tf_op jit(solution)/shard_map/ppermute | solution.py:43
  142.1 8.5 %collective-permute-start.32 = (bf16[256,512]{1,0:T(8,128)(2,1)S(1)}, bf16[256,512]{1,0:T(8,128)(2,1)S(1)}, u32[]{:S(2)}, u32[]{:S(2)}) collective-permute-start(bf16[256,512]{1,0:T(8,128)(2,1)S(1)} %collective-permute-done.31.refs_3_), channel_id=1, source_target_pairs={{0,4},{4,0},{8,12},{12,8},{16,20},{20,16},{24,28},{28,24},{1,5},{5... | collective-permute-start | bytes 786440 | tf_op jit(solution)/shard_map/ppermute | solution.py:43
  147.8 2.8 %collective-permute-start.34 = (bf16[256,512]{1,0:T(8,128)(2,1)S(1)}, bf16[256,512]{1,0:T(8,128)(2,1)S(1)}, u32[]{:S(2)}, u32[]{:S(2)}) collective-permute-start(bf16[256,512]{1,0:T(8,128)(2,1)S(1)} %collective-permute-done.33.refs_5_), channel_id=1, source_target_pairs={{0,4},{4,0},{8,12},{12,8},{16,20},{20,16},{24,28},{28,24},{1,5},{5... | collective-permute-start | bytes 786440 | tf_op jit(solution)/shard_map/ppermute | solution.py:43
  147.8 2.8 %collective-permute-start.36 = (bf16[256,512]{1,0:T(8,128)(2,1)S(1)}, bf16[256,512]{1,0:T(8,128)(2,1)S(1)}, u32[]{:S(2)}, u32[]{:S(2)}) collective-permute-start(bf16[256,512]{1,0:T(8,128)(2,1)S(1)} %collective-permute-done.35.refs_7_), channel_id=1, source_target_pairs={{0,4},{4,0},{8,12},{12,8},{16,20},{20,16},{24,28},{28,24},{1,5},{5... | collective-permute-start | bytes 786440 | tf_op jit(solution)/shard_map/ppermute | solution.py:43
  153.0 25.0 %collective-permute-start.40 = (bf16[640,256]{1,0:T(8,128)(2,1)S(1)}, bf16[640,256]{1,0:T(8,128)(2,1)S(1)}, u32[]{:S(2)}, u32[]{:S(2)}) collective-permute-start(bf16[640,256]{1,0:T(8,128)(2,1)S(1)} %get-tuple-element.86), channel_id=1, source_target_pairs={{0,2},{1,3},{2,0},{3,1},{4,6},{5,7},{6,4},{7,5},{8,10},{9,11},{10,... | collective-permute-start | bytes 983048 | tf_op jit(solution)/shard_map/ppermute | solution.py:43
  155.8 29.0 %collective-permute-start.41 = (bf16[640,256]{1,0:T(8,128)(2,1)S(1)}, bf16[640,256]{1,0:T(8,128)(2,1)S(1)}, u32[]{:S(2)}, u32[]{:S(2)}) collective-permute-start(bf16[640,256]{1,0:T(8,128)(2,1)S(1)} %get-tuple-element.87), channel_id=1, source_target_pairs={{0,3},{1,2},{2,1},{3,0},{4,7},{5,6},{6,5},{7,4},{8,11},{9,10},{10,... | collective-permute-start | bytes 983048 | tf_op jit(solution)/shard_map/ppermute | solution.py:43
  161.3 23.5 %collective-permute-start.42 = (bf16[640,256]{1,0:T(8,128)(2,1)S(1)}, bf16[640,256]{1,0:T(8,128)(2,1)S(1)}, u32[]{:S(2)}, u32[]{:S(2)}) collective-permute-start(bf16[640,256]{1,0:T(8,128)(2,1)S(1)} %get-tuple-element.88), channel_id=1, source_target_pairs={{0,1},{1,0},{2,3},{3,2},{4,5},{5,4},{6,7},{7,6},{8,9},{9,8},{10,11... | collective-permute-start | bytes 983048 | tf_op jit(solution)/shard_map/ppermute | solution.py:43
  (26 other events, 222.7 us)

commit v7 on v6

--- a/solution.py
+++ b/solution.py
@@ -532,7 +532,7 @@
         gates = ()
     gates = (sums[0],)
     terms = [sums[0]]
-    for mask in (*range(2, seq_count), 1):
+    for mask in (2, 1, *range(3, seq_count)):
         terms.append(exchange(sums[mask], "seq", mask).astype(jnp.float32))
     weight_grad = functools.reduce(lambda a, b: a + b, terms)
     token_grad = token_grads(after(rank, *gates), dkvs, weight_pieces, rows)

time: 187 us -> 186 us (level)
  transfers between devices with their start and end apart: 44 -> 44, of which waited for: 19 -> 20; matrix products, arithmetic and copies ran while one was open for 3% -> 3% of each run, Pallas kernels for 16% -> 16%
where the time goes in v7:
time: 186 us; the launch traced here: 185 us
  waiting for transfers between devices  83.6 us (45%)
  starting transfers between devices  58.3 us (31%)
  Pallas kernels  32.2 us (17%)
  other arithmetic  7.05 us (4%)
  local copies, waits for them, and re-layouts  2.95 us (2%)
    ppermute x31, waiting for transfers between devices, exchange(): return lax.ppermute(value, axis, [(i, i ^ mask) for i in range(count)])  60 us
    ppermute x12, starting transfers between devices, moved(): return lax.ppermute(value, axis, pairs)  29.2 us
    ppermute x31, starting transfers between devices, exchange(): return lax.ppermute(value, axis, [(i, i ^ mask) for i in range(count)])  25.4 us
    ppermute x12, waiting for transfers between devices, moved(): return lax.ppermute(value, axis, pairs)  23.5 us
    pallas_call x2, Pallas kernels, project(): pl.pallas_call(functools.partial(project_kernel, table), out_shape=jax.Sh...  8.77 us
    pallas_call x1, Pallas kernels, token_grads(): pl.pallas_call(functools.partial(token_kernel, tables, tuple(indices)), o...  7.21 us
    pallas_call x2, Pallas kernels, attend(): pl.pallas_call(functools.partial(attend_kernel, sizes), grid=(heads,), ou...  6.84 us
    pallas_call x2, Pallas kernels, weight_terms(): pl.pallas_call(functools.partial(weight_kernel, dests, len(pieces), bool(...  4.48 us
  transfers between devices with their start and end apart: 44, of which 20 were waited for; matrix products, arithmetic and copies ran while one was open for 3% of the time, Pallas kernels for 16%

profile of v7, /device:TPU:8, one launch (start us, length us, event | category | flops | bytes accessed | tf_op | source)
XLA Modules:
  0.0 185.4 jit_solution(7706514363761413514)
XLA Ops:
  0.6 1.4 fusion.2
  2.1 1.6 collective-permute-start
  3.6 1.5 collective-permute-start.1
  5.2 3.4 %split_columns.1.refs_0_ = bf16[8,256,640]{2,1,0:T(8,128)(2,1)} custom-call(bf16[1,256,5120]{2,1,0:T(8,128)(2,1)S(1)} %copy-done.2), custom_call_target="tpu_custom_call" | custom-call | flops 12000000000 | bytes 36000000 | tf_op jit(solution)/shard_map/split_columns/pallas_call | solution.py:195
  8.6 10.0 %collective-permute-done.near_ref.refs_2_.refs_3_ = bf16[640,512]{1,0:T(8,128)(2,1)S(1)} collective-permute-done((bf16[640,512]{1,0:T(8,128)(2,1)S(1)}, bf16[640,512]{1,0:T(8,128)(2,1)S(1)}, u32[]{:S(2)}, u32[]{:S(2)}) %collective-permute-start) | collective-permute-done | bytes 655392 | tf_op jit(solution)/shard_map/ppermute | solution.py:43
  18.6 1.2 collective-permute-done.1.far_ref.refs_3_.refs_4_
  20.5 1.5 collective-permute-start.2
  22.5 5.8 %collective-permute-done.3.refs_5_.refs_6_ = bf16[640,256]{1,0:T(8,128)(2,1)} collective-permute-done((bf16[640,256]{1,0:T(8,128)(2,1)S(1)}, bf16[640,256]{1,0:T(8,128)(2,1)}, u32[]{:S(2)}, u32[]{:S(2)}) %collective-permute-start.3) | collective-permute-done | bytes 327712 | tf_op jit(solution)/shard_map/ppermute | solution.py:43
  28.9 1.3 collective-permute-start.4
  30.3 1.5 collective-permute-start.5
  31.8 4.3 %project.2.refs_0_.refs_1_ = bf16[256,512]{1,0:T(8,128)(2,1)S(1)} custom-call(s32[2]{0:T(128)S(1)} %pad_add_fusion.1.rank_ref, bf16[8,256,640]{2,1,0:T(8,128)(2,1)} %split_columns.1.refs_0_, bf16[640,512]{1,0:T(8,128)(2,1)S(1)} %pad_maximum_fusion.1.refs_1_.refs_2_, bf16[640,512]{1,0:T(8,128)(2,1)S(1)} %collective-permute-done.near_ref.refs_2_.refs_3_, ...), custom_call_target="tpu_custom_call" | custom-call | flops 16000000000 | bytes 48000000 | tf_op jit(solution)/shard_map/project/pallas_call | solution.py:227
  36.2 3.5 %collective-permute-start.11 = (bf16[256,512]{1,0:T(8,128)(2,1)S(1)}, bf16[256,512]{1,0:T(8,128)(2,1)}, u32[]{:S(2)}, u32[]{:S(2)}) collective-permute-start(bf16[256,512]{1,0:T(8,128)(2,1)S(1)} %project.2.refs_0_.refs_1_), channel_id=1, source_target_pairs={{0,1},{1,2},{2,3},{4,5},{5,6},{6,7},{8,9},{9,10},{10,11},{12,13},{... | collective-permute-start | bytes 786440 | tf_op jit(solution)/shard_map/ppermute | solution.py:49
  39.7 7.2 %collective-permute-done.11.refs_2_.refs_3_ = bf16[256,512]{1,0:T(8,128)(2,1)} collective-permute-done((bf16[256,512]{1,0:T(8,128)(2,1)S(1)}, bf16[256,512]{1,0:T(8,128)(2,1)}, u32[]{:S(2)}, u32[]{:S(2)}) %collective-permute-start.11) | collective-permute-done | bytes 262176 | tf_op jit(solution)/shard_map/ppermute | solution.py:49
  46.9 4.2 %collective-permute-start.15 = (bf16[256,512]{1,0:T(8,128)(2,1)}, bf16[256,512]{1,0:T(8,128)(2,1)}, u32[]{:S(2)}, u32[]{:S(2)}) collective-permute-start(bf16[256,512]{1,0:T(8,128)(2,1)} %collective-permute-done.11.refs_2_.refs_3_), channel_id=1, source_target_pairs={{1,2},{2,3},{5,6},{6,7},{9,10},{10,11},{13,14},{14,15},{17,18},{18... | collective-permute-start | bytes 786440 | tf_op jit(solution)/shard_map/ppermute | solution.py:49
  51.2 1.5 halves.3
  53.6 1.2 collective-permute-start.14
  56.1 6.8 %collective-permute-done.13.refs_4_.refs_15_ = bf16[640,256]{1,0:T(8,128)(2,1)S(1)} collective-permute-done((bf16[640,256]{1,0:T(8,128)(2,1)S(1)}, bf16[640,256]{1,0:T(8,128)(2,1)S(1)}, u32[]{:S(2)}, u32[]{:S(2)}) %collective-permute-start.13) | collective-permute-done | bytes 327712 | tf_op jit(solution)/shard_map/ppermute | solution.py:43
  64.3 1.4 collective-permute-start.20
  65.7 4.5 %project.3.refs_0_.refs_1_ = bf16[256,512]{1,0:T(8,128)(2,1)S(1)} custom-call(s32[2]{0:T(128)S(1)} %pad_add_fusion.1.rank_ref, bf16[8,256,640]{2,1,0:T(8,128)(2,1)} %split_columns.1.refs_0_, bf16[640,512]{1,0:T(8,128)(2,1)S(1)} %pad_maximum_fusion.refs_1_.refs_12_, bf16[640,512]{1,0:T(8,128)(2,1)} %collective-permute-done.4.near_ref.refs_2_.refs_13_, ...), custom_call_target="tpu_custom_call" | custom-call | flops 16000000000 | bytes 48000000 | tf_op jit(solution)/shard_map/project/pallas_call | solution.py:227
  70.3 2.3 %collective-permute-start.21 = (bf16[256,512]{1,0:T(8,128)(2,1)S(1)}, bf16[256,512]{1,0:T(8,128)(2,1)}, u32[]{:S(2)}, u32[]{:S(2)}) collective-permute-start(bf16[256,512]{1,0:T(8,128)(2,1)S(1)} %project.3.refs_0_.refs_1_), channel_id=1, source_target_pairs={{0,2},{1,3},{4,6},{5,7},{8,10},{9,11},{12,14},{13,15},{16,18},{17,... | collective-permute-start | bytes 786440 | tf_op jit(solution)/shard_map/ppermute | solution.py:49
  72.6 3.6 %all-to-all-start = ((bf16[8,256,640]{2,1,0:T(8,128)(2,1)}), bf16[8,256,640]{2,1,0:T(8,128)(2,1)S(1)}, u32[]{:S(2)}, u32[]{:S(2)}) async-start(bf16[8,256,640]{2,1,0:T(8,128)(2,1)} %split_columns.1.refs_0_), calls=%async_computation | async-start | bytes 5242880 | tf_op jit(solution)/shard_map/all_to_all | solution.py:501
  76.2 3.4 %attend.2 = (bf16[1,256,2560]{2,1,0:T(8,128)(2,1)}, f32[256,512]{1,0:T(8,128)}, bf16[256,512]{1,0:T(8,128)(2,1)}, bf16[256,512]{1,0:T(8,128)(2,1)}, bf16[256,512]{1,0:T(8,128)(2,1)}) custom-call(s32[10]{0:T(128)} %pad_add_fusion.info_ref, bf16[1,256,2560]{2,1,0:T(8,128)(2,1)} %q_ref.3, bf16[1,256,2560]{2,1,0:T(8,128)(2,1)} %g_ref.3, ...), custom_call_target="tpu_custom_call" | custom-call | flops 35999997952 | bytes 108000000 | tf_op jit(solution)/shard_map/attend/pallas_call | solution.py:342
  79.6 3.6 %collective-permute-done.21.refs_4_.refs_5_ = bf16[256,512]{1,0:T(8,128)(2,1)} collective-permute-done((bf16[256,512]{1,0:T(8,128)(2,1)S(1)}, bf16[256,512]{1,0:T(8,128)(2,1)}, u32[]{:S(2)}, u32[]{:S(2)}) %collective-permute-start.21) | collective-permute-done | bytes 262176 | tf_op jit(solution)/shard_map/ppermute | solution.py:49
  83.9 2.3 %collective-permute-start.23 = (bf16[256,512]{1,0:T(8,128)(2,1)S(1)}, bf16[256,512]{1,0:T(8,128)(2,1)S(1)}, u32[]{:S(2)}, u32[]{:S(2)}) collective-permute-start(bf16[256,512]{1,0:T(8,128)(2,1)S(1)} %project.3.refs_0_.refs_1_), channel_id=1, source_target_pairs={{0,1},{1,2},{2,3},{4,5},{5,6},{6,7},{8,9},{9,10},{10,11},{12,13},{... | collective-permute-start | bytes 786440 | tf_op jit(solution)/shard_map/ppermute | solution.py:49
  87.0 3.7 %collective-permute-start.25 = (bf16[256,512]{1,0:T(8,128)(2,1)}, bf16[256,512]{1,0:T(8,128)(2,1)}, u32[]{:S(2)}, u32[]{:S(2)}) collective-permute-start(bf16[256,512]{1,0:T(8,128)(2,1)} %get-tuple-element.68), channel_id=1, source_target_pairs={{1,0},{2,1},{3,2},{5,4},{6,5},{7,6},{9,8},{10,9},{11,10},{13,12},{... | collective-permute-start | bytes 786440 | tf_op jit(solution)/shard_map/ppermute | solution.py:49
  90.7 1.7 add_convert_fusion.3
  92.4 1.5 collective-permute-start.26
  93.9 1.1 collective-permute-done.23.refs_2_.refs_3_
  96.4 3.4 %attend.3 = (bf16[1,256,2560]{2,1,0:T(8,128)(2,1)}, f32[256,512]{1,0:T(8,128)}, bf16[256,512]{1,0:T(8,128)(2,1)}, bf16[256,512]{1,0:T(8,128)(2,1)}, bf16[256,512]{1,0:T(8,128)(2,1)}) custom-call(s32[10]{0:T(128)} %pad_add_fusion.info_ref, bf16[1,256,2560]{2,1,0:T(8,128)(2,1)} %q_ref.3, ...), custom_call_target="tpu_custom_call", output_to_operand_aliasing={{0}: (11, {})} | custom-call | flops 8000000000 | bytes 24000000 | tf_op jit(solution)/shard_map/attend/pallas_call | solution.py:342
  99.9 7.0 %collective-permute-done.25 = bf16[256,512]{1,0:T(8,128)(2,1)} collective-permute-done((bf16[256,512]{1,0:T(8,128)(2,1)}, bf16[256,512]{1,0:T(8,128)(2,1)}, u32[]{:S(2)}, u32[]{:S(2)}) %collective-permute-start.25) | collective-permute-done | bytes 262176 | tf_op jit(solution)/shard_map/ppermute | solution.py:49
  106.9 1.1 add_convert_fusion.refs_0_
  108.0 1.3 collective-permute-start.37
  109.3 7.1 %collective-permute-start.27 = (bf16[256,512]{1,0:T(8,128)(2,1)}, bf16[256,512]{1,0:T(8,128)(2,1)S(1)}, u32[]{:S(2)}, u32[]{:S(2)}) collective-permute-start(bf16[256,512]{1,0:T(8,128)(2,1)} %get-tuple-element.71), channel_id=1, source_target_pairs={{1,0},{2,1},{3,2},{5,4},{6,5},{7,6},{9,8},{10,9},{11,10},{13,12},{... | collective-permute-start | bytes 786440 | tf_op jit(solution)/shard_map/ppermute | solution.py:49
  118.2 2.5 %collective-permute-done.27 = bf16[256,512]{1,0:T(8,128)(2,1)S(1)} collective-permute-done((bf16[256,512]{1,0:T(8,128)(2,1)}, bf16[256,512]{1,0:T(8,128)(2,1)S(1)}, u32[]{:S(2)}, u32[]{:S(2)}) %collective-permute-start.27) | collective-permute-done | bytes 262176 | tf_op jit(solution)/shard_map/ppermute | solution.py:49
  121.6 1.1 add_convert_fusion.2
  122.7 1.3 collective-permute-start.29
  124.0 7.6 %collective-permute-done.38 = bf16[512,512]{1,0:T(8,128)(2,1)S(1)} collective-permute-done((bf16[512,512]{1,0:T(8,128)(2,1)S(1)}, bf16[512,512]{1,0:T(8,128)(2,1)S(1)}, u32[]{:S(2)}, u32[]{:S(2)}) %collective-permute-start.38) | collective-permute-done | bytes 524320 | tf_op jit(solution)/shard_map/ppermute | solution.py:43
  133.5 1.6 collective-permute-start.33
  135.2 1.2 collective-permute-start.35
  136.3 5.6 %collective-permute-done.31.refs_3_ = bf16[256,512]{1,0:T(8,128)(2,1)S(1)} collective-permute-done((bf16[256,512]{1,0:T(8,128)(2,1)S(1)}, bf16[256,512]{1,0:T(8,128)(2,1)S(1)}, u32[]{:S(2)}, u32[]{:S(2)}) %collective-permute-start.31) | collective-permute-done | bytes 262176 | tf_op jit(solution)/shard_map/ppermute | solution.py:43
  142.0 5.6 %collective-permute-done.33.refs_5_ = bf16[256,512]{1,0:T(8,128)(2,1)S(1)} collective-permute-done((bf16[256,512]{1,0:T(8,128)(2,1)S(1)}, bf16[256,512]{1,0:T(8,128)(2,1)S(1)}, u32[]{:S(2)}, u32[]{:S(2)}) %collective-permute-start.33) | collective-permute-done | bytes 262176 | tf_op jit(solution)/shard_map/ppermute | solution.py:43
  148.1 2.2 %weight_grad.2 = (f32[640,256]{1,0:T(8,128)S(1)}, bf16[640,256]{1,0:T(8,128)(2,1)S(1)}, bf16[640,256]{1,0:T(8,128)(2,1)S(1)}, bf16[640,256]{1,0:T(8,128)(2,1)S(1)}) custom-call(s32[2]{0:T(128)S(1)} %pad_add_fusion.1.rank_ref, bf16[8,256,640]{2,1,0:T(8,128)(2,1)S(1)} %all-to-all-done.refs_0_, bf16[1024,512]{1,0:T(8,128)(2,1)S(1)} %constant_dynamic-update-slice_fusion.refs_1_, ...), custom_call_target="tpu_custom_call" | custom-call | flops 16000000000 | bytes 48000000 | tf_op jit(solution)/shard_map/weight_grad/pallas_call | solution.py:443
  150.5 2.3 %weight_grad.3 = (f32[640,256]{1,0:T(8,128)S(1)}, bf16[640,256]{1,0:T(8,128)(2,1)S(1)}, bf16[640,256]{1,0:T(8,128)(2,1)S(1)}, bf16[640,256]{1,0:T(8,128)(2,1)S(1)}) custom-call(s32[2]{0:T(128)S(1)} %pad_add_fusion.1.rank_ref, bf16[8,256,640]{2,1,0:T(8,128)(2,1)S(1)} %all-to-all-done.refs_0_, bf16[256,512]{1,0:T(8,128)(2,1)S(1)} %add_convert_fusion.1.refs_1_, ...), custom_call_target="tpu_custom_call" | custom-call | flops 16000000000 | bytes 48000000 | tf_op jit(solution)/shard_map/weight_grad/pallas_call | solution.py:443
  152.8 6.2 %collective-permute-start.41 = (bf16[640,256]{1,0:T(8,128)(2,1)S(1)}, bf16[640,256]{1,0:T(8,128)(2,1)S(1)}, u32[]{:S(2)}, u32[]{:S(2)}) collective-permute-start(bf16[640,256]{1,0:T(8,128)(2,1)S(1)} %get-tuple-element.87), channel_id=1, source_target_pairs={{0,1},{1,0},{2,3},{3,2},{4,5},{5,4},{6,7},{7,6},{8,9},{9,8},{10,11... | collective-permute-start | bytes 983048 | tf_op jit(solution)/shard_map/ppermute | solution.py:43
  159.1 1.4 collective-permute-start.42
  160.5 7.2 %token_grads.1 = bf16[256,5120]{1,0:T(8,128)(2,1)} custom-call(s32[2]{0:T(128)S(1)} %pad_add_fusion.1.rank_ref, bf16[256,512]{1,0:T(8,128)(2,1)S(1)} %add_convert_fusion.refs_0_, bf16[256,512]{1,0:T(8,128)(2,1)S(1)} %add_convert_fusion.1.refs_1_, bf16[640,512]{1,0:T(8,128)(2,1)S(1)} %pad_maximum_fusion.1.refs_1_.refs_2_, bf16[640,512]{1,0:T(8,128)(2,1)S(1)} %copy-done.4, ...), custom_call_target="tpu_custom_call" | custom-call | flops 32000000000 | bytes 96000000 | tf_op jit(solution)/shard_map/token_grads/pallas_call | solution.py:400
  167.9 12.3 %collective-permute-done.41 = bf16[640,256]{1,0:T(8,128)(2,1)S(1)} collective-permute-done((bf16[640,256]{1,0:T(8,128)(2,1)S(1)}, bf16[640,256]{1,0:T(8,128)(2,1)S(1)}, u32[]{:S(2)}, u32[]{:S(2)}) %collective-permute-start.41) | collective-permute-done | bytes 327712 | tf_op jit(solution)/shard_map/ppermute | solution.py:43
  180.2 4.2 %collective-permute-done.42 = bf16[640,256]{1,0:T(8,128)(2,1)S(1)} collective-permute-done((bf16[640,256]{1,0:T(8,128)(2,1)S(1)}, bf16[640,256]{1,0:T(8,128)(2,1)S(1)}, u32[]{:S(2)}, u32[]{:S(2)}) %collective-permute-start.42) | collective-permute-done | bytes 327712 | tf_op jit(solution)/shard_map/ppermute | solution.py:43
  (128 shorter events, 14.9 us)
Async XLA Ops:
  2.1 16.5 %collective-permute-start = (bf16[640,512]{1,0:T(8,128)(2,1)S(1)}, bf16[640,512]{1,0:T(8,128)(2,1)S(1)}, u32[]{:S(2)}, u32[]{:S(2)}) collective-permute-start(bf16[640,512]{1,0:T(8,128)(2,1)S(1)} %pad_maximum_fusion.1.refs_1_.refs_2_), channel_id=1, source_target_pairs={{0,8},{4,12},{8,0},{12,4},{16,24},{20,28},{24,16},{28,20},{1,9},{5... | collective-permute-start | bytes 1966088 | tf_op jit(solution)/shard_map/ppermute | solution.py:43
  3.6 16.2 %collective-permute-start.1 = (bf16[640,512]{1,0:T(8,128)(2,1)S(1)}, bf16[640,512]{1,0:T(8,128)(2,1)S(1)}, u32[]{:S(2)}, u32[]{:S(2)}) collective-permute-start(bf16[640,512]{1,0:T(8,128)(2,1)S(1)} %pad_maximum_fusion.1.refs_1_.refs_2_), channel_id=1, source_target_pairs={{0,16},{4,20},{8,24},{12,28},{16,0},{20,4},{24,8},{28,12},{1,17},{... | collective-permute-start | bytes 1966088 | tf_op jit(solution)/shard_map/ppermute | solution.py:43
  5.1 23.7 %collective-permute-start.6 = (bf16[640,512]{1,0:T(8,128)(2,1)S(1)}, bf16[640,512]{1,0:T(8,128)(2,1)S(1)}, u32[]{:S(2)}, u32[]{:S(2)}) collective-permute-start(bf16[640,512]{1,0:T(8,128)(2,1)S(1)} %pad_maximum_fusion.1.refs_1_.refs_2_), channel_id=1, source_target_pairs={{0,4},{4,0},{8,12},{12,8},{16,20},{20,16},{24,28},{28,24},{1,5},{5... | collective-permute-start | bytes 1966088 | tf_op jit(solution)/shard_map/ppermute | solution.py:43
  5.2 60.5 %copy-start = (bf16[640,512]{1,0:T(8,128)(2,1)}, bf16[640,512]{1,0:T(8,128)(2,1)S(1)}, u32[]{:S(2)}) copy-start(bf16[640,512]{1,0:T(8,128)(2,1)S(1)} %pad_maximum_fusion.refs_1_.refs_12_) | copy-start | bytes 1966084
  19.9 8.4 %collective-permute-start.3 = (bf16[640,256]{1,0:T(8,128)(2,1)S(1)}, bf16[640,256]{1,0:T(8,128)(2,1)}, u32[]{:S(2)}, u32[]{:S(2)}) collective-permute-start(bf16[640,256]{1,0:T(8,128)(2,1)S(1)} %get-tuple-element.49), channel_id=1, source_target_pairs={{0,8},{4,12},{8,0},{12,4},{16,24},{20,28},{24,16},{28,20},{1,9},{5... | collective-permute-start | bytes 983048 | tf_op jit(solution)/shard_map/ppermute | solution.py:43
  20.5 8.2 %collective-permute-start.2 = (bf16[640,256]{1,0:T(8,128)(2,1)S(1)}, bf16[640,256]{1,0:T(8,128)(2,1)}, u32[]{:S(2)}, u32[]{:S(2)}) collective-permute-start(bf16[640,256]{1,0:T(8,128)(2,1)S(1)} %get-tuple-element.48), channel_id=1, source_target_pairs={{0,16},{4,20},{8,24},{12,28},{16,0},{20,4},{24,8},{28,12},{1,17},{... | collective-permute-start | bytes 983048 | tf_op jit(solution)/shard_map/ppermute | solution.py:43
  22.0 9.8 %collective-permute-start.7 = (bf16[640,512]{1,0:T(8,128)(2,1)S(1)}, bf16[640,512]{1,0:T(8,128)(2,1)}, u32[]{:S(2)}, u32[]{:S(2)}) collective-permute-start(bf16[640,512]{1,0:T(8,128)(2,1)S(1)} %collective-permute-done.near_ref.refs_2_.refs_3_), channel_id=1, source_target_pairs={{0,4},{4,0},{8,12},{12,8},{16,20},{20,16},{24,28},{28,24},{1,5},{5... | collective-permute-start | bytes 1966088 | tf_op jit(solution)/shard_map/ppermute | solution.py:43
  22.0 9.8 %collective-permute-start.8 = (bf16[640,512]{1,0:T(8,128)(2,1)S(1)}, bf16[640,512]{1,0:T(8,128)(2,1)}, u32[]{:S(2)}, u32[]{:S(2)}) collective-permute-start(bf16[640,512]{1,0:T(8,128)(2,1)S(1)} %collective-permute-done.1.far_ref.refs_3_.refs_4_), channel_id=1, source_target_pairs={{0,4},{4,0},{8,12},{12,8},{16,20},{20,16},{24,28},{28,24},{1,5},{5... | collective-permute-start | bytes 1966088 | tf_op jit(solution)/shard_map/ppermute | solution.py:43
  28.3 2.0 %collective-permute-start.10 = (bf16[640,256]{1,0:T(8,128)(2,1)}, bf16[640,256]{1,0:T(8,128)(2,1)}, u32[]{:S(2)}, u32[]{:S(2)}) collective-permute-start(bf16[640,256]{1,0:T(8,128)(2,1)} %collective-permute-done.3.refs_5_.refs_6_), channel_id=1, source_target_pairs={{0,4},{4,0},{8,12},{12,8},{16,20},{20,16},{24,28},{28,24},{1,5},{5... | collective-permute-start | bytes 983048 | tf_op jit(solution)/shard_map/ppermute | solution.py:43
  28.6 3.2 %collective-permute-start.9 = (bf16[640,256]{1,0:T(8,128)(2,1)}, bf16[640,256]{1,0:T(8,128)(2,1)}, u32[]{:S(2)}, u32[]{:S(2)}) collective-permute-start(bf16[640,256]{1,0:T(8,128)(2,1)} %collective-permute-done.2.refs_4_.refs_5_), channel_id=1, source_target_pairs={{0,4},{4,0},{8,12},{12,8},{16,20},{20,16},{24,28},{28,24},{1,5},{5... | collective-permute-start | bytes 983048 | tf_op jit(solution)/shard_map/ppermute | solution.py:43
  28.9 22.2 %collective-permute-start.4 = (bf16[640,512]{1,0:T(8,128)(2,1)S(1)}, bf16[640,512]{1,0:T(8,128)(2,1)}, u32[]{:S(2)}, u32[]{:S(2)}) collective-permute-start(bf16[640,512]{1,0:T(8,128)(2,1)S(1)} %pad_maximum_fusion.refs_1_.refs_12_), channel_id=1, source_target_pairs={{0,8},{4,12},{8,0},{12,4},{16,24},{20,28},{24,16},{28,20},{1,9},{5... | collective-permute-start | bytes 1966088 | tf_op jit(solution)/shard_map/ppermute | solution.py:43
  30.3 20.8 %collective-permute-start.5 = (bf16[640,512]{1,0:T(8,128)(2,1)S(1)}, bf16[640,512]{1,0:T(8,128)(2,1)}, u32[]{:S(2)}, u32[]{:S(2)}) collective-permute-start(bf16[640,512]{1,0:T(8,128)(2,1)S(1)} %pad_maximum_fusion.refs_1_.refs_12_), channel_id=1, source_target_pairs={{0,16},{4,20},{8,24},{12,28},{16,0},{20,4},{24,8},{28,12},{1,17},{... | collective-permute-start | bytes 1966088 | tf_op jit(solution)/shard_map/ppermute | solution.py:43
  36.1 16.6 %copy-start.23 = (bf16[256,512]{1,0:T(8,128)(2,1)}, bf16[256,512]{1,0:T(8,128)(2,1)S(1)}, u32[]{:S(2)}) copy-start(bf16[256,512]{1,0:T(8,128)(2,1)S(1)} %project.2.refs_0_.refs_1_) | copy-start | bytes 786436
  36.1 15.0 %collective-permute-start.12 = (bf16[640,512]{1,0:T(8,128)(2,1)S(1)}, bf16[640,512]{1,0:T(8,128)(2,1)S(1)}, u32[]{:S(2)}, u32[]{:S(2)}) collective-permute-start(bf16[640,512]{1,0:T(8,128)(2,1)S(1)} %pad_maximum_fusion.refs_1_.refs_12_), channel_id=1, source_target_pairs={{0,4},{4,0},{8,12},{12,8},{16,20},{20,16},{24,28},{28,24},{1,5},{5... | collective-permute-start | bytes 1966088 | tf_op jit(solution)/shard_map/ppermute | solution.py:43
  36.2 10.7 %collective-permute-start.11 = (bf16[256,512]{1,0:T(8,128)(2,1)S(1)}, bf16[256,512]{1,0:T(8,128)(2,1)}, u32[]{:S(2)}, u32[]{:S(2)}) collective-permute-start(bf16[256,512]{1,0:T(8,128)(2,1)S(1)} %project.2.refs_0_.refs_1_), channel_id=1, source_target_pairs={{0,1},{1,2},{2,3},{4,5},{5,6},{6,7},{8,9},{9,10},{10,11},{12,13},{... | collective-permute-start | bytes 786440 | tf_op jit(solution)/shard_map/ppermute | solution.py:49
  39.7 15.1 %copy-start.27 = (s32[1,4]{1,0:T(1,128)S(1)}, s32[1,4]{1,0:T(1,128)}, u32[]{:S(2)}) copy-start(s32[1,4]{1,0:T(1,128)} %param.9) | copy-start | bytes 52
  46.9 9.2 %collective-permute-start.15 = (bf16[256,512]{1,0:T(8,128)(2,1)}, bf16[256,512]{1,0:T(8,128)(2,1)}, u32[]{:S(2)}, u32[]{:S(2)}) collective-permute-start(bf16[256,512]{1,0:T(8,128)(2,1)} %collective-permute-done.11.refs_2_.refs_3_), channel_id=1, source_target_pairs={{1,2},{2,3},{5,6},{6,7},{9,10},{10,11},{13,14},{14,15},{17,18},{18... | collective-permute-start | bytes 786440 | tf_op jit(solution)/shard_map/ppermute | solution.py:49
  51.1 14.6 %copy-start.9 = (bf16[640,512]{1,0:T(8,128)(2,1)}, bf16[640,512]{1,0:T(8,128)(2,1)S(1)}, u32[]{:S(2)}) copy-start(bf16[640,512]{1,0:T(8,128)(2,1)S(1)} %collective-permute-done.12.refs_6_.refs_17_) | copy-start | bytes 1966084
  51.1 14.6 %collective-permute-start.16 = (bf16[640,512]{1,0:T(8,128)(2,1)}, bf16[640,512]{1,0:T(8,128)(2,1)S(1)}, u32[]{:S(2)}, u32[]{:S(2)}) collective-permute-start(bf16[640,512]{1,0:T(8,128)(2,1)} %collective-permute-done.4.near_ref.refs_2_.refs_13_), channel_id=1, source_target_pairs={{0,4},{4,0},{8,12},{12,8},{16,20},{20,16},{24,28},{28,24},{1,5},{5... | collective-permute-start | bytes 1966088 | tf_op jit(solution)/shard_map/ppermute | solution.py:43
  52.7 13.0 %collective-permute-start.17 = (bf16[640,512]{1,0:T(8,128)(2,1)}, bf16[640,512]{1,0:T(8,128)(2,1)S(1)}, u32[]{:S(2)}, u32[]{:S(2)}) collective-permute-start(bf16[640,512]{1,0:T(8,128)(2,1)} %collective-permute-done.5.far_ref.refs_3_.refs_14_), channel_id=1, source_target_pairs={{0,4},{4,0},{8,12},{12,8},{16,20},{20,16},{24,28},{28,24},{1,5},{5... | collective-permute-start | bytes 1966088 | tf_op jit(solution)/shard_map/ppermute | solution.py:43
  53.1 9.8 %collective-permute-start.13 = (bf16[640,256]{1,0:T(8,128)(2,1)S(1)}, bf16[640,256]{1,0:T(8,128)(2,1)S(1)}, u32[]{:S(2)}, u32[]{:S(2)}) collective-permute-start(bf16[640,256]{1,0:T(8,128)(2,1)S(1)} %get-tuple-element.54), channel_id=1, source_target_pairs={{0,16},{4,20},{8,24},{12,28},{16,0},{20,4},{24,8},{28,12},{1,17},{... | collective-permute-start | bytes 983048 | tf_op jit(solution)/shard_map/ppermute | solution.py:43
  53.6 9.5 %collective-permute-start.14 = (bf16[640,256]{1,0:T(8,128)(2,1)S(1)}, bf16[640,256]{1,0:T(8,128)(2,1)S(1)}, u32[]{:S(2)}, u32[]{:S(2)}) collective-permute-start(bf16[640,256]{1,0:T(8,128)(2,1)S(1)} %get-tuple-element.55), channel_id=1, source_target_pairs={{0,8},{4,12},{8,0},{12,4},{16,24},{20,28},{24,16},{28,20},{1,9},{5... | collective-permute-start | bytes 983048 | tf_op jit(solution)/shard_map/ppermute | solution.py:43
  63.1 2.5 %collective-permute-start.18 = (bf16[640,256]{1,0:T(8,128)(2,1)S(1)}, bf16[640,256]{1,0:T(8,128)(2,1)S(1)}, u32[]{:S(2)}, u32[]{:S(2)}) collective-permute-start(bf16[640,256]{1,0:T(8,128)(2,1)S(1)} %collective-permute-done.13.refs_4_.refs_15_), channel_id=1, source_target_pairs={{0,4},{4,0},{8,12},{12,8},{16,20},{20,16},{24,28},{28,24},{1,5},{5... | collective-permute-start | bytes 983048 | tf_op jit(solution)/shard_map/ppermute | solution.py:43
  63.1 2.6 %collective-permute-start.19 = (bf16[640,256]{1,0:T(8,128)(2,1)S(1)}, bf16[640,256]{1,0:T(8,128)(2,1)S(1)}, u32[]{:S(2)}, u32[]{:S(2)}) collective-permute-start(bf16[640,256]{1,0:T(8,128)(2,1)S(1)} %collective-permute-done.14.refs_5_.refs_16_), channel_id=1, source_target_pairs={{0,4},{4,0},{8,12},{12,8},{16,20},{20,16},{24,28},{28,24},{1,5},{5... | collective-permute-start | bytes 983048 | tf_op jit(solution)/shard_map/ppermute | solution.py:43
  64.3 11.9 %collective-permute-start.20 = (bf16[256,512]{1,0:T(8,128)(2,1)}, bf16[256,512]{1,0:T(8,128)(2,1)}, u32[]{:S(2)}, u32[]{:S(2)}) collective-permute-start(bf16[256,512]{1,0:T(8,128)(2,1)} %collective-permute-done.15.refs_4_.refs_5_), channel_id=1, source_target_pairs={{2,3},{6,7},{10,11},{14,15},{18,19},{22,23},{26,27},{30,31}} | collective-permute-start | bytes 786440 | tf_op jit(solution)/shard_map/ppermute | solution.py:49
  70.3 12.9 %collective-permute-start.21 = (bf16[256,512]{1,0:T(8,128)(2,1)S(1)}, bf16[256,512]{1,0:T(8,128)(2,1)}, u32[]{:S(2)}, u32[]{:S(2)}) collective-permute-start(bf16[256,512]{1,0:T(8,128)(2,1)S(1)} %project.3.refs_0_.refs_1_), channel_id=1, source_target_pairs={{0,2},{1,3},{4,6},{5,7},{8,10},{9,11},{12,14},{13,15},{16,18},{17,... | collective-permute-start | bytes 786440 | tf_op jit(solution)/shard_map/ppermute | solution.py:49
  72.6 36.7 %all-to-all-start = ((bf16[8,256,640]{2,1,0:T(8,128)(2,1)}), bf16[8,256,640]{2,1,0:T(8,128)(2,1)S(1)}, u32[]{:S(2)}, u32[]{:S(2)}) async-start(bf16[8,256,640]{2,1,0:T(8,128)(2,1)} %split_columns.1.refs_0_), calls=%async_computation | async-start | bytes 5242880 | tf_op jit(solution)/shard_map/all_to_all | solution.py:501
  83.2 7.4 %collective-permute-start.22 = (bf16[256,512]{1,0:T(8,128)(2,1)}, bf16[256,512]{1,0:T(8,128)(2,1)S(1)}, u32[]{:S(2)}, u32[]{:S(2)}) collective-permute-start(bf16[256,512]{1,0:T(8,128)(2,1)} %get-tuple-element.60), channel_id=1, source_target_pairs={{3,2},{7,6},{11,10},{15,14},{19,18},{23,22},{27,26},{31,30}} | collective-permute-start | bytes 786440 | tf_op jit(solution)/shard_map/ppermute | solution.py:49
  83.9 11.1 %collective-permute-start.23 = (bf16[256,512]{1,0:T(8,128)(2,1)S(1)}, bf16[256,512]{1,0:T(8,128)(2,1)S(1)}, u32[]{:S(2)}, u32[]{:S(2)}) collective-permute-start(bf16[256,512]{1,0:T(8,128)(2,1)S(1)} %project.3.refs_0_.refs_1_), channel_id=1, source_target_pairs={{0,1},{1,2},{2,3},{4,5},{5,6},{6,7},{8,9},{9,10},{10,11},{12,13},{... | collective-permute-start | bytes 786440 | tf_op jit(solution)/shard_map/ppermute | solution.py:49
  86.3 8.7 %collective-permute-start.24 = (bf16[256,512]{1,0:T(8,128)(2,1)}, bf16[256,512]{1,0:T(8,128)(2,1)S(1)}, u32[]{:S(2)}, u32[]{:S(2)}) collective-permute-start(bf16[256,512]{1,0:T(8,128)(2,1)} %collective-permute-done.21.refs_4_.refs_5_), channel_id=1, source_target_pairs={{2,3},{6,7},{10,11},{14,15},{18,19},{22,23},{26,27},{30,31}} | collective-permute-start | bytes 786440 | tf_op jit(solution)/shard_map/ppermute | solution.py:49
  87.0 19.9 %collective-permute-start.25 = (bf16[256,512]{1,0:T(8,128)(2,1)}, bf16[256,512]{1,0:T(8,128)(2,1)}, u32[]{:S(2)}, u32[]{:S(2)}) collective-permute-start(bf16[256,512]{1,0:T(8,128)(2,1)} %get-tuple-element.68), channel_id=1, source_target_pairs={{1,0},{2,1},{3,2},{5,4},{6,5},{7,6},{9,8},{10,9},{11,10},{13,12},{... | collective-permute-start | bytes 786440 | tf_op jit(solution)/shard_map/ppermute | solution.py:49
  92.4 14.5 %collective-permute-start.26 = (bf16[256,512]{1,0:T(8,128)(2,1)}, bf16[256,512]{1,0:T(8,128)(2,1)}, u32[]{:S(2)}, u32[]{:S(2)}) collective-permute-start(bf16[256,512]{1,0:T(8,128)(2,1)} %add_convert_fusion.3), channel_id=1, source_target_pairs={{2,0},{3,1},{6,4},{7,5},{10,8},{11,9},{14,12},{15,13},{18,16},{19,... | collective-permute-start | bytes 786440 | tf_op jit(solution)/shard_map/ppermute | solution.py:49
  108.0 9.1 %collective-permute-start.37 = (bf16[256,512]{1,0:T(8,128)(2,1)S(1)}, bf16[256,512]{1,0:T(8,128)(2,1)}, u32[]{:S(2)}, u32[]{:S(2)}) collective-permute-start(bf16[256,512]{1,0:T(8,128)(2,1)S(1)} %add_convert_fusion.refs_0_), channel_id=1, source_target_pairs={{0,8},{4,12},{8,0},{12,4},{16,24},{20,28},{24,16},{28,20},{1,9},{5... | collective-permute-start | bytes 786440 | tf_op jit(solution)/shard_map/ppermute | solution.py:43
  109.3 11.3 %collective-permute-start.27 = (bf16[256,512]{1,0:T(8,128)(2,1)}, bf16[256,512]{1,0:T(8,128)(2,1)S(1)}, u32[]{:S(2)}, u32[]{:S(2)}) collective-permute-start(bf16[256,512]{1,0:T(8,128)(2,1)} %get-tuple-element.71), channel_id=1, source_target_pairs={{1,0},{2,1},{3,2},{5,4},{6,5},{7,6},{9,8},{10,9},{11,10},{13,12},{... | collective-permute-start | bytes 786440 | tf_op jit(solution)/shard_map/ppermute | solution.py:49
  116.5 5.1 %collective-permute-start.28 = (bf16[256,512]{1,0:T(8,128)(2,1)}, bf16[256,512]{1,0:T(8,128)(2,1)S(1)}, u32[]{:S(2)}, u32[]{:S(2)}) collective-permute-start(bf16[256,512]{1,0:T(8,128)(2,1)} %get-tuple-element.75), channel_id=1, source_target_pairs={{3,2},{7,6},{11,10},{15,14},{19,18},{23,22},{27,26},{31,30}} | collective-permute-start | bytes 786440 | tf_op jit(solution)/shard_map/ppermute | solution.py:49
  120.7 11.0 %collective-permute-start.38 = (bf16[512,512]{1,0:T(8,128)(2,1)S(1)}, bf16[512,512]{1,0:T(8,128)(2,1)S(1)}, u32[]{:S(2)}, u32[]{:S(2)}) collective-permute-start(bf16[512,512]{1,0:T(8,128)(2,1)S(1)} %pad_maximum_fusion.2), channel_id=1, source_target_pairs={{0,16},{4,20},{8,24},{12,28},{16,0},{20,4},{24,8},{28,12},{1,17},{... | collective-permute-start | bytes 1572872 | tf_op jit(solution)/shard_map/ppermute | solution.py:43
  122.7 10.0 %collective-permute-start.29 = (bf16[256,512]{1,0:T(8,128)(2,1)S(1)}, bf16[256,512]{1,0:T(8,128)(2,1)S(1)}, u32[]{:S(2)}, u32[]{:S(2)}) collective-permute-start(bf16[256,512]{1,0:T(8,128)(2,1)S(1)} %add_convert_fusion.2), channel_id=1, source_target_pairs={{2,0},{3,1},{6,4},{7,5},{10,8},{11,9},{14,12},{15,13},{18,16},{19,... | collective-permute-start | bytes 786440 | tf_op jit(solution)/shard_map/ppermute | solution.py:49
  132.7 15.4 %collective-permute-start.39 = (bf16[1024,512]{1,0:T(8,128)(2,1)S(1)}, bf16[1024,512]{1,0:T(8,128)(2,1)S(1)}, u32[]{:S(2)}, u32[]{:S(2)}) collective-permute-start(bf16[1024,512]{1,0:T(8,128)(2,1)S(1)} %constant_dynamic-update-slice_fusion.refs_1_), channel_id=1, source_target_pairs={{0,4},{4,0},{8,12},{12,8},{16,20},{20,16},{24,28},{28,24},{1,5},{5... | collective-permute-start | bytes 3145736 | tf_op jit(solution)/shard_map/ppermute | solution.py:43
  132.8 9.2 %collective-permute-start.31 = (bf16[256,512]{1,0:T(8,128)(2,1)S(1)}, bf16[256,512]{1,0:T(8,128)(2,1)S(1)}, u32[]{:S(2)}, u32[]{:S(2)}) collective-permute-start(bf16[256,512]{1,0:T(8,128)(2,1)S(1)} %add_convert_fusion.1.refs_1_), channel_id=1, source_target_pairs={{0,8},{4,12},{8,0},{12,4},{16,24},{20,28},{24,16},{28,20},{1,9},{5... | collective-permute-start | bytes 786440 | tf_op jit(solution)/shard_map/ppermute | solution.py:43
  133.5 14.1 %collective-permute-start.33 = (bf16[256,512]{1,0:T(8,128)(2,1)S(1)}, bf16[256,512]{1,0:T(8,128)(2,1)S(1)}, u32[]{:S(2)}, u32[]{:S(2)}) collective-permute-start(bf16[256,512]{1,0:T(8,128)(2,1)S(1)} %add_convert_fusion.1.refs_1_), channel_id=1, source_target_pairs={{0,16},{4,20},{8,24},{12,28},{16,0},{20,4},{24,8},{28,12},{1,17},{... | collective-permute-start | bytes 786440 | tf_op jit(solution)/shard_map/ppermute | solution.py:43
  135.2 12.4 %collective-permute-start.35 = (bf16[256,512]{1,0:T(8,128)(2,1)S(1)}, bf16[256,512]{1,0:T(8,128)(2,1)S(1)}, u32[]{:S(2)}, u32[]{:S(2)}) collective-permute-start(bf16[256,512]{1,0:T(8,128)(2,1)S(1)} %add_convert_fusion.1.refs_1_), channel_id=1, source_target_pairs={{0,24},{4,28},{8,16},{12,20},{16,8},{20,12},{24,0},{28,4},{1,25},{... | collective-permute-start | bytes 786440 | tf_op jit(solution)/shard_map/ppermute | solution.py:43
  136.3 14.0 %collective-permute-start.30 = (bf16[256,512]{1,0:T(8,128)(2,1)S(1)}, bf16[256,512]{1,0:T(8,128)(2,1)S(1)}, u32[]{:S(2)}, u32[]{:S(2)}) collective-permute-start(bf16[256,512]{1,0:T(8,128)(2,1)S(1)} %add_convert_fusion.1.refs_1_), channel_id=1, source_target_pairs={{0,4},{4,0},{8,12},{12,8},{16,20},{20,16},{24,28},{28,24},{1,5},{5... | collective-permute-start | bytes 786440 | tf_op jit(solution)/shard_map/ppermute | solution.py:43
  142.0 8.4 %collective-permute-start.32 = (bf16[256,512]{1,0:T(8,128)(2,1)S(1)}, bf16[256,512]{1,0:T(8,128)(2,1)S(1)}, u32[]{:S(2)}, u32[]{:S(2)}) collective-permute-start(bf16[256,512]{1,0:T(8,128)(2,1)S(1)} %collective-permute-done.31.refs_3_), channel_id=1, source_target_pairs={{0,4},{4,0},{8,12},{12,8},{16,20},{20,16},{24,28},{28,24},{1,5},{5... | collective-permute-start | bytes 786440 | tf_op jit(solution)/shard_map/ppermute | solution.py:43
  147.6 2.8 %collective-permute-start.34 = (bf16[256,512]{1,0:T(8,128)(2,1)S(1)}, bf16[256,512]{1,0:T(8,128)(2,1)S(1)}, u32[]{:S(2)}, u32[]{:S(2)}) collective-permute-start(bf16[256,512]{1,0:T(8,128)(2,1)S(1)} %collective-permute-done.33.refs_5_), channel_id=1, source_target_pairs={{0,4},{4,0},{8,12},{12,8},{16,20},{20,16},{24,28},{28,24},{1,5},{5... | collective-permute-start | bytes 786440 | tf_op jit(solution)/shard_map/ppermute | solution.py:43
  147.6 2.8 %collective-permute-start.36 = (bf16[256,512]{1,0:T(8,128)(2,1)S(1)}, bf16[256,512]{1,0:T(8,128)(2,1)S(1)}, u32[]{:S(2)}, u32[]{:S(2)}) collective-permute-start(bf16[256,512]{1,0:T(8,128)(2,1)S(1)} %collective-permute-done.35.refs_7_), channel_id=1, source_target_pairs={{0,4},{4,0},{8,12},{12,8},{16,20},{20,16},{24,28},{28,24},{1,5},{5... | collective-permute-start | bytes 786440 | tf_op jit(solution)/shard_map/ppermute | solution.py:43
  152.7 15.1 %collective-permute-start.40 = (bf16[640,256]{1,0:T(8,128)(2,1)S(1)}, bf16[640,256]{1,0:T(8,128)(2,1)S(1)}, u32[]{:S(2)}, u32[]{:S(2)}) collective-permute-start(bf16[640,256]{1,0:T(8,128)(2,1)S(1)} %get-tuple-element.86), channel_id=1, source_target_pairs={{0,2},{1,3},{2,0},{3,1},{4,6},{5,7},{6,4},{7,5},{8,10},{9,11},{10,... | collective-permute-start | bytes 983048 | tf_op jit(solution)/shard_map/ppermute | solution.py:43
  152.8 27.4 %collective-permute-start.41 = (bf16[640,256]{1,0:T(8,128)(2,1)S(1)}, bf16[640,256]{1,0:T(8,128)(2,1)S(1)}, u32[]{:S(2)}, u32[]{:S(2)}) collective-permute-start(bf16[640,256]{1,0:T(8,128)(2,1)S(1)} %get-tuple-element.87), channel_id=1, source_target_pairs={{0,1},{1,0},{2,3},{3,2},{4,5},{5,4},{6,7},{7,6},{8,9},{9,8},{10,11... | collective-permute-start | bytes 983048 | tf_op jit(solution)/shard_map/ppermute | solution.py:43
  159.1 25.4 %collective-permute-start.42 = (bf16[640,256]{1,0:T(8,128)(2,1)S(1)}, bf16[640,256]{1,0:T(8,128)(2,1)S(1)}, u32[]{:S(2)}, u32[]{:S(2)}) collective-permute-start(bf16[640,256]{1,0:T(8,128)(2,1)S(1)} %get-tuple-element.88), channel_id=1, source_target_pairs={{0,3},{1,2},{2,1},{3,0},{4,7},{5,6},{6,5},{7,4},{8,11},{9,10},{10,... | collective-permute-start | bytes 983048 | tf_op jit(solution)/shard_map/ppermute | solution.py:43
  (26 other events, 215.9 us)
